TPU v7x, 32 devices: a whole 2x2x4 slice. The times are simulated.
32 devices in a mesh: sp: 16 (over z, x, core), tp: 2 (over y).
Axes of the slice: x: 2, y: 2, z: 4, core: 2. Of those that a mesh axis runs over, the one named last changes fastest.
Arguments:
- tokens: bfloat16 [3072, 1024], P('sp'), may hold values from -6 to 6
- segment_ids: int32 [3072], P('sp'), may hold values from 0 to 1, as said below
- lead_hours: float32 [2], replicated, may hold values from 0.06 to 1.68
- qkv_weight: bfloat16 [3, 1024, 1024], P(None, 'sp', 'tp'), may hold values from -0.25 to 0.25
- qv_bias: bfloat16 [2, 16, 64], P(None, 'tp', 'sp'), may hold values from -3 to 3
- proj_weight: bfloat16 [1024, 1024], P('tp', 'sp'), may hold values from -1.5 to 1.5
- proj_bias: bfloat16 [1024], P('sp'), may hold values from -2 to 2
- up_weight: bfloat16 [1024, 4096], P('sp', 'tp'), may hold values from -0.1875 to 0.1875
- up_bias: bfloat16 [64, 64], P('tp', 'sp'), may hold values from -2 to 2
- down_weight: bfloat16 [4096, 1024], P('tp', 'sp'), may hold values from -0.125 to 0.125
- down_bias: bfloat16 [1024], P('sp'), may hold values from -2 to 2
- norm1_gain: bfloat16 [1024], P('sp'), may hold values from 0.5 to 1.5
- norm1_bias: bfloat16 [1024], P('sp'), may hold values from -2 to 2
- norm2_gain: bfloat16 [1024], P('sp'), may hold values from 0.5 to 1.5
- norm2_bias: bfloat16 [1024], P('sp'), may hold values from -2 to 2
- lead_weight: bfloat16 [1024], P('sp'), may hold values from -3 to 3
- lead_bias: bfloat16 [1024], P('sp'), may hold values from -3 to 3
- out_grad: bfloat16 [3072, 1024], P('sp'), may hold values from -6 to 6
Outputs:
- block_out: bfloat16 [3072, 1024], P('sp')
- input_grad: float32 [3072, 1024], P('sp')
- grad_qkv_weight: float32 [3, 1024, 1024], P(None, 'sp', 'tp')
- grad_qv_bias: float32 [2, 16, 64], P(None, 'tp', 'sp')
- grad_proj_weight: float32 [1024, 1024], P('tp', 'sp')
- grad_proj_bias: float32 [1024], P('sp')
- grad_up_weight: float32 [1024, 4096], P('sp', 'tp')
- grad_up_bias: float32 [64, 64], P('tp', 'sp')
- grad_down_weight: float32 [4096, 1024], P('tp', 'sp')
- grad_down_bias: float32 [1024], P('sp')
- grad_norm1_gain: float32 [1024], P('sp')
- grad_norm1_bias: float32 [1024], P('sp')
- grad_norm2_gain: float32 [1024], P('sp')
- grad_norm2_bias: float32 [1024], P('sp')
- grad_lead_weight: float32 [1024], P('sp')
- grad_lead_bias: float32 [1024], P('sp')
Inputs may be any that keep to these rules, and one draw needn't show every extreme that they name: `segment_ids`: sample 0 holds the first and the last patch: two runs at the two ends of the sequence. Samples 1 to 1 follow in order in between, each one run of 576 to 1152 patches, one of them exactly 1152; sample 0 holds all other patches.
All inputs are finite; a program needn't handle non-finite values.
Results may differ from a plain program's by a relative error of at most 0.025.
Values may be sent and summed in bfloat16 or wider, within the bound.
No kernel may reach another device: no remote copies, remote signals or barrier semaphores. Data moves between devices by JAX's collectives and lax.ppermute only.
A program may use at most 128 MiB of HBM per device.

v0:
```python
import jax
import jax.numpy as jnp
from jax import lax
from jax.sharding import PartitionSpec as P

HD = 64


NEGATIVE = -1e30
EPSILON = 1e-05


def shifted(block, axis, distance):
    devices = range(lax.axis_size(axis))
    route = [((i - distance) % len(devices), i) for i in devices]
    return lax.ppermute(block, axis, route)


def layer_norm(values, gain_vec, shift_vec):
    center = values - jnp.mean(values, axis=-1, keepdims=True)
    spread = jnp.mean(center * center, axis=-1, keepdims=True)
    return center * lax.rsqrt(spread + EPSILON) * gain_vec + shift_vec


def gelu_exact(values):
    return jax.nn.gelu(values, approximate=False)


def split_heads(matrix):
    return matrix.reshape(matrix.shape[0], matrix.shape[1] // HD, HD)


def head_sum(values):
    return lax.psum(values.astype(jnp.bfloat16), "tp").astype(jnp.float32)


def first_half(full_set, embedded):
    normed_one = layer_norm(
        embedded, full_set[8].astype(jnp.float32), full_set[9].astype(jnp.float32)
    ).astype(jnp.bfloat16)
    stacked = jnp.einsum("td,cde->cte", normed_one, full_set[0], preferred_element_type=jnp.float32)
    local_width = stacked.shape[2]
    bias_rows = full_set[1].reshape(2, local_width).astype(jnp.float32)
    query_rows = (stacked[0] + bias_rows[0]).astype(jnp.bfloat16)
    key_rows = stacked[1].astype(jnp.bfloat16)
    value_rows = (stacked[2] + bias_rows[1]).astype(jnp.bfloat16)
    return (normed_one, query_rows, key_rows, value_rows)


def second_half(full_set, middle):
    normed_two = layer_norm(
        middle, full_set[10].astype(jnp.float32), full_set[11].astype(jnp.float32)
    ).astype(jnp.bfloat16)
    hidden = jnp.dot(normed_two, full_set[4], preferred_element_type=jnp.float32) + full_set[
        5
    ].reshape(-1).astype(jnp.float32)
    return (normed_two, hidden)


def block_grads(
    query_block, dout_block, log_total, grad_delta, query_seg, key_block, value_block, key_seg
):
    score_scale = HD ** (-0.5)
    query_heads = split_heads(query_block)
    dout_heads = split_heads(dout_block)
    key_heads = split_heads(key_block)
    value_heads = split_heads(value_block)
    same_seg = (query_seg[:, None] == key_seg[None, :])[None]
    scores = (
        jnp.einsum("qhd,khd->hqk", query_heads, key_heads, preferred_element_type=jnp.float32)
        * score_scale
    )
    scores = jnp.where(same_seg, scores, NEGATIVE)
    attn_prob = jnp.where(same_seg, jnp.exp(scores - log_total[:, :, None]), 0.0)
    grad_prob = jnp.einsum(
        "qhd,khd->hqk", dout_heads, value_heads, preferred_element_type=jnp.float32
    )
    grad_score = (attn_prob * (grad_prob - grad_delta[:, :, None])).astype(jnp.bfloat16)
    grad_query = (
        jnp.einsum("hqk,khd->qhd", grad_score, key_heads, preferred_element_type=jnp.float32)
        * score_scale
    )
    grad_key = (
        jnp.einsum("hqk,qhd->khd", grad_score, query_heads, preferred_element_type=jnp.float32)
        * score_scale
    )
    grad_value = jnp.einsum(
        "hqk,qhd->khd",
        attn_prob.astype(jnp.bfloat16),
        dout_heads,
        preferred_element_type=jnp.float32,
    )
    return (
        grad_query.reshape(query_block.shape),
        grad_key.reshape(key_block.shape),
        grad_value.reshape(key_block.shape),
    )


def per_device(
    tokens,
    segment_ids,
    lead_hours,
    qkv_weight,
    qv_bias,
    proj_weight,
    proj_bias,
    up_weight,
    up_bias,
    down_weight,
    down_bias,
    norm1_gain,
    norm1_bias,
    norm2_gain,
    norm2_bias,
    lead_weight,
    lead_bias,
    out_grad,
):
    full_set = (
        lax.all_gather(qkv_weight, "sp", axis=1, tiled=True),
        lax.all_gather(qv_bias, "sp", axis=2, tiled=True),
        lax.all_gather(proj_weight, "sp", axis=1, tiled=True),
        lax.all_gather(proj_bias, "sp", axis=0, tiled=True),
        lax.all_gather(up_weight, "sp", axis=0, tiled=True),
        lax.all_gather(up_bias, "sp", axis=1, tiled=True),
        lax.all_gather(down_weight, "sp", axis=1, tiled=True),
        lax.all_gather(down_bias, "sp", axis=0, tiled=True),
        lax.all_gather(norm1_gain, "sp", axis=0, tiled=True),
        lax.all_gather(norm1_bias, "sp", axis=0, tiled=True),
        lax.all_gather(norm2_gain, "sp", axis=0, tiled=True),
        lax.all_gather(norm2_bias, "sp", axis=0, tiled=True),
        lax.all_gather(lead_weight, "sp", axis=0, tiled=True),
        lax.all_gather(lead_bias, "sp", axis=0, tiled=True),
    )
    seg_table = lax.all_gather(segment_ids, "sp", axis=0, tiled=True)
    local_rows = tokens.shape[0]
    cycle_size = lax.axis_size("sp")
    my_rank = lax.axis_index("sp")
    choose = segment_ids[:, None] == jnp.arange(lead_hours.shape[0], dtype=jnp.int32)[None, :]
    lead_time = jnp.sum(jnp.where(choose, lead_hours[None, :], 0.0), axis=1)
    embedded = (
        tokens.astype(jnp.float32)
        + lead_time[:, None] * full_set[12].astype(jnp.float32)
        + full_set[13].astype(jnp.float32)
    )
    normed_one, query_rows, key_rows, value_rows = first_half(full_set, embedded)
    local_width = query_rows.shape[1]
    local_heads = local_width // HD
    score_scale = HD ** (-0.5)
    query_heads = split_heads(query_rows)
    pair_rows = jnp.stack([key_rows, value_rows], axis=1)
    fold_init = (
        jnp.full((local_heads, local_rows), NEGATIVE, jnp.float32),
        jnp.zeros((local_heads, local_rows), jnp.float32),
        jnp.zeros((local_rows, local_heads, HD), jnp.float32),
    )
    key_piece = lax.all_gather(pair_rows, "sp", axis=0, tiled=True)
    piece_rows = key_piece.shape[0]
    step_rows = 512

    def key_step(block_index, inner_state):
        row_top, totals, weighted = inner_state
        key_block = lax.dynamic_slice_in_dim(key_piece, block_index * step_rows, step_rows, 0)
        key_seg = lax.dynamic_slice_in_dim(seg_table, block_index * step_rows, step_rows, 0)
        same_seg = (segment_ids[:, None] == key_seg[None, :])[None]
        scores = (
            jnp.einsum(
                "qhd,khd->hqk",
                query_heads,
                key_block[:, 0].reshape(step_rows, local_heads, HD),
                preferred_element_type=jnp.float32,
            )
            * score_scale
        )
        scores = jnp.where(same_seg, scores, NEGATIVE)
        new_top = jnp.maximum(row_top, jnp.max(scores, axis=2))
        attn_prob = jnp.where(same_seg, jnp.exp(scores - new_top[:, :, None]), 0.0)
        rescale = jnp.exp(row_top - new_top)
        totals = totals * rescale + jnp.sum(attn_prob, axis=2)
        weighted = weighted * jnp.transpose(rescale)[:, :, None] + jnp.einsum(
            "hqk,khd->qhd",
            attn_prob.astype(jnp.bfloat16),
            key_block[:, 1].reshape(step_rows, local_heads, HD),
            preferred_element_type=jnp.float32,
        )
        return (new_top, totals, weighted)

    row_top, totals, weighted = lax.fori_loop(0, piece_rows // step_rows, key_step, fold_init)
    attn_full = (weighted / jnp.transpose(totals)[:, :, None]).reshape(local_rows, local_width)
    log_total = row_top + jnp.log(totals)
    attn_out = attn_full.astype(jnp.bfloat16)
    branch = head_sum(
        jnp.dot(attn_out, full_set[2], preferred_element_type=jnp.float32)
    ) + full_set[3].astype(jnp.float32)
    middle = embedded + branch
    normed_two, hidden = second_half(full_set, middle)
    active = gelu_exact(hidden).astype(jnp.bfloat16)
    block_out = middle + (
        head_sum(jnp.dot(active, full_set[6], preferred_element_type=jnp.float32))
        + full_set[7].astype(jnp.float32)
    )
    back_set = (
        lax.all_gather(qkv_weight, "sp", axis=1, tiled=True),
        lax.all_gather(qv_bias, "sp", axis=2, tiled=True),
        lax.all_gather(proj_weight, "sp", axis=1, tiled=True),
        lax.all_gather(proj_bias, "sp", axis=0, tiled=True),
        lax.all_gather(up_weight, "sp", axis=0, tiled=True),
        lax.all_gather(up_bias, "sp", axis=1, tiled=True),
        lax.all_gather(down_weight, "sp", axis=1, tiled=True),
        lax.all_gather(down_bias, "sp", axis=0, tiled=True),
        lax.all_gather(norm1_gain, "sp", axis=0, tiled=True),
        lax.all_gather(norm1_bias, "sp", axis=0, tiled=True),
        lax.all_gather(norm2_gain, "sp", axis=0, tiled=True),
        lax.all_gather(norm2_bias, "sp", axis=0, tiled=True),
        lax.all_gather(lead_weight, "sp", axis=0, tiled=True),
        lax.all_gather(lead_bias, "sp", axis=0, tiled=True),
    )
    normed_two, hidden = second_half(back_set, middle)
    active_full, gelu_back = jax.vjp(gelu_exact, hidden)
    active = active_full.astype(jnp.bfloat16)
    grad_top = out_grad.astype(jnp.float32)
    grad_down_bias = jnp.sum(grad_top, axis=0)
    grad_down = jnp.einsum("tf,td->fd", active, out_grad, preferred_element_type=jnp.float32)
    grad_active = jnp.einsum("td,fd->tf", out_grad, back_set[6], preferred_element_type=jnp.float32)
    grad_hidden = gelu_back(grad_active)[0].astype(jnp.bfloat16)
    grad_up = jnp.einsum("td,tf->df", normed_two, grad_hidden, preferred_element_type=jnp.float32)
    grad_up_bias = jnp.sum(grad_hidden.astype(jnp.float32), axis=0).reshape(back_set[5].shape)
    grad_norm_two = head_sum(
        jnp.einsum("tf,df->td", grad_hidden, back_set[4], preferred_element_type=jnp.float32)
    )
    gain_two = back_set[10].astype(jnp.float32)
    shift_two = back_set[11].astype(jnp.float32)
    norm_out, norm_two_back = jax.vjp(layer_norm, middle, gain_two, shift_two)
    grad_mid_norm, grad_gain_two, grad_bias_two = norm_two_back(grad_norm_two)
    grad_middle = grad_top + grad_mid_norm
    grad_branch = grad_middle.astype(jnp.bfloat16)
    grad_proj_bias = jnp.sum(grad_branch.astype(jnp.float32), axis=0)
    grad_proj = jnp.einsum("te,td->ed", attn_out, grad_branch, preferred_element_type=jnp.float32)
    grad_attn = jnp.einsum(
        "td,ed->te", grad_branch, back_set[2], preferred_element_type=jnp.float32
    ).astype(jnp.bfloat16)
    grad_delta = jnp.transpose(
        jnp.sum(
            (grad_attn.astype(jnp.float32) * attn_full).reshape(local_rows, local_heads, HD), axis=2
        )
    )
    normed_one, query_rows, key_rows, value_rows = first_half(back_set, embedded)

    def cycle_turn(turn_index, cycle_state):
        pair_block, grad_pair, grad_query = cycle_state
        owner_rank = (my_rank - turn_index) % cycle_size
        key_seg = lax.dynamic_slice_in_dim(seg_table, owner_rank * local_rows, local_rows, 0)
        add_query, add_key, add_value = block_grads(
            query_rows,
            grad_attn,
            log_total,
            grad_delta,
            segment_ids,
            pair_block[:, 0],
            pair_block[:, 1],
            key_seg,
        )
        grad_pair = grad_pair + jnp.stack([add_key, add_value], axis=1)
        pair_block = shifted(pair_block, "sp", 1)
        grad_pair = shifted(grad_pair.astype(jnp.bfloat16), "sp", 1).astype(grad_pair.dtype)
        return (pair_block, grad_pair, grad_query + add_query)

    pair_start = jnp.stack([key_rows, value_rows], axis=1)
    cycle_init = (
        pair_start,
        jnp.zeros((local_rows, 2, local_width), jnp.float32),
        jnp.zeros((local_rows, local_width), jnp.float32),
    )
    pair_end, grad_pair, grad_query = lax.fori_loop(0, cycle_size, cycle_turn, cycle_init)
    grad_key = grad_pair[:, 0]
    grad_value = grad_pair[:, 1]
    grad_stack = jnp.stack(
        [
            grad_query.astype(jnp.bfloat16),
            grad_key.astype(jnp.bfloat16),
            grad_value.astype(jnp.bfloat16),
        ],
        axis=0,
    )
    grad_qkv = jnp.einsum("td,cte->cde", normed_one, grad_stack, preferred_element_type=jnp.float32)
    grad_qv_bias = jnp.stack(
        [
            jnp.sum(grad_stack[0].astype(jnp.float32), axis=0),
            jnp.sum(grad_stack[2].astype(jnp.float32), axis=0),
        ],
        axis=0,
    ).reshape(2, local_heads, HD)
    grad_norm_one = head_sum(
        jnp.einsum("cte,cde->td", grad_stack, back_set[0], preferred_element_type=jnp.float32)
    )
    gain_one = back_set[8].astype(jnp.float32)
    shift_one = back_set[9].astype(jnp.float32)
    norm_first, norm_one_back = jax.vjp(layer_norm, embedded, gain_one, shift_one)
    grad_start_norm, grad_gain_one, grad_bias_one = norm_one_back(grad_norm_one)
    grad_embedded = grad_middle + grad_start_norm
    grad_lead_w = jnp.sum(grad_embedded * lead_time[:, None], axis=0)
    grad_lead_b = jnp.sum(grad_embedded, axis=0)
    shards = (
        lax.psum_scatter(grad_qkv, "sp", scatter_dimension=1, tiled=True),
        lax.psum_scatter(grad_qv_bias, "sp", scatter_dimension=2, tiled=True),
        lax.psum_scatter(grad_proj, "sp", scatter_dimension=1, tiled=True),
        lax.psum_scatter(grad_proj_bias, "sp", scatter_dimension=0, tiled=True),
        lax.psum_scatter(grad_up, "sp", scatter_dimension=0, tiled=True),
        lax.psum_scatter(grad_up_bias, "sp", scatter_dimension=1, tiled=True),
        lax.psum_scatter(grad_down, "sp", scatter_dimension=1, tiled=True),
        lax.psum_scatter(grad_down_bias, "sp", scatter_dimension=0, tiled=True),
        lax.psum_scatter(grad_gain_one, "sp", scatter_dimension=0, tiled=True),
        lax.psum_scatter(grad_bias_one, "sp", scatter_dimension=0, tiled=True),
        lax.psum_scatter(grad_gain_two, "sp", scatter_dimension=0, tiled=True),
        lax.psum_scatter(grad_bias_two, "sp", scatter_dimension=0, tiled=True),
        lax.psum_scatter(grad_lead_w, "sp", scatter_dimension=0, tiled=True),
        lax.psum_scatter(grad_lead_b, "sp", scatter_dimension=0, tiled=True),
    )
    return (
        block_out.astype(jnp.bfloat16),
        grad_embedded,
        shards[0],
        shards[1],
        shards[2],
        shards[3],
        shards[4],
        shards[5],
        shards[6],
        shards[7],
        shards[8],
        shards[9],
        shards[10],
        shards[11],
        shards[12],
        shards[13],
    )


def solution(mesh):
    placed = (
        P("sp", None),
        P("sp"),
        P(),
        P(None, "sp", "tp"),
        P(None, "tp", "sp"),
        P("tp", "sp"),
        P("sp"),
        P("sp", "tp"),
        P("tp", "sp"),
        P("tp", "sp"),
        P("sp"),
        P("sp"),
        P("sp"),
        P("sp"),
        P("sp"),
        P("sp"),
        P("sp"),
        P("sp", None),
    )
    return jax.shard_map(
        per_device,
        mesh=mesh,
        in_specs=placed,
        out_specs=(
            P("sp", None),
            P("sp", None),
            P(None, "sp", "tp"),
            P(None, "tp", "sp"),
            P("tp", "sp"),
            P("sp"),
            P("sp", "tp"),
            P("tp", "sp"),
            P("tp", "sp"),
            P("sp"),
            P("sp"),
            P("sp"),
            P("sp"),
            P("sp"),
            P("sp"),
            P("sp"),
        ),
        check_vma=False,
    )
```

profile of v0, /device:TPU:0, one launch (start us, length us, event | category | flops | bytes accessed | tf_op | source)
XLA Modules:
  0.0 1232.3 jit_solution(5032956503079393849)
XLA Ops:
  16.7 63.3 %all-reduce.21 = (bf16[1024]{0:T(1024)(128)(2,1)}, bf16[1024]{0:T(1024)(128)(2,1)}, bf16[1024]{0:T(1024)(128)(2,1)}, bf16[1024]{0:T(1024)(128)(2,1)S(1)}, bf16[1...) all-reduce(bf16[1024]{0:T(1024)(128)(2,1)S(1)} %dynamic-update-slic, ...), channel_id=1, replica_groups=mesh['sp'=16,'tp'=2] {'sp'}, use_global_device_ids=true, to_apply=%add.7 | all-reduce | flops 8192 | bytes 32768
  80.6 17.2 %all_gather.64 = bf16[2,8,64]{1,0,2:T(2,128)(2,1)S(1)} all-gather(bf16[2,8,4]{1,0,2:T(2,128)(2,1)S(1)} %copy.82), channel_id=1, replica_groups=mesh['sp'=16,'tp'=2] {'sp'}, dimensions={2}, use_global_device_ids=true | all-gather | bytes 2176 | tf_op jit(solution)/shard_map/all_gather | solution.py:122
  102.1 2.9 convolution_bitcast_fusion.1
  108.5 60.7 %all-reduce.2 = s32[3072]{0:T(1024)} all-reduce(s32[3072]{0:T(1024)S(1)} %dynamic-update-slice.2), channel_id=1, replica_groups=mesh['sp'=16,'tp'=2] {'sp'}, use_global_device_ids=true, to_apply=%add.2 | all-reduce | flops 3072 | bytes 24576
  169.6 75.6 %while.38 = (s32[]{:T(128)}, f32[8,192]{1,0:T(8,128)S(1)}, f32[8,192]{1,0:T(8,128)S(1)}, f32[192,8,64]{0,2,1:T(8,128)}, s32[192]{0:T(256)}, /*index=5*/s32[3072]...) while((s32[]{:T(128)}, f32[8,192]{1,0:T(8,128)S(1)}, ...), condition=%wide.region_6.7_spmd.clone, body=%wide.region_3.6_spmd.clone.sunk | while | flops 211952640 | bytes 16161743 | solution.py:189
  178.2 2.8 fusion.125
  190.6 3.0 fusion.125
  203.3 3.0 fusion.125
  215.9 3.0 fusion.125
  228.5 3.0 fusion.125
  241.1 3.0 fusion.125
  246.4 2.7 convolution_convert_fusion.2
  250.5 17.3 %all-gather = bf16[16,4,32]{2,1,0:T(4,128)(2,1)S(1)} all-gather(bf16[1,4,32]{2,1,0:T(4,128)(2,1)S(1)} %bitcast.185), channel_id=1, replica_groups=mesh['sp'=16,'tp'=2] {'sp'}, dimensions={0}, use_global_device_ids=true | all-gather | bytes 4352 | tf_op jit(solution)/shard_map/all_gather | solution.py:126
  275.1 50.1 %all-gather.13.cloned.1.call-done = bf16[1024,2048]{1,0:T(8,128)(2,1)} async-done(((bf16[64,2048]{1,0:T(8,128)(2,1)}), bf16[1024,2048]{1,0:T(8,128)(2,1)}) %all-gather.13.cloned.1.call-update) | async-done | bytes 4194320 | tf_op jit(solution)/shard_map/all_gather | solution.py:125
  325.2 4.6 convolution_add_fusion
  329.8 46.7 %all-gather.15.cloned.1.call-done = bf16[2048,1024]{0,1:T(8,128)(2,1)} async-done(((bf16[2048,64]{0,1:T(8,128)(2,1)}), bf16[2048,1024]{0,1:T(8,128)(2,1)}) %all-gather.15.cloned.1.call-update) | async-done | bytes 4194320 | tf_op jit(solution)/shard_map/all_gather | solution.py:127
  376.5 9.0 convert_reduce_fusion
  386.4 2.3 convolution_convert_fusion
  392.1 4.6 convolution_convert_fusion.1
  396.6 16.5 %all-reduce.30.cloned.1.call-done = bf16[192,1024]{1,0:T(8,128)(2,1)} async-done(((bf16[192,1024]{1,0:T(8,128)(2,1)}), bf16[192,1024]{1,0:T(8,128)(2,1)}) %all-reduce.30.cloned.1.call-update) | async-done | bytes 393232 | tf_op jit(solution)/shard_map/psum | solution.py:34
  413.1 2.2 fusion.33
  420.0 311.1 %while.39 = (s32[]{:T(128)}, bf16[192,2,512]{0,2,1:T(8,128)(2,1)}, f32[192,2,512]{0,2,1:T(8,128)S(1)}, f32[192,512]{0,1:T(8,128)S(1)}, s32[192]{0:T(256)}, /*ind...) while((s32[]{:T(128)}, bf16[192,2,512]{0,2,1:T(8,128)(2,1)}, ...), condition=%wide.region_16.17_spmd.clone, body=%wide.region_15.16_spmd.clone.sunk | while | flops 192516112 | bytes 17022400 | solution.py:275
  429.9 9.4 collective-permute-done.1
  447.8 11.0 collective-permute-done.1
  467.2 11.0 collective-permute-done.1
  486.7 11.0 collective-permute-done.1
  506.1 11.0 collective-permute-done.1
  525.5 11.0 collective-permute-done.1
  545.0 11.0 collective-permute-done.1
  564.4 11.0 collective-permute-done.1
  583.9 11.0 collective-permute-done.1
  603.3 11.0 collective-permute-done.1
  622.8 11.0 collective-permute-done.1
  642.2 11.0 collective-permute-done.1
  661.7 11.0 collective-permute-done.1
  681.1 11.0 collective-permute-done.1
  700.6 11.0 collective-permute-done.1
  720.0 11.0 collective-permute-done.1
  731.5 3.8 fusion.26
  735.5 4.0 convolution_bitcast_fusion
  739.4 9.4 copy.97
  753.1 4.7 fusion.56
  759.0 4.5 fusion.66
  771.3 66.5 %all-reduce.20 = (f32[2,8,64]{1,0,2:T(2,128)S(1)}, f32[1024]{0:T(1024)S(1)}, f32[32,64]{1,0:T(8,128)S(1)}, f32[1024]{0:T(1024)S(1)}, f32[1024]{0:T(1024)S(1)}, /...) all-reduce(f32[2,8,64]{1,0,2:T(2,128)S(1)} %copy.98, ...), channel_id=3, replica_groups=mesh['sp'=16,'tp'=2] {'sp'}, use_global_device_ids=true, to_apply=%region_23.24.clone | all-reduce | flops 11264 | bytes 90112
  843.7 97.8 %all-reduce.32.cloned.1.call-done = f32[3,1024,512]{2,0,1:T(4,128)} async-done(((f32[3,1024,512]{2,0,1:T(4,128)}), f32[3,1024,512]{2,0,1:T(4,128)}) %all-reduce.32.cloned.1.call-update) | async-done | bytes 6291472
  943.6 63.6 %reduce-scatter.5.cloned.1.call-done = f32[512,64]{0,1:T(8,128)} async-done(((f32[512,1024]{0,1:T(8,128)}), f32[512,64]{0,1:T(8,128)}) %reduce-scatter.5.cloned.1.call-update) | async-done | bytes 131088 | tf_op jit(solution)/shard_map/reduce_scatter | solution.py:307
  1007.2 108.8 %reduce-scatter.7.cloned.1.call-done = f32[64,2048]{1,0:T(8,128)} async-done(((f32[1024,2048]{1,0:T(8,128)}), f32[64,2048]{1,0:T(8,128)}) %reduce-scatter.7.cloned.1.call-update) | async-done | bytes 524304 | tf_op jit(solution)/shard_map/reduce_scatter | solution.py:309
  1116.0 109.4 %reduce-scatter.9.cloned.1.call-done = f32[2048,64]{0,1:T(8,128)} async-done(((f32[2048,1024]{0,1:T(8,128)}), f32[2048,64]{0,1:T(8,128)}) %reduce-scatter.9.cloned.1.call-update) | async-done | bytes 524304 | tf_op jit(solution)/shard_map/reduce_scatter | solution.py:311
  (570 shorter events, 247.5 us)
Async XLA Ops:
  7.2 94.3 %all-gather.7.cloned.1.call-start = ((), (), s32[]{:S(2)}) async-start(), calls=%async_computation.3 | async-start | bytes 3342336 | tf_op jit(solution)/shard_map/all_gather | solution.py:121
  7.9 161.7 %all-gather.9.cloned.1.call-start = ((), (), s32[]{:S(2)}) async-start(), calls=%async_computation.4 | async-start | bytes 6684672 | tf_op jit(solution)/shard_map/all_gather | solution.py:158
  106.0 140.4 %all-gather.11.cloned.1.call-start = ((), (), s32[]{:S(2)}) async-start(), calls=%async_computation.5 | async-start | bytes 1114112 | tf_op jit(solution)/shard_map/all_gather | solution.py:123
  106.7 165.5 %all-reduce.28.cloned.1.call-start = ((), (), s32[]{:S(2)}) async-start(), calls=%async_computation.6 | async-start | bytes 786432 | tf_op jit(solution)/shard_map/psum | solution.py:34
  249.2 76.0 %all-gather.13.cloned.1.call-start = ((), (), s32[]{:S(2)}) async-start(), calls=%async_computation.7 | async-start | bytes 4456448 | tf_op jit(solution)/shard_map/all_gather | solution.py:125
  249.8 126.8 %all-gather.15.cloned.1.call-start = ((), (), s32[]{:S(2)}) async-start(), calls=%async_computation.8 | async-start | bytes 4456448 | tf_op jit(solution)/shard_map/all_gather | solution.py:127
  250.4 162.8 %all-reduce.30.cloned.1.call-start = ((), (), s32[]{:S(2)}) async-start(), calls=%async_computation.9 | async-start | bytes 786432 | tf_op jit(solution)/shard_map/psum | solution.py:34
  250.5 74.7 %copy-start.26 = (f32[1024]{0:T(1024)}, f32[1024]{0:T(1024)S(1)}, u32[]{:S(2)}) copy-start(f32[1024]{0:T(1024)S(1)} %convert_element_type.239) | copy-start | bytes 12292
  273.6 141.7 %copy-start.30 = (f32[192]{0:T(256)}, f32[192]{0:T(256)S(1)}, u32[]{:S(2)}) copy-start(f32[192]{0:T(256)S(1)} %broadcast_multiply_fusion) | copy-start | bytes 2308
  275.1 140.2 %copy-start.34 = (f32[192]{0:T(256)}, f32[192]{0:T(256)S(1)}, u32[]{:S(2)}) copy-start(f32[192]{0:T(256)S(1)} %fusion.51) | copy-start | bytes 2308
  275.1 101.4 %copy-start.10 = (bf16[192,1024]{1,0:T(8,128)(2,1)S(1)}, bf16[192,1024]{1,0:T(8,128)(2,1)}, u32[]{:S(2)}) copy-start(bf16[192,1024]{1,0:T(8,128)(2,1)} %param.39) | copy-start | bytes 1179652
  388.7 377.4 %all-reduce.34.cloned.1.call-start = ((), (), s32[]{:S(2)}) async-start(), calls=%async_computation.14 | async-start | bytes 1572864 | tf_op jit(solution)/shard_map/psum | solution.py:34
  421.1 18.4 %collective-permute-start = (bf16[192,2,512]{0,2,1:T(8,128)(2,1)S(1)}, bf16[192,2,512]{0,2,1:T(8,128)(2,1)}, u32[]{:S(2)}, u32[]{:S(2)}) collective-permute-start(bf16[192,2,512]{0,2,1:T(8,128)(2,1)S(1)} %copy.138), channel_id=1, source_target_pairs={{30,0},{0,2},{2,4},{4,6},{6,8},{8,10},{10,12},{12,14},{14,16},{16,... | collective-permute-start | bytes 1179656 | tf_op jit(solution)/shard_map/while/body/eval_jaxpr/ppermute | solution.py:16
  427.8 11.5 collective-permute-start.1
  440.5 18.3 %collective-permute-start = (bf16[192,2,512]{0,2,1:T(8,128)(2,1)S(1)}, bf16[192,2,512]{0,2,1:T(8,128)(2,1)}, u32[]{:S(2)}, u32[]{:S(2)}) collective-permute-start(bf16[192,2,512]{0,2,1:T(8,128)(2,1)S(1)} %copy.138), channel_id=1, source_target_pairs={{30,0},{0,2},{2,4},{4,6},{6,8},{8,10},{10,12},{12,14},{14,16},{16,... | collective-permute-start | bytes 1179656 | tf_op jit(solution)/shard_map/while/body/eval_jaxpr/ppermute | solution.py:16
  447.3 11.5 collective-permute-start.1
  460.0 18.4 %collective-permute-start = (bf16[192,2,512]{0,2,1:T(8,128)(2,1)S(1)}, bf16[192,2,512]{0,2,1:T(8,128)(2,1)}, u32[]{:S(2)}, u32[]{:S(2)}) collective-permute-start(bf16[192,2,512]{0,2,1:T(8,128)(2,1)S(1)} %copy.138), channel_id=1, source_target_pairs={{30,0},{0,2},{2,4},{4,6},{6,8},{8,10},{10,12},{12,14},{14,16},{16,... | collective-permute-start | bytes 1179656 | tf_op jit(solution)/shard_map/while/body/eval_jaxpr/ppermute | solution.py:16
  466.7 11.5 collective-permute-start.1
  479.4 18.3 %collective-permute-start = (bf16[192,2,512]{0,2,1:T(8,128)(2,1)S(1)}, bf16[192,2,512]{0,2,1:T(8,128)(2,1)}, u32[]{:S(2)}, u32[]{:S(2)}) collective-permute-start(bf16[192,2,512]{0,2,1:T(8,128)(2,1)S(1)} %copy.138), channel_id=1, source_target_pairs={{30,0},{0,2},{2,4},{4,6},{6,8},{8,10},{10,12},{12,14},{14,16},{16,... | collective-permute-start | bytes 1179656 | tf_op jit(solution)/shard_map/while/body/eval_jaxpr/ppermute | solution.py:16
  486.1 11.5 collective-permute-start.1
  498.8 18.3 %collective-permute-start = (bf16[192,2,512]{0,2,1:T(8,128)(2,1)S(1)}, bf16[192,2,512]{0,2,1:T(8,128)(2,1)}, u32[]{:S(2)}, u32[]{:S(2)}) collective-permute-start(bf16[192,2,512]{0,2,1:T(8,128)(2,1)S(1)} %copy.138), channel_id=1, source_target_pairs={{30,0},{0,2},{2,4},{4,6},{6,8},{8,10},{10,12},{12,14},{14,16},{16,... | collective-permute-start | bytes 1179656 | tf_op jit(solution)/shard_map/while/body/eval_jaxpr/ppermute | solution.py:16
  505.6 11.5 collective-permute-start.1
  518.3 18.4 %collective-permute-start = (bf16[192,2,512]{0,2,1:T(8,128)(2,1)S(1)}, bf16[192,2,512]{0,2,1:T(8,128)(2,1)}, u32[]{:S(2)}, u32[]{:S(2)}) collective-permute-start(bf16[192,2,512]{0,2,1:T(8,128)(2,1)S(1)} %copy.138), channel_id=1, source_target_pairs={{30,0},{0,2},{2,4},{4,6},{6,8},{8,10},{10,12},{12,14},{14,16},{16,... | collective-permute-start | bytes 1179656 | tf_op jit(solution)/shard_map/while/body/eval_jaxpr/ppermute | solution.py:16
  525.0 11.5 collective-permute-start.1
  537.7 18.4 %collective-permute-start = (bf16[192,2,512]{0,2,1:T(8,128)(2,1)S(1)}, bf16[192,2,512]{0,2,1:T(8,128)(2,1)}, u32[]{:S(2)}, u32[]{:S(2)}) collective-permute-start(bf16[192,2,512]{0,2,1:T(8,128)(2,1)S(1)} %copy.138), channel_id=1, source_target_pairs={{30,0},{0,2},{2,4},{4,6},{6,8},{8,10},{10,12},{12,14},{14,16},{16,... | collective-permute-start | bytes 1179656 | tf_op jit(solution)/shard_map/while/body/eval_jaxpr/ppermute | solution.py:16
  544.5 11.5 collective-permute-start.1
  557.2 18.4 %collective-permute-start = (bf16[192,2,512]{0,2,1:T(8,128)(2,1)S(1)}, bf16[192,2,512]{0,2,1:T(8,128)(2,1)}, u32[]{:S(2)}, u32[]{:S(2)}) collective-permute-start(bf16[192,2,512]{0,2,1:T(8,128)(2,1)S(1)} %copy.138), channel_id=1, source_target_pairs={{30,0},{0,2},{2,4},{4,6},{6,8},{8,10},{10,12},{12,14},{14,16},{16,... | collective-permute-start | bytes 1179656 | tf_op jit(solution)/shard_map/while/body/eval_jaxpr/ppermute | solution.py:16
  563.9 11.5 collective-permute-start.1
  576.6 18.4 %collective-permute-start = (bf16[192,2,512]{0,2,1:T(8,128)(2,1)S(1)}, bf16[192,2,512]{0,2,1:T(8,128)(2,1)}, u32[]{:S(2)}, u32[]{:S(2)}) collective-permute-start(bf16[192,2,512]{0,2,1:T(8,128)(2,1)S(1)} %copy.138), channel_id=1, source_target_pairs={{30,0},{0,2},{2,4},{4,6},{6,8},{8,10},{10,12},{12,14},{14,16},{16,... | collective-permute-start | bytes 1179656 | tf_op jit(solution)/shard_map/while/body/eval_jaxpr/ppermute | solution.py:16
  583.4 11.5 collective-permute-start.1
  596.1 18.4 %collective-permute-start = (bf16[192,2,512]{0,2,1:T(8,128)(2,1)S(1)}, bf16[192,2,512]{0,2,1:T(8,128)(2,1)}, u32[]{:S(2)}, u32[]{:S(2)}) collective-permute-start(bf16[192,2,512]{0,2,1:T(8,128)(2,1)S(1)} %copy.138), channel_id=1, source_target_pairs={{30,0},{0,2},{2,4},{4,6},{6,8},{8,10},{10,12},{12,14},{14,16},{16,... | collective-permute-start | bytes 1179656 | tf_op jit(solution)/shard_map/while/body/eval_jaxpr/ppermute | solution.py:16
  602.8 11.5 collective-permute-start.1
  615.5 18.4 %collective-permute-start = (bf16[192,2,512]{0,2,1:T(8,128)(2,1)S(1)}, bf16[192,2,512]{0,2,1:T(8,128)(2,1)}, u32[]{:S(2)}, u32[]{:S(2)}) collective-permute-start(bf16[192,2,512]{0,2,1:T(8,128)(2,1)S(1)} %copy.138), channel_id=1, source_target_pairs={{30,0},{0,2},{2,4},{4,6},{6,8},{8,10},{10,12},{12,14},{14,16},{16,... | collective-permute-start | bytes 1179656 | tf_op jit(solution)/shard_map/while/body/eval_jaxpr/ppermute | solution.py:16
  622.3 11.5 collective-permute-start.1
  635.0 18.4 %collective-permute-start = (bf16[192,2,512]{0,2,1:T(8,128)(2,1)S(1)}, bf16[192,2,512]{0,2,1:T(8,128)(2,1)}, u32[]{:S(2)}, u32[]{:S(2)}) collective-permute-start(bf16[192,2,512]{0,2,1:T(8,128)(2,1)S(1)} %copy.138), channel_id=1, source_target_pairs={{30,0},{0,2},{2,4},{4,6},{6,8},{8,10},{10,12},{12,14},{14,16},{16,... | collective-permute-start | bytes 1179656 | tf_op jit(solution)/shard_map/while/body/eval_jaxpr/ppermute | solution.py:16
  641.7 11.5 collective-permute-start.1
  654.4 18.4 %collective-permute-start = (bf16[192,2,512]{0,2,1:T(8,128)(2,1)S(1)}, bf16[192,2,512]{0,2,1:T(8,128)(2,1)}, u32[]{:S(2)}, u32[]{:S(2)}) collective-permute-start(bf16[192,2,512]{0,2,1:T(8,128)(2,1)S(1)} %copy.138), channel_id=1, source_target_pairs={{30,0},{0,2},{2,4},{4,6},{6,8},{8,10},{10,12},{12,14},{14,16},{16,... | collective-permute-start | bytes 1179656 | tf_op jit(solution)/shard_map/while/body/eval_jaxpr/ppermute | solution.py:16
  661.2 11.5 collective-permute-start.1
  673.8 18.4 %collective-permute-start = (bf16[192,2,512]{0,2,1:T(8,128)(2,1)S(1)}, bf16[192,2,512]{0,2,1:T(8,128)(2,1)}, u32[]{:S(2)}, u32[]{:S(2)}) collective-permute-start(bf16[192,2,512]{0,2,1:T(8,128)(2,1)S(1)} %copy.138), channel_id=1, source_target_pairs={{30,0},{0,2},{2,4},{4,6},{6,8},{8,10},{10,12},{12,14},{14,16},{16,... | collective-permute-start | bytes 1179656 | tf_op jit(solution)/shard_map/while/body/eval_jaxpr/ppermute | solution.py:16
  680.6 11.5 collective-permute-start.1
  693.3 18.4 %collective-permute-start = (bf16[192,2,512]{0,2,1:T(8,128)(2,1)S(1)}, bf16[192,2,512]{0,2,1:T(8,128)(2,1)}, u32[]{:S(2)}, u32[]{:S(2)}) collective-permute-start(bf16[192,2,512]{0,2,1:T(8,128)(2,1)S(1)} %copy.138), channel_id=1, source_target_pairs={{30,0},{0,2},{2,4},{4,6},{6,8},{8,10},{10,12},{12,14},{14,16},{16,... | collective-permute-start | bytes 1179656 | tf_op jit(solution)/shard_map/while/body/eval_jaxpr/ppermute | solution.py:16
  700.1 11.5 collective-permute-start.1
  712.7 18.4 %collective-permute-start = (bf16[192,2,512]{0,2,1:T(8,128)(2,1)S(1)}, bf16[192,2,512]{0,2,1:T(8,128)(2,1)}, u32[]{:S(2)}, u32[]{:S(2)}) collective-permute-start(bf16[192,2,512]{0,2,1:T(8,128)(2,1)S(1)} %copy.138), channel_id=1, source_target_pairs={{30,0},{0,2},{2,4},{4,6},{6,8},{8,10},{10,12},{12,14},{14,16},{16,... | collective-permute-start | bytes 1179656 | tf_op jit(solution)/shard_map/while/body/eval_jaxpr/ppermute | solution.py:16
  719.5 11.5 collective-permute-start.1
  735.4 206.2 %all-reduce.32.cloned.1.call-start = ((), (), s32[]{:S(2)}) async-start(), calls=%async_computation.13 | async-start | bytes 16777216
  748.9 258.3 %reduce-scatter.5.cloned.1.call-start = ((), (), s32[]{:S(2)}) async-start(), calls=%async_computation.10 | async-start | bytes 2228224 | tf_op jit(solution)/shard_map/reduce_scatter | solution.py:307
  751.9 364.1 %reduce-scatter.7.cloned.1.call-start = ((), (), s32[]{:S(2)}) async-start(), calls=%async_computation.11 | async-start | bytes 8912896 | tf_op jit(solution)/shard_map/reduce_scatter | solution.py:309
  757.8 467.6 %reduce-scatter.9.cloned.1.call-start = ((), (), s32[]{:S(2)}) async-start(), calls=%async_computation.12 | async-start | bytes 8912896 | tf_op jit(solution)/shard_map/reduce_scatter | solution.py:311
  (66 other events, 408.1 us)
Sparse Core Ops, SparseCore 0:
  10.2 48.2 all-gather.6
  106.1 61.1 all-gather.8
  169.4 36.6 all-gather.10
  249.3 22.8 all-reduce.27
  274.4 50.7 all-gather.12
  327.4 49.0 all-gather.14
  388.9 24.2 all-reduce.29
  735.5 30.6 all-reduce.33
  770.4 171.1 all-reduce.31
  945.7 61.4 reduce-scatter.4
  1012.4 103.5 reduce-scatter.6
  1121.0 104.3 reduce-scatter.8
where the time goes:
time: 1240 us; the launch traced here: 1230 us
  waiting for transfers between devices  671 us (54%)
  blocking collectives  225 us (18%)
  matrix products  147 us (12%)
  local copies, waits for them, and re-layouts  102 us (8%)
  other arithmetic  64.4 us (5%)
  between operations  17.6 us (1%)
    unnamed x3, blocking collectives  190 us
    ppermute x32, waiting for transfers between devices, shifted(): return lax.ppermute(block, axis, route)  175 us
    reduce_scatter x1, waiting for transfers between devices, per_device(): lax.psum_scatter(grad_down, 'sp', scatter_dimension=1, tiled=True)  109 us
    reduce_scatter x1, waiting for transfers between devices, per_device(): lax.psum_scatter(grad_up, 'sp', scatter_dimension=0, tiled=True)  109 us
    unnamed x13, waiting for transfers between devices  100 us
    reduce_scatter x1, waiting for transfers between devices, per_device(): lax.psum_scatter(grad_proj, 'sp', scatter_dimension=1, tiled=True)  63.6 us
    all_gather x1, waiting for transfers between devices, per_device(): lax.all_gather(up_weight, 'sp', axis=0, tiled=True)  50.1 us
    all_gather x1, waiting for transfers between devices, per_device(): lax.all_gather(down_weight, 'sp', axis=1, tiled=True)  46.7 us
  transfers between devices with their start and end apart: 44, of which 25 were waited for; matrix products, arithmetic and copies ran while one was open for 21% of the time, Pallas kernels for 0%

commit v1 on v0

v1 whole, which is shorter than its diff:
```python
import functools

import jax
import jax.numpy as jnp
from jax import lax
from jax.experimental import pallas as pl
from jax.experimental.pallas import tpu as pltpu
from jax.sharding import PartitionSpec as P

HD = 64
EPSILON = 1e-05
EXCLUDED = -1e30
F32 = jnp.float32
BF16 = jnp.bfloat16
NN = (((1,), (0,)), ((), ()))
NT = (((1,), (1,)), ((), ()))
TN = (((0,), (0,)), ((), ()))


def dot(left, right, dims=NN):
    return lax.dot_general(left, right, dims, preferred_element_type=F32)


class Grid:
    def __init__(self):
        self.sp = lax.axis_size("sp")
        chips = self.sp // 2
        self.nx = 2 if chips <= 8 else 4
        self.nz = chips // self.nx
        self.chips = chips
        me = lax.axis_index("sp")
        self.core = me % 2
        self.x = (me // 2) % self.nx
        self.z = me // (2 * self.nx)

    def _move(self, block, dz, dx, flip):
        pairs = []
        for i in range(self.sp):
            z, x, c = i // (2 * self.nx), (i // 2) % self.nx, i % 2
            to = (((z + dz) % self.nz) * self.nx + (x + dx) % self.nx) * 2 + (1 - c if flip else c)
            pairs.append((i, to))
        return lax.ppermute(block, "sp", pairs)

    def zshift(self, block, k):
        return self._move(block, k, 0, False)

    def xshift(self, block, k):
        return self._move(block, 0, k, False)

    def cswap(self, block):
        return self._move(block, 0, 0, True)

    def yswap(self, block):
        return lax.ppermute(block, "tp", [(0, 1), (1, 0)])

    def gather(self, block):
        columns = [block] + [self.zshift(block, k) for k in range(1, self.nz)]
        return [[b] + [self.xshift(b, j) for j in range(1, self.nx)] for b in columns]

    def scatter(self, pieces):
        total = pieces[:, 0].astype(F32)
        for j in range(1, self.nx):
            total = total + self.xshift(pieces[:, j], -j).astype(F32)
        low = total.astype(pieces.dtype)
        mine = total[0]
        for k in range(1, self.nz):
            mine = mine + self.zshift(low[k], -k).astype(F32)
        return mine


def normalize(values):
    center = values - jnp.mean(values, axis=-1, keepdims=True)
    spread = jnp.mean(center * center, axis=-1, keepdims=True)
    scale = lax.rsqrt(spread + EPSILON)
    return center * scale, scale


def norm_back(normed, scale, gain, grad):
    scaled = grad * gain
    mean_one = jnp.mean(scaled, axis=-1, keepdims=True)
    mean_two = jnp.mean(scaled * normed, axis=-1, keepdims=True)
    return (scaled - mean_one - normed * mean_two) * scale


def lane_in_head(shape, head):
    lanes = lax.broadcasted_iota(jnp.int32, shape, 1)
    return (lanes // HD) == (head % 2)


def pair_lanes(pair):
    return slice(pair * 2 * HD, (pair + 1) * 2 * HD)


def attend_kernel(chips, heads, q_ref, qcode_ref, kcode_ref, *refs):
    kv_refs = refs[:chips]
    out_ref, lse_ref = refs[chips : chips + 2]
    kaug, vturn, qaug, acc, stat = refs[chips + 2 :]
    rows = q_ref.shape[0]
    width = heads * HD
    for i in range(chips):
        code = kcode_ref[pl.ds(i * rows, rows), :]
        for p in range(heads // 2):
            keys = kv_refs[i][:, pair_lanes(p)]
            for h in (2 * p, 2 * p + 1):
                kaug[h, pl.ds(i * rows, rows), :] = jnp.where(lane_in_head(keys.shape, h), keys, code)
        vturn[i] = jnp.transpose(kv_refs[i][:, width:])
    for p in range(heads // 2):
        part = q_ref[:, pair_lanes(p)]
        for h in (2 * p, 2 * p + 1):
            qaug[h] = jnp.where(lane_in_head(part.shape, h), part, qcode_ref[...])
    acc[...] = jnp.zeros_like(acc)
    stat[0] = jnp.full(stat.shape[1:], EXCLUDED, F32)
    stat[1] = jnp.zeros(stat.shape[1:], F32)

    def chunk(i, carry):
        for h in range(heads):
            scores = dot(kaug[h, pl.ds(i * rows, rows), :], qaug[h], NT)
            top = stat[0, h : h + 1, :]
            new_top = jnp.maximum(top, jnp.max(scores, axis=0, keepdims=True))
            weight = jnp.exp(scores - new_top)
            rescale = jnp.exp(top - new_top)
            stat[0, h : h + 1, :] = new_top
            stat[1, h : h + 1, :] = stat[1, h : h + 1, :] * rescale + jnp.sum(weight, axis=0, keepdims=True)
            span = slice(h * HD, (h + 1) * HD)
            acc[span, :] = acc[span, :] * rescale + dot(vturn[i, span, :], weight.astype(BF16))
        return carry

    lax.fori_loop(0, chips, chunk, 0)
    for h in range(heads):
        span = slice(h * HD, (h + 1) * HD)
        acc[span, :] = acc[span, :] / stat[1, h : h + 1, :]
    out_ref[...] = jnp.transpose(acc[...])
    lse_ref[...] = stat[0] + jnp.log(jnp.maximum(stat[1], 1e-37))


def attend(q, qcode, kcode, kv_pieces):
    rows, width = q.shape
    heads = width // HD
    chips = len(kv_pieces)
    return pl.pallas_call(
        functools.partial(attend_kernel, chips, heads),
        out_shape=(jax.ShapeDtypeStruct((rows, width), F32), jax.ShapeDtypeStruct((8, rows), F32)),
        scratch_shapes=[
            pltpu.VMEM((heads, chips * rows, 2 * HD), BF16),
            pltpu.VMEM((chips, width, rows), BF16),
            pltpu.VMEM((heads, rows, 2 * HD), BF16),
            pltpu.VMEM((width, rows), F32),
            pltpu.VMEM((2, 8, rows), F32),
        ],
        compiler_params=pltpu.CompilerParams(vmem_limit_bytes=48 * 1024 * 1024),
        cost_estimate=pl.CostEstimate(
            flops=4 * rows * rows * chips * width, bytes_accessed=4 * rows * width * chips, transcendentals=rows * rows * chips * heads
        ),
        name="attend",
    )(q, qcode, kcode, *kv_pieces)


def attend_back_kernel(chips, heads, q_ref, qcode_ref, kcode_ref, dout_ref, lse_ref, delta_ref, *refs):
    kv_refs = refs[:chips]
    dq_ref, dkv_ref = refs[chips : chips + 2]
    kaug, kturn, vals, qaug, qmask, domask, acc = refs[chips + 2 :]
    rows = q_ref.shape[0]
    width = heads * HD
    for i in range(chips):
        span = pl.ds(i * rows, rows)
        code = kcode_ref[span, :]
        for p in range(heads // 2):
            keys = kv_refs[i][:, pair_lanes(p)]
            for h in (2 * p, 2 * p + 1):
                kaug[h, span, :] = jnp.where(lane_in_head(keys.shape, h), keys, code)
        kturn[i] = jnp.transpose(kv_refs[i][:, :width])
        vals[span, :] = kv_refs[i][:, width:]
    for p in range(heads // 2):
        part = q_ref[:, pair_lanes(p)]
        dpart = dout_ref[:, pair_lanes(p)]
        for h in (2 * p, 2 * p + 1):
            inside = lane_in_head(part.shape, h)
            qaug[h] = jnp.where(inside, part, qcode_ref[...])
            qmask[h] = jnp.where(inside, part, jnp.zeros_like(part))
            domask[h] = jnp.where(inside, dpart, jnp.zeros_like(dpart))
    acc[...] = jnp.zeros_like(acc)

    def chunk(i, carry):
        span = pl.ds(i * rows, rows)
        for p in range(heads // 2):
            dkey = dval = None
            for h in (2 * p, 2 * p + 1):
                scores = dot(kaug[h, span, :], qaug[h], NT)
                prob = jnp.exp(scores - lse_ref[h : h + 1, :])
                dprob = dot(vals[span, pair_lanes(p)], domask[h], NT)
                dscore = (prob * (dprob - delta_ref[h : h + 1, :])).astype(BF16)
                add_val = dot(prob.astype(BF16), domask[h])
                add_key = dot(dscore, qmask[h])
                dval = add_val if dval is None else dval + add_val
                dkey = add_key if dkey is None else dkey + add_key
                turn = slice(h * HD, (h + 1) * HD)
                acc[turn, :] += dot(kturn[i, turn, :], dscore)
            dkv_ref[i, :, pair_lanes(p)] = dkey.astype(BF16)
            dkv_ref[i, :, slice(width + p * 2 * HD, width + (p + 1) * 2 * HD)] = dval.astype(BF16)
        return carry

    lax.fori_loop(0, chips, chunk, 0)
    dq_ref[...] = (jnp.transpose(acc[...]) * (HD ** (-0.5))).astype(BF16)


def attend_back(q, qcode, kcode, dout, lse, delta, kv_pieces):
    rows, width = q.shape
    heads = width // HD
    chips = len(kv_pieces)
    return pl.pallas_call(
        functools.partial(attend_back_kernel, chips, heads),
        out_shape=(
            jax.ShapeDtypeStruct((rows, width), BF16),
            jax.ShapeDtypeStruct((chips, rows, 2 * width), BF16),
        ),
        scratch_shapes=[
            pltpu.VMEM((heads, chips * rows, 2 * HD), BF16),
            pltpu.VMEM((chips, width, rows), BF16),
            pltpu.VMEM((chips * rows, width), BF16),
            pltpu.VMEM((heads, rows, 2 * HD), BF16),
            pltpu.VMEM((heads, rows, 2 * HD), BF16),
            pltpu.VMEM((heads, rows, 2 * HD), BF16),
            pltpu.VMEM((width, rows), F32),
        ],
        compiler_params=pltpu.CompilerParams(vmem_limit_bytes=56 * 1024 * 1024),
        cost_estimate=pl.CostEstimate(
            flops=10 * rows * rows * chips * width, bytes_accessed=8 * rows * width * chips, transcendentals=rows * rows * chips * heads
        ),
        name="attend_back",
    )(q, qcode, kcode, dout, lse, delta, *kv_pieces)


def per_device(
    tokens,
    segment_ids,
    lead_hours,
    qkv_weight,
    qv_bias,
    proj_weight,
    proj_bias,
    up_weight,
    up_bias,
    down_weight,
    down_bias,
    norm1_gain,
    norm1_bias,
    norm2_gain,
    norm2_bias,
    lead_weight,
    lead_bias,
    out_grad,
):
    grid = Grid()
    core, chips = grid.core, grid.chips
    rows, width = tokens.shape
    part = norm1_gain.shape[0]
    low_core = core == 0

    def by_core(own, other):
        return jnp.where(low_core, own, other), jnp.where(low_core, other, own)

    def core_half(array, axis):
        half = array.shape[axis] // 2
        first = lax.slice_in_dim(array, 0, half, axis=axis)
        second = lax.slice_in_dim(array, half, 2 * half, axis=axis)
        return jnp.where(low_core, first, second), jnp.where(low_core, second, first)

    def spread(shard):
        keep, send = core_half(shard, shard.ndim - 1)
        keep = jnp.swapaxes(keep, 0, 1).reshape(part, -1) if keep.ndim == 3 else keep
        send = jnp.swapaxes(send, 0, 1).reshape(part, -1) if send.ndim == 3 else send
        return jnp.concatenate(by_core(keep, grid.cswap(send)), axis=0)

    def collect(block):
        pieces = grid.gather(block)
        return jnp.concatenate([p for line in pieces for p in line], axis=0)

    vectors = [lead_weight, lead_bias, norm1_gain, norm1_bias, proj_bias, norm2_gain, norm2_bias, down_bias]
    n_vec = len(vectors)
    flat = jnp.concatenate(vectors + [qv_bias.reshape(-1), up_bias.reshape(-1), segment_ids.astype(BF16)])
    sizes = (n_vec * part, qv_bias.size, up_bias.size, rows)
    pack = jnp.pad(flat, (0, -flat.size % 1024)).reshape(-1, 128)
    both = jnp.stack(by_core(pack, grid.cswap(pack)))
    table = jnp.stack([p for line in grid.gather(both) for p in line]).reshape(chips, 2, -1)
    order = jnp.arange(chips)
    chip_of = ((grid.z - order // grid.nx) % grid.nz) * grid.nx + (grid.x - order % grid.nx) % grid.nx
    at = 0
    vec_table = table[:, :, : sizes[0]].reshape(chips, 2, n_vec, part)
    vecs = jnp.transpose(vec_table, (2, 0, 1, 3)).reshape(n_vec, width).astype(F32)
    at += sizes[0]
    heads_local = qv_bias.shape[1]
    bias_table = table[:, :, at : at + sizes[1] + sizes[2]].reshape(chips, -1)
    place = (jnp.arange(chips)[:, None] == chip_of[None, :]).astype(BF16)
    bias_abs = dot(place, bias_table).reshape(2 * chips, -1)
    qv_all = jnp.transpose(bias_abs[:, : sizes[1]].reshape(2 * chips, 2, heads_local, -1), (1, 2, 0, 3)).reshape(
        2, heads_local * HD
    )
    up_all = jnp.transpose(bias_abs[:, sizes[1] :].reshape(2 * chips, up_bias.shape[0], -1), (1, 0, 2)).reshape(1, -1)
    qv_full = core_half(qv_all, 1)[0]
    up_full = core_half(up_all, 1)[0]
    at += sizes[1] + sizes[2]
    seg_table = table[:, :, at : at + rows]
    key_seg = jnp.concatenate(core_half(seg_table, 1), axis=1).reshape(-1).astype(jnp.int32)
    query_seg = key_seg[: 2 * rows]
    lanes = jnp.arange(2 * HD, dtype=jnp.int32) % HD
    kcode = jnp.where(key_seg[:, None] == lanes[None, :], 0.0, EXCLUDED).astype(BF16)
    qcode = (query_seg[:, None] == lanes[None, :]).astype(BF16)

    group = 2 * part
    feature = jnp.arange(width)
    source = jnp.sum(
        jnp.where((feature // group)[:, None] == order[None, :], chip_of[None, :], 0), axis=1
    ) * group + feature % group
    turn = (feature[:, None] == source[None, :]).astype(BF16)

    w_qkv = collect(spread(qkv_weight))
    tokens_two = jnp.concatenate([tokens, grid.cswap(tokens)], axis=0)
    grad_two = jnp.concatenate([out_grad, grid.cswap(out_grad)], axis=0)
    turned = dot(jnp.concatenate([tokens_two, grad_two], axis=0), turn)
    choose = query_seg[:, None] == jnp.arange(lead_hours.shape[0], dtype=jnp.int32)[None, :]
    lead_time = jnp.sum(jnp.where(choose, lead_hours[None, :], 0.0), axis=1)
    embedded_two = turned[: 2 * rows] + lead_time[:, None] * vecs[0] + vecs[1]
    gz = turned[2 * rows :].astype(BF16)
    embedded = embedded_two[:rows]
    n1, s1 = normalize(embedded_two)
    normed_one = (n1 * vecs[2] + vecs[3]).astype(BF16)
    local = qv_full.shape[1]
    qkv = dot(normed_one, w_qkv)
    q = ((qkv[:, :local] + qv_full[0]).astype(BF16) * jnp.asarray(HD ** (-0.5), BF16))
    kv = jnp.concatenate([qkv[:, local : 2 * local], qkv[:, 2 * local :] + qv_full[1]], axis=1).astype(BF16)
    kv_pieces = [p for line in grid.gather(kv) for p in line]

    w_proj = collect(spread(jnp.transpose(proj_weight)))
    w_up = collect(spread(up_weight))
    w_down = collect(spread(jnp.transpose(down_weight)))

    attn_full, lse = attend(q, qcode, kcode, kv_pieces)
    attn_out = attn_full.astype(BF16)

    def pair_sum(partial):
        mine = partial[:rows] + grid.cswap(partial[rows:].astype(BF16)).astype(F32)
        low = mine.astype(BF16)
        return low.astype(F32) + grid.yswap(low).astype(F32)

    def core_pair(block):
        return jnp.concatenate([block, grid.cswap(block)], axis=0)

    middle = embedded + (pair_sum(dot(attn_out, w_proj, NT)) + vecs[4])
    n2, s2 = normalize(middle)
    normed_two = core_pair((n2 * vecs[5] + vecs[6]).astype(BF16))
    hidden = dot(normed_two, w_up) + up_full
    cdf = 0.5 * (1.0 + lax.erf(hidden * (0.5**0.5)))
    active = (hidden * cdf).astype(BF16)
    slope = cdf + hidden * (jnp.exp(-0.5 * hidden * hidden) * ((0.5 / jnp.pi) ** 0.5))
    grad_hidden = (dot(gz, w_down) * slope).astype(BF16)
    grad_n2 = pair_sum(dot(grad_hidden, w_up, NT))
    block_out = middle + (pair_sum(dot(active, w_down, NT)) + vecs[7])
    block_out = dot(block_out.astype(BF16), turn, NT).astype(BF16)

    def give(gradient):
        pieces = gradient.astype(BF16).reshape(grid.nz, grid.nx, 2 * part, -1)
        mine = grid.scatter(pieces)
        keep, send = core_half(mine, 0)
        other = grid.cswap(send.astype(BF16)).astype(F32)
        return by_core(keep, other)

    d_up = give(dot(normed_two, grad_hidden, TN))
    d_down = give(dot(gz, active, TN))

    grad_top = gz[:rows].astype(F32)
    grad_middle = grad_top + norm_back(n2, s2, vecs[5], grad_n2)
    grad_branch = core_pair(grad_middle.astype(BF16))
    d_proj = give(dot(grad_branch, attn_out, TN))
    grad_attn = dot(grad_branch, w_proj).astype(BF16)
    delta = jnp.sum((grad_attn.astype(F32) * attn_full).reshape(2 * rows, -1, HD), axis=2)
    delta = jnp.pad(jnp.transpose(delta), ((0, 8 - delta.shape[1]), (0, 0)))
    grad_q, grad_kv_all = attend_back(q, qcode, kcode, grad_attn, lse, delta, kv_pieces)
    grad_kv = grid.scatter(grad_kv_all.reshape((grid.nz, grid.nx) + grad_kv_all.shape[1:])).astype(BF16)
    grad_stack = jnp.concatenate([grad_q, grad_kv], axis=1)
    d_qkv = give(dot(normed_one, grad_stack, TN))
    grad_n1 = pair_sum(dot(grad_stack, w_qkv, NT))
    input_grad = grad_middle + norm_back(n1[:rows], s1[:rows], vecs[2], grad_n1)

    sums = jnp.stack(
        [
            jnp.sum(input_grad * lead_time[:rows, None], axis=0),
            jnp.sum(input_grad, axis=0),
            jnp.sum(grad_n1 * n1[:rows], axis=0),
            jnp.sum(grad_n1, axis=0),
            jnp.sum(grad_branch[:rows].astype(F32), axis=0),
            jnp.sum(grad_n2 * n2, axis=0),
            jnp.sum(grad_n2, axis=0),
            jnp.sum(grad_top, axis=0),
        ]
    )
    sums = sums + grid.cswap(sums)
    sums = jnp.transpose(sums.reshape(n_vec, grid.nz, grid.nx, group), (1, 2, 0, 3))
    sums = core_half(grid.scatter(sums), 1)[0]
    bias_sums = jnp.concatenate(
        [jnp.sum(grad_hidden.astype(F32), axis=0), jnp.sum(grad_stack.astype(F32), axis=0)]
    ).reshape(1, -1)
    total = bias_sums
    for j in range(1, grid.nx):
        total = total + grid.xshift(bias_sums, j)
    whole = total
    for k in range(1, grid.nz):
        whole = whole + grid.zshift(total, k)
    low_half, high_half = by_core(whole, grid.cswap(whole))
    me = lax.axis_index("sp")
    n_up = grad_hidden.shape[1]

    def piece(low, high, start, size):
        both_halves = jnp.concatenate([low[0, start : start + size], high[0, start : start + size]])
        table_rows = both_halves.reshape(-1, HD)
        return lax.dynamic_slice_in_dim(table_rows, me * (HD // grid.sp), HD // grid.sp, 1)

    g_up_bias = piece(low_half, high_half, 0, n_up)
    g_q_bias = piece(low_half, high_half, n_up, local)
    g_v_bias = piece(low_half, high_half, n_up + 2 * local, local)

    input_grad = lax.dot_general(
        input_grad, turn.astype(F32), NT, precision=lax.Precision.HIGHEST, preferred_element_type=F32
    )
    g_qkv = jnp.concatenate([h.reshape(part, 3, local) for h in d_qkv], axis=2)
    return (
        block_out,
        input_grad,
        jnp.swapaxes(g_qkv, 0, 1),
        jnp.stack([g_q_bias, g_v_bias]),
        jnp.transpose(jnp.concatenate(d_proj, axis=1)),
        sums[4],
        jnp.concatenate(d_up, axis=1),
        g_up_bias,
        jnp.transpose(jnp.concatenate(d_down, axis=1)),
        sums[7],
        sums[2],
        sums[3],
        sums[5],
        sums[6],
        sums[0],
        sums[1],
    )


def solution(mesh):
    placed = (
        P("sp", None),
        P("sp"),
        P(),
        P(None, "sp", "tp"),
        P(None, "tp", "sp"),
        P("tp", "sp"),
        P("sp"),
        P("sp", "tp"),
        P("tp", "sp"),
        P("tp", "sp"),
        P("sp"),
        P("sp"),
        P("sp"),
        P("sp"),
        P("sp"),
        P("sp"),
        P("sp"),
        P("sp", None),
    )
    return jax.shard_map(
        per_device,
        mesh=mesh,
        in_specs=placed,
        out_specs=(
            P("sp", None),
            P("sp", None),
            P(None, "sp", "tp"),
            P(None, "tp", "sp"),
            P("tp", "sp"),
            P("sp"),
            P("sp", "tp"),
            P("tp", "sp"),
            P("tp", "sp"),
            P("sp"),
            P("sp"),
            P("sp"),
            P("sp"),
            P("sp"),
            P("sp"),
            P("sp"),
        ),
        check_vma=False,
    )
```

time: 1240 us -> 471 us (0.38)
  waiting for transfers between devices: 671 us -> 239 us
  blocking collectives: 225 us -> 0 us
  matrix products: 147 us -> 20.1 us
  starting transfers between devices: 2.62 us -> 109 us
  local copies, waits for them, and re-layouts: 102 us -> 31.3 us
  Pallas kernels: 0 us -> 35 us
  other arithmetic: 64.4 us -> 29.9 us
  between operations: 17.6 us -> 2.43 us
    reduce_scatter x3 -> x0, waiting for transfers between devices: 282 us -> none  [the longest x1 109 us: per_device(): lax.psum_scatter(grad_down, 'sp', scatter_dimension=1, tiled=True)]
    unnamed x3 -> x0, blocking collectives: 190 us -> none
    dot_general x104 -> x16, matrix products: 147 us -> 20.1 us  [the longest x15 16.8 us: dot(): return lax.dot_general(left, right, dims, preferred_element_type=F32)]
    ppermute x32 -> x93, starting transfers between devices: 1.66 us -> 109 us  [the longest x89 104 us: _move(): return lax.ppermute(block, 'sp', pairs)]
    unnamed x13 -> x0, waiting for transfers between devices: 100 us -> none
    all_gather x5 -> x0, waiting for transfers between devices: 96.9 us -> none  [the longest x1 50.1 us: per_device(): lax.all_gather(up_weight, 'sp', axis=0, tiled=True)]
    ppermute x32 -> x93, waiting for transfers between devices: 175 us -> 239 us  [the longest x89 213 us: _move(): return lax.ppermute(block, 'sp', pairs)]
    while x68 -> x0, local copies, waits for them, and re-layouts: 35.5 us -> none
  transfers between devices with their start and end apart: 44 -> 93, of which waited for: 25 -> 44; matrix products, arithmetic and copies ran while one was open for 21% -> 14% of each run, Pallas kernels for 0% -> 7%
where the time goes in v1:
time: 471 us; the launch traced here: 467 us
  waiting for transfers between devices  239 us (51%)
  starting transfers between devices  109 us (23%)
  Pallas kernels  35 us (7%)
  local copies, waits for them, and re-layouts  31.3 us (7%)
  other arithmetic  29.9 us (6%)
  matrix products  20.1 us (4%)
    ppermute x89, waiting for transfers between devices, _move(): return lax.ppermute(block, 'sp', pairs)  213 us
    ppermute x89, starting transfers between devices, _move(): return lax.ppermute(block, 'sp', pairs)  104 us
    ppermute x4, waiting for transfers between devices, yswap(): return lax.ppermute(block, 'tp', [(0, 1), (1, 0)])  26 us
    pallas_call x1, Pallas kernels, attend_back(): pl.pallas_call(functools.partial(attend_back_kernel, chips, heads), out_s...  20.1 us
    dot_general x15, matrix products, dot(): return lax.dot_general(left, right, dims, preferred_element_type=F32)  16.8 us
    pallas_call x1, Pallas kernels, attend(): pl.pallas_call(functools.partial(attend_kernel, chips, heads), out_shape=...  14.9 us
  transfers between devices with their start and end apart: 93, of which 44 were waited for; matrix products, arithmetic and copies ran while one was open for 14% of the time, Pallas kernels for 7%

profile of v1, /device:TPU:0, one launch (start us, length us, event | category | flops | bytes accessed | tf_op | source)
XLA Modules:
  0.0 467.2 jit_solution(10167064950911867978)
XLA Ops:
  3.1 5.4 %concatenate.92 = bf16[896]{0:T(1024)(128)(2,1)S(1)} concatenate(bf16[64]{0:T(256)(128)(2,1)} %param.33, bf16[64]{0:T(256)(128)(2,1)} %param.34, bf16[64]{0:T(256)(128)(2,1)} %param.29, bf16[64]{0:T(256)(128)(2,1)} %param.30, bf16[64]{0:T(256)(128)(2,1)} %param.24, bf16[64]{0:T(256)(128)(2,1)} %param.31, bf16[64]{0:T(256)(128)(2,1)} %param.32, bf16[64]{0:T(256)(128)(2,1)} %param.28, ...), dimensions={0} | concatenate | bytes 3584 | tf_op jit(solution)/shard_map/concatenate | solution.py:280
  13.6 4.7 %collective-permute-start.8 = (bf16[2,8,128]{2,1,0:T(8,128)(2,1)S(1)}, bf16[2,8,128]{2,1,0:T(8,128)(2,1)S(1)}, u32[]{:S(2)}, u32[]{:S(2)}) collective-permute-start(bf16[2,8,128]{2,1,0:T(8,128)(2,1)S(1)} %pad_maximum_fusion.16), channel_id=1, source_target_pairs={{0,24},{2,26},{4,28},{6,30},{8,0},{10,2},{12,4},{14,6},{16,8},{18,... | collective-permute-start | bytes 12296 | tf_op jit(solution)/shard_map/ppermute | solution.py:42
  19.8 2.1 collective-permute-done.3
  23.0 4.4 collective-permute-done.4
  46.4 6.1 %collective-permute-done.27 = bf16[128,256]{1,0:T(8,128)(2,1)S(1)} collective-permute-done((bf16[128,256]{1,0:T(8,128)(2,1)S(1)}, bf16[128,256]{1,0:T(8,128)(2,1)S(1)}, u32[]{:S(2)}, u32[]{:S(2)}) %collective-permute-start.27) | collective-permute-done | bytes 65568 | tf_op jit(solution)/shard_map/ppermute | solution.py:42
  57.8 3.8 collective-permute-done.11
  66.3 6.5 %collective-permute-done.14 = bf16[128,768]{1,0:T(8,128)(2,1)S(1)} collective-permute-done((bf16[128,768]{1,0:T(8,128)(2,1)S(1)}, bf16[128,768]{1,0:T(8,128)(2,1)S(1)}, u32[]{:S(2)}, u32[]{:S(2)}) %collective-permute-start.14) | collective-permute-done | bytes 196640 | tf_op jit(solution)/shard_map/ppermute | solution.py:42
  76.3 3.0 fusion.97
  80.6 7.2 %collective-permute-done.15 = bf16[128,768]{1,0:T(8,128)(2,1)S(1)} collective-permute-done((bf16[128,768]{1,0:T(8,128)(2,1)S(1)}, bf16[128,768]{1,0:T(8,128)(2,1)S(1)}, u32[]{:S(2)}, u32[]{:S(2)}) %collective-permute-start.15) | collective-permute-done | bytes 196640 | tf_op jit(solution)/shard_map/ppermute | solution.py:42
  89.2 3.6 collective-permute-start.23
  93.5 2.4 collective-permute-start.29
  97.3 30.4 %collective-permute-done.29 = bf16[128,256]{1,0:T(8,128)(2,1)S(1)} collective-permute-done((bf16[128,256]{1,0:T(8,128)(2,1)S(1)}, bf16[128,256]{1,0:T(8,128)(2,1)S(1)}, u32[]{:S(2)}, u32[]{:S(2)}) %collective-permute-start.29) | collective-permute-done | bytes 65568 | tf_op jit(solution)/shard_map/ppermute | solution.py:42
  129.2 3.2 collective-permute-done.30
  133.8 2.8 collective-permute-done.32
  142.5 5.8 %collective-permute-done.46 = bf16[128,1024]{1,0:T(8,128)(2,1)S(1)} collective-permute-done((bf16[128,1024]{1,0:T(8,128)(2,1)S(1)}, bf16[128,1024]{1,0:T(8,128)(2,1)S(1)}, u32[]{:S(2)}, u32[]{:S(2)}) %collective-permute-start.46) | collective-permute-done | bytes 262176 | tf_op jit(solution)/shard_map/ppermute | solution.py:42
  148.3 2.3 collective-permute-start.50
  150.6 3.3 collective-permute-start.48
  154.0 4.9 %collective-permute-done.24.refs_7_ = bf16[384,512]{1,0:T(8,128)(2,1)S(1)} collective-permute-done((bf16[384,512]{1,0:T(8,128)(2,1)S(1)}, bf16[384,512]{1,0:T(8,128)(2,1)S(1)}, u32[]{:S(2)}, u32[]{:S(2)}) %collective-permute-start.24) | collective-permute-done | bytes 393248 | tf_op jit(solution)/shard_map/ppermute | solution.py:42
  159.1 8.2 %collective-permute-done.22.refs_5_ = bf16[384,512]{1,0:T(8,128)(2,1)S(1)} collective-permute-done((bf16[384,512]{1,0:T(8,128)(2,1)S(1)}, bf16[384,512]{1,0:T(8,128)(2,1)S(1)}, u32[]{:S(2)}, u32[]{:S(2)}) %collective-permute-start.22) | collective-permute-done | bytes 393248 | tf_op jit(solution)/shard_map/ppermute | solution.py:42
  168.8 6.9 %collective-permute-done.20.refs_3_ = bf16[384,512]{1,0:T(8,128)(2,1)S(1)} collective-permute-done((bf16[384,512]{1,0:T(8,128)(2,1)S(1)}, bf16[384,512]{1,0:T(8,128)(2,1)S(1)}, u32[]{:S(2)}, u32[]{:S(2)}) %collective-permute-start.20) | collective-permute-done | bytes 393248 | tf_op jit(solution)/shard_map/ppermute | solution.py:42
  177.2 14.9 %attend.1 = (f32[384,256]{1,0:T(8,128)S(1)}, f32[8,384]{1,0:T(8,128)S(1)}) custom-call(bf16[384,256]{1,0:T(8,128)(2,1)S(1)} %get-tuple-element.115.q_ref, bf16[384,128]{1,0:T(8,128)(2,1)S(1)} %compare_convert_fusion.qcode_ref, bf16[3072,128]{1,0:T(8,128)(2,1)S(1)} %select_convert_fusion.kcode_ref, bf16[384,512]{1,0:T(8,128)(2,1)S(1)} %pad_maximum_fusion.8.refs_0_, ...), custom_call_target="tpu_custom_call" | custom-call | flops 1207959552 | bytes 3145728 | tf_op jit(solution)/shard_map/attend/pallas_call | solution.py:140
  193.8 3.0 collective-permute-start.42
  200.2 3.4 collective-permute-done.42
  204.2 10.4 %collective-permute-done.40 = bf16[128,1024]{1,0:T(8,128)(2,1)S(1)} collective-permute-done((bf16[128,1024]{1,0:T(8,128)(2,1)S(1)}, bf16[128,1024]{1,0:T(8,128)(2,1)S(1)}, u32[]{:S(2)}, u32[]{:S(2)}) %collective-permute-start.40) | collective-permute-done | bytes 262176 | tf_op jit(solution)/shard_map/ppermute | solution.py:42
  218.4 7.7 %collective-permute-done.34 = bf16[192,1024]{1,0:T(8,128)(2,1)S(1)} collective-permute-done((bf16[192,1024]{1,0:T(8,128)(2,1)S(1)}, bf16[192,1024]{1,0:T(8,128)(2,1)S(1)}, u32[]{:S(2)}, u32[]{:S(2)}) %collective-permute-start.34) | collective-permute-done | bytes 393248 | tf_op jit(solution)/shard_map/ppermute | solution.py:54
  241.2 8.2 %collective-permute-done.55 = bf16[192,1024]{1,0:T(8,128)(2,1)S(1)} collective-permute-done((bf16[192,1024]{1,0:T(8,128)(2,1)S(1)}, bf16[192,1024]{1,0:T(8,128)(2,1)S(1)}, u32[]{:S(2)}, u32[]{:S(2)}) %collective-permute-start.55) | collective-permute-done | bytes 393248 | tf_op jit(solution)/shard_map/ppermute | solution.py:54
  250.4 2.9 convert_reduce_fusion.3
  253.3 3.5 collective-permute-done.53
  258.6 2.7 collective-permute-done.88
  262.8 4.1 collective-permute-start.89
  267.4 15.6 %collective-permute-done.83 = bf16[4,128,1024]{2,1,0:T(8,128)(2,1)S(1)} collective-permute-done((bf16[4,128,1024]{2,1,0:T(8,128)(2,1)S(1)}, bf16[4,128,1024]{2,1,0:T(8,128)(2,1)S(1)}, u32[]{:S(2)}, u32[]{:S(2)}) %collective-permute-start.83) | collective-permute-done | bytes 1048608 | tf_op jit(solution)/shard_map/ppermute | solution.py:42
  285.8 4.1 collective-permute-start.84
  289.9 8.1 %collective-permute-start.86 = (bf16[128,1024]{1,0:T(8,128)(2,1)}, bf16[128,1024]{1,0:T(8,128)(2,1)}, u32[]{:S(2)}, u32[]{:S(2)}) collective-permute-start(bf16[128,1024]{1,0:T(8,128)(2,1)} %get-tuple-element.120), channel_id=1, source_target_pairs={{0,8},{2,10},{4,12},{6,14},{8,16},{10,18},{12,20},{14,22},{16,24},... | collective-permute-start | bytes 786440 | tf_op jit(solution)/shard_map/ppermute | solution.py:42
  301.0 20.1 %attend_back.1 = (bf16[384,256]{1,0:T(8,128)(2,1)}, bf16[8,384,512]{2,1,0:T(8,128)(2,1)}) custom-call(bf16[384,256]{1,0:T(8,128)(2,1)} %copy-done.2, bf16[384,128]{1,0:T(8,128)(2,1)} %copy-done.3, bf16[3072,128]{1,0:T(8,128)(2,1)} %copy-done, bf16[384,256]{1,0:T(8,128)(2,1)} %get-tuple-element.164.dout_ref, f32[8,384]{1,0:T(8,128)} %copy-done.11, ...), custom_call_target="tpu_custom_call" | custom-call | flops 3019898880 | bytes 6291456 | tf_op jit(solution)/shard_map/attend_back/pallas_call | solution.py:210
  328.0 9.5 %collective-permute-done.85 = bf16[128,1024]{1,0:T(8,128)(2,1)S(1)} collective-permute-done((bf16[128,1024]{1,0:T(8,128)(2,1)S(1)}, bf16[128,1024]{1,0:T(8,128)(2,1)S(1)}, u32[]{:S(2)}, u32[]{:S(2)}) %collective-permute-start.85) | collective-permute-done | bytes 262176 | tf_op jit(solution)/shard_map/ppermute | solution.py:42
  343.5 4.1 collective-permute-done.76
  349.0 16.2 %collective-permute-done.57 = bf16[4,384,512]{2,1,0:T(8,128)(2,1)S(1)} collective-permute-done((bf16[4,384,512]{2,1,0:T(8,128)(2,1)S(1)}, bf16[4,384,512]{2,1,0:T(8,128)(2,1)S(1)}, u32[]{:S(2)}, u32[]{:S(2)}) %collective-permute-start.57) | collective-permute-done | bytes 1572896 | tf_op jit(solution)/shard_map/ppermute | solution.py:42
  365.9 3.0 collective-permute-start.58
  372.2 11.4 %collective-permute-done.58 = bf16[384,512]{1,0:T(8,128)(2,1)S(1)} collective-permute-done((bf16[384,512]{1,0:T(8,128)(2,1)S(1)}, bf16[384,512]{1,0:T(8,128)(2,1)S(1)}, u32[]{:S(2)}, u32[]{:S(2)}) %collective-permute-start.58) | collective-permute-done | bytes 393248 | tf_op jit(solution)/shard_map/ppermute | solution.py:42
  383.6 4.5 collective-permute-done.60
  388.1 14.4 %collective-permute-done.59 = bf16[384,512]{1,0:T(8,128)(2,1)S(1)} collective-permute-done((bf16[384,512]{1,0:T(8,128)(2,1)S(1)}, bf16[384,512]{1,0:T(8,128)(2,1)S(1)}, u32[]{:S(2)}, u32[]{:S(2)}) %collective-permute-start.59) | collective-permute-done | bytes 393248 | tf_op jit(solution)/shard_map/ppermute | solution.py:42
  406.6 2.4 collective-permute-start.71
  410.6 2.9 collective-permute-done.70
  431.1 6.6 %collective-permute-done.62 = bf16[192,1024]{1,0:T(8,128)(2,1)S(1)} collective-permute-done((bf16[192,1024]{1,0:T(8,128)(2,1)S(1)}, bf16[192,1024]{1,0:T(8,128)(2,1)S(1)}, u32[]{:S(2)}, u32[]{:S(2)}) %collective-permute-start.62) | collective-permute-done | bytes 393248 | tf_op jit(solution)/shard_map/ppermute | solution.py:54
  445.3 2.3 collective-permute-start.80
  448.6 3.3 fusion
  452.6 3.0 collective-permute-start.65
  455.7 8.5 %collective-permute-done.65 = bf16[128,768]{1,0:T(8,128)(2,1)S(1)} collective-permute-done((bf16[128,768]{1,0:T(8,128)(2,1)S(1)}, bf16[128,768]{1,0:T(8,128)(2,1)S(1)}, u32[]{:S(2)}, u32[]{:S(2)}) %collective-permute-start.65) | collective-permute-done | bytes 196640 | tf_op jit(solution)/shard_map/ppermute | solution.py:42
  (437 shorter events, 147.1 us)
Async XLA Ops:
  9.8 31.9 %collective-permute-start.25 = (bf16[64,256]{1,0:T(8,128)(2,1)S(1)}, bf16[64,256]{1,0:T(8,128)(2,1)S(1)}, u32[]{:S(2)}, u32[]{:S(2)}) collective-permute-start(bf16[64,256]{1,0:T(8,128)(2,1)S(1)} %broadcast_select_fusion.12), channel_id=1, source_target_pairs={{0,2},{2,0},{4,6},{6,4},{8,10},{10,8},{12,14},{14,12},{16,18},{18,... | collective-permute-start | bytes 98312 | tf_op jit(solution)/shard_map/ppermute | solution.py:42
  10.9 43.9 %collective-permute-start.36 = (bf16[64,1024]{1,0:T(8,128)(2,1)S(1)}, bf16[64,1024]{1,0:T(8,128)(2,1)S(1)}, u32[]{:S(2)}, u32[]{:S(2)}) collective-permute-start(bf16[64,1024]{1,0:T(8,128)(2,1)S(1)} %broadcast_select_fusion.6), channel_id=1, source_target_pairs={{0,2},{2,0},{4,6},{6,4},{8,10},{10,8},{12,14},{14,12},{16,18},{18,... | collective-permute-start | bytes 393224 | tf_op jit(solution)/shard_map/ppermute | solution.py:42
  13.6 15.3 %collective-permute-start.8 = (bf16[2,8,128]{2,1,0:T(8,128)(2,1)S(1)}, bf16[2,8,128]{2,1,0:T(8,128)(2,1)S(1)}, u32[]{:S(2)}, u32[]{:S(2)}) collective-permute-start(bf16[2,8,128]{2,1,0:T(8,128)(2,1)S(1)} %pad_maximum_fusion.16), channel_id=1, source_target_pairs={{0,24},{2,26},{4,28},{6,30},{8,0},{10,2},{12,4},{14,6},{16,8},{18,... | collective-permute-start | bytes 12296 | tf_op jit(solution)/shard_map/ppermute | solution.py:42
  28.9 23.8 %collective-permute-start.44 = (bf16[64,1024]{1,0:T(8,128)(2,1)S(1)}, bf16[64,1024]{1,0:T(8,128)(2,1)S(1)}, u32[]{:S(2)}, u32[]{:S(2)}) collective-permute-start(bf16[64,1024]{1,0:T(8,128)(2,1)S(1)} %broadcast_select_fusion.2), channel_id=1, source_target_pairs={{0,2},{2,0},{4,6},{6,4},{8,10},{10,8},{12,14},{14,12},{16,18},{18,... | collective-permute-start | bytes 393224 | tf_op jit(solution)/shard_map/ppermute | solution.py:42
  29.0 23.5 %collective-permute-start.10 = (bf16[64,768]{1,0:T(8,128)(2,1)S(1)}, bf16[64,768]{1,0:T(8,128)(2,1)S(1)}, u32[]{:S(2)}, u32[]{:S(2)}) collective-permute-start(bf16[64,768]{1,0:T(8,128)(2,1)S(1)} %bitcast.267), channel_id=1, source_target_pairs={{0,2},{2,0},{4,6},{6,4},{8,10},{10,8},{12,14},{14,12},{16,18},{18,... | collective-permute-start | bytes 294920 | tf_op jit(solution)/shard_map/ppermute | solution.py:42
  38.2 36.1 %collective-permute-start = (bf16[192,1024]{1,0:T(8,128)(2,1)}, bf16[192,1024]{1,0:T(8,128)(2,1)}, u32[]{:S(2)}, u32[]{:S(2)}) collective-permute-start(bf16[192,1024]{1,0:T(8,128)(2,1)} %param.18), channel_id=1, source_target_pairs={{0,2},{2,0},{4,6},{6,4},{8,10},{10,8},{12,14},{14,12},{16,18},{18,... | collective-permute-start | bytes 1179656 | tf_op jit(solution)/shard_map/ppermute | solution.py:42
  52.5 22.3 %collective-permute-start.1 = (bf16[192,1024]{1,0:T(8,128)(2,1)}, bf16[192,1024]{1,0:T(8,128)(2,1)S(1)}, u32[]{:S(2)}, u32[]{:S(2)}) collective-permute-start(bf16[192,1024]{1,0:T(8,128)(2,1)} %param.35), channel_id=1, source_target_pairs={{0,2},{2,0},{4,6},{6,4},{8,10},{10,8},{12,14},{14,12},{16,18},{18,... | collective-permute-start | bytes 1179656 | tf_op jit(solution)/shard_map/ppermute | solution.py:42
  63.0 30.4 %collective-permute-start.31 = (bf16[128,256]{1,0:T(8,128)(2,1)S(1)}, bf16[128,256]{1,0:T(8,128)(2,1)S(1)}, u32[]{:S(2)}, u32[]{:S(2)}) collective-permute-start(bf16[128,256]{1,0:T(8,128)(2,1)S(1)} %pad_maximum_fusion.14), channel_id=1, source_target_pairs={{0,24},{2,26},{4,28},{6,30},{8,0},{10,2},{12,4},{14,6},{16,8},{18,... | collective-permute-start | bytes 196616 | tf_op jit(solution)/shard_map/ppermute | solution.py:42
  64.7 31.1 %collective-permute-start.28 = (bf16[128,256]{1,0:T(8,128)(2,1)S(1)}, bf16[128,256]{1,0:T(8,128)(2,1)S(1)}, u32[]{:S(2)}, u32[]{:S(2)}) collective-permute-start(bf16[128,256]{1,0:T(8,128)(2,1)S(1)} %collective-permute-done.27), channel_id=1, source_target_pairs={{0,4},{2,6},{4,0},{6,2},{8,12},{10,14},{12,8},{14,10},{16,20},{18,... | collective-permute-start | bytes 196616 | tf_op jit(solution)/shard_map/ppermute | solution.py:42
  74.3 13.6 %collective-permute-start.17 = (bf16[128,768]{1,0:T(8,128)(2,1)S(1)}, bf16[128,768]{1,0:T(8,128)(2,1)S(1)}, u32[]{:S(2)}, u32[]{:S(2)}) collective-permute-start(bf16[128,768]{1,0:T(8,128)(2,1)S(1)} %collective-permute-done.16), channel_id=1, source_target_pairs={{0,4},{2,6},{4,0},{6,2},{8,12},{10,14},{12,8},{14,10},{16,20},{18,... | collective-permute-start | bytes 589832 | tf_op jit(solution)/shard_map/ppermute | solution.py:42
  89.2 50.7 %collective-permute-start.23 = (bf16[384,512]{1,0:T(8,128)(2,1)S(1)}, bf16[384,512]{1,0:T(8,128)(2,1)S(1)}, u32[]{:S(2)}, u32[]{:S(2)}) collective-permute-start(bf16[384,512]{1,0:T(8,128)(2,1)S(1)} %pad_maximum_fusion.8.refs_0_), channel_id=1, source_target_pairs={{0,24},{2,26},{4,28},{6,30},{8,0},{10,2},{12,4},{14,6},{16,8},{18,... | collective-permute-start | bytes 1179656 | tf_op jit(solution)/shard_map/ppermute | solution.py:42
  92.8 47.6 %collective-permute-start.21 = (bf16[384,512]{1,0:T(8,128)(2,1)S(1)}, bf16[384,512]{1,0:T(8,128)(2,1)S(1)}, u32[]{:S(2)}, u32[]{:S(2)}) collective-permute-start(bf16[384,512]{1,0:T(8,128)(2,1)S(1)} %pad_maximum_fusion.8.refs_0_), channel_id=1, source_target_pairs={{0,16},{2,18},{4,20},{6,22},{8,24},{10,26},{12,28},{14,30},{16,0},... | collective-permute-start | bytes 1179656 | tf_op jit(solution)/shard_map/ppermute | solution.py:42
  92.8 49.1 %collective-permute-start.19 = (bf16[384,512]{1,0:T(8,128)(2,1)S(1)}, bf16[384,512]{1,0:T(8,128)(2,1)S(1)}, u32[]{:S(2)}, u32[]{:S(2)}) collective-permute-start(bf16[384,512]{1,0:T(8,128)(2,1)S(1)} %pad_maximum_fusion.8.refs_0_), channel_id=1, source_target_pairs={{0,8},{2,10},{4,12},{6,14},{8,16},{10,18},{12,20},{14,22},{16,24},... | collective-permute-start | bytes 1179656 | tf_op jit(solution)/shard_map/ppermute | solution.py:42
  93.5 34.2 %collective-permute-start.29 = (bf16[128,256]{1,0:T(8,128)(2,1)S(1)}, bf16[128,256]{1,0:T(8,128)(2,1)S(1)}, u32[]{:S(2)}, u32[]{:S(2)}) collective-permute-start(bf16[128,256]{1,0:T(8,128)(2,1)S(1)} %pad_maximum_fusion.14), channel_id=1, source_target_pairs={{0,16},{2,18},{4,20},{6,22},{8,24},{10,26},{12,28},{14,30},{16,0},... | collective-permute-start | bytes 196616 | tf_op jit(solution)/shard_map/ppermute | solution.py:42
  95.8 42.6 %collective-permute-start.45 = (bf16[128,1024]{1,0:T(8,128)(2,1)S(1)}, bf16[128,1024]{1,0:T(8,128)(2,1)S(1)}, u32[]{:S(2)}, u32[]{:S(2)}) collective-permute-start(bf16[128,1024]{1,0:T(8,128)(2,1)S(1)} %pad_maximum_fusion.10), channel_id=1, source_target_pairs={{0,4},{2,6},{4,0},{6,2},{8,12},{10,14},{12,8},{14,10},{16,20},{18,... | collective-permute-start | bytes 786440 | tf_op jit(solution)/shard_map/ppermute | solution.py:42
  139.9 19.0 %collective-permute-start.24 = (bf16[384,512]{1,0:T(8,128)(2,1)S(1)}, bf16[384,512]{1,0:T(8,128)(2,1)S(1)}, u32[]{:S(2)}, u32[]{:S(2)}) collective-permute-start(bf16[384,512]{1,0:T(8,128)(2,1)S(1)} %collective-permute-done.23.refs_6_), channel_id=1, source_target_pairs={{0,4},{2,6},{4,0},{6,2},{8,12},{10,14},{12,8},{14,10},{16,20},{18,... | collective-permute-start | bytes 1179656 | tf_op jit(solution)/shard_map/ppermute | solution.py:42
  140.4 26.9 %collective-permute-start.22 = (bf16[384,512]{1,0:T(8,128)(2,1)S(1)}, bf16[384,512]{1,0:T(8,128)(2,1)S(1)}, u32[]{:S(2)}, u32[]{:S(2)}) collective-permute-start(bf16[384,512]{1,0:T(8,128)(2,1)S(1)} %collective-permute-done.21.refs_4_), channel_id=1, source_target_pairs={{0,4},{2,6},{4,0},{6,2},{8,12},{10,14},{12,8},{14,10},{16,20},{18,... | collective-permute-start | bytes 1179656 | tf_op jit(solution)/shard_map/ppermute | solution.py:42
  141.9 33.8 %collective-permute-start.20 = (bf16[384,512]{1,0:T(8,128)(2,1)S(1)}, bf16[384,512]{1,0:T(8,128)(2,1)S(1)}, u32[]{:S(2)}, u32[]{:S(2)}) collective-permute-start(bf16[384,512]{1,0:T(8,128)(2,1)S(1)} %collective-permute-done.19.refs_2_), channel_id=1, source_target_pairs={{0,4},{2,6},{4,0},{6,2},{8,12},{10,14},{12,8},{14,10},{16,20},{18,... | collective-permute-start | bytes 1179656 | tf_op jit(solution)/shard_map/ppermute | solution.py:42
  148.3 50.4 %collective-permute-start.50 = (bf16[128,1024]{1,0:T(8,128)(2,1)S(1)}, bf16[128,1024]{1,0:T(8,128)(2,1)S(1)}, u32[]{:S(2)}, u32[]{:S(2)}) collective-permute-start(bf16[128,1024]{1,0:T(8,128)(2,1)S(1)} %pad_maximum_fusion.10), channel_id=1, source_target_pairs={{0,24},{2,26},{4,28},{6,30},{8,0},{10,2},{12,4},{14,6},{16,8},{18,... | collective-permute-start | bytes 786440 | tf_op jit(solution)/shard_map/ppermute | solution.py:42
  150.6 43.2 %collective-permute-start.48 = (bf16[128,1024]{1,0:T(8,128)(2,1)S(1)}, bf16[128,1024]{1,0:T(8,128)(2,1)S(1)}, u32[]{:S(2)}, u32[]{:S(2)}) collective-permute-start(bf16[128,1024]{1,0:T(8,128)(2,1)S(1)} %pad_maximum_fusion.10), channel_id=1, source_target_pairs={{0,16},{2,18},{4,20},{6,22},{8,24},{10,26},{12,28},{14,30},{16,0},... | collective-permute-start | bytes 786440 | tf_op jit(solution)/shard_map/ppermute | solution.py:42
  158.9 38.0 %collective-permute-start.38 = (bf16[128,1024]{1,0:T(8,128)(2,1)S(1)}, bf16[128,1024]{1,0:T(8,128)(2,1)S(1)}, u32[]{:S(2)}, u32[]{:S(2)}) collective-permute-start(bf16[128,1024]{1,0:T(8,128)(2,1)S(1)} %pad_maximum_fusion.9), channel_id=1, source_target_pairs={{0,8},{2,10},{4,12},{6,14},{8,16},{10,18},{12,20},{14,22},{16,24},... | collective-permute-start | bytes 786440 | tf_op jit(solution)/shard_map/ppermute | solution.py:42
  167.3 25.5 %collective-permute-start.37 = (bf16[128,1024]{1,0:T(8,128)(2,1)S(1)}, bf16[128,1024]{1,0:T(8,128)(2,1)S(1)}, u32[]{:S(2)}, u32[]{:S(2)}) collective-permute-start(bf16[128,1024]{1,0:T(8,128)(2,1)S(1)} %pad_maximum_fusion.9), channel_id=1, source_target_pairs={{0,4},{2,6},{4,0},{6,2},{8,12},{10,14},{12,8},{14,10},{16,20},{18,... | collective-permute-start | bytes 786440 | tf_op jit(solution)/shard_map/ppermute | solution.py:42
  175.7 22.4 %collective-permute-start.47 = (bf16[128,1024]{1,0:T(8,128)(2,1)S(1)}, bf16[128,1024]{1,0:T(8,128)(2,1)S(1)}, u32[]{:S(2)}, u32[]{:S(2)}) collective-permute-start(bf16[128,1024]{1,0:T(8,128)(2,1)S(1)} %collective-permute-done.46), channel_id=1, source_target_pairs={{0,4},{2,6},{4,0},{6,2},{8,12},{10,14},{12,8},{14,10},{16,20},{18,... | collective-permute-start | bytes 786440 | tf_op jit(solution)/shard_map/ppermute | solution.py:42
  192.8 22.4 %collective-permute-start.33 = (bf16[192,1024]{1,0:T(8,128)(2,1)S(1)}, bf16[192,1024]{1,0:T(8,128)(2,1)S(1)}, u32[]{:S(2)}, u32[]{:S(2)}) collective-permute-start(bf16[192,1024]{1,0:T(8,128)(2,1)S(1)} %slice.803), channel_id=1, source_target_pairs={{0,2},{2,0},{4,6},{6,4},{8,10},{10,8},{12,14},{14,12},{16,18},{18,... | collective-permute-start | bytes 1179656 | tf_op jit(solution)/shard_map/ppermute | solution.py:42
  196.8 17.8 %collective-permute-start.40 = (bf16[128,1024]{1,0:T(8,128)(2,1)S(1)}, bf16[128,1024]{1,0:T(8,128)(2,1)S(1)}, u32[]{:S(2)}, u32[]{:S(2)}) collective-permute-start(bf16[128,1024]{1,0:T(8,128)(2,1)S(1)} %pad_maximum_fusion.9), channel_id=1, source_target_pairs={{0,16},{2,18},{4,20},{6,22},{8,24},{10,26},{12,28},{14,30},{16,0},... | collective-permute-start | bytes 786440 | tf_op jit(solution)/shard_map/ppermute | solution.py:42
  198.1 18.6 %collective-permute-start.49 = (bf16[128,1024]{1,0:T(8,128)(2,1)S(1)}, bf16[128,1024]{1,0:T(8,128)(2,1)S(1)}, u32[]{:S(2)}, u32[]{:S(2)}) collective-permute-start(bf16[128,1024]{1,0:T(8,128)(2,1)S(1)} %collective-permute-done.48), channel_id=1, source_target_pairs={{0,4},{2,6},{4,0},{6,2},{8,12},{10,14},{12,8},{14,10},{16,20},{18,... | collective-permute-start | bytes 786440 | tf_op jit(solution)/shard_map/ppermute | solution.py:42
  198.7 19.7 %collective-permute-start.39 = (bf16[128,1024]{1,0:T(8,128)(2,1)S(1)}, bf16[128,1024]{1,0:T(8,128)(2,1)S(1)}, u32[]{:S(2)}, u32[]{:S(2)}) collective-permute-start(bf16[128,1024]{1,0:T(8,128)(2,1)S(1)} %collective-permute-done.38), channel_id=1, source_target_pairs={{0,4},{2,6},{4,0},{6,2},{8,12},{10,14},{12,8},{14,10},{16,20},{18,... | collective-permute-start | bytes 786440 | tf_op jit(solution)/shard_map/ppermute | solution.py:42
  203.6 24.4 %collective-permute-start.51 = (bf16[128,1024]{1,0:T(8,128)(2,1)S(1)}, bf16[128,1024]{1,0:T(8,128)(2,1)S(1)}, u32[]{:S(2)}, u32[]{:S(2)}) collective-permute-start(bf16[128,1024]{1,0:T(8,128)(2,1)S(1)} %collective-permute-done.50), channel_id=1, source_target_pairs={{0,4},{2,6},{4,0},{6,2},{8,12},{10,14},{12,8},{14,10},{16,20},{18,... | collective-permute-start | bytes 786440 | tf_op jit(solution)/shard_map/ppermute | solution.py:42
  214.6 13.5 %collective-permute-start.43 = (bf16[128,1024]{1,0:T(8,128)(2,1)S(1)}, bf16[128,1024]{1,0:T(8,128)(2,1)S(1)}, u32[]{:S(2)}, u32[]{:S(2)}) collective-permute-start(bf16[128,1024]{1,0:T(8,128)(2,1)S(1)} %collective-permute-done.42), channel_id=1, source_target_pairs={{0,4},{2,6},{4,0},{6,2},{8,12},{10,14},{12,8},{14,10},{16,20},{18,... | collective-permute-start | bytes 786440 | tf_op jit(solution)/shard_map/ppermute | solution.py:42
  235.3 26.1 %collective-permute-start.88 = (bf16[4,128,1024]{2,1,0:T(8,128)(2,1)S(1)}, bf16[4,128,1024]{2,1,0:T(8,128)(2,1)S(1)}, u32[]{:S(2)}, u32[]{:S(2)}) collective-permute-start(bf16[4,128,1024]{2,1,0:T(8,128)(2,1)S(1)} %slice_bitcast_fusion.2), channel_id=1, source_target_pairs={{0,4},{2,6},{4,0},{6,2},{8,12},{10,14},{12,8},{14,10},{16,20},{18,... | collective-permute-start | bytes 3145736 | tf_op jit(solution)/shard_map/ppermute | solution.py:42
  239.0 44.1 %collective-permute-start.83 = (bf16[4,128,1024]{2,1,0:T(8,128)(2,1)S(1)}, bf16[4,128,1024]{2,1,0:T(8,128)(2,1)S(1)}, u32[]{:S(2)}, u32[]{:S(2)}) collective-permute-start(bf16[4,128,1024]{2,1,0:T(8,128)(2,1)S(1)} %slice_bitcast_fusion.4), channel_id=1, source_target_pairs={{0,4},{2,6},{4,0},{6,2},{8,12},{10,14},{12,8},{14,10},{16,20},{18,... | collective-permute-start | bytes 3145736 | tf_op jit(solution)/shard_map/ppermute | solution.py:42
  240.6 16.1 %collective-permute-start.53 = (bf16[192,1024]{1,0:T(8,128)(2,1)S(1)}, bf16[192,1024]{1,0:T(8,128)(2,1)S(1)}, u32[]{:S(2)}, u32[]{:S(2)}) collective-permute-start(bf16[192,1024]{1,0:T(8,128)(2,1)S(1)} %fusion.27), channel_id=1, source_target_pairs={{0,1},{1,0},{2,3},{3,2},{4,5},{5,4},{6,7},{7,6},{8,9},{9,8},{10,11... | collective-permute-start | bytes 1179656 | tf_op jit(solution)/shard_map/ppermute | solution.py:54
  253.3 36.6 %collective-permute-start.56 = (bf16[192,1024]{1,0:T(8,128)(2,1)S(1)}, bf16[192,1024]{1,0:T(8,128)(2,1)S(1)}, u32[]{:S(2)}, u32[]{:S(2)}) collective-permute-start(bf16[192,1024]{1,0:T(8,128)(2,1)S(1)} %get-tuple-element.79), channel_id=1, source_target_pairs={{0,2},{2,0},{4,6},{6,4},{8,10},{10,8},{12,14},{14,12},{16,18},{18,... | collective-permute-start | bytes 1179656 | tf_op jit(solution)/shard_map/ppermute | solution.py:42
  262.8 60.5 %collective-permute-start.89 = (bf16[128,1024]{1,0:T(8,128)(2,1)}, bf16[128,1024]{1,0:T(8,128)(2,1)}, u32[]{:S(2)}, u32[]{:S(2)}) collective-permute-start(bf16[128,1024]{1,0:T(8,128)(2,1)} %get-tuple-element.116), channel_id=1, source_target_pairs={{0,24},{2,26},{4,28},{6,30},{8,0},{10,2},{12,4},{14,6},{16,8},{18,... | collective-permute-start | bytes 786440 | tf_op jit(solution)/shard_map/ppermute | solution.py:42
  266.9 57.7 %collective-permute-start.91 = (bf16[128,1024]{1,0:T(8,128)(2,1)}, bf16[128,1024]{1,0:T(8,128)(2,1)}, u32[]{:S(2)}, u32[]{:S(2)}) collective-permute-start(bf16[128,1024]{1,0:T(8,128)(2,1)} %get-tuple-element.117), channel_id=1, source_target_pairs={{0,8},{2,10},{4,12},{6,14},{8,16},{10,18},{12,20},{14,22},{16,24},... | collective-permute-start | bytes 786440 | tf_op jit(solution)/shard_map/ppermute | solution.py:42
  266.9 58.2 %collective-permute-start.90 = (bf16[128,1024]{1,0:T(8,128)(2,1)}, bf16[128,1024]{1,0:T(8,128)(2,1)}, u32[]{:S(2)}, u32[]{:S(2)}) collective-permute-start(bf16[128,1024]{1,0:T(8,128)(2,1)} %get-tuple-element.118), channel_id=1, source_target_pairs={{0,16},{2,18},{4,20},{6,22},{8,24},{10,26},{12,28},{14,30},{16,0},... | collective-permute-start | bytes 786440 | tf_op jit(solution)/shard_map/ppermute | solution.py:42
  285.8 42.1 %collective-permute-start.84 = (bf16[128,1024]{1,0:T(8,128)(2,1)}, bf16[128,1024]{1,0:T(8,128)(2,1)}, u32[]{:S(2)}, u32[]{:S(2)}) collective-permute-start(bf16[128,1024]{1,0:T(8,128)(2,1)} %get-tuple-element.119), channel_id=1, source_target_pairs={{0,24},{2,26},{4,28},{6,30},{8,0},{10,2},{12,4},{14,6},{16,8},{18,... | collective-permute-start | bytes 786440 | tf_op jit(solution)/shard_map/ppermute | solution.py:42
  289.9 38.1 %collective-permute-start.86 = (bf16[128,1024]{1,0:T(8,128)(2,1)}, bf16[128,1024]{1,0:T(8,128)(2,1)}, u32[]{:S(2)}, u32[]{:S(2)}) collective-permute-start(bf16[128,1024]{1,0:T(8,128)(2,1)} %get-tuple-element.120), channel_id=1, source_target_pairs={{0,8},{2,10},{4,12},{6,14},{8,16},{10,18},{12,20},{14,22},{16,24},... | collective-permute-start | bytes 786440 | tf_op jit(solution)/shard_map/ppermute | solution.py:42
  323.7 13.8 %collective-permute-start.85 = (bf16[128,1024]{1,0:T(8,128)(2,1)S(1)}, bf16[128,1024]{1,0:T(8,128)(2,1)S(1)}, u32[]{:S(2)}, u32[]{:S(2)}) collective-permute-start(bf16[128,1024]{1,0:T(8,128)(2,1)S(1)} %copy-done.24), channel_id=1, source_target_pairs={{0,16},{2,18},{4,20},{6,22},{8,24},{10,26},{12,28},{14,30},{16,0},... | collective-permute-start | bytes 786440 | tf_op jit(solution)/shard_map/ppermute | solution.py:42
  324.5 14.3 %collective-permute-start.73 = (bf16[4,128,256]{2,1,0:T(8,128)(2,1)S(1)}, bf16[4,128,256]{2,1,0:T(8,128)(2,1)S(1)}, u32[]{:S(2)}, u32[]{:S(2)}) collective-permute-start(bf16[4,128,256]{2,1,0:T(8,128)(2,1)S(1)} %slice_bitcast_fusion.21), channel_id=1, source_target_pairs={{0,4},{2,6},{4,0},{6,2},{8,12},{10,14},{12,8},{14,10},{16,20},{18,... | collective-permute-start | bytes 786440 | tf_op jit(solution)/shard_map/ppermute | solution.py:42
  325.1 40.1 %collective-permute-start.57 = (bf16[4,384,512]{2,1,0:T(8,128)(2,1)S(1)}, bf16[4,384,512]{2,1,0:T(8,128)(2,1)S(1)}, u32[]{:S(2)}, u32[]{:S(2)}) collective-permute-start(bf16[4,384,512]{2,1,0:T(8,128)(2,1)S(1)} %slice_bitcast_fusion), channel_id=1, source_target_pairs={{0,4},{2,6},{4,0},{6,2},{8,12},{10,14},{12,8},{14,10},{16,20},{18,... | collective-permute-start | bytes 4718600 | tf_op jit(solution)/shard_map/ppermute | solution.py:42
  327.9 13.2 %collective-permute-start.92 = (bf16[64,1024]{1,0:T(8,128)(2,1)S(1)}, bf16[64,1024]{1,0:T(8,128)(2,1)S(1)}, u32[]{:S(2)}, u32[]{:S(2)}) collective-permute-start(bf16[64,1024]{1,0:T(8,128)(2,1)S(1)} %select_convert_fusion.1), channel_id=1, source_target_pairs={{0,2},{2,0},{4,6},{6,4},{8,10},{10,8},{12,14},{14,12},{16,18},{18,... | collective-permute-start | bytes 393224 | tf_op jit(solution)/shard_map/ppermute | solution.py:42
  349.0 22.5 %collective-permute-start.77 = (bf16[64,256]{1,0:T(8,128)(2,1)S(1)}, bf16[64,256]{1,0:T(8,128)(2,1)S(1)}, u32[]{:S(2)}, u32[]{:S(2)}) collective-permute-start(bf16[64,256]{1,0:T(8,128)(2,1)S(1)} %select_convert_fusion.4), channel_id=1, source_target_pairs={{0,2},{2,0},{4,6},{6,4},{8,10},{10,8},{12,14},{14,12},{16,18},{18,... | collective-permute-start | bytes 98312 | tf_op jit(solution)/shard_map/ppermute | solution.py:42
  365.9 17.6 %collective-permute-start.58 = (bf16[384,512]{1,0:T(8,128)(2,1)S(1)}, bf16[384,512]{1,0:T(8,128)(2,1)S(1)}, u32[]{:S(2)}, u32[]{:S(2)}) collective-permute-start(bf16[384,512]{1,0:T(8,128)(2,1)S(1)} %get-tuple-element.111), channel_id=1, source_target_pairs={{0,24},{2,26},{4,28},{6,30},{8,0},{10,2},{12,4},{14,6},{16,8},{18,... | collective-permute-start | bytes 1179656 | tf_op jit(solution)/shard_map/ppermute | solution.py:42
  368.9 19.1 %collective-permute-start.60 = (bf16[384,512]{1,0:T(8,128)(2,1)S(1)}, bf16[384,512]{1,0:T(8,128)(2,1)S(1)}, u32[]{:S(2)}, u32[]{:S(2)}) collective-permute-start(bf16[384,512]{1,0:T(8,128)(2,1)S(1)} %get-tuple-element.112), channel_id=1, source_target_pairs={{0,8},{2,10},{4,12},{6,14},{8,16},{10,18},{12,20},{14,22},{16,24},... | collective-permute-start | bytes 1179656 | tf_op jit(solution)/shard_map/ppermute | solution.py:42
  369.3 33.2 %collective-permute-start.59 = (bf16[384,512]{1,0:T(8,128)(2,1)S(1)}, bf16[384,512]{1,0:T(8,128)(2,1)S(1)}, u32[]{:S(2)}, u32[]{:S(2)}) collective-permute-start(bf16[384,512]{1,0:T(8,128)(2,1)S(1)} %get-tuple-element.113), channel_id=1, source_target_pairs={{0,16},{2,18},{4,20},{6,22},{8,24},{10,26},{12,28},{14,30},{16,0},... | collective-permute-start | bytes 1179656 | tf_op jit(solution)/shard_map/ppermute | solution.py:42
  410.5 14.8 %collective-permute-start.61 = (bf16[192,1024]{1,0:T(8,128)(2,1)S(1)}, bf16[192,1024]{1,0:T(8,128)(2,1)}, u32[]{:S(2)}, u32[]{:S(2)}) collective-permute-start(bf16[192,1024]{1,0:T(8,128)(2,1)S(1)} %slice.800), channel_id=1, source_target_pairs={{0,2},{2,0},{4,6},{6,4},{8,10},{10,8},{12,14},{14,12},{16,18},{18,... | collective-permute-start | bytes 1179656 | tf_op jit(solution)/shard_map/ppermute | solution.py:42
  415.5 24.3 %collective-permute-start.63 = (bf16[4,128,768]{2,1,0:T(8,128)(2,1)}, bf16[4,128,768]{2,1,0:T(8,128)(2,1)}, u32[]{:S(2)}, u32[]{:S(2)}) collective-permute-start(bf16[4,128,768]{2,1,0:T(8,128)(2,1)} %slice_bitcast_fusion.6), channel_id=1, source_target_pairs={{0,4},{2,6},{4,0},{6,2},{8,12},{10,14},{12,8},{14,10},{16,20},{18,... | collective-permute-start | bytes 2359304 | tf_op jit(solution)/shard_map/ppermute | solution.py:42
  (81 other events, 1773.2 us)

commit v2 on v1

v2 whole, which is shorter than its diff:
```python
import functools

import jax
import jax.numpy as jnp
from jax import lax
from jax.experimental import pallas as pl
from jax.experimental.pallas import tpu as pltpu
from jax.sharding import PartitionSpec as P

HD = 64
EPSILON = 1e-05
EXCLUDED = -1e30
F32 = jnp.float32
BF16 = jnp.bfloat16
NN = (((1,), (0,)), ((), ()))
NT = (((1,), (1,)), ((), ()))
TN = (((0,), (0,)), ((), ()))


def dot(left, right, dims=NN):
    return lax.dot_general(left, right, dims, preferred_element_type=F32)


class Grid:
    def __init__(self):
        self.sp = lax.axis_size("sp")
        self.nz = 4
        self.nx = self.sp // (2 * self.nz)
        self.chips = self.nz * self.nx
        me = lax.axis_index("sp")
        self.me = me
        self.core = me % 2
        self.x = (me // 2) % self.nx
        self.z = me // (2 * self.nx)
        self.y = lax.axis_index("tp")

    def _move(self, block, dz, dx, flip):
        pairs = []
        for i in range(self.sp):
            z, x, c = i // (2 * self.nx), (i // 2) % self.nx, i % 2
            to = (((z + dz) % self.nz) * self.nx + (x + dx) % self.nx) * 2 + (1 - c if flip else c)
            pairs.append((i, to))
        return lax.ppermute(block, "sp", pairs)

    def zshift(self, block, k):
        return self._move(block, k, 0, False)

    def xshift(self, block, k):
        return self._move(block, 0, k, False)

    def cswap(self, block):
        return self._move(block, 0, 0, True)

    def yswap(self, block):
        return lax.ppermute(block, "tp", [(0, 1), (1, 0)])

    def _pairs(self, route):
        pairs = []
        for chip in range(self.chips):
            for (c, y), (to_c, to_y) in route:
                pairs.append(((chip * 2 + c) * 2 + y, (chip * 2 + to_c) * 2 + to_y))
        return pairs

    def spin(self, block, back=False):
        route = []
        for b in (0, 1):
            route += [((b, b), (b, 1 - b)), ((1 - b, b), (b, b))]
        if back:
            route = [(to, at) for at, to in route]
        return lax.ppermute(block, ("sp", "tp"), self._pairs(route))

    def cross(self, block):
        route = [((1 - b, b), (b, 1 - b)) for b in (0, 1)]
        return lax.ppermute(block, ("sp", "tp"), self._pairs(route))

    def far_z(self, k):
        return (self.z + k) % self.nz

    def far_x(self, j):
        return (self.x + j) % self.nx

    def gather(self, block):
        columns = [block] + [self.zshift(block, k) for k in range(1, self.nz)]
        return [p for b in columns for p in [b] + [self.xshift(b, j) for j in range(1, self.nx)]]

    def chip_order(self):
        order = jnp.arange(self.chips)
        return self.far_z(-(order // self.nx)) * self.nx + self.far_x(-(order % self.nx))

    def scatter(self, pieces):
        total = pick(pieces, self.x, 1).astype(F32)
        for j in range(1, self.nx):
            total = total + self.xshift(pick(pieces, self.far_x(j), 1), j).astype(F32)
        low = total.astype(pieces.dtype)
        mine = pick(total, self.z, 0)
        for k in range(1, self.nz):
            mine = mine + self.zshift(pick(low, self.far_z(k), 0), k).astype(F32)
        return mine


def pick(array, index, axis):
    return lax.dynamic_index_in_dim(array, index, axis, keepdims=False)


def normalize(values):
    center = values - jnp.mean(values, axis=-1, keepdims=True)
    spread = jnp.mean(center * center, axis=-1, keepdims=True)
    scale = lax.rsqrt(spread + EPSILON)
    return center * scale, scale


def norm_back(normed, scale, gain, grad):
    scaled = grad * gain
    mean_one = jnp.mean(scaled, axis=-1, keepdims=True)
    mean_two = jnp.mean(scaled * normed, axis=-1, keepdims=True)
    return (scaled - mean_one - normed * mean_two) * scale


def place_kernel(axis, starts_ref, *refs):
    pieces, out_ref = refs[:-1], refs[-1]
    for i, piece in enumerate(pieces):
        size = piece.shape[axis]
        span = pl.ds(pl.multiple_of(starts_ref[i], size), size)
        if axis == 0:
            out_ref[span, :] = piece[...]
        else:
            out_ref[:, span] = piece[...]


def place(pieces, starts, axis):
    shape = list(pieces[0].shape)
    shape[axis] *= len(pieces)
    vmem = pl.BlockSpec(memory_space=pltpu.VMEM)
    return pl.pallas_call(
        functools.partial(place_kernel, axis),
        out_shape=jax.ShapeDtypeStruct(tuple(shape), pieces[0].dtype),
        in_specs=[pl.BlockSpec(memory_space=pltpu.SMEM)] + [vmem] * len(pieces),
        out_specs=vmem,
        compiler_params=pltpu.CompilerParams(vmem_limit_bytes=32 * 1024 * 1024),
        name="place",
    )(jnp.stack(starts).astype(jnp.int32), *pieces)


def place_qkv_kernel(starts_ref, *refs):
    pieces, out_ref = refs[:-1], refs[-1]
    for i, piece in enumerate(pieces):
        size = piece.shape[1] // 3
        span = pl.ds(pl.multiple_of(starts_ref[i], size), size)
        for c in range(3):
            out_ref[c, :, span] = piece[:, c * size : (c + 1) * size].astype(F32)


def place_qkv(pieces, starts):
    rows, columns = pieces[0].shape
    vmem = pl.BlockSpec(memory_space=pltpu.VMEM)
    return pl.pallas_call(
        place_qkv_kernel,
        out_shape=jax.ShapeDtypeStruct((3, rows, columns // 3 * len(pieces)), F32),
        in_specs=[pl.BlockSpec(memory_space=pltpu.SMEM)] + [vmem] * len(pieces),
        out_specs=vmem,
        name="place_qkv",
    )(jnp.stack(starts).astype(jnp.int32), *pieces)


def lane_in_head(shape, head):
    lanes = lax.broadcasted_iota(jnp.int32, shape, 1)
    return (lanes // HD) == (head % 2)


def pair_lanes(pair):
    return slice(pair * 2 * HD, (pair + 1) * 2 * HD)


STEP = 384


def attend_kernel(pieces, heads, q_ref, qcode_ref, kcode_ref, *refs):
    kv_refs = refs[:pieces]
    out_ref, lse_ref = refs[pieces : pieces + 2]
    kaug, vturn, qaug, acc, stat = refs[pieces + 2 :]
    width = heads * HD
    steps = kv_refs[0].shape[0] // STEP
    for n in range(pieces * steps):
        block = kv_refs[n // steps]
        rows = pl.ds((n % steps) * STEP, STEP)
        span = pl.ds(n * STEP, STEP)
        code = kcode_ref[span, :]
        for p in range(heads // 2):
            keys = block[rows, pair_lanes(p)]
            for h in (2 * p, 2 * p + 1):
                kaug[h, span, :] = jnp.where(lane_in_head(keys.shape, h), keys, code)
        vturn[n] = jnp.transpose(block[rows, width:])
    for p in range(heads // 2):
        part = q_ref[:, pair_lanes(p)]
        for h in (2 * p, 2 * p + 1):
            qaug[h] = jnp.where(lane_in_head(part.shape, h), part, qcode_ref[...])
    acc[...] = jnp.zeros_like(acc)
    stat[0] = jnp.full(stat.shape[1:], EXCLUDED, F32)
    stat[1] = jnp.zeros(stat.shape[1:], F32)

    def chunk(i, carry):
        for h in range(heads):
            scores = dot(kaug[h, pl.ds(i * STEP, STEP), :], qaug[h], NT)
            top = stat[0, h : h + 1, :]
            new_top = jnp.maximum(top, jnp.max(scores, axis=0, keepdims=True))
            weight = jnp.exp(scores - new_top)
            rescale = jnp.exp(top - new_top)
            stat[0, h : h + 1, :] = new_top
            stat[1, h : h + 1, :] = stat[1, h : h + 1, :] * rescale + jnp.sum(weight, axis=0, keepdims=True)
            span = slice(h * HD, (h + 1) * HD)
            acc[span, :] = acc[span, :] * rescale + dot(vturn[i, span, :], weight.astype(BF16))
        return carry

    lax.fori_loop(0, pieces * steps, chunk, 0)
    for h in range(heads):
        span = slice(h * HD, (h + 1) * HD)
        acc[span, :] = acc[span, :] / stat[1, h : h + 1, :]
    out_ref[...] = jnp.transpose(acc[...])
    lse_ref[...] = stat[0] + jnp.log(jnp.maximum(stat[1], 1e-37))


def attend(q, qcode, kcode, kv_pieces):
    rows, width = q.shape
    heads = width // HD
    keys = kcode.shape[0]
    return pl.pallas_call(
        functools.partial(attend_kernel, len(kv_pieces), heads),
        out_shape=(jax.ShapeDtypeStruct((rows, width), F32), jax.ShapeDtypeStruct((8, rows), F32)),
        scratch_shapes=[
            pltpu.VMEM((heads, keys, 2 * HD), BF16),
            pltpu.VMEM((keys // STEP, width, STEP), BF16),
            pltpu.VMEM((heads, rows, 2 * HD), BF16),
            pltpu.VMEM((width, rows), F32),
            pltpu.VMEM((2, 8, rows), F32),
        ],
        compiler_params=pltpu.CompilerParams(vmem_limit_bytes=48 * 1024 * 1024),
        cost_estimate=pl.CostEstimate(
            flops=4 * rows * keys * width, bytes_accessed=4 * keys * width, transcendentals=rows * keys * heads
        ),
        name="attend",
    )(q, qcode, kcode, *kv_pieces)


def attend_back_kernel(pieces, heads, q_ref, qcode_ref, kcode_ref, dout_ref, lse_ref, delta_ref, *refs):
    kv_refs = refs[:pieces]
    dq_ref, dkv_ref = refs[pieces : pieces + 2]
    kaug, kturn, vals, qaug, qmask, domask, acc = refs[pieces + 2 :]
    width = heads * HD
    steps = kv_refs[0].shape[0] // STEP
    for n in range(pieces * steps):
        block = kv_refs[n // steps]
        rows = pl.ds((n % steps) * STEP, STEP)
        span = pl.ds(n * STEP, STEP)
        code = kcode_ref[span, :]
        for p in range(heads // 2):
            keys = block[rows, pair_lanes(p)]
            for h in (2 * p, 2 * p + 1):
                kaug[h, span, :] = jnp.where(lane_in_head(keys.shape, h), keys, code)
        kturn[n] = jnp.transpose(block[rows, :width])
        vals[span, :] = block[rows, width:]
    for p in range(heads // 2):
        part = q_ref[:, pair_lanes(p)]
        dpart = dout_ref[:, pair_lanes(p)]
        for h in (2 * p, 2 * p + 1):
            inside = lane_in_head(part.shape, h)
            qaug[h] = jnp.where(inside, part, qcode_ref[...])
            qmask[h] = jnp.where(inside, part, jnp.zeros_like(part))
            domask[h] = jnp.where(inside, dpart, jnp.zeros_like(dpart))
    acc[...] = jnp.zeros_like(acc)

    def chunk(i, carry):
        span = pl.ds(i * STEP, STEP)
        for p in range(heads // 2):
            dkey = dval = None
            for h in (2 * p, 2 * p + 1):
                scores = dot(kaug[h, span, :], qaug[h], NT)
                prob = jnp.exp(scores - lse_ref[h : h + 1, :])
                dprob = dot(vals[span, pair_lanes(p)], domask[h], NT)
                dscore = (prob * (dprob - delta_ref[h : h + 1, :])).astype(BF16)
                add_val = dot(prob.astype(BF16), domask[h])
                add_key = dot(dscore, qmask[h])
                dval = add_val if dval is None else dval + add_val
                dkey = add_key if dkey is None else dkey + add_key
                turn = slice(h * HD, (h + 1) * HD)
                acc[turn, :] += dot(kturn[i, turn, :], dscore)
            dkv_ref[i, :, pair_lanes(p)] = dkey.astype(BF16)
            dkv_ref[i, :, slice(width + p * 2 * HD, width + (p + 1) * 2 * HD)] = dval.astype(BF16)
        return carry

    lax.fori_loop(0, pieces * steps, chunk, 0)
    dq_ref[...] = (jnp.transpose(acc[...]) * (HD ** (-0.5))).astype(BF16)


def attend_back(q, qcode, kcode, dout, lse, delta, kv_pieces):
    rows, width = q.shape
    heads = width // HD
    keys = kcode.shape[0]
    return pl.pallas_call(
        functools.partial(attend_back_kernel, len(kv_pieces), heads),
        out_shape=(
            jax.ShapeDtypeStruct((rows, width), BF16),
            jax.ShapeDtypeStruct((keys // STEP, STEP, 2 * width), BF16),
        ),
        scratch_shapes=[
            pltpu.VMEM((heads, keys, 2 * HD), BF16),
            pltpu.VMEM((keys // STEP, width, STEP), BF16),
            pltpu.VMEM((keys, width), BF16),
            pltpu.VMEM((heads, rows, 2 * HD), BF16),
            pltpu.VMEM((heads, rows, 2 * HD), BF16),
            pltpu.VMEM((heads, rows, 2 * HD), BF16),
            pltpu.VMEM((width, rows), F32),
        ],
        compiler_params=pltpu.CompilerParams(vmem_limit_bytes=56 * 1024 * 1024),
        cost_estimate=pl.CostEstimate(
            flops=10 * rows * keys * width, bytes_accessed=8 * keys * width, transcendentals=rows * keys * heads
        ),
        name="attend_back",
    )(q, qcode, kcode, dout, lse, delta, *kv_pieces)


def after(block, *before):
    return lax.optimization_barrier((block,) + before)[0]


def per_device(
    tokens,
    segment_ids,
    lead_hours,
    qkv_weight,
    qv_bias,
    proj_weight,
    proj_bias,
    up_weight,
    up_bias,
    down_weight,
    down_bias,
    norm1_gain,
    norm1_bias,
    norm2_gain,
    norm2_bias,
    lead_weight,
    lead_bias,
    out_grad,
):
    grid = Grid()
    nz, nx, chips, sp = grid.nz, grid.nx, grid.chips, grid.sp
    core, y = grid.core, grid.y
    full_rows, width = tokens.shape
    rows = full_rows // 2
    part = norm1_gain.shape[0]
    at_home = core == y

    def split(array, axis, index):
        half = array.shape[axis] // 2
        first = lax.slice_in_dim(array, 0, half, axis=axis)
        second = lax.slice_in_dim(array, half, 2 * half, axis=axis)
        return jnp.where(index == 0, first, second), jnp.where(index == 0, second, first)

    def in_order(own, other, index):
        return jnp.where(index == 0, own, other), jnp.where(index == 0, other, own)

    vectors = [lead_weight, lead_bias, norm1_gain, norm1_bias, proj_bias, norm2_gain, norm2_bias, down_bias]
    n_vec = len(vectors)
    pack = jnp.concatenate(
        [
            jnp.stack(vectors),
            qv_bias.reshape(-1, part),
            up_bias.reshape(-1, part),
            segment_ids.astype(BF16).reshape(-1, part),
        ],
        axis=0,
    )
    n_qv, n_up = qv_bias.size // part, up_bias.size // part
    both = jnp.stack(in_order(pack, grid.cswap(pack), core))
    table = jnp.stack(grid.gather(both)).reshape(chips, -1)
    chip_of = grid.chip_order()
    in_place = (jnp.arange(chips)[:, None] == chip_of[None, :]).astype(BF16)
    table = dot(in_place, table).reshape(sp, -1, part)
    vecs = jnp.transpose(table[:, :n_vec], (1, 0, 2)).reshape(n_vec, width)
    heads_local = qv_bias.shape[1]
    qv_all = jnp.transpose(
        table[:, n_vec : n_vec + n_qv].reshape(sp, 2, heads_local, -1), (1, 2, 0, 3)
    ).reshape(2, heads_local * HD)
    up_all = jnp.transpose(
        table[:, n_vec + n_qv : n_vec + n_qv + n_up].reshape(sp, up_bias.shape[0], -1), (1, 0, 2)
    ).reshape(1, -1)
    up_full = split(up_all, 1, core)[0]
    qv_far = grid.yswap(qv_all)
    qv_mine = jnp.where(at_home, qv_all, qv_far).reshape(2, nz, -1)
    qv_full = pick(qv_mine, grid.z, 1)
    local = qv_full.shape[1]

    seg_rows = table[:, n_vec + n_qv + n_up :].reshape(sp * 2, rows)
    n_key = nx * 2 * 2 * nz
    n = jnp.arange(n_key)
    k, r, w, j = n % nz, (n // nz) % 2, (n // (2 * nz)) % 2, n // (4 * nz)
    key_at = ((grid.far_z(-k) * nx + grid.far_x(-j)) * 2 + (core + r) % 2) * 2 + (y + w) % 2
    take = (key_at[:, None] == jnp.arange(2 * sp)[None, :]).astype(BF16)
    key_seg = dot(take, seg_rows.astype(BF16)).astype(jnp.int32).reshape(-1)
    query_seg = key_seg[: 2 * nz * rows]
    lanes = jnp.arange(2 * HD, dtype=jnp.int32) % HD
    kcode = jnp.where(key_seg[:, None] == lanes[None, :], 0.0, EXCLUDED).astype(BF16)
    qcode = (query_seg[:, None] == lanes[None, :]).astype(BF16)

    shard = jnp.transpose(qkv_weight.reshape(3, part, nz, -1), (2, 1, 0, 3)).reshape(nz, part, -1)
    wq_z = [pick(shard, grid.z, 0)] + [grid.zshift(pick(shard, grid.far_z(k), 0), k) for k in range(1, nz)]

    own_tokens = split(tokens, 0, y)[0]
    token_z = jnp.concatenate([own_tokens] + [grid.zshift(own_tokens, k) for k in range(1, nz)])
    tokens_all = jnp.concatenate([token_z, grid.cswap(token_z)])

    wq_z = jnp.stack(wq_z)
    wq_x = jnp.stack([wq_z] + [grid.xshift(wq_z, j) for j in range(1, nx)])
    wq_spin, wq_cross = grid.spin(wq_x), grid.cross(wq_x)
    wq_same = jnp.where(at_home, wq_x, wq_spin)
    wq_other = jnp.where(at_home, wq_spin, wq_cross)
    starts, pieces = [], []
    for p, block in ((core, wq_same), (1 - core, wq_other)):
        for j in range(nx):
            for k in range(nz):
                starts.append(((grid.far_z(-k) * nx + grid.far_x(-j)) * 2 + p) * part)
                pieces.append(block[j, k])
    w_qkv = place(pieces, starts, 0)

    choose = query_seg[:, None] == jnp.arange(lead_hours.shape[0], dtype=jnp.int32)[None, :]
    lead_time = jnp.sum(jnp.where(choose, lead_hours[None, :], 0.0), axis=1)
    embedded_all = tokens_all.astype(F32) + lead_time[:, None] * vecs[0] + vecs[1]
    embedded = embedded_all[:rows]
    n1_all, s1_all = normalize(embedded_all)
    n1, s1 = n1_all[:rows], s1_all[:rows]
    normed_one = (n1_all * vecs[2] + vecs[3]).astype(BF16)
    qkv = dot(normed_one, w_qkv)
    q = (qkv[:, :local] + qv_full[0]).astype(BF16) * jnp.asarray(HD ** (-0.5), BF16)
    kv = jnp.concatenate([qkv[:, local : 2 * local], qkv[:, 2 * local :] + qv_full[1]], axis=1).astype(BF16)
    kv_far = grid.yswap(kv)
    kv_pieces = [kv, kv_far]
    for j in range(1, nx):
        kv_pieces += [grid.xshift(kv, j), grid.xshift(kv_far, j)]

    def spread(shard):
        keep, send = split(shard, 1, core)
        return jnp.concatenate(in_order(keep, grid.cswap(send), core), axis=0)

    chip_starts = [chip_of[i] * (2 * part) for i in range(chips)]
    w_up = place(grid.gather(spread(up_weight)), chip_starts, 0)
    w_down = place(grid.gather(spread(jnp.transpose(down_weight))), chip_starts, 0)

    wp = grid.gather(jnp.transpose(proj_weight))
    wp_half = jnp.concatenate(wp)
    wp_rows = jnp.concatenate(in_order(wp_half, grid.yswap(wp_half), y), axis=1)
    wp_far = grid.cswap(wp_rows)
    starts, pieces = [], []
    for p, block in ((core, wp_rows), (1 - core, wp_far)):
        for i in range(chips):
            starts.append((chip_of[i] * 2 + p) * part)
            pieces.append(block[i * part : (i + 1) * part])
    w_proj = place(pieces, starts, 0)

    attn_full, lse = attend(q, qcode, kcode, kv_pieces)
    blocks = attn_full.astype(BF16).reshape(2, nz, rows, local)
    home = jnp.stack([blocks[:, 0]] + [grid.zshift(blocks[:, k], -k) for k in range(1, nz)])
    home_far = grid.cswap(home[:, 1])
    starts, pieces = [], []
    for c, block in ((core, home[:, 0]), (1 - core, home_far)):
        for k in range(nz):
            starts.append((c * nz + grid.far_z(k)) * local)
            pieces.append(block[k])
    attn_out = place(pieces, starts, 1)

    def all_four(block):
        two = jnp.concatenate([block, grid.yswap(block)], axis=0)
        return jnp.concatenate([two, grid.cswap(two)], axis=0)

    def sum_four(partial):
        half = partial[: 2 * rows] + grid.cswap(partial[2 * rows :].astype(BF16)).astype(F32)
        return half[:rows] + grid.yswap(half[rows:].astype(BF16)).astype(F32)

    middle = embedded + (dot(attn_out, w_proj, NT) + vecs[4])
    n2, s2 = normalize(middle)
    normed_two = all_four((n2 * vecs[5] + vecs[6]).astype(BF16))
    gz_own, gz_far = split(out_grad, 0, y)
    gz_two = jnp.concatenate([gz_own, gz_far], axis=0)
    gz = jnp.concatenate([gz_two, grid.cswap(gz_two)], axis=0)
    hidden = dot(normed_two, w_up) + up_full
    cdf = 0.5 * (1.0 + lax.erf(hidden * (0.5**0.5)))
    active = (hidden * cdf).astype(BF16)
    slope = cdf + hidden * (jnp.exp(-0.5 * hidden * hidden) * ((0.5 / jnp.pi) ** 0.5))
    grad_hidden = (dot(gz, w_down) * slope).astype(BF16)
    grad_n2 = sum_four(dot(grad_hidden, w_up, NT))
    block_out = (middle + (sum_four(dot(active, w_down, NT)) + vecs[7])).astype(BF16)
    block_out = jnp.concatenate(in_order(block_out, grid.yswap(block_out), y), axis=0)

    def give(gradient):
        mine = grid.scatter(gradient.astype(BF16).reshape(nz, nx, 2 * part, -1))
        keep, send = split(mine, 0, core)
        other = grid.cswap(send.astype(BF16)).astype(F32)
        return jnp.concatenate(in_order(keep, other, core), axis=1)

    d_up = give(dot(normed_two, grad_hidden, TN))
    d_down = give(dot(gz, active, TN))

    grad_top = gz_own.astype(F32)
    grad_middle = grad_top + norm_back(n2, s2, vecs[5], grad_n2)
    grad_branch = grad_middle.astype(BF16)
    grad_attn = dot(grad_branch, w_proj).astype(BF16)
    near, send = split(grad_attn, 1, core)
    far = grid.cswap(send)
    pair = jnp.stack([near, far]).reshape(2, rows, nz, local)
    d_out = jnp.stack(
        [pick(pair, grid.z, 2)] + [grid.zshift(pick(pair, grid.far_z(k), 2), k) for k in range(1, nz)], axis=1
    ).reshape(2 * nz * rows, local)
    delta = jnp.sum((d_out.astype(F32) * attn_full).reshape(2 * nz * rows, -1, HD), axis=2)
    delta = jnp.pad(jnp.transpose(delta), ((0, 8 - delta.shape[1]), (0, 0)))
    grad_q, grad_kv_all = attend_back(q, qcode, kcode, d_out, lse, delta, kv_pieces)
    grad_kv_all = grad_kv_all.reshape(nx, 2, 2 * nz * rows, 2 * local)
    two = grad_kv_all[0].astype(F32)
    for j in range(1, nx):
        two = two + grid.xshift(grad_kv_all[j], -j).astype(F32)
    grad_kv = (two[0] + grid.yswap(two[1].astype(BF16)).astype(F32)).astype(BF16)
    grad_stack = jnp.concatenate([grad_q, grad_kv], axis=1)

    part_n1 = dot(grad_stack, w_qkv, NT).astype(BF16)
    part_n1 = (part_n1[: nz * rows].astype(F32) + grid.cswap(part_n1[nz * rows :]).astype(F32)).reshape(nz, rows, width)
    low = part_n1.astype(BF16)
    grad_n1 = part_n1[0]
    for k in range(1, nz):
        grad_n1 = grad_n1 + grid.zshift(low[k], -k).astype(F32)

    dp = dot(grad_branch, attn_out, TN).astype(BF16).reshape(chips, 2, part, 2, -1)
    dp = pick(dp, core, 1).astype(F32) + grid.cswap(pick(dp, 1 - core, 1)).astype(F32)
    dp_low = dp.astype(BF16)
    dp = pick(dp, y, 2) + grid.yswap(pick(dp_low, 1 - y, 2)).astype(F32)
    d_proj = grid.scatter(dp.astype(BF16).reshape(nz, nx, part, -1))

    dw = dot(normed_one, grad_stack, TN).astype(BF16).reshape(nz, nx, 2, part, -1)
    dw_same, dw_other = pick(dw, core, 2), pick(dw, 1 - core, 2)
    from_spin = grid.spin(jnp.where(at_home, dw_other, dw_same), back=True)
    from_cross = grid.cross(dw_other)
    dw = from_spin.astype(F32) + jnp.where(at_home, dw_same, from_cross).astype(F32)
    dw_low = dw.astype(BF16)
    dw = pick(dw, grid.x, 1)
    for j in range(1, nx):
        dw = dw + grid.xshift(pick(dw_low, grid.far_x(j), 1), j).astype(F32)
    dw = dw.astype(BF16)
    dw_pieces = [pick(dw, grid.z, 0)] + [grid.zshift(pick(dw, grid.far_z(k), 0), k) for k in range(1, nz)]
    g_qkv = place_qkv(dw_pieces, [grid.far_z(-k) * local for k in range(nz)])

    input_grad = grad_middle + norm_back(n1, s1, vecs[2], grad_n1)
    lead_own = lead_time[:rows, None]
    sums = jnp.stack(
        [
            jnp.sum(input_grad * lead_own, axis=0),
            jnp.sum(input_grad, axis=0),
            jnp.sum(grad_n1 * n1, axis=0),
            jnp.sum(grad_n1, axis=0),
            jnp.sum(grad_branch.astype(F32), axis=0),
            jnp.sum(grad_n2 * n2, axis=0),
            jnp.sum(grad_n2, axis=0),
            jnp.sum(grad_top, axis=0),
        ]
    )
    sums = sums + grid.yswap(sums)
    sums = sums + grid.cswap(sums)
    sums = grid.scatter(jnp.transpose(sums.reshape(n_vec, nz, nx, 2 * part), (1, 2, 0, 3)))
    sums = split(sums, 1, core)[0]

    up_sum = jnp.sum(grad_hidden.astype(F32), axis=0)
    stack_sum = jnp.sum(grad_stack.astype(F32), axis=0)
    qv_sum = jnp.concatenate([stack_sum[:local], stack_sum[2 * local :]])
    qv_sum = qv_sum + grid.yswap(qv_sum)
    bias = jnp.concatenate([up_sum, qv_sum])
    bias_x = bias
    for j in range(1, nx):
        bias_x = bias_x + grid.xshift(bias, j)
    bias_z = jnp.stack([bias_x] + [grid.zshift(bias_x, k) for k in range(1, nz)])
    n_hidden = grad_hidden.shape[1]
    up_sum = jnp.sum(bias_z[:, :n_hidden], axis=0)
    to_z = (jnp.arange(nz)[:, None] == grid.far_z(-jnp.arange(nz))[None, :]).astype(F32)
    qv_sum = jnp.sum(to_z[:, :, None] * bias_z[None, :, n_hidden:], axis=1)
    bias = jnp.concatenate([up_sum, qv_sum.reshape(-1)])
    bias_far = grid.cswap(bias)
    up_sum = jnp.concatenate(in_order(bias[:n_hidden], bias_far[:n_hidden], core)).reshape(-1, HD)
    qv_sum = jnp.where(at_home, bias[n_hidden:], bias_far[n_hidden:]).reshape(nz, 2, -1, HD)
    qv_sum = jnp.transpose(qv_sum, (1, 0, 2, 3)).reshape(2, -1, HD)
    each = HD // sp
    g_up_bias = lax.dynamic_slice_in_dim(up_sum, grid.me * each, each, 1)
    g_qv_bias = lax.dynamic_slice_in_dim(qv_sum, grid.me * each, each, 2)

    input_grad = input_grad.astype(BF16)
    input_grad = jnp.concatenate(in_order(input_grad, grid.yswap(input_grad), y), axis=0).astype(F32)
    return (
        block_out,
        input_grad,
        g_qkv,
        g_qv_bias,
        jnp.transpose(d_proj),
        sums[4],
        d_up,
        g_up_bias,
        jnp.transpose(d_down),
        sums[7],
        sums[2],
        sums[3],
        sums[5],
        sums[6],
        sums[0],
        sums[1],
    )


def solution(mesh):
    placed = (
        P("sp", None),
        P("sp"),
        P(),
        P(None, "sp", "tp"),
        P(None, "tp", "sp"),
        P("tp", "sp"),
        P("sp"),
        P("sp", "tp"),
        P("tp", "sp"),
        P("tp", "sp"),
        P("sp"),
        P("sp"),
        P("sp"),
        P("sp"),
        P("sp"),
        P("sp"),
        P("sp"),
        P("sp", None),
    )
    return jax.shard_map(
        per_device,
        mesh=mesh,
        in_specs=placed,
        out_specs=(
            P("sp", None),
            P("sp", None),
            P(None, "sp", "tp"),
            P(None, "tp", "sp"),
            P("tp", "sp"),
            P("sp"),
            P("sp", "tp"),
            P("tp", "sp"),
            P("tp", "sp"),
            P("sp"),
            P("sp"),
            P("sp"),
            P("sp"),
            P("sp"),
            P("sp"),
            P("sp"),
        ),
        check_vma=False,
    )
```

time: 471 us -> 422 us (0.90)
  waiting for transfers between devices: 239 us -> 151 us
  starting transfers between devices: 109 us -> 123 us
  between operations: 2.43 us -> 12.9 us
  local copies, waits for them, and re-layouts: 31.3 us -> 41.3 us
    ppermute x89 -> x88, waiting for transfers between devices: 213 us -> 105 us  [_move(): return lax.ppermute(block, 'sp', pairs)]
    ppermute x4 -> x12, waiting for transfers between devices: 26 us -> 39.3 us  [yswap(): return lax.ppermute(block, 'tp', [(0, 1), (1, 0)])]
    concatenate x11 -> x3, local copies, waits for them, and re-layouts: 10.9 us -> 1.52 us  [the longest x1 0.83 us: per_device(): jnp.concatenate([jnp.stack(vectors), qv_bias.reshape(-1, part), up_bias.r...]
    unnamed x108 -> x162, local copies, waits for them, and re-layouts: 5.69 us -> 13.2 us
    ppermute x0 -> x4, waiting for transfers between devices: none -> 7.27 us  [the longest x2 7.27 us: spin(): return lax.ppermute(block, ('sp', 'tp'), self._pairs(route))]
    ppermute x0 -> x4, starting transfers between devices: none -> 6.27 us  [the longest x2 3.87 us: spin(): return lax.ppermute(block, ('sp', 'tp'), self._pairs(route))]
    reshape x12, local copies, waits for them, and re-layouts: 0.91 us -> 6.33 us  [the longest x1 3.31 us: per_device(): dot(grad_branch, attn_out, TN).astype(BF16).reshape(chips, 2, part, 2, -1)]
    ppermute x4 -> x12, starting transfers between devices: 5.33 us -> 9.92 us  [yswap(): return lax.ppermute(block, 'tp', [(0, 1), (1, 0)])]
  transfers between devices with their start and end apart: 93 -> 104, of which waited for: 44 -> 39; matrix products, arithmetic and copies ran while one was open for 14% -> 19% of each run, Pallas kernels for 7% -> 9%
where the time goes in v2:
time: 422 us; the launch traced here: 417 us
  waiting for transfers between devices  151 us (36%)
  starting transfers between devices  123 us (29%)
  local copies, waits for them, and re-layouts  41.3 us (10%)
  Pallas kernels  36.7 us (9%)
  other arithmetic  33.8 us (8%)
  matrix products  17.4 us (4%)
  between operations  12.9 us (3%)
    ppermute x88, starting transfers between devices, _move(): return lax.ppermute(block, 'sp', pairs)  107 us
    ppermute x88, waiting for transfers between devices, _move(): return lax.ppermute(block, 'sp', pairs)  105 us
    ppermute x12, waiting for transfers between devices, yswap(): return lax.ppermute(block, 'tp', [(0, 1), (1, 0)])  39.3 us
    dot_general x14, matrix products, dot(): return lax.dot_general(left, right, dims, preferred_element_type=F32)  17.4 us
    pallas_call x1, Pallas kernels, attend_back(): pl.pallas_call(functools.partial(attend_back_kernel, len(kv_pieces), head...  17.3 us
    unnamed x162, local copies, waits for them, and re-layouts  13.2 us
    pallas_call x1, Pallas kernels, attend(): pl.pallas_call(functools.partial(attend_kernel, len(kv_pieces), heads), o...  12.9 us
    ppermute x12, starting transfers between devices, yswap(): return lax.ppermute(block, 'tp', [(0, 1), (1, 0)])  9.92 us
  transfers between devices with their start and end apart: 104, of which 39 were waited for; matrix products, arithmetic and copies ran while one was open for 19% of the time, Pallas kernels for 9%

profile of v2, /device:TPU:0, one launch (start us, length us, event | category | flops | bytes accessed | tf_op | source)
XLA Modules:
  0.0 416.6 jit_solution(14016558101002842151)
XLA Ops:
  4.6 4.7 %collective-permute-start.31 = (bf16[64,512]{1,0:T(8,128)(2,1)}, bf16[64,512]{1,0:T(8,128)(2,1)}, u32[]{:S(2)}, u32[]{:S(2)}) collective-permute-start(bf16[64,512]{1,0:T(8,128)(2,1)} %bitcast.105), channel_id=1, source_target_pairs={{0,24},{2,26},{4,28},{6,30},{8,0},{10,2},{12,4},{14,6},{16,8},{18,... | collective-permute-start | bytes 196616 | tf_op jit(solution)/shard_map/ppermute | solution.py:43
  28.9 3.0 collective-permute-start.29
  37.4 2.1 select_convert_fusion.kcode_ref
  42.2 2.6 collective-permute-start.27
  55.2 2.1 collective-permute-done.28
  68.0 3.4 collective-permute-start.16
  71.4 2.6 collective-permute-start.51
  74.5 6.5 %collective-permute-done.16 = bf16[2,4,64,384]{3,2,1,0:T(8,128)(2,1)S(1)} collective-permute-done((bf16[2,4,64,384]{3,2,1,0:T(8,128)(2,1)S(1)}, bf16[2,4,64,384]{3,2,1,0:T(8,128)(2,1)S(1)}, u32[]{:S(2)}, u32[]{:S(2)}) %collective-permute-start.16) | collective-permute-done | bytes 393248 | tf_op jit(solution)/shard_map/ppermute | solution.py:70
  81.0 2.5 collective-permute-start.3
  84.4 7.8 %collective-permute-done.33 = bf16[512,512]{1,0:T(8,128)(2,1)S(1)} collective-permute-done((bf16[512,512]{1,0:T(8,128)(2,1)S(1)}, bf16[512,512]{1,0:T(8,128)(2,1)S(1)}, u32[]{:S(2)}, u32[]{:S(2)}) %collective-permute-start.33) | collective-permute-done | bytes 524320 | tf_op jit(solution)/shard_map/ppermute | solution.py:55
  97.7 9.4 %collective-permute-done.19.refs_1_ = bf16[768,256]{1,0:T(8,128)(2,1)S(1)} collective-permute-done((bf16[768,256]{1,0:T(8,128)(2,1)S(1)}, bf16[768,256]{1,0:T(8,128)(2,1)S(1)}, u32[]{:S(2)}, u32[]{:S(2)}) %collective-permute-start.19) | collective-permute-done | bytes 393248 | tf_op jit(solution)/shard_map/ppermute | solution.py:55
  108.3 2.4 subtract_multiply_fusion
  114.0 5.2 %collective-permute-done.21.refs_3_ = bf16[768,256]{1,0:T(8,128)(2,1)S(1)} collective-permute-done((bf16[768,256]{1,0:T(8,128)(2,1)S(1)}, bf16[768,256]{1,0:T(8,128)(2,1)S(1)}, u32[]{:S(2)}, u32[]{:S(2)}) %collective-permute-start.21) | collective-permute-done | bytes 393248 | tf_op jit(solution)/shard_map/ppermute | solution.py:43
  119.2 12.9 %attend.1 = (f32[768,128]{1,0:T(8,128)S(1)}, f32[8,768]{1,0:T(8,128)S(1)}) custom-call(bf16[768,128]{1,0:T(8,128)(2,1)S(1)} %get-tuple-element.99.q_ref, bf16[768,128]{1,0:T(8,128)(2,1)S(1)} %compare_convert_fusion.qcode_ref, bf16[3072,128]{1,0:T(8,128)(2,1)S(1)} %copy-done.2, bf16[768,256]{1,0:T(8,128)(2,1)S(1)} %pad_maximum_fusion.7.refs_0_, ...), custom_call_target="tpu_custom_call" | custom-call | flops 1207959552 | bytes 1572864 | tf_op jit(solution)/shard_map/attend/pallas_call | solution.py:226
  133.5 4.6 %collective-permute-done.24 = bf16[2,96,128]{2,1,0:T(8,128)(2,1)S(1)} collective-permute-done((bf16[2,96,128]{2,1,0:T(8,128)(2,1)S(1)}, bf16[2,96,128]{2,1,0:T(8,128)(2,1)S(1)}, u32[]{:S(2)}, u32[]{:S(2)}) %collective-permute-start.24) | collective-permute-done | bytes 49184 | tf_op jit(solution)/shard_map/ppermute | solution.py:43
  139.6 3.6 collective-permute-done.23
  143.9 3.3 collective-permute-done.22
  148.7 2.5 collective-permute-start.43
  162.4 11.6 %collective-permute-done.41.refs_4_ = bf16[128,1024]{1,0:T(8,128)(2,1)S(1)} collective-permute-done((bf16[128,1024]{1,0:T(8,128)(2,1)S(1)}, bf16[128,1024]{1,0:T(8,128)(2,1)S(1)}, u32[]{:S(2)}, u32[]{:S(2)}) %collective-permute-start.41) | collective-permute-done | bytes 262176 | tf_op jit(solution)/shard_map/ppermute | solution.py:43
  192.9 3.1 collective-permute-done.42.refs_5_
  196.1 4.5 %collective-permute-done.40.refs_3_ = bf16[128,1024]{1,0:T(8,128)(2,1)} collective-permute-done((bf16[128,1024]{1,0:T(8,128)(2,1)}, bf16[128,1024]{1,0:T(8,128)(2,1)}, u32[]{:S(2)}, u32[]{:S(2)}) %collective-permute-start.40) | collective-permute-done | bytes 262176 | tf_op jit(solution)/shard_map/ppermute | solution.py:43
  202.0 2.1 multiply_convert_fusion
  205.2 2.3 convert_reduce_fusion
  213.4 2.3 convolution_convert_fusion.1
  220.2 5.6 %collective-permute-done.58 = bf16[96,1024]{1,0:T(8,128)(2,1)S(1)} collective-permute-done((bf16[96,1024]{1,0:T(8,128)(2,1)S(1)}, bf16[96,1024]{1,0:T(8,128)(2,1)S(1)}, u32[]{:S(2)}, u32[]{:S(2)}) %collective-permute-start.58) | collective-permute-done | bytes 196640 | tf_op jit(solution)/shard_map/ppermute | solution.py:55
  226.1 2.4 collective-permute-done.54
  229.9 2.1 convolution_convert_fusion.2
  232.1 3.3 reshape.538
  235.6 2.1 collective-permute-start.61
  237.7 9.9 %collective-permute-start.60 = (bf16[2,96,128]{2,1,0:T(8,128)(2,1)S(1)}, bf16[2,96,128]{2,1,0:T(8,128)(2,1)S(1)}, u32[]{:S(2)}, u32[]{:S(2)}) collective-permute-start(bf16[2,96,128]{2,1,0:T(8,128)(2,1)S(1)} %get-tuple-element.168), channel_id=1, source_target_pairs={{0,8},{2,10},{4,12},{6,14},{8,16},{10,18},{12,20},{14,22},{16,24},... | collective-permute-start | bytes 147464 | tf_op jit(solution)/shard_map/ppermute | solution.py:43
  247.7 2.5 constant_dynamic-slice_fusion.6
  253.2 17.3 %attend_back.1 = (bf16[768,128]{1,0:T(8,128)(2,1)}, bf16[8,384,256]{2,1,0:T(8,128)(2,1)}) custom-call(bf16[768,128]{1,0:T(8,128)(2,1)} %copy-done.10, bf16[768,128]{1,0:T(8,128)(2,1)} %copy-done.11, bf16[3072,128]{1,0:T(8,128)(2,1)} %select_convert_fusion.kcode_ref, bf16[768,128]{1,0:T(8,128)(2,1)} %bitcast.391, f32[8,768]{1,0:T(8,128)} %copy-done.15, ...), custom_call_target="tpu_custom_call" | custom-call | flops 3019898880 | bytes 3145728 | tf_op jit(solution)/shard_map/attend_back/pallas_call | solution.py:298
  277.4 3.7 collective-permute-start.102
  282.8 5.4 %collective-permute-done.100 = bf16[128,1024]{1,0:T(8,128)(2,1)S(1)} collective-permute-done((bf16[128,1024]{1,0:T(8,128)(2,1)S(1)}, bf16[128,1024]{1,0:T(8,128)(2,1)S(1)}, u32[]{:S(2)}, u32[]{:S(2)}) %collective-permute-start.100) | collective-permute-done | bytes 262176 | tf_op jit(solution)/shard_map/ppermute | solution.py:43
  288.2 7.9 %collective-permute-start.95 = (bf16[128,1024]{1,0:T(8,128)(2,1)S(1)}, bf16[128,1024]{1,0:T(8,128)(2,1)S(1)}, u32[]{:S(2)}, u32[]{:S(2)}) collective-permute-start(bf16[128,1024]{1,0:T(8,128)(2,1)S(1)} %get-tuple-element.103), channel_id=1, source_target_pairs={{0,8},{2,10},{4,12},{6,14},{8,16},{10,18},{12,20},{14,22},{16,24},... | collective-permute-start | bytes 786440 | tf_op jit(solution)/shard_map/ppermute | solution.py:43
  296.1 14.7 %collective-permute-done.101 = bf16[128,1024]{1,0:T(8,128)(2,1)S(1)} collective-permute-done((bf16[128,1024]{1,0:T(8,128)(2,1)S(1)}, bf16[128,1024]{1,0:T(8,128)(2,1)S(1)}, u32[]{:S(2)}, u32[]{:S(2)}) %collective-permute-start.101) | collective-permute-done | bytes 262176 | tf_op jit(solution)/shard_map/ppermute | solution.py:43
  311.7 14.1 %collective-permute-done.96 = bf16[128,1024]{1,0:T(8,128)(2,1)S(1)} collective-permute-done((bf16[128,1024]{1,0:T(8,128)(2,1)S(1)}, bf16[128,1024]{1,0:T(8,128)(2,1)S(1)}, u32[]{:S(2)}, u32[]{:S(2)}) %collective-permute-start.96) | collective-permute-done | bytes 262176 | tf_op jit(solution)/shard_map/ppermute | solution.py:43
  329.8 9.1 %collective-permute-done.64 = bf16[768,256]{1,0:T(8,128)(2,1)S(1)} collective-permute-done((bf16[768,256]{1,0:T(8,128)(2,1)S(1)}, bf16[768,256]{1,0:T(8,128)(2,1)S(1)}, u32[]{:S(2)}, u32[]{:S(2)}) %collective-permute-start.64) | collective-permute-done | bytes 393248 | tf_op jit(solution)/shard_map/ppermute | solution.py:55
  350.3 2.1 collective-permute-done.79
  357.6 2.2 collective-permute-start.65
  370.6 2.4 collective-permute-done.66
  373.0 4.9 %collective-permute-done.68 = bf16[96,1024]{1,0:T(8,128)(2,1)S(1)} collective-permute-done((bf16[96,1024]{1,0:T(8,128)(2,1)S(1)}, bf16[96,1024]{1,0:T(8,128)(2,1)S(1)}, u32[]{:S(2)}, u32[]{:S(2)}) %collective-permute-start.68) | collective-permute-done | bytes 196640 | tf_op jit(solution)/shard_map/ppermute | solution.py:43
  377.9 8.5 %collective-permute-done.67 = bf16[96,1024]{1,0:T(8,128)(2,1)S(1)} collective-permute-done((bf16[96,1024]{1,0:T(8,128)(2,1)S(1)}, bf16[96,1024]{1,0:T(8,128)(2,1)S(1)}, u32[]{:S(2)}, u32[]{:S(2)}) %collective-permute-start.67) | collective-permute-done | bytes 196640 | tf_op jit(solution)/shard_map/ppermute | solution.py:43
  389.6 3.8 collective-permute-start.87
  396.7 2.2 collective-permute-start.75
  398.9 2.5 collective-permute-start.74
  402.5 2.9 collective-permute-start.93
  412.0 3.4 collective-permute-done.69
  (549 shorter events, 161.1 us)
Async XLA Ops:
  4.1 12.8 %collective-permute-start.4 = (bf16[14,64]{1,0:T(8,128)(2,1)S(1)}, bf16[14,64]{1,0:T(8,128)(2,1)S(1)}, u32[]{:S(2)}, u32[]{:S(2)}) collective-permute-start(bf16[14,64]{1,0:T(8,128)(2,1)S(1)} %concatenate.72), channel_id=1, source_target_pairs={{0,2},{2,0},{4,6},{6,4},{8,10},{10,8},{12,14},{14,12},{16,18},{18,... | collective-permute-start | bytes 5384 | tf_op jit(solution)/shard_map/ppermute | solution.py:43
  4.6 55.6 %collective-permute-start.31 = (bf16[64,512]{1,0:T(8,128)(2,1)}, bf16[64,512]{1,0:T(8,128)(2,1)}, u32[]{:S(2)}, u32[]{:S(2)}) collective-permute-start(bf16[64,512]{1,0:T(8,128)(2,1)} %bitcast.105), channel_id=1, source_target_pairs={{0,24},{2,26},{4,28},{6,30},{8,0},{10,2},{12,4},{14,6},{16,8},{18,... | collective-permute-start | bytes 196616 | tf_op jit(solution)/shard_map/ppermute | solution.py:43
  28.9 25.4 %collective-permute-start.29 = (bf16[64,512]{1,0:T(8,128)(2,1)}, bf16[64,512]{1,0:T(8,128)(2,1)S(1)}, u32[]{:S(2)}, u32[]{:S(2)}) collective-permute-start(bf16[64,512]{1,0:T(8,128)(2,1)} %bitcast.105), channel_id=1, source_target_pairs={{0,16},{2,18},{4,20},{6,22},{8,24},{10,26},{12,28},{14,30},{16,0},... | collective-permute-start | bytes 196616 | tf_op jit(solution)/shard_map/ppermute | solution.py:43
  49.3 24.8 %collective-permute-start.2 = (bf16[96,1024]{1,0:T(8,128)(2,1)S(1)}, bf16[96,1024]{1,0:T(8,128)(2,1)S(1)}, u32[]{:S(2)}, u32[]{:S(2)}) collective-permute-start(bf16[96,1024]{1,0:T(8,128)(2,1)S(1)} %get-tuple-element.89), channel_id=1, source_target_pairs={{0,24},{2,26},{4,28},{6,30},{8,0},{10,2},{12,4},{14,6},{16,8},{18,... | collective-permute-start | bytes 589832 | tf_op jit(solution)/shard_map/ppermute | solution.py:43
  51.1 20.3 %collective-permute-start.1 = (bf16[96,1024]{1,0:T(8,128)(2,1)S(1)}, bf16[96,1024]{1,0:T(8,128)(2,1)S(1)}, u32[]{:S(2)}, u32[]{:S(2)}) collective-permute-start(bf16[96,1024]{1,0:T(8,128)(2,1)S(1)} %get-tuple-element.89), channel_id=1, source_target_pairs={{0,16},{2,18},{4,20},{6,22},{8,24},{10,26},{12,28},{14,30},{16,0},... | collective-permute-start | bytes 589832 | tf_op jit(solution)/shard_map/ppermute | solution.py:43
  54.3 13.8 %collective-permute-start = (bf16[96,1024]{1,0:T(8,128)(2,1)S(1)}, bf16[96,1024]{1,0:T(8,128)(2,1)S(1)}, u32[]{:S(2)}, u32[]{:S(2)}) collective-permute-start(bf16[96,1024]{1,0:T(8,128)(2,1)S(1)} %get-tuple-element.89), channel_id=1, source_target_pairs={{0,8},{2,10},{4,12},{6,14},{8,16},{10,18},{12,20},{14,22},{16,24},... | collective-permute-start | bytes 589832 | tf_op jit(solution)/shard_map/ppermute | solution.py:43
  66.5 29.4 %collective-permute-start.37 = (bf16[64,1024]{1,0:T(8,128)(2,1)}, bf16[64,1024]{1,0:T(8,128)(2,1)S(1)}, u32[]{:S(2)}, u32[]{:S(2)}) collective-permute-start(bf16[64,1024]{1,0:T(8,128)(2,1)} %broadcast_select_fusion.16), channel_id=1, source_target_pairs={{0,2},{2,0},{4,6},{6,4},{8,10},{10,8},{12,14},{14,12},{16,18},{18,... | collective-permute-start | bytes 393224 | tf_op jit(solution)/shard_map/ppermute | solution.py:43
  68.0 12.9 %collective-permute-start.16 = (bf16[2,4,64,384]{3,2,1,0:T(8,128)(2,1)S(1)}, bf16[2,4,64,384]{3,2,1,0:T(8,128)(2,1)S(1)}, u32[]{:S(2)}, u32[]{:S(2)}) collective-permute-start(bf16[2,4,64,384]{3,2,1,0:T(8,128)(2,1)S(1)} %pad_maximum_fusion.6), channel_id=1, source_target_pairs={{0,1},{2,0},{3,2},{1,3},{4,5},{6,4},{7,6},{5,7},{8,9},{10,8},{11,1... | collective-permute-start | bytes 1179656 | tf_op jit(solution)/shard_map/ppermute | solution.py:70
  71.4 81.7 %collective-permute-start.51 = (bf16[128,1024]{1,0:T(8,128)(2,1)S(1)}, bf16[128,1024]{1,0:T(8,128)(2,1)S(1)}, u32[]{:S(2)}, u32[]{:S(2)}) collective-permute-start(bf16[128,1024]{1,0:T(8,128)(2,1)S(1)} %pad_maximum_fusion.16.refs_0_), channel_id=1, source_target_pairs={{0,24},{2,26},{4,28},{6,30},{8,0},{10,2},{12,4},{14,6},{16,8},{18,... | collective-permute-start | bytes 786440 | tf_op jit(solution)/shard_map/ppermute | solution.py:43
  74.1 18.1 %collective-permute-start.33 = (bf16[512,512]{1,0:T(8,128)(2,1)S(1)}, bf16[512,512]{1,0:T(8,128)(2,1)S(1)}, u32[]{:S(2)}, u32[]{:S(2)}) collective-permute-start(bf16[512,512]{1,0:T(8,128)(2,1)S(1)} %copy-done.40), channel_id=1, source_target_pairs={{0,1},{1,0},{2,3},{3,2},{4,5},{5,4},{6,7},{7,6},{8,9},{9,8},{10,11... | collective-permute-start | bytes 1572872 | tf_op jit(solution)/shard_map/ppermute | solution.py:55
  74.2 79.9 %collective-permute-start.49 = (bf16[128,1024]{1,0:T(8,128)(2,1)S(1)}, bf16[128,1024]{1,0:T(8,128)(2,1)}, u32[]{:S(2)}, u32[]{:S(2)}) collective-permute-start(bf16[128,1024]{1,0:T(8,128)(2,1)S(1)} %pad_maximum_fusion.16.refs_0_), channel_id=1, source_target_pairs={{0,16},{2,18},{4,20},{6,22},{8,24},{10,26},{12,28},{14,30},{16,0},... | collective-permute-start | bytes 786440 | tf_op jit(solution)/shard_map/ppermute | solution.py:43
  81.0 11.5 %collective-permute-start.3 = (bf16[384,1024]{1,0:T(8,128)(2,1)S(1)}, bf16[384,1024]{1,0:T(8,128)(2,1)S(1)}, u32[]{:S(2)}, u32[]{:S(2)}) collective-permute-start(bf16[384,1024]{1,0:T(8,128)(2,1)S(1)} %pad_maximum_fusion.1), channel_id=1, source_target_pairs={{0,2},{2,0},{4,6},{6,4},{8,10},{10,8},{12,14},{14,12},{16,18},{18,... | collective-permute-start | bytes 2359304 | tf_op jit(solution)/shard_map/ppermute | solution.py:43
  92.4 18.3 %collective-permute-start.34 = (bf16[512,1024]{1,0:T(8,128)(2,1)S(1)}, bf16[512,1024]{1,0:T(8,128)(2,1)S(1)}, u32[]{:S(2)}, u32[]{:S(2)}) collective-permute-start(bf16[512,1024]{1,0:T(8,128)(2,1)S(1)} %pad_maximum_fusion), channel_id=1, source_target_pairs={{0,2},{2,0},{4,6},{6,4},{8,10},{10,8},{12,14},{14,12},{16,18},{18,... | collective-permute-start | bytes 3145736 | tf_op jit(solution)/shard_map/ppermute | solution.py:43
  95.6 11.6 %collective-permute-start.19 = (bf16[768,256]{1,0:T(8,128)(2,1)S(1)}, bf16[768,256]{1,0:T(8,128)(2,1)S(1)}, u32[]{:S(2)}, u32[]{:S(2)}) collective-permute-start(bf16[768,256]{1,0:T(8,128)(2,1)S(1)} %pad_maximum_fusion.7.refs_0_), channel_id=1, source_target_pairs={{0,1},{1,0},{2,3},{3,2},{4,5},{5,4},{6,7},{7,6},{8,9},{9,8},{10,11... | collective-permute-start | bytes 1179656 | tf_op jit(solution)/shard_map/ppermute | solution.py:55
  96.5 16.5 %collective-permute-start.20 = (bf16[768,256]{1,0:T(8,128)(2,1)S(1)}, bf16[768,256]{1,0:T(8,128)(2,1)S(1)}, u32[]{:S(2)}, u32[]{:S(2)}) collective-permute-start(bf16[768,256]{1,0:T(8,128)(2,1)S(1)} %pad_maximum_fusion.7.refs_0_), channel_id=1, source_target_pairs={{0,4},{2,6},{4,0},{6,2},{8,12},{10,14},{12,8},{14,10},{16,20},{18,... | collective-permute-start | bytes 1179656 | tf_op jit(solution)/shard_map/ppermute | solution.py:43
  107.1 12.0 %collective-permute-start.21 = (bf16[768,256]{1,0:T(8,128)(2,1)S(1)}, bf16[768,256]{1,0:T(8,128)(2,1)S(1)}, u32[]{:S(2)}, u32[]{:S(2)}) collective-permute-start(bf16[768,256]{1,0:T(8,128)(2,1)S(1)} %collective-permute-done.19.refs_1_), channel_id=1, source_target_pairs={{0,4},{2,6},{4,0},{6,2},{8,12},{10,14},{12,8},{14,10},{16,20},{18,... | collective-permute-start | bytes 1179656 | tf_op jit(solution)/shard_map/ppermute | solution.py:43
  110.7 43.5 %collective-permute-start.47 = (bf16[128,1024]{1,0:T(8,128)(2,1)S(1)}, bf16[128,1024]{1,0:T(8,128)(2,1)}, u32[]{:S(2)}, u32[]{:S(2)}) collective-permute-start(bf16[128,1024]{1,0:T(8,128)(2,1)S(1)} %pad_maximum_fusion.16.refs_0_), channel_id=1, source_target_pairs={{0,8},{2,10},{4,12},{6,14},{8,16},{10,18},{12,20},{14,22},{16,24},... | collective-permute-start | bytes 786440 | tf_op jit(solution)/shard_map/ppermute | solution.py:43
  113.0 42.4 %collective-permute-start.46 = (bf16[128,1024]{1,0:T(8,128)(2,1)S(1)}, bf16[128,1024]{1,0:T(8,128)(2,1)S(1)}, u32[]{:S(2)}, u32[]{:S(2)}) collective-permute-start(bf16[128,1024]{1,0:T(8,128)(2,1)S(1)} %pad_maximum_fusion.16.refs_0_), channel_id=1, source_target_pairs={{0,4},{2,6},{4,0},{6,2},{8,12},{10,14},{12,8},{14,10},{16,20},{18,... | collective-permute-start | bytes 786440 | tf_op jit(solution)/shard_map/ppermute | solution.py:43
  154.2 19.9 %collective-permute-start.41 = (bf16[128,1024]{1,0:T(8,128)(2,1)S(1)}, bf16[128,1024]{1,0:T(8,128)(2,1)S(1)}, u32[]{:S(2)}, u32[]{:S(2)}) collective-permute-start(bf16[128,1024]{1,0:T(8,128)(2,1)S(1)} %pad_maximum_fusion.15.refs_0_), channel_id=1, source_target_pairs={{0,16},{2,18},{4,20},{6,22},{8,24},{10,26},{12,28},{14,30},{16,0},... | collective-permute-start | bytes 786440 | tf_op jit(solution)/shard_map/ppermute | solution.py:43
  154.2 21.4 %collective-permute-start.39 = (bf16[128,1024]{1,0:T(8,128)(2,1)S(1)}, bf16[128,1024]{1,0:T(8,128)(2,1)}, u32[]{:S(2)}, u32[]{:S(2)}) collective-permute-start(bf16[128,1024]{1,0:T(8,128)(2,1)S(1)} %pad_maximum_fusion.15.refs_0_), channel_id=1, source_target_pairs={{0,8},{2,10},{4,12},{6,14},{8,16},{10,18},{12,20},{14,22},{16,24},... | collective-permute-start | bytes 786440 | tf_op jit(solution)/shard_map/ppermute | solution.py:43
  155.4 21.4 %collective-permute-start.52 = (bf16[128,1024]{1,0:T(8,128)(2,1)S(1)}, bf16[128,1024]{1,0:T(8,128)(2,1)}, u32[]{:S(2)}, u32[]{:S(2)}) collective-permute-start(bf16[128,1024]{1,0:T(8,128)(2,1)S(1)} %collective-permute-done.51.refs_6_), channel_id=1, source_target_pairs={{0,4},{2,6},{4,0},{6,2},{8,12},{10,14},{12,8},{14,10},{16,20},{18,... | collective-permute-start | bytes 786440 | tf_op jit(solution)/shard_map/ppermute | solution.py:43
  158.0 19.6 %collective-permute-start.50 = (bf16[128,1024]{1,0:T(8,128)(2,1)}, bf16[128,1024]{1,0:T(8,128)(2,1)}, u32[]{:S(2)}, u32[]{:S(2)}) collective-permute-start(bf16[128,1024]{1,0:T(8,128)(2,1)} %collective-permute-done.49.refs_4_), channel_id=1, source_target_pairs={{0,4},{2,6},{4,0},{6,2},{8,12},{10,14},{12,8},{14,10},{16,20},{18,... | collective-permute-start | bytes 786440 | tf_op jit(solution)/shard_map/ppermute | solution.py:43
  159.9 18.9 %collective-permute-start.48 = (bf16[128,1024]{1,0:T(8,128)(2,1)}, bf16[128,1024]{1,0:T(8,128)(2,1)}, u32[]{:S(2)}, u32[]{:S(2)}) collective-permute-start(bf16[128,1024]{1,0:T(8,128)(2,1)} %collective-permute-done.47.refs_2_), channel_id=1, source_target_pairs={{0,4},{2,6},{4,0},{6,2},{8,12},{10,14},{12,8},{14,10},{16,20},{18,... | collective-permute-start | bytes 786440 | tf_op jit(solution)/shard_map/ppermute | solution.py:43
  174.1 27.9 %collective-permute-start.36 = (bf16[192,1024]{1,0:T(8,128)(2,1)}, bf16[192,1024]{1,0:T(8,128)(2,1)}, u32[]{:S(2)}, u32[]{:S(2)}) collective-permute-start(bf16[192,1024]{1,0:T(8,128)(2,1)} %pad_maximum_fusion.8), channel_id=1, source_target_pairs={{0,2},{2,0},{4,6},{6,4},{8,10},{10,8},{12,14},{14,12},{16,18},{18,... | collective-permute-start | bytes 1179656 | tf_op jit(solution)/shard_map/ppermute | solution.py:43
  175.6 17.3 %collective-permute-start.38 = (bf16[128,1024]{1,0:T(8,128)(2,1)S(1)}, bf16[128,1024]{1,0:T(8,128)(2,1)}, u32[]{:S(2)}, u32[]{:S(2)}) collective-permute-start(bf16[128,1024]{1,0:T(8,128)(2,1)S(1)} %pad_maximum_fusion.15.refs_0_), channel_id=1, source_target_pairs={{0,4},{2,6},{4,0},{6,2},{8,12},{10,14},{12,8},{14,10},{16,20},{18,... | collective-permute-start | bytes 786440 | tf_op jit(solution)/shard_map/ppermute | solution.py:43
  176.8 16.1 %collective-permute-start.44 = (bf16[128,1024]{1,0:T(8,128)(2,1)}, bf16[128,1024]{1,0:T(8,128)(2,1)}, u32[]{:S(2)}, u32[]{:S(2)}) collective-permute-start(bf16[128,1024]{1,0:T(8,128)(2,1)} %copy-done.6), channel_id=1, source_target_pairs={{0,4},{2,6},{4,0},{6,2},{8,12},{10,14},{12,8},{14,10},{16,20},{18,... | collective-permute-start | bytes 786440 | tf_op jit(solution)/shard_map/ppermute | solution.py:43
  177.6 18.5 %collective-permute-start.42 = (bf16[128,1024]{1,0:T(8,128)(2,1)}, bf16[128,1024]{1,0:T(8,128)(2,1)}, u32[]{:S(2)}, u32[]{:S(2)}) collective-permute-start(bf16[128,1024]{1,0:T(8,128)(2,1)} %copy-done.8), channel_id=1, source_target_pairs={{0,4},{2,6},{4,0},{6,2},{8,12},{10,14},{12,8},{14,10},{16,20},{18,... | collective-permute-start | bytes 786440 | tf_op jit(solution)/shard_map/ppermute | solution.py:43
  178.8 21.7 %collective-permute-start.40 = (bf16[128,1024]{1,0:T(8,128)(2,1)}, bf16[128,1024]{1,0:T(8,128)(2,1)}, u32[]{:S(2)}, u32[]{:S(2)}) collective-permute-start(bf16[128,1024]{1,0:T(8,128)(2,1)} %collective-permute-done.39.refs_2_), channel_id=1, source_target_pairs={{0,4},{2,6},{4,0},{6,2},{8,12},{10,14},{12,8},{14,10},{16,20},{18,... | collective-permute-start | bytes 786440 | tf_op jit(solution)/shard_map/ppermute | solution.py:43
  192.9 12.4 %collective-permute-start.56 = (bf16[192,1024]{1,0:T(8,128)(2,1)S(1)}, bf16[192,1024]{1,0:T(8,128)(2,1)S(1)}, u32[]{:S(2)}, u32[]{:S(2)}) collective-permute-start(bf16[192,1024]{1,0:T(8,128)(2,1)S(1)} %copy-done.42), channel_id=1, source_target_pairs={{0,2},{2,0},{4,6},{6,4},{8,10},{10,8},{12,14},{14,12},{16,18},{18,... | collective-permute-start | bytes 1179656 | tf_op jit(solution)/shard_map/ppermute | solution.py:43
  212.2 63.0 %collective-permute-start.99 = (bf16[4,128,1024]{2,1,0:T(8,128)(2,1)}, bf16[4,128,1024]{2,1,0:T(8,128)(2,1)}, u32[]{:S(2)}, u32[]{:S(2)}) collective-permute-start(bf16[4,128,1024]{2,1,0:T(8,128)(2,1)} %dynamic-slice_bitcast_fusion), channel_id=1, source_target_pairs={{0,4},{2,6},{4,0},{6,2},{8,12},{10,14},{12,8},{14,10},{16,20},{18,... | collective-permute-start | bytes 3145736 | tf_op jit(solution)/shard_map/ppermute | solution.py:43
  216.9 64.1 %collective-permute-start.94 = (bf16[4,128,1024]{2,1,0:T(8,128)(2,1)}, bf16[4,128,1024]{2,1,0:T(8,128)(2,1)}, u32[]{:S(2)}, u32[]{:S(2)}) collective-permute-start(bf16[4,128,1024]{2,1,0:T(8,128)(2,1)} %dynamic-slice_bitcast_fusion.1), channel_id=1, source_target_pairs={{0,4},{2,6},{4,0},{6,2},{8,12},{10,14},{12,8},{14,10},{16,20},{18,... | collective-permute-start | bytes 3145736 | tf_op jit(solution)/shard_map/ppermute | solution.py:43
  235.5 14.9 %collective-permute-start.62 = (bf16[2,96,128]{2,1,0:T(8,128)(2,1)S(1)}, bf16[2,96,128]{2,1,0:T(8,128)(2,1)S(1)}, u32[]{:S(2)}, u32[]{:S(2)}) collective-permute-start(bf16[2,96,128]{2,1,0:T(8,128)(2,1)S(1)} %get-tuple-element.166), channel_id=1, source_target_pairs={{0,24},{2,26},{4,28},{6,30},{8,0},{10,2},{12,4},{14,6},{16,8},{18,... | collective-permute-start | bytes 147464 | tf_op jit(solution)/shard_map/ppermute | solution.py:43
  235.6 15.2 %collective-permute-start.61 = (bf16[2,96,128]{2,1,0:T(8,128)(2,1)S(1)}, bf16[2,96,128]{2,1,0:T(8,128)(2,1)S(1)}, u32[]{:S(2)}, u32[]{:S(2)}) collective-permute-start(bf16[2,96,128]{2,1,0:T(8,128)(2,1)S(1)} %get-tuple-element.167), channel_id=1, source_target_pairs={{0,16},{2,18},{4,20},{6,22},{8,24},{10,26},{12,28},{14,30},{16,0},... | collective-permute-start | bytes 147464 | tf_op jit(solution)/shard_map/ppermute | solution.py:43
  237.7 13.9 %collective-permute-start.60 = (bf16[2,96,128]{2,1,0:T(8,128)(2,1)S(1)}, bf16[2,96,128]{2,1,0:T(8,128)(2,1)S(1)}, u32[]{:S(2)}, u32[]{:S(2)}) collective-permute-start(bf16[2,96,128]{2,1,0:T(8,128)(2,1)S(1)} %get-tuple-element.168), channel_id=1, source_target_pairs={{0,8},{2,10},{4,12},{6,14},{8,16},{10,18},{12,20},{14,22},{16,24},... | collective-permute-start | bytes 147464 | tf_op jit(solution)/shard_map/ppermute | solution.py:43
  250.4 23.0 %collective-permute-start.55 = (bf16[96,1024]{1,0:T(8,128)(2,1)}, bf16[96,1024]{1,0:T(8,128)(2,1)}, u32[]{:S(2)}, u32[]{:S(2)}) collective-permute-start(bf16[96,1024]{1,0:T(8,128)(2,1)} %get-tuple-element.133), channel_id=1, source_target_pairs={{0,1},{1,0},{2,3},{3,2},{4,5},{5,4},{6,7},{7,6},{8,9},{9,8},{10,11... | collective-permute-start | bytes 589832 | tf_op jit(solution)/shard_map/ppermute | solution.py:55
  250.8 78.5 %collective-permute-start.82 = (bf16[8,64,2,512]{3,1,0,2:T(8,128)(2,1)S(1)}, bf16[8,64,2,512]{3,1,0,2:T(8,128)(2,1)S(1)}, u32[]{:S(2)}, u32[]{:S(2)}) collective-permute-start(bf16[8,64,2,512]{3,1,0,2:T(8,128)(2,1)S(1)} %bitcast.384), channel_id=1, source_target_pairs={{0,2},{2,0},{4,6},{6,4},{8,10},{10,8},{12,14},{14,12},{16,18},{18,... | collective-permute-start | bytes 3145736 | tf_op jit(solution)/shard_map/ppermute | solution.py:43
  272.1 55.3 %collective-permute-start.63 = (bf16[2,768,256]{2,1,0:T(8,128)(2,1)S(1)}, bf16[2,768,256]{2,1,0:T(8,128)(2,1)S(1)}, u32[]{:S(2)}, u32[]{:S(2)}) collective-permute-start(bf16[2,768,256]{2,1,0:T(8,128)(2,1)S(1)} %bitcast.390), channel_id=1, source_target_pairs={{0,4},{2,6},{4,0},{6,2},{8,12},{10,14},{12,8},{14,10},{16,20},{18,... | collective-permute-start | bytes 2359304 | tf_op jit(solution)/shard_map/ppermute | solution.py:43
  277.4 18.8 %collective-permute-start.102 = (bf16[128,1024]{1,0:T(8,128)(2,1)S(1)}, bf16[128,1024]{1,0:T(8,128)(2,1)S(1)}, u32[]{:S(2)}, u32[]{:S(2)}) collective-permute-start(bf16[128,1024]{1,0:T(8,128)(2,1)S(1)} %get-tuple-element.101), channel_id=1, source_target_pairs={{0,24},{2,26},{4,28},{6,30},{8,0},{10,2},{12,4},{14,6},{16,8},{18,... | collective-permute-start | bytes 786440 | tf_op jit(solution)/shard_map/ppermute | solution.py:43
  281.0 29.8 %collective-permute-start.101 = (bf16[128,1024]{1,0:T(8,128)(2,1)S(1)}, bf16[128,1024]{1,0:T(8,128)(2,1)S(1)}, u32[]{:S(2)}, u32[]{:S(2)}) collective-permute-start(bf16[128,1024]{1,0:T(8,128)(2,1)S(1)} %get-tuple-element.102), channel_id=1, source_target_pairs={{0,16},{2,18},{4,20},{6,22},{8,24},{10,26},{12,28},{14,30},{16,0},... | collective-permute-start | bytes 786440 | tf_op jit(solution)/shard_map/ppermute | solution.py:43
  288.2 22.8 %collective-permute-start.95 = (bf16[128,1024]{1,0:T(8,128)(2,1)S(1)}, bf16[128,1024]{1,0:T(8,128)(2,1)S(1)}, u32[]{:S(2)}, u32[]{:S(2)}) collective-permute-start(bf16[128,1024]{1,0:T(8,128)(2,1)S(1)} %get-tuple-element.103), channel_id=1, source_target_pairs={{0,8},{2,10},{4,12},{6,14},{8,16},{10,18},{12,20},{14,22},{16,24},... | collective-permute-start | bytes 786440 | tf_op jit(solution)/shard_map/ppermute | solution.py:43
  296.1 15.6 %collective-permute-start.97 = (bf16[128,1024]{1,0:T(8,128)(2,1)S(1)}, bf16[128,1024]{1,0:T(8,128)(2,1)S(1)}, u32[]{:S(2)}, u32[]{:S(2)}) collective-permute-start(bf16[128,1024]{1,0:T(8,128)(2,1)S(1)} %get-tuple-element.104), channel_id=1, source_target_pairs={{0,24},{2,26},{4,28},{6,30},{8,0},{10,2},{12,4},{14,6},{16,8},{18,... | collective-permute-start | bytes 786440 | tf_op jit(solution)/shard_map/ppermute | solution.py:43
  310.8 14.9 %collective-permute-start.96 = (bf16[128,1024]{1,0:T(8,128)(2,1)S(1)}, bf16[128,1024]{1,0:T(8,128)(2,1)S(1)}, u32[]{:S(2)}, u32[]{:S(2)}) collective-permute-start(bf16[128,1024]{1,0:T(8,128)(2,1)S(1)} %get-tuple-element.105), channel_id=1, source_target_pairs={{0,16},{2,18},{4,20},{6,22},{8,24},{10,26},{12,28},{14,30},{16,0},... | collective-permute-start | bytes 786440 | tf_op jit(solution)/shard_map/ppermute | solution.py:43
  311.0 15.0 %collective-permute-start.103 = (bf16[64,1024]{1,0:T(8,128)(2,1)S(1)}, bf16[64,1024]{1,0:T(8,128)(2,1)S(1)}, u32[]{:S(2)}, u32[]{:S(2)}) collective-permute-start(bf16[64,1024]{1,0:T(8,128)(2,1)S(1)} %select_convert_fusion.1), channel_id=1, source_target_pairs={{0,2},{2,0},{4,6},{6,4},{8,10},{10,8},{12,14},{14,12},{16,18},{18,... | collective-permute-start | bytes 393224 | tf_op jit(solution)/shard_map/ppermute | solution.py:43
  340.9 20.7 %collective-permute-start.83 = (bf16[8,64,512]{2,1,0:T(8,128)(2,1)}, bf16[8,64,512]{2,1,0:T(8,128)(2,1)S(1)}, u32[]{:S(2)}, u32[]{:S(2)}) collective-permute-start(bf16[8,64,512]{2,1,0:T(8,128)(2,1)} %fusion.9), channel_id=1, source_target_pairs={{0,1},{1,0},{2,3},{3,2},{4,5},{5,4},{6,7},{7,6},{8,9},{9,8},{10,11... | collective-permute-start | bytes 1572872 | tf_op jit(solution)/shard_map/ppermute | solution.py:55
  364.7 29.3 %collective-permute-start.72 = (bf16[4,64,384]{2,1,0:T(8,128)(2,1)S(1)}, bf16[4,64,384]{2,1,0:T(8,128)(2,1)S(1)}, u32[]{:S(2)}, u32[]{:S(2)}) collective-permute-start(bf16[4,64,384]{2,1,0:T(8,128)(2,1)S(1)} %fusion.25), channel_id=1, source_target_pairs={{0,4},{2,6},{4,0},{6,2},{8,12},{10,14},{12,8},{14,10},{16,20},{18,... | collective-permute-start | bytes 589832 | tf_op jit(solution)/shard_map/ppermute | solution.py:43
  369.3 17.0 %collective-permute-start.67 = (bf16[96,1024]{1,0:T(8,128)(2,1)S(1)}, bf16[96,1024]{1,0:T(8,128)(2,1)S(1)}, u32[]{:S(2)}, u32[]{:S(2)}) collective-permute-start(bf16[96,1024]{1,0:T(8,128)(2,1)S(1)} %get-tuple-element.126), channel_id=1, source_target_pairs={{0,16},{2,18},{4,20},{6,22},{8,24},{10,26},{12,28},{14,30},{16,0},... | collective-permute-start | bytes 589832 | tf_op jit(solution)/shard_map/ppermute | solution.py:43
  389.6 11.9 %collective-permute-start.85 = (bf16[64,512]{1,0:T(8,128)(2,1)S(1)}, bf16[64,512]{1,0:T(8,128)(2,1)S(1)}, u32[]{:S(2)}, u32[]{:S(2)}) collective-permute-start(bf16[64,512]{1,0:T(8,128)(2,1)S(1)} %get-tuple-element.158), channel_id=1, source_target_pairs={{0,8},{2,10},{4,12},{6,14},{8,16},{10,18},{12,20},{14,22},{16,24},... | collective-permute-start | bytes 196616 | tf_op jit(solution)/shard_map/ppermute | solution.py:43
  389.6 12.0 %collective-permute-start.87 = (bf16[64,512]{1,0:T(8,128)(2,1)S(1)}, bf16[64,512]{1,0:T(8,128)(2,1)S(1)}, u32[]{:S(2)}, u32[]{:S(2)}) collective-permute-start(bf16[64,512]{1,0:T(8,128)(2,1)S(1)} %get-tuple-element.159), channel_id=1, source_target_pairs={{0,24},{2,26},{4,28},{6,30},{8,0},{10,2},{12,4},{14,6},{16,8},{18,... | collective-permute-start | bytes 196616 | tf_op jit(solution)/shard_map/ppermute | solution.py:43
  (131 other events, 1735.8 us)

commit v3 on v2

v3 whole, which is shorter than its diff:
```python
import functools

import jax
import jax.numpy as jnp
from jax import lax
from jax.experimental import pallas as pl
from jax.experimental.pallas import tpu as pltpu
from jax.sharding import PartitionSpec as P

HD = 64
EPSILON = 1e-05
EXCLUDED = -1e30
F32 = jnp.float32
BF16 = jnp.bfloat16
NN = (((1,), (0,)), ((), ()))
NT = (((1,), (1,)), ((), ()))
TN = (((0,), (0,)), ((), ()))


def dot(left, right, dims=NN):
    return lax.dot_general(left, right, dims, preferred_element_type=F32)


SP = ("z", "x", "core")


class Grid:
    def __init__(self):
        self.nz = lax.axis_size("z")
        self.nx = lax.axis_size("x")
        self.chips = self.nz * self.nx
        self.sp = 2 * self.chips
        me = lax.axis_index(SP)
        self.me = me
        self.core = me % 2
        self.x = (me // 2) % self.nx
        self.z = me // (2 * self.nx)
        self.y = lax.axis_index("tp")

    def _move(self, block, dz, dx, flip):
        pairs = []
        for i in range(self.sp):
            z, x, c = i // (2 * self.nx), (i // 2) % self.nx, i % 2
            to = (((z + dz) % self.nz) * self.nx + (x + dx) % self.nx) * 2 + (1 - c if flip else c)
            pairs.append((i, to))
        return lax.ppermute(block, SP, pairs)

    def zshift(self, block, k):
        return self._move(block, k, 0, False)

    def xshift(self, block, k):
        return self._move(block, 0, k, False)

    def cswap(self, block):
        return self._move(block, 0, 0, True)

    def yswap(self, block):
        return lax.ppermute(block, "tp", [(0, 1), (1, 0)])

    def _pairs(self, route):
        pairs = []
        for chip in range(self.chips):
            for (c, y), (to_c, to_y) in route:
                pairs.append(((chip * 2 + c) * 2 + y, (chip * 2 + to_c) * 2 + to_y))
        return pairs

    def spin(self, block, back=False):
        route = []
        for b in (0, 1):
            route += [((b, b), (b, 1 - b)), ((1 - b, b), (b, b))]
        if back:
            route = [(to, at) for at, to in route]
        return lax.ppermute(block, SP + ("tp",), self._pairs(route))

    def cross(self, block):
        route = [((1 - b, b), (b, 1 - b)) for b in (0, 1)]
        return lax.ppermute(block, SP + ("tp",), self._pairs(route))

    def far_z(self, k):
        return (self.z + k) % self.nz

    def far_x(self, j):
        return (self.x + j) % self.nx

    def gather(self, block):
        columns = [block] + [self.zshift(block, k) for k in range(1, self.nz)]
        return [p for b in columns for p in [b] + [self.xshift(b, j) for j in range(1, self.nx)]]

    def chip_order(self):
        order = jnp.arange(self.chips)
        return self.far_z(-(order // self.nx)) * self.nx + self.far_x(-(order % self.nx))

    def scatter(self, pieces):
        total = pick(pieces, self.x, 1).astype(F32)
        for j in range(1, self.nx):
            total = total + self.xshift(pick(pieces, self.far_x(j), 1), j).astype(F32)
        low = total.astype(pieces.dtype)
        mine = pick(total, self.z, 0)
        for k in range(1, self.nz):
            mine = mine + self.zshift(pick(low, self.far_z(k), 0), k).astype(F32)
        return mine


def pick(array, index, axis):
    return lax.dynamic_index_in_dim(array, index, axis, keepdims=False)


def normalize(values):
    center = values - jnp.mean(values, axis=-1, keepdims=True)
    spread = jnp.mean(center * center, axis=-1, keepdims=True)
    scale = lax.rsqrt(spread + EPSILON)
    return center * scale, scale


def norm_back(normed, scale, gain, grad):
    scaled = grad * gain
    mean_one = jnp.mean(scaled, axis=-1, keepdims=True)
    mean_two = jnp.mean(scaled * normed, axis=-1, keepdims=True)
    return (scaled - mean_one - normed * mean_two) * scale


def place_qkv_kernel(starts_ref, *refs):
    pieces, out_ref = refs[:-1], refs[-1]
    for i, piece in enumerate(pieces):
        size = out_ref.shape[2] // len(pieces)
        span = pl.ds(pl.multiple_of(starts_ref[i], size), size)
        for c in range(3):
            out_ref[c, :, span] = piece[:, c * size : (c + 1) * size].astype(F32)


def place_qkv(pieces, starts, columns):
    rows = pieces[0].shape[0]
    vmem = pl.BlockSpec(memory_space=pltpu.VMEM)
    return pl.pallas_call(
        place_qkv_kernel,
        out_shape=jax.ShapeDtypeStruct((3, rows, columns * len(pieces)), F32),
        in_specs=[pl.BlockSpec(memory_space=pltpu.SMEM)] + [vmem] * len(pieces),
        out_specs=vmem,
        name="place_qkv",
    )(jnp.stack(starts).astype(jnp.int32), *pieces)


def lane_in_head(shape, head):
    lanes = lax.broadcasted_iota(jnp.int32, shape, 1)
    return (lanes // HD) == (head % 2)


def pair_lanes(pair):
    return slice(pair * 2 * HD, (pair + 1) * 2 * HD)


STEP = 384
SMEM = pl.BlockSpec(memory_space=pltpu.SMEM)


def in_vmem(count):
    return [pl.BlockSpec(memory_space=pltpu.VMEM)] * count


def local_kernel(kernel, name, out_shape, operands, scalars=1, scratch=(), flops=0, megabytes=48):
    single = not isinstance(out_shape, tuple)
    return pl.pallas_call(
        kernel,
        out_shape=out_shape,
        in_specs=[SMEM] * scalars + in_vmem(len(operands) - scalars),
        out_specs=in_vmem(1)[0] if single else tuple(in_vmem(len(out_shape))),
        scratch_shapes=list(scratch),
        compiler_params=pltpu.CompilerParams(vmem_limit_bytes=megabytes * 1024 * 1024),
        cost_estimate=pl.CostEstimate(flops=flops, bytes_accessed=1 << 16, transcendentals=0),
        name=name,
    )(*operands)


def shape(dims, kind=BF16):
    return jax.ShapeDtypeStruct(tuple(dims), kind)


def turned(index, size):
    return lax.rem(index + size, size)


def enter_kernel(nz, nx, n_vec, part, at_ref, hour_ref, *refs):
    token_refs, refs = refs[: nz + 1], refs[nz + 1 :]
    pack_refs, refs = refs[: nx - 1], refs[nx - 1 :]
    weight_refs, refs = refs[:2], refs[2:]
    normed_ref, unit_ref, scale_ref, lead_ref, first_ref, vec_ref, weight_ref, q_ref, kv_ref = refs[:9]
    packs = refs[9]
    z, x, c = at_ref[0], at_ref[1], at_ref[2]
    rows, width = first_ref.shape
    tall = packs.shape[3]
    local = q_ref.shape[1]
    aux = slice(width, width + 128)
    for k in range(nz):
        packs[0, 0, k] = token_refs[k][:tall, aux]
        packs[0, 1, k] = token_refs[nz][k, :tall, aux]
    for j in range(1, nx):
        packs[j] = pack_refs[j - 1][...]
    for dev in range(2 * nz * nx):
        dev_z, dev_x, dev_c = dev // (2 * nx), (dev // 2) % nx, dev % 2
        block = packs[turned(x - dev_x, nx), turned(c - dev_c, 2), turned(z - dev_z, nz)]
        vec_ref[:, dev * part : (dev + 1) * part] = block[:n_vec, 64 : 64 + part].astype(F32)
    for n in range(2 * nz):
        ref = token_refs[n] if n < nz else token_refs[nz].at[n - nz]
        span = slice(n * rows, (n + 1) * rows)
        segment = ref[:, aux][:, :1].astype(F32)
        lead = jnp.zeros_like(segment)
        for i in range(hour_ref.shape[0]):
            lead = jnp.where(segment == float(i), hour_ref[i], lead)
        lead_ref[span, :] = lead
        value = ref[:, :width].astype(F32) + lead * vec_ref[0:1, :] + vec_ref[1:2, :]
        if n == 0:
            first_ref[...] = value
        unit, scale = normalize(value)
        scale_ref[span, :] = scale
        unit_ref[span, :] = unit.astype(BF16)
        normed_ref[span, :] = (unit * vec_ref[2:3, :] + vec_ref[3:4, :]).astype(BF16)
    for p, ref in enumerate(weight_refs):
        parity = c if p == 0 else 1 - c
        for j in range(nx):
            for k in range(nz):
                row = ((turned(z - k, nz) * nx + turned(x - j, nx)) * 2 + parity) * part
                weight_ref[pl.ds(pl.multiple_of(row, part), part), :] = ref[j, k]
    made = dot(normed_ref[...], weight_ref[...])
    q_ref[...] = made[:, :local]
    kv_ref[...] = made[:, local:].astype(BF16)


def enter(at, hours, tokens, packs, same, other, n_vec, part):
    nz, nx = len(tokens) - 1, len(packs) + 1
    rows, wide = tokens[0].shape
    width = wide - 128
    count = 2 * nz * rows
    local = same.shape[-1] // 3
    tall = packs[0].shape[2]
    return local_kernel(
        functools.partial(enter_kernel, nz, nx, n_vec, part),
        "enter",
        (
            shape((count, width)),
            shape((count, width)),
            shape((count, 1), F32),
            shape((count, 1), F32),
            shape((rows, width), F32),
            shape((n_vec, width), F32),
            shape((width, 3 * local)),
            shape((count, local), F32),
            shape((count, 2 * local)),
        ),
        (at, hours, *tokens, *packs, same, other),
        scalars=2,
        scratch=[pltpu.VMEM((nx, 2, nz, tall, 128), BF16)],
    )


def attend_kernel(pieces, heads, nz, at_ref, q_ref, bias_ref, qcode_ref, kcode_ref, *refs):
    kv_refs = refs[:pieces]
    out_ref, lse_ref, low_ref, send_ref = refs[pieces : pieces + 4]
    kaug, vturn, qaug, acc, stat = refs[pieces + 4 :]
    width = heads * HD
    count = q_ref.shape[0]
    rows = count // (2 * nz)
    steps = kv_refs[0].shape[0] // STEP
    low_ref[...] = (q_ref[...] + bias_ref[0:1, :]).astype(BF16) * jnp.asarray(HD ** (-0.5), BF16)
    for n in range(pieces * steps):
        block = kv_refs[n // steps]
        span_in = pl.ds((n % steps) * STEP, STEP)
        span = pl.ds(n * STEP, STEP)
        code = kcode_ref[span, :]
        for p in range(heads // 2):
            keys = block[span_in, pair_lanes(p)]
            for h in (2 * p, 2 * p + 1):
                kaug[h, span, :] = jnp.where(lane_in_head(keys.shape, h), keys, code)
        vturn[n] = jnp.transpose(block[span_in, width:])
    for p in range(heads // 2):
        part = low_ref[:, pair_lanes(p)]
        for h in (2 * p, 2 * p + 1):
            qaug[h] = jnp.where(lane_in_head(part.shape, h), part, qcode_ref[...])
    acc[...] = jnp.zeros_like(acc)
    stat[0] = jnp.full(stat.shape[1:], EXCLUDED, F32)
    stat[1] = jnp.zeros(stat.shape[1:], F32)

    def chunk(i, carry):
        for h in range(heads):
            scores = dot(kaug[h, pl.ds(i * STEP, STEP), :], qaug[h], NT)
            top = stat[0, h : h + 1, :]
            new_top = jnp.maximum(top, jnp.max(scores, axis=0, keepdims=True))
            weight = jnp.exp(scores - new_top)
            rescale = jnp.exp(top - new_top)
            stat[0, h : h + 1, :] = new_top
            stat[1, h : h + 1, :] = stat[1, h : h + 1, :] * rescale + jnp.sum(weight, axis=0, keepdims=True)
            span = slice(h * HD, (h + 1) * HD)
            acc[span, :] = acc[span, :] * rescale + dot(vturn[i, span, :], weight.astype(BF16))
        return carry

    lax.fori_loop(0, pieces * steps, chunk, 0)
    for h in range(heads):
        span = slice(h * HD, (h + 1) * HD)
        acc[span, :] = acc[span, :] / stat[1, h : h + 1, :]
    out_ref[...] = jnp.transpose(acc[...])
    lse_ref[...] = stat[0] + jnp.log(jnp.maximum(stat[1], 1e-37))
    z = at_ref[0]
    for r in range(2):
        for k in range(nz):
            span = slice((r * nz + k) * rows, (r * nz + k + 1) * rows)
            send_ref[turned(z - k, nz), r] = (out_ref[span, :] + bias_ref[1:2, :]).astype(BF16)


def attend(at, nz, q, bias, qcode, kcode, kv_pieces):
    count, width = q.shape
    heads = width // HD
    keys = kcode.shape[0]
    return local_kernel(
        functools.partial(attend_kernel, len(kv_pieces), heads, nz),
        "attend",
        (
            shape((count, width), F32),
            shape((8, count), F32),
            shape((count, width)),
            shape((nz, 2, count // (2 * nz), width)),
        ),
        (at, q, bias, qcode, kcode, *kv_pieces),
        scratch=[
            pltpu.VMEM((heads, keys, 2 * HD), BF16),
            pltpu.VMEM((keys // STEP, width, STEP), BF16),
            pltpu.VMEM((heads, count, 2 * HD), BF16),
            pltpu.VMEM((width, count), F32),
            pltpu.VMEM((2, 8, count), F32),
        ],
    )


def attend_back_kernel(
    nx, heads, nz, at_ref, q_ref, qcode_ref, kcode_ref, got_ref, full_ref, lse_ref, *refs
):
    pieces = 2 * nx
    kv_refs = refs[:pieces]
    dq_ref, dkv_refs = refs[pieces], refs[pieces + 1 : pieces + 1 + nx]
    kaug, kturn, vals, qaug, qmask, domask, acc, dout, delta = refs[pieces + 1 + nx :]
    width = heads * HD
    count = q_ref.shape[0]
    rows = count // (2 * nz)
    steps = kv_refs[0].shape[0] // STEP
    z = at_ref[0]
    for r in range(2):
        for k in range(nz):
            span = slice((r * nz + k) * rows, (r * nz + k + 1) * rows)
            dout[span, :] = got_ref[turned(z - k, nz), r]
    product = dout[...].astype(F32) * full_ref[...]
    head_rows = lax.broadcasted_iota(jnp.int32, (8, width), 0)
    head_lanes = lax.broadcasted_iota(jnp.int32, (8, width), 1) // HD
    delta[...] = lax.dot_general(
        (head_rows == head_lanes).astype(F32),
        product,
        NT,
        precision=lax.Precision.HIGHEST,
        preferred_element_type=F32,
    )
    for n in range(pieces * steps):
        block = kv_refs[n // steps]
        span_in = pl.ds((n % steps) * STEP, STEP)
        span = pl.ds(n * STEP, STEP)
        code = kcode_ref[span, :]
        for p in range(heads // 2):
            keys = block[span_in, pair_lanes(p)]
            for h in (2 * p, 2 * p + 1):
                kaug[h, span, :] = jnp.where(lane_in_head(keys.shape, h), keys, code)
        kturn[n] = jnp.transpose(block[span_in, :width])
        vals[span, :] = block[span_in, width:]
    for p in range(heads // 2):
        part = q_ref[:, pair_lanes(p)]
        dpart = dout[:, pair_lanes(p)]
        for h in (2 * p, 2 * p + 1):
            inside = lane_in_head(part.shape, h)
            qaug[h] = jnp.where(inside, part, qcode_ref[...])
            qmask[h] = jnp.where(inside, part, jnp.zeros_like(part))
            domask[h] = jnp.where(inside, dpart, jnp.zeros_like(dpart))
    acc[...] = jnp.zeros_like(acc)
    each = 2 * steps
    for j in range(nx):

        def chunk(n, carry, j=j):
            i = j * each + n
            span = pl.ds(i * STEP, STEP)
            span_out = pl.ds(n * STEP, STEP)
            for p in range(heads // 2):
                dkey = dval = None
                for h in (2 * p, 2 * p + 1):
                    scores = dot(kaug[h, span, :], qaug[h], NT)
                    prob = jnp.exp(scores - lse_ref[h : h + 1, :])
                    dprob = dot(vals[span, pair_lanes(p)], domask[h], NT)
                    dscore = (prob * (dprob - delta[h : h + 1, :])).astype(BF16)
                    add_val = dot(prob.astype(BF16), domask[h])
                    add_key = dot(dscore, qmask[h])
                    dval = add_val if dval is None else dval + add_val
                    dkey = add_key if dkey is None else dkey + add_key
                    turn = slice(h * HD, (h + 1) * HD)
                    acc[turn, :] += dot(kturn[i, turn, :], dscore)
                dkv_refs[j][span_out, pair_lanes(p)] = dkey.astype(BF16)
                dkv_refs[j][span_out, slice(width + p * 2 * HD, width + (p + 1) * 2 * HD)] = dval.astype(BF16)
            return carry

        lax.fori_loop(0, each, chunk, 0)
    dq_ref[...] = (jnp.transpose(acc[...]) * (HD ** (-0.5))).astype(BF16)


def attend_back(at, nz, q, qcode, kcode, got, full, lse, kv_pieces):
    count, width = q.shape
    heads = width // HD
    keys = kcode.shape[0]
    nx = len(kv_pieces) // 2
    return local_kernel(
        functools.partial(attend_back_kernel, nx, heads, nz),
        "attend_back",
        (shape((count, width)),) + (shape((2 * count, 2 * width)),) * nx,
        (at, q, qcode, kcode, got, full, lse, *kv_pieces),
        scratch=[
            pltpu.VMEM((heads, keys, 2 * HD), BF16),
            pltpu.VMEM((keys // STEP, width, STEP), BF16),
            pltpu.VMEM((keys, width), BF16),
            pltpu.VMEM((heads, count, 2 * HD), BF16),
            pltpu.VMEM((heads, count, 2 * HD), BF16),
            pltpu.VMEM((heads, count, 2 * HD), BF16),
            pltpu.VMEM((width, count), F32),
            pltpu.VMEM((count, width), BF16),
            pltpu.VMEM((8, count), F32),
        ],
        megabytes=56,
    )


def whole_proj_kernel(nz, nx, part, at_ref, own_ref, far_ref, out_ref):
    z, x, c, y = at_ref[0], at_ref[1], at_ref[2], at_ref[3]
    half = out_ref.shape[1] // 2
    for p, ref in enumerate((own_ref, far_ref)):
        parity = c if p == 0 else 1 - c
        for w in range(2):
            column = pl.multiple_of(turned(y - w, 2) * half, half)
            for j in range(nx):
                for k in range(nz):
                    row = ((turned(z - k, nz) * nx + turned(x - j, nx)) * 2 + parity) * part
                    out_ref[pl.ds(pl.multiple_of(row, part), part), pl.ds(column, half)] = ref[w, j, k]


def whole_proj(at, own, far):
    _, nx, nz, part, half = own.shape
    return local_kernel(
        functools.partial(whole_proj_kernel, nz, nx, part),
        "whole_proj",
        shape((2 * nx * nz * part, 2 * half)),
        (at, own, far),
    )


def project_kernel(at_ref, got_ref, far_ref, weight_ref, first_ref, vec_ref, *refs):
    attn_ref, unit_ref, scale_ref, normed_ref, middle_ref = refs
    nz, _, _, local = got_ref.shape
    c = at_ref[2]
    for block in range(2):
        base = (c if block == 0 else 1 - c) * nz
        for z in range(nz):
            lane = pl.multiple_of((base + z) * local, local)
            attn_ref[:, pl.ds(lane, local)] = got_ref[z, 0] if block == 0 else far_ref[z]
    middle = first_ref[...] + (dot(attn_ref[...], weight_ref[...], NT) + vec_ref[4:5, :])
    middle_ref[...] = middle
    unit, scale = normalize(middle)
    unit_ref[...] = unit
    scale_ref[...] = scale
    normed_ref[...] = (unit * vec_ref[5:6, :] + vec_ref[6:7, :]).astype(BF16)


def project(at, got, far, weight, first, vecs):
    rows, width = first.shape
    return local_kernel(
        project_kernel,
        "project",
        (
            shape((rows, width)),
            shape((rows, width), F32),
            shape((rows, 1), F32),
            shape((rows, width)),
            shape((rows, width), F32),
        ),
        (at, got, far, weight, first, vecs),
    )


def feed_kernel(bias_ref, own_ref, near_ref, far_ref, gz_ref, weight, *refs):
    normed_ref, act_ref, gh_ref, sum_ref, keep_n_ref, send_n_ref, keep_o_ref, send_o_ref = refs[:8]
    back, out = refs[8:]
    rows = own_ref.shape[0]
    hidden_size = act_ref.shape[1]
    normed_ref[:rows, :] = own_ref[...]
    normed_ref[rows : 2 * rows, :] = near_ref[...]
    normed_ref[2 * rows :, :] = far_ref[...]
    step = 256
    for n in range(hidden_size // step):
        up = slice(n * step, (n + 1) * step)
        down = slice(hidden_size + n * step, hidden_size + (n + 1) * step)
        value = dot(normed_ref[...], weight[:, up]) + bias_ref[:, up]
        cdf = 0.5 * (1.0 + lax.erf(value * (0.5**0.5)))
        act = (value * cdf).astype(BF16)
        slope = cdf + value * (jnp.exp(-0.5 * value * value) * ((0.5 / jnp.pi) ** 0.5))
        low = (dot(gz_ref[...], weight[:, down]) * slope).astype(BF16)
        act_ref[:, up] = act
        gh_ref[:, up] = low
        sum_ref[:, up] = jnp.sum(low.astype(F32), axis=0, keepdims=True)
        add_back = dot(low, weight[:, up], NT)
        add_out = dot(act, weight[:, down], NT)
        if n == 0:
            back[...] = add_back
            out[...] = add_out
        else:
            back[...] += add_back
            out[...] += add_out
    keep_n_ref[...] = back[: 2 * rows, :]
    send_n_ref[...] = back[2 * rows :, :].astype(BF16)
    keep_o_ref[...] = out[: 2 * rows, :]
    send_o_ref[...] = out[2 * rows :, :].astype(BF16)


def feed(bias, own, near, far, gz, weight):
    count, width = gz.shape
    hidden_size = bias.shape[1]
    half = count // 2
    return local_kernel(
        feed_kernel,
        "feed",
        (
            shape((count, width)),
            shape((count, hidden_size)),
            shape((count, hidden_size)),
            shape((1, hidden_size), F32),
            shape((half, width), F32),
            shape((half, width)),
            shape((half, width), F32),
            shape((half, width)),
        ),
        (bias, own, near, far, gz, weight),
        scalars=0,
        scratch=[pltpu.VMEM((count, width), F32), pltpu.VMEM((count, width), F32)],
        megabytes=56,
    )


def outer_kernel(normed_ref, gh_ref, gz_ref, act_ref, out_ref):
    hidden_size = gh_ref.shape[1]
    step = 256
    for base, left_ref, right_ref in ((0, normed_ref, gh_ref), (hidden_size, gz_ref, act_ref)):
        for n in range(hidden_size // step):
            made = dot(left_ref[...], right_ref[:, n * step : (n + 1) * step], TN)
            out_ref[:, base + n * step : base + (n + 1) * step] = made.astype(BF16)


def outer(normed, gh, gz, act):
    return local_kernel(
        outer_kernel, "outer", shape((normed.shape[1], 2 * gh.shape[1])), (normed, gh, gz, act), scalars=0
    )


def branch_kernel(at_ref, half_ref, near_ref, unit_ref, scale_ref, vec_ref, gz_ref, weight_ref, *refs):
    middle_ref, branch_ref, mine_ref, send_ref, sum_ref = refs
    rows = half_ref.shape[0] // 2
    nz, _, local = mine_ref.shape
    c = at_ref[2]
    grad = half_ref[:rows, :] + near_ref[...].astype(F32)
    top = gz_ref[...].astype(F32)
    unit = unit_ref[...]
    middle = top + norm_back(unit, scale_ref[...], vec_ref[5:6, :], grad)
    middle_ref[...] = middle
    low = middle.astype(BF16)
    branch_ref[...] = low
    made = dot(low, weight_ref[...]).astype(BF16)
    for h in range(2):
        for z in range(nz):
            block = made[:, (h * nz + z) * local : (h * nz + z + 1) * local]

            @pl.when(c == h)
            def _():
                mine_ref[z] = block

            @pl.when(c != h)
            def _():
                send_ref[z] = block

    sum_ref[...] = jnp.concatenate(
        [
            jnp.sum(low.astype(F32), axis=0, keepdims=True),
            jnp.sum(grad * unit, axis=0, keepdims=True),
            jnp.sum(grad, axis=0, keepdims=True),
            jnp.sum(top, axis=0, keepdims=True),
        ],
        axis=0,
    )


def branch(at, nz, half, near, unit, scale, vecs, gz, weight):
    rows, width = unit.shape
    local = width // (2 * nz)
    return local_kernel(
        branch_kernel,
        "branch",
        (
            shape((rows, width), F32),
            shape((rows, width)),
            shape((nz, rows, local)),
            shape((nz, rows, local)),
            shape((4, width), F32),
        ),
        (at, half, near, unit, scale, vecs, gz, weight),
    )


def leave_kernel(dq_ref, two_ref, near_ref, weight_ref, stack_ref, full_ref, send_ref):
    count, local = dq_ref.shape
    stack_ref[:, :local] = dq_ref[...]
    stack_ref[:, local:] = (two_ref[:count, :] + near_ref[...].astype(F32)).astype(BF16)
    full_ref[...] = dot(stack_ref[...], weight_ref[...], NT)
    send_ref[...] = full_ref[count // 2 :, :].astype(BF16)


def leave(dq, two, near, weight):
    count, local = dq.shape
    width = weight.shape[0]
    return local_kernel(
        leave_kernel,
        "leave",
        (shape((count, 3 * local)), shape((count, width), F32), shape((count // 2, width))),
        (dq, two, near, weight),
        scalars=0,
    )


def close_kernel(rows, full_ref, unit_ref, scale_ref, lead_ref, vec_ref, middle_ref, normed_ref, stack_ref, *refs):
    sum_ref, bias_ref, out_ref = refs
    count, width = full_ref.shape
    lead_row = jnp.zeros((4, width), F32)
    for n in range(count // rows):
        span = slice(n * rows, (n + 1) * rows)
        grad = full_ref[span, :]
        unit = unit_ref[span, :].astype(F32)
        back = norm_back(unit, scale_ref[span, :], vec_ref[2:3, :], grad)
        if n == 0:
            back = back + middle_ref[...]
        lead_row = lead_row + jnp.concatenate(
            [
                jnp.sum(back * lead_ref[span, :], axis=0, keepdims=True),
                jnp.sum(back, axis=0, keepdims=True),
                jnp.sum(grad * unit, axis=0, keepdims=True),
                jnp.sum(grad, axis=0, keepdims=True),
            ],
            axis=0,
        )
    sum_ref[...] = lead_row
    bias_ref[...] = jnp.sum(stack_ref[...].astype(F32), axis=0, keepdims=True)
    out_ref[...] = dot(normed_ref[...], stack_ref[...], TN).astype(BF16)


def close(rows, full, unit, scale, lead, vecs, middle, normed, stack):
    width = full.shape[1]
    return local_kernel(
        functools.partial(close_kernel, rows),
        "close",
        (shape((4, width), F32), shape((1, stack.shape[1]), F32), shape((width, stack.shape[1]))),
        (full, unit, scale, lead, vecs, middle, normed, stack),
        scalars=0,
    )


def after(block, *before):
    return lax.optimization_barrier((block,) + before)[0]


def per_device(
    tokens,
    segment_ids,
    lead_hours,
    qkv_weight,
    qv_bias,
    proj_weight,
    proj_bias,
    up_weight,
    up_bias,
    down_weight,
    down_bias,
    norm1_gain,
    norm1_bias,
    norm2_gain,
    norm2_bias,
    lead_weight,
    lead_bias,
    out_grad,
):
    grid = Grid()
    nz, nx, chips, sp = grid.nz, grid.nx, grid.chips, grid.sp
    core, y = grid.core, grid.y
    at = jnp.stack([grid.z, grid.x, core, y]).astype(jnp.int32)
    full_rows, width = tokens.shape
    rows = full_rows // 2
    part = norm1_gain.shape[0]
    each = HD // sp
    at_home = core == y

    def split(array, axis, index):
        half = array.shape[axis] // 2
        first = lax.slice_in_dim(array, 0, half, axis=axis)
        second = lax.slice_in_dim(array, half, 2 * half, axis=axis)
        return jnp.where(index == 0, first, second), jnp.where(index == 0, second, first)

    def in_order(own, other, index):
        return jnp.where(index == 0, own, other), jnp.where(index == 0, other, own)

    shard = jnp.transpose(qkv_weight.reshape(3, part, nz, -1), (2, 1, 0, 3)).reshape(nz, part, -1)
    wq_z = [pick(shard, grid.z, 0)] + [grid.zshift(pick(shard, grid.far_z(k), 0), k) for k in range(1, nz)]

    vectors = [lead_weight, lead_bias, norm1_gain, norm1_bias, proj_bias, norm2_gain, norm2_bias, down_bias]
    n_vec = len(vectors)
    n_qv, n_up = qv_bias.size // part, up_bias.size // part
    pack = jnp.concatenate(
        [
            jnp.stack(vectors),
            qv_bias.reshape(-1, part),
            up_bias.reshape(-1, part),
            segment_ids.astype(BF16).reshape(-1, part),
        ],
        axis=0,
    )
    pack_rows = pack.shape[0]
    tall = -(-pack_rows // 16) * 16
    pack = jnp.pad(pack, ((0, rows - pack_rows), (63, 128 - 64 - part)))
    own_segments = split(segment_ids, 0, y)[0]
    beside = jnp.concatenate([own_segments.astype(BF16)[:, None], pack], axis=1)
    own_tokens = jnp.concatenate([split(tokens, 0, y)[0], beside], axis=1)
    token_far = [grid.zshift(own_tokens, k) for k in range(1, nz)]
    token_z = jnp.stack([own_tokens] + token_far)
    token_c = grid.cswap(token_z)
    packs_own = jnp.stack([token_z[:, :tall, width:], token_c[:, :tall, width:]])
    packs_far = [grid.xshift(packs_own, j) for j in range(1, nx)]

    wq_z = jnp.stack(wq_z)
    wq_x = jnp.stack([wq_z] + [grid.xshift(wq_z, j) for j in range(1, nx)])
    wq_spin, wq_cross = grid.spin(wq_x), grid.cross(wq_x)
    wq_same = jnp.where(at_home, wq_x, wq_spin)
    wq_other = jnp.where(at_home, wq_spin, wq_cross)

    normed_one, unit_one, scale_one, lead, embedded, vecs, w_qkv, q_raw, kv = enter(
        at, lead_hours, [own_tokens] + token_far + [token_c], packs_far, wq_same, wq_other, n_vec, part
    )
    local = q_raw.shape[1]
    kv_far = grid.yswap(kv)
    kv_pieces = [kv, kv_far]
    for j in range(1, nx):
        kv_pieces += [grid.xshift(kv, j), grid.xshift(kv_far, j)]

    table = jnp.stack([packs_own] + packs_far)[:, :, :, n_vec:pack_rows, 64 : 64 + part].reshape(sp, -1)
    n = jnp.arange(sp)
    rel_j, rel_r, rel_k = n // (2 * nz), (n // nz) % 2, n % nz
    device = (grid.far_z(-rel_k) * nx + grid.far_x(-rel_j)) * 2 + (core + rel_r) % 2
    in_place = (jnp.arange(sp)[:, None] == device[None, :]).astype(BF16)
    table = dot(in_place, table).reshape(sp, -1, part)
    heads_local = qv_bias.shape[1]
    qv_all = jnp.transpose(table[:, :n_qv].reshape(sp, 2, heads_local, -1), (1, 2, 0, 3)).reshape(2, heads_local * HD)
    qv_far = grid.yswap(qv_all)
    qv_full = pick(jnp.where(at_home, qv_all, qv_far).reshape(2, nz, -1), grid.z, 1)
    seg_rows = table[:, n_qv + n_up :].reshape(sp * 2, rows)
    n = jnp.arange(nx * 2 * 2 * nz)
    k, r, w, j = n % nz, (n // nz) % 2, (n // (2 * nz)) % 2, n // (4 * nz)
    key_at = ((grid.far_z(-k) * nx + grid.far_x(-j)) * 2 + (core + r) % 2) * 2 + (y + w) % 2
    take = (key_at[:, None] == jnp.arange(2 * sp)[None, :]).astype(BF16)
    key_seg = dot(take, seg_rows.astype(BF16)).astype(jnp.int32).reshape(-1)
    query_seg = key_seg[: 2 * nz * rows]
    lanes = jnp.arange(2 * HD, dtype=jnp.int32) % HD
    kcode = jnp.where(key_seg[:, None] == lanes[None, :], 0.0, EXCLUDED).astype(BF16)
    qcode = (query_seg[:, None] == lanes[None, :]).astype(BF16)
    up_all = jnp.transpose(table[:, n_qv : n_qv + n_up].reshape(sp, up_bias.shape[0], -1), (1, 0, 2)).reshape(1, -1)
    up_full = split(up_all, 1, core)[0]

    up_shard, down_shard, _ = lax.optimization_barrier((up_weight, down_weight, wq_z))
    up_keep, up_send = split(up_shard, 1, core)
    down_keep, down_send = split(jnp.transpose(down_shard), 1, core)
    ff_far = grid.cswap(jnp.concatenate([up_send, down_send], axis=1))
    ff = jnp.concatenate(in_order(jnp.concatenate([up_keep, down_keep], axis=1), ff_far, core), axis=0)
    w_ff = lax.all_gather(after(ff, *token_far), ("z", "x"), axis=0, tiled=True)

    gz_own, gz_far = split(after(out_grad, kv), 0, y)
    gz_two = jnp.concatenate([gz_own, gz_far], axis=0)
    gz = jnp.concatenate([gz_two, grid.cswap(gz_two)], axis=0)

    wp = jnp.transpose(after(proj_weight, wq_spin, token_c))
    wp_z = jnp.stack([wp] + [grid.zshift(wp, k) for k in range(1, nz)])
    wp_z = after(wp_z, kv)
    wp_x = jnp.stack([wp_z] + [grid.xshift(wp_z, j) for j in range(1, nx)])
    wp_x = after(wp_x, kv_far)
    wp_own = jnp.stack([wp_x, grid.yswap(wp_x)])
    w_proj = whole_proj(at, wp_own, grid.cswap(wp_own))

    q_raw, up_full, gz = lax.optimization_barrier((q_raw, up_full, gz))
    attn_full, lse, q, attn_send = attend(at, nz, q_raw, qv_full, qcode, kcode, kv_pieces)
    attn_got = lax.all_to_all(attn_send, "z", 0, 0, tiled=True)
    attn_far = grid.cswap(attn_got[:, 1])
    attn_out, n2, s2, normed, middle = project(at, attn_got, attn_far, w_proj, embedded, vecs)
    near = grid.yswap(normed)
    far = grid.cswap(jnp.concatenate([normed, near], axis=0))
    normed_two, active, grad_hidden, up_sum, keep_n, send_n, keep_o, send_o = feed(up_full, normed, near, far, gz, w_ff)

    half_n = keep_n + grid.cswap(send_n).astype(F32)
    near_n = grid.yswap(half_n[rows:].astype(BF16))
    d_ff = lax.psum_scatter(
        outer(normed_two, grad_hidden, gz, active), ("z", "x"), scatter_dimension=0, tiled=True
    )
    grad_middle, grad_branch, mine, send, sums_two = branch(
        at, nz, half_n, near_n, n2, s2, vecs, gz[:rows], w_proj
    )
    theirs = grid.cswap(send)
    got = lax.all_to_all(jnp.stack([mine, theirs], axis=1), "z", 0, 0, tiled=True)

    back = attend_back(at, nz, q, qcode, kcode, got, attn_full, lse, kv_pieces)
    grad_q, grad_kv = back[0], back[1].astype(F32)
    for j in range(1, nx):
        grad_kv = grad_kv + grid.xshift(back[1 + j], -j).astype(F32)
    count = 2 * nz * rows
    near_kv = grid.yswap(grad_kv[count:].astype(BF16))
    grad_stack, part_full, part_send = leave(grad_q, grad_kv, near_kv, w_qkv)

    part_n1 = (part_full[: nz * rows] + grid.cswap(part_send).astype(F32)).reshape(nz, rows, width)
    low = part_n1.astype(BF16)
    n1_far = [grid.zshift(low[k], -k) for k in range(1, nz)]

    sums_one, stack_sum, d_wqkv = close(
        rows, part_full, unit_one, scale_one, lead, vecs, grad_middle, normed_one, grad_stack
    )
    up_column = jnp.transpose(up_sum.reshape(-1, sp, each), (1, 0, 2)).reshape(1, -1)
    sums = jnp.concatenate([sums_one, sums_two, up_column], axis=0)
    sums_far = grid.cswap(sums)
    up_both = jnp.concatenate(in_order(sums[n_vec:], sums_far[n_vec:], core), axis=0)
    sums = jnp.concatenate(
        [sums[:n_vec] + sums_far[:n_vec], jnp.where(y == 0, up_both, 0.0), jnp.where(y == 0, 0.0, up_both)], axis=0
    )
    n_sums = n_vec + 4
    qv_sum = jnp.concatenate([stack_sum[0, :local], stack_sum[0, 2 * local :]]).reshape(-1, sp, each)
    n_bias = qv_sum.shape[0] * each
    qv_column = jnp.pad(jnp.transpose(qv_sum, (1, 0, 2)).reshape(sp, n_bias), ((0, 0), (0, part - n_bias)))
    columns = jnp.concatenate([jnp.transpose(sums), qv_column.reshape(-1, 1)], axis=1).astype(BF16)
    columns = jnp.pad(columns, ((0, 0), (0, 128 - columns.shape[1])))
    dw = jnp.concatenate([d_wqkv, columns], axis=1).reshape(nz, nx, 2, part, -1)
    dw_same, dw_other = pick(dw, core, 2), pick(dw, 1 - core, 2)
    from_spin = grid.spin(jnp.where(at_home, dw_other, dw_same), back=True)
    from_cross = grid.cross(dw_other)
    dw = from_spin.astype(F32) + jnp.where(at_home, dw_same, from_cross).astype(F32)
    dw_low = dw.astype(BF16)
    dw = pick(dw, grid.x, 1)
    for j in range(1, nx):
        dw = dw + grid.xshift(pick(dw_low, grid.far_x(j), 1), j).astype(F32)
    dw = lax.all_to_all(dw.astype(BF16), "z", 0, 0, tiled=True)
    g_qkv = place_qkv([dw[k] for k in range(nz)], [jnp.int32(k * local) for k in range(nz)], local)
    tails = dw[:, :, 3 * local :].astype(F32)
    sums = jnp.transpose(jnp.sum(tails[:, :, :n_sums], axis=0))
    up_rows = jnp.where(y == 0, sums[n_vec : n_vec + 2], sums[n_vec + 2 : n_vec + 4])
    g_up_bias = up_rows.reshape(-1, each)
    qv_tail = tails[:, :n_bias, n_sums].reshape(nz, 2, -1, each)
    g_qv_bias = jnp.transpose(qv_tail, (1, 0, 2, 3)).reshape(2, -1, each)

    grad_n1 = part_n1[0]
    for block in n1_far:
        grad_n1 = grad_n1 + block.astype(F32)
    input_grad = grad_middle + norm_back(unit_one[:rows].astype(F32), scale_one[:rows], vecs[2], grad_n1)
    input_grad = input_grad.astype(BF16)
    input_grad = jnp.concatenate(in_order(input_grad, grid.yswap(input_grad), y), axis=0).astype(F32)

    half_o = keep_o + grid.cswap(after(send_o, grad_branch)).astype(F32)
    block_out = half_o[:rows] + grid.yswap(half_o[rows:].astype(BF16)).astype(F32)
    block_out = (middle + (block_out + vecs[7])).astype(BF16)
    block_out = jnp.concatenate(in_order(block_out, grid.yswap(block_out), y), axis=0)
    dp = dot(grad_branch, after(attn_out, got), TN).astype(BF16).reshape(chips, 2, part, -1)
    dp = pick(dp, core, 1).astype(F32) + grid.cswap(pick(dp, 1 - core, 1)).astype(F32)
    dp_keep, dp_send = split(dp, 2, y)
    dp = dp_keep + grid.yswap(dp_send.astype(BF16)).astype(F32)
    d_proj = grid.scatter(dp.astype(BF16).reshape(nz, nx, part, -1))

    keep, send = split(after(d_ff, grad_n1), 0, core)
    low_cols, high_cols = in_order(keep, grid.cswap(send), core)
    n_hidden = grad_hidden.shape[1]
    d_up = jnp.concatenate([low_cols[:, :n_hidden], high_cols[:, :n_hidden]], axis=1).astype(F32)
    d_down = jnp.concatenate([low_cols[:, n_hidden:], high_cols[:, n_hidden:]], axis=1).astype(F32)
    return (
        block_out,
        input_grad,
        g_qkv,
        g_qv_bias,
        jnp.transpose(d_proj),
        sums[4],
        d_up,
        g_up_bias,
        jnp.transpose(d_down),
        sums[7],
        sums[2],
        sums[3],
        sums[5],
        sums[6],
        sums[0],
        sums[1],
    )


def solution(mesh):
    sp = mesh.shape["sp"]
    nz = 4
    devices = mesh.devices.reshape(nz, sp // (2 * nz), 2, mesh.shape["tp"])
    fine = jax.sharding.Mesh(devices, SP + ("tp",))
    line = P(SP)
    placed = (
        P(SP, None),
        line,
        P(),
        P(None, SP, "tp"),
        P(None, "tp", SP),
        P("tp", SP),
        line,
        P(SP, "tp"),
        P("tp", SP),
        P("tp", SP),
    ) + (line,) * 7 + (P(SP, None),)
    given = (
        P(SP, None),
        P(SP, None),
        P(None, SP, "tp"),
        P(None, "tp", SP),
        P("tp", SP),
        line,
        P(SP, "tp"),
        P("tp", SP),
        P("tp", SP),
    ) + (line,) * 7
    return jax.shard_map(per_device, mesh=fine, in_specs=placed, out_specs=given, check_vma=False)
```

time: 422 us -> 334 us (0.79)
  starting transfers between devices: 123 us -> 69.4 us
  waiting for transfers between devices: 151 us -> 121 us
  Pallas kernels: 36.7 us -> 61.2 us
  local copies, waits for them, and re-layouts: 41.3 us -> 24.9 us
  matrix products: 17.4 us -> 1.05 us
  blocking collectives: 0 us -> 9.17 us
    ppermute x92 -> x40, starting transfers between devices: 113 us -> 49.5 us  [the longest x36 46.3 us: _move(): return lax.ppermute(block, SP, pairs)]
    ppermute x92 -> x40, waiting for transfers between devices: 112 us -> 87.3 us  [the longest x36 81.2 us: _move(): return lax.ppermute(block, SP, pairs)]
    pallas_call x7 -> x10, Pallas kernels: 35 us -> 59.5 us  [local_kernel(): pl.pallas_call(kernel, out_shape=out_shape, in_specs=[SMEM] * scalars + i...]
    dot_general x14 -> x3, matrix products: 17.4 us -> 1.05 us  [dot(): return lax.dot_general(left, right, dims, preferred_element_type=F32)]
    all_to_all x0 -> x1, blocking collectives: none -> 9.17 us  [per_device(): attn_got = lax.all_to_all(attn_send, 'z', 0, 0, tiled=True)]
    all_to_all x0 -> x2, starting transfers between devices: none -> 7.5 us  [the longest x1 4.13 us: per_device(): dw = lax.all_to_all(dw.astype(BF16), 'z', 0, 0, tiled=True)]
    ppermute x12 -> x10, waiting for transfers between devices: 39.3 us -> 34.1 us  [yswap(): return lax.ppermute(block, 'tp', [(0, 1), (1, 0)])]
    reduce_sum x13 -> x2, other arithmetic: 6.47 us -> 1.37 us  [the longest x1 1.36 us: norm_back(): mean_one = jnp.mean(scaled, axis=-1, keepdims=True)]
  transfers between devices with their start and end apart: 104 -> 54, of which waited for: 39 -> 25; matrix products, arithmetic and copies ran while one was open for 19% -> 11% of each run, Pallas kernels for 9% -> 15%
where the time goes in v3:
time: 334 us; the launch traced here: 333 us
  waiting for transfers between devices  121 us (36%)
  starting transfers between devices  69.4 us (21%)
  Pallas kernels  61.2 us (18%)
  other arithmetic  30.2 us (9%)
  local copies, waits for them, and re-layouts  24.9 us (7%)
  between operations  15.4 us (5%)
  blocking collectives  9.17 us (3%)
    ppermute x36, waiting for transfers between devices, _move(): return lax.ppermute(block, SP, pairs)  81.2 us
    pallas_call x10, Pallas kernels, local_kernel(): pl.pallas_call(kernel, out_shape=out_shape, in_specs=[SMEM] * scalars + i...  59.5 us
    ppermute x36, starting transfers between devices, _move(): return lax.ppermute(block, SP, pairs)  46.3 us
    ppermute x10, waiting for transfers between devices, yswap(): return lax.ppermute(block, 'tp', [(0, 1), (1, 0)])  34.1 us
    unnamed x133, local copies, waits for them, and re-layouts  13.2 us
    ppermute x10, starting transfers between devices, yswap(): return lax.ppermute(block, 'tp', [(0, 1), (1, 0)])  12.3 us
    all_to_all x1, blocking collectives, per_device(): attn_got = lax.all_to_all(attn_send, 'z', 0, 0, tiled=True)  9.17 us
  transfers between devices with their start and end apart: 54, of which 25 were waited for; matrix products, arithmetic and copies ran while one was open for 11% of the time, Pallas kernels for 15%

profile of v3, /device:TPU:0, one launch (start us, length us, event | category | flops | bytes accessed | tf_op | source)
XLA Modules:
  0.0 332.7 jit_solution(14992410780542983392)
XLA Ops:
  8.9 3.1 collective-permute-start.5
  12.0 2.6 collective-permute-start.6
  16.2 2.0 collective-permute-done.6
  21.5 2.9 collective-permute-start.1
  25.6 5.2 %collective-permute-done.refs_1_ = bf16[96,1152]{1,0:T(8,128)(2,1)S(1)} collective-permute-done((bf16[96,1152]{1,0:T(8,128)(2,1)S(1)}, bf16[96,1152]{1,0:T(8,128)(2,1)S(1)}, u32[]{:S(2)}, u32[]{:S(2)}) %collective-permute-start) | collective-permute-done | bytes 221216 | tf_op jit(solution)/shard_map/ppermute | solution.py:46
  30.8 9.1 %collective-permute-done.1.refs_2_ = bf16[96,1152]{1,0:T(8,128)(2,1)S(1)} collective-permute-done((bf16[96,1152]{1,0:T(8,128)(2,1)S(1)}, bf16[96,1152]{1,0:T(8,128)(2,1)S(1)}, u32[]{:S(2)}, u32[]{:S(2)}) %collective-permute-start.1) | collective-permute-done | bytes 221216 | tf_op jit(solution)/shard_map/ppermute | solution.py:46
  41.9 5.6 %collective-permute-done.8 = bf16[4,64,384]{2,1,0:T(8,128)(2,1)S(1)} collective-permute-done((bf16[4,64,384]{2,1,0:T(8,128)(2,1)S(1)}, bf16[4,64,384]{2,1,0:T(8,128)(2,1)S(1)}, u32[]{:S(2)}, u32[]{:S(2)}) %collective-permute-start.8) | collective-permute-done | bytes 196640 | tf_op jit(solution)/shard_map/ppermute | solution.py:46
  51.5 5.8 %collective-permute-done.9 = bf16[2,4,64,384]{3,2,1,0:T(8,128)(2,1)S(1)} collective-permute-done((bf16[2,4,64,384]{3,2,1,0:T(8,128)(2,1)S(1)}, bf16[2,4,64,384]{3,2,1,0:T(8,128)(2,1)S(1)}, u32[]{:S(2)}, u32[]{:S(2)}) %collective-permute-start.9) | collective-permute-done | bytes 393248 | tf_op jit(solution)/shard_map/ppermute | solution.py:73
  57.4 5.1 %collective-permute-start.17 = (bf16[64,512]{1,0:T(8,128)(2,1)}, bf16[64,512]{1,0:T(8,128)(2,1)S(1)}, u32[]{:S(2)}, u32[]{:S(2)}) collective-permute-start(bf16[64,512]{1,0:T(8,128)(2,1)} %bitcast.173), channel_id=1, source_target_pairs={{0,8},{2,10},{4,12},{6,14},{8,16},{10,18},{12,20},{14,22},{16,24},... | collective-permute-start | bytes 196616 | tf_op jit(solution)/shard_map/ppermute | solution.py:46
  62.8 2.2 collective-permute-start.19
  65.0 4.2 %enter.1 = (bf16[768,1024]{1,0:T(8,128)(2,1)}, bf16[768,1024]{1,0:T(8,128)(2,1)}, f32[768,1]{1,0:T(8,128)S(1)}, f32[768,1]{1,0:T(8,128)S(1)}, f32[96,1024]{1,0:T...) custom-call(s32[4]{0:T(128)S(1)} %pad_add_fusion.at_ref, ...), custom_call_target="tpu_custom_call" | custom-call | bytes 65536 | tf_op jit(solution)/shard_map/enter/pallas_call | solution.py:162
  72.3 3.8 %collective-permute-start.13 = (bf16[768,256]{1,0:T(8,128)(2,1)S(1)}, bf16[768,256]{1,0:T(8,128)(2,1)S(1)}, u32[]{:S(2)}, u32[]{:S(2)}) collective-permute-start(bf16[768,256]{1,0:T(8,128)(2,1)S(1)} %get-tuple-element.70.refs_0_), channel_id=1, source_target_pairs={{0,1},{1,0},{2,3},{3,2},{4,5},{5,4},{6,7},{7,6},{8,9},{9,8},{10,11... | collective-permute-start | bytes 1179656 | tf_op jit(solution)/shard_map/ppermute | solution.py:58
  83.7 13.4 %collective-permute-done.20 = bf16[4,64,512]{2,1,0:T(8,128)(2,1)S(1)} collective-permute-done((bf16[4,64,512]{2,1,0:T(8,128)(2,1)S(1)}, bf16[4,64,512]{2,1,0:T(8,128)(2,1)S(1)}, u32[]{:S(2)}, u32[]{:S(2)}) %collective-permute-start.20) | collective-permute-done | bytes 262176 | tf_op jit(solution)/shard_map/ppermute | solution.py:46
  97.2 2.6 collective-permute-start.21
  101.2 2.5 collective-permute-start.15
  103.7 6.0 %collective-permute-done.21 = bf16[2,4,64,512]{3,2,1,0:T(8,128)(2,1)S(1)} collective-permute-done((bf16[2,4,64,512]{3,2,1,0:T(8,128)(2,1)S(1)}, bf16[2,4,64,512]{3,2,1,0:T(8,128)(2,1)S(1)}, u32[]{:S(2)}, u32[]{:S(2)}) %collective-permute-start.21) | collective-permute-done | bytes 524320 | tf_op jit(solution)/shard_map/ppermute | solution.py:58
  110.0 1.9 pad_maximum_fusion.2.gz_ref
  111.9 8.4 %collective-permute-done.15.refs_3_ = bf16[768,256]{1,0:T(8,128)(2,1)S(1)} collective-permute-done((bf16[768,256]{1,0:T(8,128)(2,1)S(1)}, bf16[768,256]{1,0:T(8,128)(2,1)S(1)}, u32[]{:S(2)}, u32[]{:S(2)}) %collective-permute-start.15) | collective-permute-done | bytes 393248 | tf_op jit(solution)/shard_map/ppermute | solution.py:46
  120.4 13.6 %attend.1 = (f32[768,128]{1,0:T(8,128)S(1)}, f32[8,768]{1,0:T(8,128)S(1)}, bf16[768,128]{1,0:T(8,128)(2,1)S(1)}, bf16[4,2,96,128]{3,2,1,0:T(8,128)(2,1)S(1)}) custom-call(s32[4]{0:T(128)S(1)} %pad_add_fusion.at_ref, f32[768,128]{1,0:T(8,128)S(1)} %get-tuple-element.72.q_ref, f32[2,128]{1,0:T(2,128)S(1)} %fusion.24.bias_ref, ...), custom_call_target="tpu_custom_call" | custom-call | bytes 65536 | tf_op jit(solution)/shard_map/attend/pallas_call | solution.py:162
  134.0 9.2 %all_to_all.15.got_ref = bf16[4,2,96,128]{3,2,1,0:T(8,128)(2,1)S(1)} all-to-all(bf16[4,2,96,128]{3,2,1,0:T(8,128)(2,1)S(1)} %get-tuple-element.73), channel_id=1, replica_groups=mesh['z'=4,'x'=2,'core'=2,'tp'=2] {'z'}, dimensions={0} | all-to-all | bytes 393216 | tf_op jit(solution)/shard_map/all_to_all | solution.py:798
  147.4 6.4 %collective-permute-done.23.near_ref = bf16[96,1024]{1,0:T(8,128)(2,1)S(1)} collective-permute-done((bf16[96,1024]{1,0:T(8,128)(2,1)S(1)}, bf16[96,1024]{1,0:T(8,128)(2,1)S(1)}, u32[]{:S(2)}, u32[]{:S(2)}) %collective-permute-start.23) | collective-permute-done | bytes 196640 | tf_op jit(solution)/shard_map/ppermute | solution.py:58
  153.9 1.8 collective-permute-done.24.far_ref
  155.8 8.4 %feed.1 = (bf16[384,1024]{1,0:T(8,128)(2,1)}, bf16[384,1024]{1,0:T(8,128)(2,1)}, bf16[384,1024]{1,0:T(8,128)(2,1)}, f32[1,1024]{1,0:T(1,128)}, f32[192,1024]{1,0...) custom-call(f32[1,1024]{1,0:T(1,128)} %broadcast_select_fusion.20.bias_ref, ...), custom_call_target="tpu_custom_call" | custom-call | bytes 65536 | tf_op jit(solution)/shard_map/feed/pallas_call | solution.py:162
  164.4 1.8 collective-permute-done.26
  168.2 6.3 %collective-permute-done.27.near_ref = bf16[96,1024]{1,0:T(8,128)(2,1)S(1)} collective-permute-done((bf16[96,1024]{1,0:T(8,128)(2,1)S(1)}, bf16[96,1024]{1,0:T(8,128)(2,1)S(1)}, u32[]{:S(2)}, u32[]{:S(2)}) %collective-permute-start.27) | collective-permute-done | bytes 196640 | tf_op jit(solution)/shard_map/ppermute | solution.py:58
  178.6 3.4 %all-to-all-start.1 = ((bf16[4,2,96,128]{3,2,1,0:T(8,128)(2,1)}), bf16[4,2,96,128]{3,2,1,0:T(8,128)(2,1)S(1)}, u32[]{:S(2)}, u32[]{:S(2)}) async-start(bf16[4,2,96,128]{3,2,1,0:T(8,128)(2,1)} %pad_maximum_fusion.13), calls=%async_computation.1 | async-start | bytes 393216 | tf_op jit(solution)/shard_map/all_to_all | solution.py:814
  186.9 4.5 %outer.1 = bf16[1024,2048]{1,0:T(8,128)(2,1)} custom-call(bf16[384,1024]{1,0:T(8,128)(2,1)S(1)} %copy-done.10, bf16[384,1024]{1,0:T(8,128)(2,1)S(1)} %copy-done.12, bf16[384,1024]{1,0:T(8,128)(2,1)S(1)} %copy-done, bf16[384,1024]{1,0:T(8,128)(2,1)S(1)} %copy-done.11), custom_call_target="tpu_custom_call" | custom-call | bytes 65536 | tf_op jit(solution)/shard_map/outer/pallas_call | solution.py:162
  192.3 17.4 %attend_back.1 = (bf16[768,128]{1,0:T(8,128)(2,1)}, bf16[1536,256]{1,0:T(8,128)(2,1)}, bf16[1536,256]{1,0:T(8,128)(2,1)}) custom-call(s32[4]{0:T(128)} %copy-done.32, bf16[768,128]{1,0:T(8,128)(2,1)} %copy-done.26, bf16[768,128]{1,0:T(8,128)(2,1)} %copy-done.3, bf16[3072,128]{1,0:T(8,128)(2,1)} %copy-done.1, bf16[4,2,96,128]{3,2,1,0:T(8,128)(2,1)} %copy-done.44, ...), custom_call_target="tpu_custom_call" | custom-call | bytes 65536 | tf_op jit(solution)/shard_map/attend_back/pallas_call | solution.py:162
  217.0 5.1 %collective-permute-done.29 = bf16[96,1024]{1,0:T(8,128)(2,1)S(1)} collective-permute-done((bf16[96,1024]{1,0:T(8,128)(2,1)S(1)}, bf16[96,1024]{1,0:T(8,128)(2,1)S(1)}, u32[]{:S(2)}, u32[]{:S(2)}) %collective-permute-start.29) | collective-permute-done | bytes 196640 | tf_op jit(solution)/shard_map/ppermute | solution.py:58
  222.9 12.6 %collective-permute-done.32 = bf16[1536,256]{1,0:T(8,128)(2,1)} collective-permute-done((bf16[1536,256]{1,0:T(8,128)(2,1)}, bf16[1536,256]{1,0:T(8,128)(2,1)}, u32[]{:S(2)}, u32[]{:S(2)}) %collective-permute-start.32) | collective-permute-done | bytes 786464 | tf_op jit(solution)/shard_map/ppermute | solution.py:46
  237.7 1.8 convert_add_fusion
  243.1 6.0 %collective-permute-done.33.near_ref = bf16[768,256]{1,0:T(8,128)(2,1)S(1)} collective-permute-done((bf16[768,256]{1,0:T(8,128)(2,1)S(1)}, bf16[768,256]{1,0:T(8,128)(2,1)S(1)}, u32[]{:S(2)}, u32[]{:S(2)}) %collective-permute-start.33) | collective-permute-done | bytes 393248 | tf_op jit(solution)/shard_map/ppermute | solution.py:58
  249.1 2.8 leave.1
  251.9 4.9 %close.1 = (f32[4,1024]{1,0:T(4,128)S(1)}, f32[1,384]{1,0:T(1,128)S(1)}, bf16[1024,384]{1,0:T(8,128)(2,1)S(1)}) custom-call(f32[768,1024]{1,0:T(8,128)} %get-tuple-element.104.full_ref, bf16[768,1024]{1,0:T(8,128)(2,1)S(1)} %copy-done.2, f32[768,1]{1,0:T(8,128)S(1)} %copy-done.16, f32[768,1]{1,0:T(8,128)S(1)} %copy-done.18, ...), custom_call_target="tpu_custom_call" | custom-call | bytes 65536 | tf_op jit(solution)/shard_map/close/pallas_call | solution.py:162
  261.5 3.1 collective-permute-start.34
  266.0 1.7 collective-permute-start.45
  268.3 1.7 collective-permute-start.42
  270.0 4.5 %collective-permute-done.45 = bf16[4,64,512]{2,1,0:T(8,128)(2,1)S(1)} collective-permute-done((bf16[4,64,512]{2,1,0:T(8,128)(2,1)S(1)}, bf16[4,64,512]{2,1,0:T(8,128)(2,1)S(1)}, u32[]{:S(2)}, u32[]{:S(2)}) %collective-permute-start.45) | collective-permute-done | bytes 262176 | tf_op jit(solution)/shard_map/ppermute | solution.py:46
  276.0 2.9 collective-permute-start.46
  278.9 2.3 collective-permute-start.47
  282.4 1.7 collective-permute-start.35
  285.8 4.1 %all-to-all-start.2 = ((bf16[4,64,512]{2,1,0:T(8,128)(2,1)}), bf16[4,64,512]{2,1,0:T(8,128)(2,1)}, u32[]{:S(2)}, u32[]{:S(2)}) async-start(bf16[4,64,512]{2,1,0:T(8,128)(2,1)} %fusion.2), calls=%async_computation.2 | async-start | bytes 524288 | tf_op jit(solution)/shard_map/all_to_all | solution.py:853
  290.9 3.0 collective-permute-start.48
  294.0 12.5 %collective-permute-done.36 = bf16[96,1024]{1,0:T(8,128)(2,1)} collective-permute-done((bf16[96,1024]{1,0:T(8,128)(2,1)}, bf16[96,1024]{1,0:T(8,128)(2,1)}, u32[]{:S(2)}, u32[]{:S(2)}) %collective-permute-start.36) | collective-permute-done | bytes 196640 | tf_op jit(solution)/shard_map/ppermute | solution.py:46
  309.1 1.7 fusion.16
  310.8 4.2 %collective-permute-done.38 = bf16[96,1024]{1,0:T(8,128)(2,1)S(1)} collective-permute-done((bf16[96,1024]{1,0:T(8,128)(2,1)S(1)}, bf16[96,1024]{1,0:T(8,128)(2,1)S(1)}, u32[]{:S(2)}, u32[]{:S(2)}) %collective-permute-start.38) | collective-permute-done | bytes 196640 | tf_op jit(solution)/shard_map/ppermute | solution.py:58
  319.9 1.6 slice_bitcast_fusion.1
  321.5 1.7 place_qkv.1
  (343 shorter events, 77.9 us)
Async XLA Ops:
  7.2 148.5 %all-gather.2.cloned.1.call-start = ((), (), s32[]{:S(2)}) async-start(), calls=%async_computation.4 | async-start | bytes 4718592 | tf_op jit(solution)/shard_map/all_gather | solution.py:782
  8.9 7.3 %collective-permute-start.5 = (bf16[64,384]{1,0:T(8,128)(2,1)S(1)}, bf16[64,384]{1,0:T(8,128)(2,1)S(1)}, u32[]{:S(2)}, u32[]{:S(2)}) collective-permute-start(bf16[64,384]{1,0:T(8,128)(2,1)S(1)} %get-tuple-element.240), channel_id=1, source_target_pairs={{0,8},{2,10},{4,12},{6,14},{8,16},{10,18},{12,20},{14,22},{16,24},... | collective-permute-start | bytes 147464 | tf_op jit(solution)/shard_map/ppermute | solution.py:46
  12.0 6.2 %collective-permute-start.6 = (bf16[64,384]{1,0:T(8,128)(2,1)S(1)}, bf16[64,384]{1,0:T(8,128)(2,1)S(1)}, u32[]{:S(2)}, u32[]{:S(2)}) collective-permute-start(bf16[64,384]{1,0:T(8,128)(2,1)S(1)} %get-tuple-element.239), channel_id=1, source_target_pairs={{0,16},{2,18},{4,20},{6,22},{8,24},{10,26},{12,28},{14,30},{16,0},... | collective-permute-start | bytes 147464 | tf_op jit(solution)/shard_map/ppermute | solution.py:46
  19.5 5.2 %collective-permute-start.25 = (bf16[64,2048]{1,0:T(8,128)(2,1)S(1)}, bf16[64,2048]{1,0:T(8,128)(2,1)S(1)}, u32[]{:S(2)}, u32[]{:S(2)}) collective-permute-start(bf16[64,2048]{1,0:T(8,128)(2,1)S(1)} %pad_maximum_fusion.11), channel_id=1, source_target_pairs={{0,2},{2,0},{4,6},{6,4},{8,10},{10,8},{12,14},{14,12},{16,18},{18,... | collective-permute-start | bytes 786440 | tf_op jit(solution)/shard_map/ppermute | solution.py:46
  20.6 10.2 %collective-permute-start = (bf16[96,1152]{1,0:T(8,128)(2,1)S(1)}, bf16[96,1152]{1,0:T(8,128)(2,1)S(1)}, u32[]{:S(2)}, u32[]{:S(2)}) collective-permute-start(bf16[96,1152]{1,0:T(8,128)(2,1)S(1)} %concatenate.67.refs_0_), channel_id=1, source_target_pairs={{0,8},{2,10},{4,12},{6,14},{8,16},{10,18},{12,20},{14,22},{16,24},... | collective-permute-start | bytes 663560 | tf_op jit(solution)/shard_map/ppermute | solution.py:46
  21.5 18.5 %collective-permute-start.1 = (bf16[96,1152]{1,0:T(8,128)(2,1)S(1)}, bf16[96,1152]{1,0:T(8,128)(2,1)S(1)}, u32[]{:S(2)}, u32[]{:S(2)}) collective-permute-start(bf16[96,1152]{1,0:T(8,128)(2,1)S(1)} %concatenate.67.refs_0_), channel_id=1, source_target_pairs={{0,16},{2,18},{4,20},{6,22},{8,24},{10,26},{12,28},{14,30},{16,0},... | collective-permute-start | bytes 663560 | tf_op jit(solution)/shard_map/ppermute | solution.py:46
  24.4 15.6 %collective-permute-start.2 = (bf16[96,1152]{1,0:T(8,128)(2,1)S(1)}, bf16[96,1152]{1,0:T(8,128)(2,1)S(1)}, u32[]{:S(2)}, u32[]{:S(2)}) collective-permute-start(bf16[96,1152]{1,0:T(8,128)(2,1)S(1)} %concatenate.67.refs_0_), channel_id=1, source_target_pairs={{0,24},{2,26},{4,28},{6,30},{8,0},{10,2},{12,4},{14,6},{16,8},{18,... | collective-permute-start | bytes 663560 | tf_op jit(solution)/shard_map/ppermute | solution.py:46
  40.1 9.8 %collective-permute-start.3 = (bf16[4,96,1152]{2,1,0:T(8,128)(2,1)S(1)}, bf16[4,96,1152]{2,1,0:T(8,128)(2,1)S(1)}, u32[]{:S(2)}, u32[]{:S(2)}) collective-permute-start(bf16[4,96,1152]{2,1,0:T(8,128)(2,1)S(1)} %pad_maximum_fusion.1), channel_id=1, source_target_pairs={{0,2},{2,0},{4,6},{6,4},{8,10},{10,8},{12,14},{14,12},{16,18},{18,... | collective-permute-start | bytes 2654216 | tf_op jit(solution)/shard_map/ppermute | solution.py:46
  40.2 7.3 %collective-permute-start.8 = (bf16[4,64,384]{2,1,0:T(8,128)(2,1)S(1)}, bf16[4,64,384]{2,1,0:T(8,128)(2,1)S(1)}, u32[]{:S(2)}, u32[]{:S(2)}) collective-permute-start(bf16[4,64,384]{2,1,0:T(8,128)(2,1)S(1)} %copy-done.50), channel_id=1, source_target_pairs={{0,4},{2,6},{4,0},{6,2},{8,12},{10,14},{12,8},{14,10},{16,20},{18,... | collective-permute-start | bytes 589832 | tf_op jit(solution)/shard_map/ppermute | solution.py:46
  47.6 9.7 %collective-permute-start.9 = (bf16[2,4,64,384]{3,2,1,0:T(8,128)(2,1)S(1)}, bf16[2,4,64,384]{3,2,1,0:T(8,128)(2,1)S(1)}, u32[]{:S(2)}, u32[]{:S(2)}) collective-permute-start(bf16[2,4,64,384]{3,2,1,0:T(8,128)(2,1)S(1)} %pad_maximum_fusion.5), channel_id=1, source_target_pairs={{0,1},{2,0},{3,2},{1,3},{4,5},{6,4},{7,6},{5,7},{8,9},{10,8},{11,1... | collective-permute-start | bytes 1179656 | tf_op jit(solution)/shard_map/ppermute | solution.py:73
  49.2 8.1 %collective-permute-start.10 = (bf16[2,4,64,384]{3,2,1,0:T(8,128)(2,1)S(1)}, bf16[2,4,64,384]{3,2,1,0:T(8,128)(2,1)S(1)}, u32[]{:S(2)}, u32[]{:S(2)}) collective-permute-start(bf16[2,4,64,384]{3,2,1,0:T(8,128)(2,1)S(1)} %pad_maximum_fusion.5), channel_id=1, source_target_pairs={{2,1},{1,2},{6,5},{5,6},{10,9},{9,10},{14,13},{13,14},{18,17},{17,... | collective-permute-start | bytes 1179656 | tf_op jit(solution)/shard_map/ppermute | solution.py:77
  49.9 15.0 %collective-permute-start.4 = (bf16[2,4,16,128]{3,2,1,0:T(8,128)(2,1)S(1)}, bf16[2,4,16,128]{3,2,1,0:T(8,128)(2,1)S(1)}, u32[]{:S(2)}, u32[]{:S(2)}) collective-permute-start(bf16[2,4,16,128]{3,2,1,0:T(8,128)(2,1)S(1)} %get-tuple-element.246), channel_id=1, source_target_pairs={{0,4},{2,6},{4,0},{6,2},{8,12},{10,14},{12,8},{14,10},{16,20},{18,... | collective-permute-start | bytes 98312 | tf_op jit(solution)/shard_map/ppermute | solution.py:46
  57.4 23.4 %collective-permute-start.17 = (bf16[64,512]{1,0:T(8,128)(2,1)}, bf16[64,512]{1,0:T(8,128)(2,1)S(1)}, u32[]{:S(2)}, u32[]{:S(2)}) collective-permute-start(bf16[64,512]{1,0:T(8,128)(2,1)} %bitcast.173), channel_id=1, source_target_pairs={{0,8},{2,10},{4,12},{6,14},{8,16},{10,18},{12,20},{14,22},{16,24},... | collective-permute-start | bytes 196616 | tf_op jit(solution)/shard_map/ppermute | solution.py:46
  62.5 18.3 %collective-permute-start.18 = (bf16[64,512]{1,0:T(8,128)(2,1)}, bf16[64,512]{1,0:T(8,128)(2,1)S(1)}, u32[]{:S(2)}, u32[]{:S(2)}) collective-permute-start(bf16[64,512]{1,0:T(8,128)(2,1)} %bitcast.174), channel_id=1, source_target_pairs={{0,16},{2,18},{4,20},{6,22},{8,24},{10,26},{12,28},{14,30},{16,0},... | collective-permute-start | bytes 196616 | tf_op jit(solution)/shard_map/ppermute | solution.py:46
  62.8 18.1 %collective-permute-start.19 = (bf16[64,512]{1,0:T(8,128)(2,1)}, bf16[64,512]{1,0:T(8,128)(2,1)}, u32[]{:S(2)}, u32[]{:S(2)}) collective-permute-start(bf16[64,512]{1,0:T(8,128)(2,1)} %bitcast.175), channel_id=1, source_target_pairs={{0,24},{2,26},{4,28},{6,30},{8,0},{10,2},{12,4},{14,6},{16,8},{18,... | collective-permute-start | bytes 196616 | tf_op jit(solution)/shard_map/ppermute | solution.py:46
  72.3 24.8 %collective-permute-start.13 = (bf16[768,256]{1,0:T(8,128)(2,1)S(1)}, bf16[768,256]{1,0:T(8,128)(2,1)S(1)}, u32[]{:S(2)}, u32[]{:S(2)}) collective-permute-start(bf16[768,256]{1,0:T(8,128)(2,1)S(1)} %get-tuple-element.70.refs_0_), channel_id=1, source_target_pairs={{0,1},{1,0},{2,3},{3,2},{4,5},{5,4},{6,7},{7,6},{8,9},{9,8},{10,11... | collective-permute-start | bytes 1179656 | tf_op jit(solution)/shard_map/ppermute | solution.py:58
  76.2 35.8 %collective-permute-start.14 = (bf16[768,256]{1,0:T(8,128)(2,1)S(1)}, bf16[768,256]{1,0:T(8,128)(2,1)S(1)}, u32[]{:S(2)}, u32[]{:S(2)}) collective-permute-start(bf16[768,256]{1,0:T(8,128)(2,1)S(1)} %get-tuple-element.70.refs_0_), channel_id=1, source_target_pairs={{0,4},{2,6},{4,0},{6,2},{8,12},{10,14},{12,8},{14,10},{16,20},{18,... | collective-permute-start | bytes 1179656 | tf_op jit(solution)/shard_map/ppermute | solution.py:46
  80.8 29.2 %collective-permute-start.11 = (bf16[192,1024]{1,0:T(8,128)(2,1)}, bf16[192,1024]{1,0:T(8,128)(2,1)}, u32[]{:S(2)}, u32[]{:S(2)}) collective-permute-start(bf16[192,1024]{1,0:T(8,128)(2,1)} %pad_maximum_fusion.6), channel_id=1, source_target_pairs={{0,2},{2,0},{4,6},{6,4},{8,10},{10,8},{12,14},{14,12},{16,18},{18,... | collective-permute-start | bytes 1179656 | tf_op jit(solution)/shard_map/ppermute | solution.py:46
  81.7 15.4 %collective-permute-start.20 = (bf16[4,64,512]{2,1,0:T(8,128)(2,1)S(1)}, bf16[4,64,512]{2,1,0:T(8,128)(2,1)S(1)}, u32[]{:S(2)}, u32[]{:S(2)}) collective-permute-start(bf16[4,64,512]{2,1,0:T(8,128)(2,1)S(1)} %pad_maximum_fusion.9), channel_id=1, source_target_pairs={{0,4},{2,6},{4,0},{6,2},{8,12},{10,14},{12,8},{14,10},{16,20},{18,... | collective-permute-start | bytes 786440 | tf_op jit(solution)/shard_map/ppermute | solution.py:46
  83.3 26.6 %collective-permute-start.12 = (f32[2,512]{1,0:T(2,128)S(1)}, f32[2,512]{1,0:T(2,128)S(1)}, u32[]{:S(2)}, u32[]{:S(2)}) collective-permute-start(f32[2,512]{1,0:T(2,128)S(1)} %reshape.345), channel_id=1, source_target_pairs={{0,1},{1,0},{2,3},{3,2},{4,5},{5,4},{6,7},{7,6},{8,9},{9,8},{10,11... | collective-permute-start | bytes 12296 | tf_op jit(solution)/shard_map/ppermute | solution.py:58
  97.2 12.6 %collective-permute-start.21 = (bf16[2,4,64,512]{3,2,1,0:T(8,128)(2,1)S(1)}, bf16[2,4,64,512]{3,2,1,0:T(8,128)(2,1)S(1)}, u32[]{:S(2)}, u32[]{:S(2)}) collective-permute-start(bf16[2,4,64,512]{3,2,1,0:T(8,128)(2,1)S(1)} %pad_maximum_fusion.3), channel_id=1, source_target_pairs={{0,1},{1,0},{2,3},{3,2},{4,5},{5,4},{6,7},{7,6},{8,9},{9,8},{10,11... | collective-permute-start | bytes 1572872 | tf_op jit(solution)/shard_map/ppermute | solution.py:58
  101.2 19.2 %collective-permute-start.15 = (bf16[768,256]{1,0:T(8,128)(2,1)S(1)}, bf16[768,256]{1,0:T(8,128)(2,1)S(1)}, u32[]{:S(2)}, u32[]{:S(2)}) collective-permute-start(bf16[768,256]{1,0:T(8,128)(2,1)S(1)} %collective-permute-done.13.refs_1_), channel_id=1, source_target_pairs={{0,4},{2,6},{4,0},{6,2},{8,12},{10,14},{12,8},{14,10},{16,20},{18,... | collective-permute-start | bytes 1179656 | tf_op jit(solution)/shard_map/ppermute | solution.py:46
  109.9 33.4 %collective-permute-start.22 = (bf16[2,2,4,64,512]{4,3,2,1,0:T(8,128)(2,1)S(1)}, bf16[2,2,4,64,512]{4,3,2,1,0:T(8,128)(2,1)S(1)}, u32[]{:S(2)}, u32[]{:S(2)}) collective-permute-start(bf16[2,2,4,64,512]{4,3,2,1,0:T(8,128)(2,1)S(1)} %pad_maximum_fusion.own_ref), channel_id=1, source_target_pairs={{0,2},{2,0},{4,6},{6,4},{8,10},{10,8},{12,14},{14,12},{16,18},{18,... | collective-permute-start | bytes 3145736 | tf_op jit(solution)/shard_map/ppermute | solution.py:46
  146.8 7.0 %collective-permute-start.23 = (bf16[96,1024]{1,0:T(8,128)(2,1)S(1)}, bf16[96,1024]{1,0:T(8,128)(2,1)S(1)}, u32[]{:S(2)}, u32[]{:S(2)}) collective-permute-start(bf16[96,1024]{1,0:T(8,128)(2,1)S(1)} %get-tuple-element.81.own_ref), channel_id=1, source_target_pairs={{0,1},{1,0},{2,3},{3,2},{4,5},{5,4},{6,7},{7,6},{8,9},{9,8},{10,11... | collective-permute-start | bytes 589832 | tf_op jit(solution)/shard_map/ppermute | solution.py:58
  167.5 7.0 %collective-permute-start.27 = (bf16[96,1024]{1,0:T(8,128)(2,1)S(1)}, bf16[96,1024]{1,0:T(8,128)(2,1)S(1)}, u32[]{:S(2)}, u32[]{:S(2)}) collective-permute-start(bf16[96,1024]{1,0:T(8,128)(2,1)S(1)} %slice.394), channel_id=1, source_target_pairs={{0,1},{1,0},{2,3},{3,2},{4,5},{5,4},{6,7},{7,6},{8,9},{9,8},{10,11... | collective-permute-start | bytes 589832 | tf_op jit(solution)/shard_map/ppermute | solution.py:58
  178.6 13.0 %all-to-all-start.1 = ((bf16[4,2,96,128]{3,2,1,0:T(8,128)(2,1)}), bf16[4,2,96,128]{3,2,1,0:T(8,128)(2,1)S(1)}, u32[]{:S(2)}, u32[]{:S(2)}) async-start(bf16[4,2,96,128]{3,2,1,0:T(8,128)(2,1)} %pad_maximum_fusion.13), calls=%async_computation.1 | async-start | bytes 393216 | tf_op jit(solution)/shard_map/all_to_all | solution.py:814
  182.0 136.7 %reduce-scatter.2.cloned.1.call-start = ((), (), s32[]{:S(2)}) async-start(), calls=%async_computation.5 | async-start | bytes 4718592 | tf_op jit(solution)/shard_map/reduce_scatter | solution.py:807
  191.4 23.2 %collective-permute-start.28 = (bf16[192,1024]{1,0:T(8,128)(2,1)}, bf16[192,1024]{1,0:T(8,128)(2,1)S(1)}, u32[]{:S(2)}, u32[]{:S(2)}) collective-permute-start(bf16[192,1024]{1,0:T(8,128)(2,1)} %get-tuple-element.93), channel_id=1, source_target_pairs={{0,2},{2,0},{4,6},{6,4},{8,10},{10,8},{12,14},{14,12},{16,18},{18,... | collective-permute-start | bytes 1179656 | tf_op jit(solution)/shard_map/ppermute | solution.py:46
  209.8 25.7 %collective-permute-start.32 = (bf16[1536,256]{1,0:T(8,128)(2,1)}, bf16[1536,256]{1,0:T(8,128)(2,1)}, u32[]{:S(2)}, u32[]{:S(2)}) collective-permute-start(bf16[1536,256]{1,0:T(8,128)(2,1)} %get-tuple-element.102), channel_id=1, source_target_pairs={{0,4},{2,6},{4,0},{6,2},{8,12},{10,14},{12,8},{14,10},{16,20},{18,... | collective-permute-start | bytes 2359304 | tf_op jit(solution)/shard_map/ppermute | solution.py:46
  214.6 23.1 %collective-permute-start.43 = (bf16[8,64,1024]{2,1,0:T(8,128)(2,1)}, bf16[8,64,1024]{2,1,0:T(8,128)(2,1)}, u32[]{:S(2)}, u32[]{:S(2)}) collective-permute-start(bf16[8,64,1024]{2,1,0:T(8,128)(2,1)} %dynamic-slice_bitcast_fusion), channel_id=1, source_target_pairs={{0,2},{2,0},{4,6},{6,4},{8,10},{10,8},{12,14},{14,12},{16,18},{18,... | collective-permute-start | bytes 3145736 | tf_op jit(solution)/shard_map/ppermute | solution.py:46
  214.8 7.3 %collective-permute-start.29 = (bf16[96,1024]{1,0:T(8,128)(2,1)S(1)}, bf16[96,1024]{1,0:T(8,128)(2,1)S(1)}, u32[]{:S(2)}, u32[]{:S(2)}) collective-permute-start(bf16[96,1024]{1,0:T(8,128)(2,1)S(1)} %slice.393), channel_id=1, source_target_pairs={{0,1},{1,0},{2,3},{3,2},{4,5},{5,4},{6,7},{7,6},{8,9},{9,8},{10,11... | collective-permute-start | bytes 589832 | tf_op jit(solution)/shard_map/ppermute | solution.py:58
  222.2 37.6 %collective-permute-start.30 = (bf16[96,1024]{1,0:T(8,128)(2,1)S(1)}, bf16[96,1024]{1,0:T(8,128)(2,1)}, u32[]{:S(2)}, u32[]{:S(2)}) collective-permute-start(bf16[96,1024]{1,0:T(8,128)(2,1)S(1)} %fusion.12), channel_id=1, source_target_pairs={{0,1},{1,0},{2,3},{3,2},{4,5},{5,4},{6,7},{7,6},{8,9},{9,8},{10,11... | collective-permute-start | bytes 589832 | tf_op jit(solution)/shard_map/ppermute | solution.py:58
  237.0 12.1 %collective-permute-start.33 = (bf16[768,256]{1,0:T(8,128)(2,1)S(1)}, bf16[768,256]{1,0:T(8,128)(2,1)S(1)}, u32[]{:S(2)}, u32[]{:S(2)}) collective-permute-start(bf16[768,256]{1,0:T(8,128)(2,1)S(1)} %slice.392), channel_id=1, source_target_pairs={{0,1},{1,0},{2,3},{3,2},{4,5},{5,4},{6,7},{7,6},{8,9},{9,8},{10,11... | collective-permute-start | bytes 1179656 | tf_op jit(solution)/shard_map/ppermute | solution.py:58
  241.6 23.0 %collective-permute-start.44 = (bf16[8,64,512]{2,1,0:T(8,128)(2,1)}, bf16[8,64,512]{2,1,0:T(8,128)(2,1)}, u32[]{:S(2)}, u32[]{:S(2)}) collective-permute-start(bf16[8,64,512]{2,1,0:T(8,128)(2,1)} %select_convert_fusion.1), channel_id=1, source_target_pairs={{0,1},{1,0},{2,3},{3,2},{4,5},{5,4},{6,7},{7,6},{8,9},{9,8},{10,11... | collective-permute-start | bytes 1572872 | tf_op jit(solution)/shard_map/ppermute | solution.py:58
  258.8 9.2 %collective-permute-start.40 = (bf16[4,2,64,512]{3,2,0,1:T(8,128)(2,1)S(1)}, bf16[4,2,64,512]{3,2,0,1:T(8,128)(2,1)S(1)}, u32[]{:S(2)}, u32[]{:S(2)}) collective-permute-start(bf16[4,2,64,512]{3,2,0,1:T(8,128)(2,1)S(1)} %bitcast_select_fusion.1), channel_id=1, source_target_pairs={{1,0},{0,2},{2,3},{3,1},{5,4},{4,6},{6,7},{7,5},{9,8},{8,10},{10,1... | collective-permute-start | bytes 1572872 | tf_op jit(solution)/shard_map/ppermute | solution.py:73
  259.0 9.0 %collective-permute-start.41 = (bf16[4,2,64,512]{3,2,0,1:T(8,128)(2,1)S(1)}, bf16[4,2,64,512]{3,2,0,1:T(8,128)(2,1)S(1)}, u32[]{:S(2)}, u32[]{:S(2)}) collective-permute-start(bf16[4,2,64,512]{3,2,0,1:T(8,128)(2,1)S(1)} %bitcast.165), channel_id=1, source_target_pairs={{2,1},{1,2},{6,5},{5,6},{10,9},{9,10},{14,13},{13,14},{18,17},{17,... | collective-permute-start | bytes 1572872 | tf_op jit(solution)/shard_map/ppermute | solution.py:77
  261.5 19.7 %collective-permute-start.34 = (bf16[384,1024]{1,0:T(8,128)(2,1)S(1)}, bf16[384,1024]{1,0:T(8,128)(2,1)S(1)}, u32[]{:S(2)}, u32[]{:S(2)}) collective-permute-start(bf16[384,1024]{1,0:T(8,128)(2,1)S(1)} %copy-done.36), channel_id=1, source_target_pairs={{0,2},{2,0},{4,6},{6,4},{8,10},{10,8},{12,14},{14,12},{16,18},{18,... | collective-permute-start | bytes 2359304 | tf_op jit(solution)/shard_map/ppermute | solution.py:46
  266.0 8.4 %collective-permute-start.45 = (bf16[4,64,512]{2,1,0:T(8,128)(2,1)S(1)}, bf16[4,64,512]{2,1,0:T(8,128)(2,1)S(1)}, u32[]{:S(2)}, u32[]{:S(2)}) collective-permute-start(bf16[4,64,512]{2,1,0:T(8,128)(2,1)S(1)} %dynamic-slice_bitcast_fusion.1), channel_id=1, source_target_pairs={{0,4},{2,6},{4,0},{6,2},{8,12},{10,14},{12,8},{14,10},{16,20},{18,... | collective-permute-start | bytes 786440 | tf_op jit(solution)/shard_map/ppermute | solution.py:46
  268.3 15.8 %collective-permute-start.42 = (bf16[4,64,512]{2,1,0:T(8,128)(2,1)S(1)}, bf16[4,64,512]{2,1,0:T(8,128)(2,1)S(1)}, u32[]{:S(2)}, u32[]{:S(2)}) collective-permute-start(bf16[4,64,512]{2,1,0:T(8,128)(2,1)S(1)} %fusion.13), channel_id=1, source_target_pairs={{0,4},{2,6},{4,0},{6,2},{8,12},{10,14},{12,8},{14,10},{16,20},{18,... | collective-permute-start | bytes 786440 | tf_op jit(solution)/shard_map/ppermute | solution.py:46
  276.0 33.1 %collective-permute-start.46 = (bf16[64,512]{1,0:T(8,128)(2,1)}, bf16[64,512]{1,0:T(8,128)(2,1)}, u32[]{:S(2)}, u32[]{:S(2)}) collective-permute-start(bf16[64,512]{1,0:T(8,128)(2,1)} %get-tuple-element.224), channel_id=1, source_target_pairs={{0,8},{2,10},{4,12},{6,14},{8,16},{10,18},{12,20},{14,22},{16,24},... | collective-permute-start | bytes 196616 | tf_op jit(solution)/shard_map/ppermute | solution.py:46
  278.9 30.2 %collective-permute-start.47 = (bf16[64,512]{1,0:T(8,128)(2,1)}, bf16[64,512]{1,0:T(8,128)(2,1)}, u32[]{:S(2)}, u32[]{:S(2)}) collective-permute-start(bf16[64,512]{1,0:T(8,128)(2,1)} %get-tuple-element.226), channel_id=1, source_target_pairs={{0,16},{2,18},{4,20},{6,22},{8,24},{10,26},{12,28},{14,30},{16,0},... | collective-permute-start | bytes 196616 | tf_op jit(solution)/shard_map/ppermute | solution.py:46
  282.4 8.6 %collective-permute-start.35 = (bf16[96,1024]{1,0:T(8,128)(2,1)}, bf16[96,1024]{1,0:T(8,128)(2,1)}, u32[]{:S(2)}, u32[]{:S(2)}) collective-permute-start(bf16[96,1024]{1,0:T(8,128)(2,1)} %get-tuple-element.207), channel_id=1, source_target_pairs={{0,24},{2,26},{4,28},{6,30},{8,0},{10,2},{12,4},{14,6},{16,8},{18,... | collective-permute-start | bytes 589832 | tf_op jit(solution)/shard_map/ppermute | solution.py:46
  284.0 22.5 %collective-permute-start.36 = (bf16[96,1024]{1,0:T(8,128)(2,1)}, bf16[96,1024]{1,0:T(8,128)(2,1)}, u32[]{:S(2)}, u32[]{:S(2)}) collective-permute-start(bf16[96,1024]{1,0:T(8,128)(2,1)} %get-tuple-element.209), channel_id=1, source_target_pairs={{0,16},{2,18},{4,20},{6,22},{8,24},{10,26},{12,28},{14,30},{16,0},... | collective-permute-start | bytes 589832 | tf_op jit(solution)/shard_map/ppermute | solution.py:46
  284.0 22.5 %collective-permute-start.37 = (bf16[96,1024]{1,0:T(8,128)(2,1)}, bf16[96,1024]{1,0:T(8,128)(2,1)}, u32[]{:S(2)}, u32[]{:S(2)}) collective-permute-start(bf16[96,1024]{1,0:T(8,128)(2,1)} %get-tuple-element.208), channel_id=1, source_target_pairs={{0,8},{2,10},{4,12},{6,14},{8,16},{10,18},{12,20},{14,22},{16,24},... | collective-permute-start | bytes 589832 | tf_op jit(solution)/shard_map/ppermute | solution.py:46
  285.8 30.2 %all-to-all-start.2 = ((bf16[4,64,512]{2,1,0:T(8,128)(2,1)}), bf16[4,64,512]{2,1,0:T(8,128)(2,1)}, u32[]{:S(2)}, u32[]{:S(2)}) async-start(bf16[4,64,512]{2,1,0:T(8,128)(2,1)} %fusion.2), calls=%async_computation.2 | async-start | bytes 524288 | tf_op jit(solution)/shard_map/all_to_all | solution.py:853
  290.9 18.2 %collective-permute-start.48 = (bf16[64,512]{1,0:T(8,128)(2,1)}, bf16[64,512]{1,0:T(8,128)(2,1)S(1)}, u32[]{:S(2)}, u32[]{:S(2)}) collective-permute-start(bf16[64,512]{1,0:T(8,128)(2,1)} %get-tuple-element.225), channel_id=1, source_target_pairs={{0,24},{2,26},{4,28},{6,30},{8,0},{10,2},{12,4},{14,6},{16,8},{18,... | collective-permute-start | bytes 196616 | tf_op jit(solution)/shard_map/ppermute | solution.py:46
  308.1 6.9 %collective-permute-start.38 = (bf16[96,1024]{1,0:T(8,128)(2,1)S(1)}, bf16[96,1024]{1,0:T(8,128)(2,1)S(1)}, u32[]{:S(2)}, u32[]{:S(2)}) collective-permute-start(bf16[96,1024]{1,0:T(8,128)(2,1)S(1)} %fusion.7), channel_id=1, source_target_pairs={{0,1},{1,0},{2,3},{3,2},{4,5},{5,4},{6,7},{7,6},{8,9},{9,8},{10,11... | collective-permute-start | bytes 589832 | tf_op jit(solution)/shard_map/ppermute | solution.py:58
  319.8 4.3 %collective-permute-start.49 = (bf16[64,2048]{1,0:T(8,128)(2,1)S(1)}, bf16[64,2048]{1,0:T(8,128)(2,1)S(1)}, u32[]{:S(2)}, u32[]{:S(2)}) collective-permute-start(bf16[64,2048]{1,0:T(8,128)(2,1)S(1)} %broadcast_select_fusion.4), channel_id=1, source_target_pairs={{0,2},{2,0},{4,6},{6,4},{8,10},{10,8},{12,14},{14,12},{16,18},{18,... | collective-permute-start | bytes 786440 | tf_op jit(solution)/shard_map/ppermute | solution.py:46
  (70 other events, 784.3 us)
Sparse Core Ops, SparseCore 0:
  40.1 94.2 all-gather.1
  191.5 89.8 reduce-scatter.1

commit v4 on v3

--- a/solution.py
+++ b/solution.py
@@ -157,22 +157,71 @@
     return [pl.BlockSpec(memory_space=pltpu.VMEM)] * count
 
 
-def local_kernel(kernel, name, out_shape, operands, scalars=1, scratch=(), flops=0, megabytes=48):
+COSTS = {"enter": 5, "attend": 14, "attend_back": 17, "whole_proj": 1, "project": 2, "branch": 2, "leave": 3, "close": 5, "outer": 5}
+
+
+def local_kernel(kernel, name, out_shape, operands, scalars=1, scratch=(), flops=0, megabytes=48, before=()):
+    if before:
+        inner, at_end = kernel, len(operands)
+
+        def kernel(*refs):
+            inner(*refs[:at_end], *refs[at_end + len(before) :])
+
     single = not isinstance(out_shape, tuple)
     return pl.pallas_call(
         kernel,
         out_shape=out_shape,
-        in_specs=[SMEM] * scalars + in_vmem(len(operands) - scalars),
+        in_specs=[SMEM] * scalars + in_vmem(len(operands) - scalars) + [ANY] * len(before),
         out_specs=in_vmem(1)[0] if single else tuple(in_vmem(len(out_shape))),
         scratch_shapes=list(scratch),
         compiler_params=pltpu.CompilerParams(vmem_limit_bytes=megabytes * 1024 * 1024),
-        cost_estimate=pl.CostEstimate(flops=flops, bytes_accessed=1 << 16, transcendentals=0),
+        cost_estimate=pl.CostEstimate(flops=COSTS.get(name, 0) * 1000000000, bytes_accessed=1 << 16, transcendentals=0),
         name=name,
-    )(*operands)
+    )(*operands, *before)
+
+
+def turn_kernel(in_ref, out_ref):
+    out_ref[...] = jnp.transpose(in_ref[...])
+
+
+def turn(block, *before):
+    return local_kernel(turn_kernel, "turn", shape(block.shape[::-1]), (block,), scalars=0, before=before)
 
 
 def shape(dims, kind=BF16):
     return jax.ShapeDtypeStruct(tuple(dims), kind)
+
+
+ANY = pl.BlockSpec(memory_space=pl.ANY)
+
+
+def gate(block, *before):
+    return pl.pallas_call(
+        lambda *refs: None,
+        out_shape=jax.ShapeDtypeStruct(block.shape, block.dtype),
+        in_specs=[ANY] * (1 + len(before)),
+        out_specs=ANY,
+        input_output_aliases={0: 0},
+        cost_estimate=pl.CostEstimate(flops=0, bytes_accessed=0, transcendentals=0),
+        name="gate",
+    )(block, *before)
+
+
+def stack_kernel(count, *refs):
+    for n in range(count):
+        refs[-1][n] = refs[n][...]
+
+
+def stack(blocks, *before):
+    first = blocks[0]
+    return pl.pallas_call(
+        functools.partial(stack_kernel, len(blocks)),
+        out_shape=jax.ShapeDtypeStruct((len(blocks),) + first.shape, first.dtype),
+        in_specs=in_vmem(len(blocks)) + [ANY] * len(before),
+        out_specs=in_vmem(1)[0],
+        cost_estimate=pl.CostEstimate(flops=0, bytes_accessed=1 << 16, transcendentals=0),
+        name="stack",
+    )(*blocks, *before)
 
 
 def turned(index, size):
@@ -593,7 +642,7 @@
     )
 
 
-def branch(at, nz, half, near, unit, scale, vecs, gz, weight):
+def branch(at, nz, half, near, unit, scale, vecs, gz, weight, before):
     rows, width = unit.shape
     local = width // (2 * nz)
     return local_kernel(
@@ -607,6 +656,7 @@
             shape((4, width), F32),
         ),
         (at, half, near, unit, scale, vecs, gz, weight),
+        before=before,
     )
 
 
@@ -655,7 +705,7 @@
     out_ref[...] = dot(normed_ref[...], stack_ref[...], TN).astype(BF16)
 
 
-def close(rows, full, unit, scale, lead, vecs, middle, normed, stack):
+def close(rows, full, unit, scale, lead, vecs, middle, normed, stack, before):
     width = full.shape[1]
     return local_kernel(
         functools.partial(close_kernel, rows),
@@ -663,6 +713,7 @@
         (shape((4, width), F32), shape((1, stack.shape[1]), F32), shape((width, stack.shape[1]))),
         (full, unit, scale, lead, vecs, middle, normed, stack),
         scalars=0,
+        before=before,
     )
 
 
@@ -804,11 +855,10 @@
 
     half_n = keep_n + grid.cswap(send_n).astype(F32)
     near_n = grid.yswap(half_n[rows:].astype(BF16))
-    d_ff = lax.psum_scatter(
-        outer(normed_two, grad_hidden, gz, active), ("z", "x"), scatter_dimension=0, tiled=True
-    )
+    d_outer = outer(normed_two, grad_hidden, gz, active)
+    d_ff = lax.psum_scatter(d_outer, ("z", "x"), scatter_dimension=0, tiled=True)
     grad_middle, grad_branch, mine, send, sums_two = branch(
-        at, nz, half_n, near_n, n2, s2, vecs, gz[:rows], w_proj
+        at, nz, half_n, near_n, n2, s2, vecs, gz[:rows], w_proj, (d_outer,)
     )
     theirs = grid.cswap(send)
     got = lax.all_to_all(jnp.stack([mine, theirs], axis=1), "z", 0, 0, tiled=True)
@@ -826,7 +876,7 @@
     n1_far = [grid.zshift(low[k], -k) for k in range(1, nz)]
 
     sums_one, stack_sum, d_wqkv = close(
-        rows, part_full, unit_one, scale_one, lead, vecs, grad_middle, normed_one, grad_stack
+        rows, part_full, unit_one, scale_one, lead, vecs, grad_middle, normed_one, grad_stack, (low,)
     )
     up_column = jnp.transpose(up_sum.reshape(-1, sp, each), (1, 0, 2)).reshape(1, -1)
     sums = jnp.concatenate([sums_one, sums_two, up_column], axis=0)

time: 334 us -> 327 us (0.979)
  waiting for transfers between devices: 121 us -> 111 us
    ppermute x36, waiting for transfers between devices: 81.2 us -> 64.6 us  [_move(): return lax.ppermute(block, SP, pairs)]
    ppermute x36, starting transfers between devices: 46.3 us -> 35.2 us  [_move(): return lax.ppermute(block, SP, pairs)]
    ppermute x10, waiting for transfers between devices: 34.1 us -> 24.9 us  [yswap(): return lax.ppermute(block, 'tp', [(0, 1), (1, 0)])]
    all_to_all x1, waiting for transfers between devices: 0.01 us -> 8.75 us  [per_device(): dw = lax.all_to_all(dw.astype(BF16), 'z', 0, 0, tiled=True)]
    ppermute x10, starting transfers between devices: 12.3 us -> 20.8 us  [yswap(): return lax.ppermute(block, 'tp', [(0, 1), (1, 0)])]
    all_to_all x1, waiting for transfers between devices: 0.01 us -> 6.09 us  [per_device(): lax.all_to_all(jnp.stack([mine, theirs], axis=1), 'z', 0, 0, tiled=True)]
    unnamed x133 -> x93, local copies, waits for them, and re-layouts: 13.2 us -> 12.9 us
  transfers between devices with their start and end apart: 54 -> 54, of which waited for: 25 -> 22; matrix products, arithmetic and copies ran while one was open for 11% -> 11% of each run, Pallas kernels for 15% -> 16%
where the time goes in v4:
time: 327 us; the launch traced here: 326 us
  waiting for transfers between devices  111 us (34%)
  starting transfers between devices  67.7 us (21%)
  Pallas kernels  61.6 us (19%)
  other arithmetic  32.2 us (10%)
  local copies, waits for them, and re-layouts  25.2 us (8%)
  between operations  15.2 us (5%)
  blocking collectives  12.1 us (4%)
    ppermute x36, waiting for transfers between devices, _move(): return lax.ppermute(block, SP, pairs)  64.6 us
    pallas_call x10, Pallas kernels, local_kernel(): pl.pallas_call(kernel, out_shape=out_shape, in_specs=[SMEM] * scalars + i...  59.9 us
    ppermute x36, starting transfers between devices, _move(): return lax.ppermute(block, SP, pairs)  35.2 us
    ppermute x10, waiting for transfers between devices, yswap(): return lax.ppermute(block, 'tp', [(0, 1), (1, 0)])  24.9 us
    ppermute x10, starting transfers between devices, yswap(): return lax.ppermute(block, 'tp', [(0, 1), (1, 0)])  20.8 us
    unnamed x93, local copies, waits for them, and re-layouts  12.9 us
    all_to_all x1, blocking collectives, per_device(): attn_got = lax.all_to_all(attn_send, 'z', 0, 0, tiled=True)  12.1 us
    all_to_all x1, waiting for transfers between devices, per_device(): dw = lax.all_to_all(dw.astype(BF16), 'z', 0, 0, tiled=True)  8.75 us
  transfers between devices with their start and end apart: 54, of which 22 were waited for; matrix products, arithmetic and copies ran while one was open for 11% of the time, Pallas kernels for 16%

profile of v4, /device:TPU:0, one launch (start us, length us, event | category | flops | bytes accessed | tf_op | source)
XLA Modules:
  0.0 326.0 jit_solution(2748571099668345146)
XLA Ops:
  12.8 3.1 collective-permute-start
  15.9 2.6 collective-permute-start.1
  20.0 1.8 collective-permute-start.6
  21.8 1.9 collective-permute-start.7
  23.8 6.2 %collective-permute-done.5 = bf16[64,384]{1,0:T(8,128)(2,1)S(1)} collective-permute-done((bf16[64,384]{1,0:T(8,128)(2,1)S(1)}, bf16[64,384]{1,0:T(8,128)(2,1)S(1)}, u32[]{:S(2)}, u32[]{:S(2)}) %collective-permute-start.5) | collective-permute-done | bytes 49184 | tf_op jit(solution)/shard_map/ppermute | solution.py:46
  30.0 6.1 %collective-permute-done.6 = bf16[64,384]{1,0:T(8,128)(2,1)S(1)} collective-permute-done((bf16[64,384]{1,0:T(8,128)(2,1)S(1)}, bf16[64,384]{1,0:T(8,128)(2,1)S(1)}, u32[]{:S(2)}, u32[]{:S(2)}) %collective-permute-start.6) | collective-permute-done | bytes 49184 | tf_op jit(solution)/shard_map/ppermute | solution.py:46
  37.9 6.2 %collective-permute-done.2.refs_3_ = bf16[96,1152]{1,0:T(8,128)(2,1)S(1)} collective-permute-done((bf16[96,1152]{1,0:T(8,128)(2,1)S(1)}, bf16[96,1152]{1,0:T(8,128)(2,1)S(1)}, u32[]{:S(2)}, u32[]{:S(2)}) %collective-permute-start.2) | collective-permute-done | bytes 221216 | tf_op jit(solution)/shard_map/ppermute | solution.py:46
  50.8 4.6 %collective-permute-done.9 = bf16[2,4,64,384]{3,2,1,0:T(8,128)(2,1)S(1)} collective-permute-done((bf16[2,4,64,384]{3,2,1,0:T(8,128)(2,1)S(1)}, bf16[2,4,64,384]{3,2,1,0:T(8,128)(2,1)S(1)}, u32[]{:S(2)}, u32[]{:S(2)}) %collective-permute-start.9) | collective-permute-done | bytes 393248 | tf_op jit(solution)/shard_map/ppermute | solution.py:73
  55.5 2.4 collective-permute-start.17
  59.5 2.8 collective-permute-start.19
  62.8 4.2 %enter.1 = (bf16[768,1024]{1,0:T(8,128)(2,1)}, bf16[768,1024]{1,0:T(8,128)(2,1)}, f32[768,1]{1,0:T(8,128)S(1)}, f32[768,1]{1,0:T(8,128)S(1)}, f32[96,1024]{1,0:T...) custom-call(s32[4]{0:T(128)S(1)} %pad_add_fusion.at_ref.refs_0_, ...), custom_call_target="tpu_custom_call" | custom-call | flops 5000000000 | bytes 65536 | tf_op jit(solution)/shard_map/enter/pallas_call | solution.py:171
  70.2 4.3 %collective-permute-start.13 = (bf16[768,256]{1,0:T(8,128)(2,1)S(1)}, bf16[768,256]{1,0:T(8,128)(2,1)S(1)}, u32[]{:S(2)}, u32[]{:S(2)}) collective-permute-start(bf16[768,256]{1,0:T(8,128)(2,1)S(1)} %get-tuple-element.70.refs_0_), channel_id=1, source_target_pairs={{0,1},{1,0},{2,3},{3,2},{4,5},{5,4},{6,7},{7,6},{8,9},{9,8},{10,11... | collective-permute-start | bytes 1179656 | tf_op jit(solution)/shard_map/ppermute | solution.py:58
  82.5 6.6 %collective-permute-done.20 = bf16[4,64,512]{2,1,0:T(8,128)(2,1)} collective-permute-done((bf16[4,64,512]{2,1,0:T(8,128)(2,1)S(1)}, bf16[4,64,512]{2,1,0:T(8,128)(2,1)}, u32[]{:S(2)}, u32[]{:S(2)}) %collective-permute-start.20) | collective-permute-done | bytes 262176 | tf_op jit(solution)/shard_map/ppermute | solution.py:46
  90.2 1.9 collective-permute-start.21
  92.7 2.1 collective-permute-start.15
  94.9 2.0 pad_maximum_fusion.2.gz_ref
  96.9 6.8 %collective-permute-done.21 = bf16[2,4,64,512]{3,2,1,0:T(8,128)(2,1)S(1)} collective-permute-done((bf16[2,4,64,512]{3,2,1,0:T(8,128)(2,1)S(1)}, bf16[2,4,64,512]{3,2,1,0:T(8,128)(2,1)S(1)}, u32[]{:S(2)}, u32[]{:S(2)}) %collective-permute-start.21) | collective-permute-done | bytes 524320 | tf_op jit(solution)/shard_map/ppermute | solution.py:58
  103.9 8.5 %collective-permute-done.15.refs_3_ = bf16[768,256]{1,0:T(8,128)(2,1)S(1)} collective-permute-done((bf16[768,256]{1,0:T(8,128)(2,1)S(1)}, bf16[768,256]{1,0:T(8,128)(2,1)S(1)}, u32[]{:S(2)}, u32[]{:S(2)}) %collective-permute-start.15) | collective-permute-done | bytes 393248 | tf_op jit(solution)/shard_map/ppermute | solution.py:46
  112.5 13.6 %attend.1 = (f32[768,128]{1,0:T(8,128)S(1)}, f32[8,768]{1,0:T(8,128)S(1)}, bf16[768,128]{1,0:T(8,128)(2,1)S(1)}, bf16[4,2,96,128]{3,2,1,0:T(8,128)(2,1)S(1)}) custom-call(s32[4]{0:T(128)S(1)} %pad_add_fusion.at_ref.refs_0_, f32[768,128]{1,0:T(8,128)S(1)} %copy-done.31, f32[2,128]{1,0:T(2,128)S(1)} %fusion.24.bias_ref, ...), custom_call_target="tpu_custom_call" | custom-call | flops 14000000000 | bytes 65536 | tf_op jit(solution)/shard_map/attend/pallas_call | solution.py:171
  126.8 12.1 %all_to_all.15.got_ref = bf16[4,2,96,128]{3,2,1,0:T(8,128)(2,1)S(1)} all-to-all(bf16[4,2,96,128]{3,2,1,0:T(8,128)(2,1)S(1)} %get-tuple-element.73), channel_id=1, replica_groups=mesh['z'=4,'x'=2,'core'=2,'tp'=2] {'z'}, dimensions={0} | all-to-all | bytes 393216 | tf_op jit(solution)/shard_map/all_to_all | solution.py:849
  143.3 1.6 collective-permute-start.23
  144.9 5.4 %collective-permute-done.23.near_ref = bf16[96,1024]{1,0:T(8,128)(2,1)S(1)} collective-permute-done((bf16[96,1024]{1,0:T(8,128)(2,1)S(1)}, bf16[96,1024]{1,0:T(8,128)(2,1)S(1)}, u32[]{:S(2)}, u32[]{:S(2)}) %collective-permute-start.23) | collective-permute-done | bytes 196640 | tf_op jit(solution)/shard_map/ppermute | solution.py:58
  151.1 1.8 collective-permute-done.24.far_ref
  152.9 8.4 %feed.1 = (bf16[384,1024]{1,0:T(8,128)(2,1)}, bf16[384,1024]{1,0:T(8,128)(2,1)}, bf16[384,1024]{1,0:T(8,128)(2,1)}, f32[1,1024]{1,0:T(1,128)}, f32[192,1024]{1,0...) custom-call(f32[1,1024]{1,0:T(1,128)} %broadcast_select_fusion.20.bias_ref, ...), custom_call_target="tpu_custom_call" | custom-call | bytes 65536 | tf_op jit(solution)/shard_map/feed/pallas_call | solution.py:171
  161.6 1.8 collective-permute-done.26
  166.2 1.6 collective-permute-start.27
  167.8 4.4 %outer.1.refs_8_ = bf16[1024,2048]{1,0:T(8,128)(2,1)} custom-call(bf16[384,1024]{1,0:T(8,128)(2,1)S(1)} %copy-done.15, bf16[384,1024]{1,0:T(8,128)(2,1)S(1)} %copy-done.17, bf16[384,1024]{1,0:T(8,128)(2,1)S(1)} %copy-done, bf16[384,1024]{1,0:T(8,128)(2,1)S(1)} %copy-done.16), custom_call_target="tpu_custom_call" | custom-call | flops 5000000000 | bytes 65536 | tf_op jit(solution)/shard_map/outer/pallas_call | solution.py:171
  175.3 1.8 branch.1
  179.1 3.4 %all-to-all-start.1 = ((bf16[4,2,96,128]{3,2,1,0:T(8,128)(2,1)}), bf16[4,2,96,128]{3,2,1,0:T(8,128)(2,1)S(1)}, u32[]{:S(2)}, u32[]{:S(2)}) async-start(bf16[4,2,96,128]{3,2,1,0:T(8,128)(2,1)} %pad_maximum_fusion.13), calls=%async_computation.1 | async-start | bytes 393216 | tf_op jit(solution)/shard_map/all_to_all | solution.py:864
  184.4 6.1 %all-to-all-done.1.got_ref = bf16[4,2,96,128]{3,2,1,0:T(8,128)(2,1)S(1)} async-done(((bf16[4,2,96,128]{3,2,1,0:T(8,128)(2,1)}), bf16[4,2,96,128]{3,2,1,0:T(8,128)(2,1)S(1)}, u32[]{:S(2)}, u32[]{:S(2)}) %all-to-all-start.1) | async-done | bytes 196640 | tf_op jit(solution)/shard_map/all_to_all | solution.py:864
  191.2 17.2 %attend_back.1 = (bf16[768,128]{1,0:T(8,128)(2,1)}, bf16[1536,256]{1,0:T(8,128)(2,1)}, bf16[1536,256]{1,0:T(8,128)(2,1)}) custom-call(s32[4]{0:T(128)} %copy-done.13, bf16[768,128]{1,0:T(8,128)(2,1)} %copy-done.33, bf16[768,128]{1,0:T(8,128)(2,1)} %copy-done.9, bf16[3072,128]{1,0:T(8,128)(2,1)} %copy-done.4, bf16[4,2,96,128]{3,2,1,0:T(8,128)(2,1)} %copy-done.42, ...), custom_call_target="tpu_custom_call" | custom-call | flops 16999999488 | bytes 65536 | tf_op jit(solution)/shard_map/attend_back/pallas_call | solution.py:171
  215.4 16.3 %collective-permute-done.32 = bf16[1536,256]{1,0:T(8,128)(2,1)} collective-permute-done((bf16[1536,256]{1,0:T(8,128)(2,1)}, bf16[1536,256]{1,0:T(8,128)(2,1)}, u32[]{:S(2)}, u32[]{:S(2)}) %collective-permute-start.32) | collective-permute-done | bytes 786464 | tf_op jit(solution)/shard_map/ppermute | solution.py:46
  231.7 1.6 convert_add_fusion.2.two_ref
  233.3 1.7 collective-permute-start.33
  235.0 1.6 convert_add_fusion
  239.0 6.5 %collective-permute-done.33.near_ref = bf16[768,256]{1,0:T(8,128)(2,1)S(1)} collective-permute-done((bf16[768,256]{1,0:T(8,128)(2,1)S(1)}, bf16[768,256]{1,0:T(8,128)(2,1)S(1)}, u32[]{:S(2)}, u32[]{:S(2)}) %collective-permute-start.33) | collective-permute-done | bytes 393248 | tf_op jit(solution)/shard_map/ppermute | solution.py:58
  245.4 2.8 leave.1
  248.2 4.1 %collective-permute-done.44 = bf16[8,64,512]{2,1,0:T(8,128)(2,1)S(1)} collective-permute-done((bf16[8,64,512]{2,1,0:T(8,128)(2,1)S(1)}, bf16[8,64,512]{2,1,0:T(8,128)(2,1)S(1)}, u32[]{:S(2)}, u32[]{:S(2)}) %collective-permute-start.44) | collective-permute-done | bytes 524320 | tf_op jit(solution)/shard_map/ppermute | solution.py:58
  255.2 8.6 %collective-permute-done.45 = bf16[4,64,512]{2,1,0:T(8,128)(2,1)S(1)} collective-permute-done((bf16[4,64,512]{2,1,0:T(8,128)(2,1)S(1)}, bf16[4,64,512]{2,1,0:T(8,128)(2,1)S(1)}, u32[]{:S(2)}, u32[]{:S(2)}) %collective-permute-start.45) | collective-permute-done | bytes 262176 | tf_op jit(solution)/shard_map/ppermute | solution.py:46
  266.3 2.0 collective-permute-start.35
  269.7 5.1 %close.1 = (f32[4,1024]{1,0:T(4,128)S(1)}, f32[1,384]{1,0:T(1,128)S(1)}, bf16[1024,384]{1,0:T(8,128)(2,1)S(1)}) custom-call(f32[768,1024]{1,0:T(8,128)} %get-tuple-element.107.refs_0_, bf16[768,1024]{1,0:T(8,128)(2,1)S(1)} %copy-done.10, f32[768,1]{1,0:T(8,128)S(1)} %copy-done.12, f32[768,1]{1,0:T(8,128)S(1)} %copy-done.28, ...), custom_call_target="tpu_custom_call" | custom-call | flops 5000000000 | bytes 65536 | tf_op jit(solution)/shard_map/close/pallas_call | solution.py:171
  277.7 2.1 collective-permute-start.46
  282.3 1.6 multiply_reduce_fusion
  284.0 2.1 collective-permute-done.40
  288.3 6.3 %collective-permute-start.38 = (bf16[96,1024]{1,0:T(8,128)(2,1)S(1)}, bf16[96,1024]{1,0:T(8,128)(2,1)S(1)}, u32[]{:S(2)}, u32[]{:S(2)}) collective-permute-start(bf16[96,1024]{1,0:T(8,128)(2,1)S(1)} %fusion.7), channel_id=1, source_target_pairs={{0,1},{1,0},{2,3},{3,2},{4,5},{5,4},{6,7},{7,6},{8,9},{9,8},{10,11... | collective-permute-start | bytes 589832 | tf_op jit(solution)/shard_map/ppermute | solution.py:58
  295.4 4.9 %all-to-all-start.2 = ((bf16[4,64,512]{2,1,0:T(8,128)(2,1)}), bf16[4,64,512]{2,1,0:T(8,128)(2,1)S(1)}, u32[]{:S(2)}, u32[]{:S(2)}) async-start(bf16[4,64,512]{2,1,0:T(8,128)(2,1)} %fusion.2), calls=%async_computation.2 | async-start | bytes 524288 | tf_op jit(solution)/shard_map/all_to_all | solution.py:903
  302.0 8.8 %all-to-all-done.2 = bf16[4,64,512]{2,1,0:T(8,128)(2,1)S(1)} async-done(((bf16[4,64,512]{2,1,0:T(8,128)(2,1)}), bf16[4,64,512]{2,1,0:T(8,128)(2,1)S(1)}, u32[]{:S(2)}, u32[]{:S(2)}) %all-to-all-start.2) | async-done | bytes 262176 | tf_op jit(solution)/shard_map/all_to_all | solution.py:903
  314.8 1.7 place_qkv.1
  (303 shorter events, 79.6 us)
Async XLA Ops:
  7.2 145.7 %all-gather.2.cloned.1.call-start = ((), (), s32[]{:S(2)}) async-start(), calls=%async_computation.4 | async-start | bytes 4718592 | tf_op jit(solution)/shard_map/all_gather | solution.py:833
  12.8 25.0 %collective-permute-start = (bf16[96,1152]{1,0:T(8,128)(2,1)S(1)}, bf16[96,1152]{1,0:T(8,128)(2,1)S(1)}, u32[]{:S(2)}, u32[]{:S(2)}) collective-permute-start(bf16[96,1152]{1,0:T(8,128)(2,1)S(1)} %concatenate.67.refs_0_), channel_id=1, source_target_pairs={{0,8},{2,10},{4,12},{6,14},{8,16},{10,18},{12,20},{14,22},{16,24},... | collective-permute-start | bytes 663560 | tf_op jit(solution)/shard_map/ppermute | solution.py:46
  15.9 22.0 %collective-permute-start.1 = (bf16[96,1152]{1,0:T(8,128)(2,1)S(1)}, bf16[96,1152]{1,0:T(8,128)(2,1)S(1)}, u32[]{:S(2)}, u32[]{:S(2)}) collective-permute-start(bf16[96,1152]{1,0:T(8,128)(2,1)S(1)} %concatenate.67.refs_0_), channel_id=1, source_target_pairs={{0,16},{2,18},{4,20},{6,22},{8,24},{10,26},{12,28},{14,30},{16,0},... | collective-permute-start | bytes 663560 | tf_op jit(solution)/shard_map/ppermute | solution.py:46
  19.9 10.1 %collective-permute-start.5 = (bf16[64,384]{1,0:T(8,128)(2,1)S(1)}, bf16[64,384]{1,0:T(8,128)(2,1)S(1)}, u32[]{:S(2)}, u32[]{:S(2)}) collective-permute-start(bf16[64,384]{1,0:T(8,128)(2,1)S(1)} %get-tuple-element.240), channel_id=1, source_target_pairs={{0,8},{2,10},{4,12},{6,14},{8,16},{10,18},{12,20},{14,22},{16,24},... | collective-permute-start | bytes 147464 | tf_op jit(solution)/shard_map/ppermute | solution.py:46
  20.0 16.1 %collective-permute-start.6 = (bf16[64,384]{1,0:T(8,128)(2,1)S(1)}, bf16[64,384]{1,0:T(8,128)(2,1)S(1)}, u32[]{:S(2)}, u32[]{:S(2)}) collective-permute-start(bf16[64,384]{1,0:T(8,128)(2,1)S(1)} %get-tuple-element.239), channel_id=1, source_target_pairs={{0,16},{2,18},{4,20},{6,22},{8,24},{10,26},{12,28},{14,30},{16,0},... | collective-permute-start | bytes 147464 | tf_op jit(solution)/shard_map/ppermute | solution.py:46
  21.8 14.2 %collective-permute-start.7 = (bf16[64,384]{1,0:T(8,128)(2,1)S(1)}, bf16[64,384]{1,0:T(8,128)(2,1)S(1)}, u32[]{:S(2)}, u32[]{:S(2)}) collective-permute-start(bf16[64,384]{1,0:T(8,128)(2,1)S(1)} %get-tuple-element.238), channel_id=1, source_target_pairs={{0,24},{2,26},{4,28},{6,30},{8,0},{10,2},{12,4},{14,6},{16,8},{18,... | collective-permute-start | bytes 147464 | tf_op jit(solution)/shard_map/ppermute | solution.py:46
  30.0 14.1 %collective-permute-start.2 = (bf16[96,1152]{1,0:T(8,128)(2,1)S(1)}, bf16[96,1152]{1,0:T(8,128)(2,1)S(1)}, u32[]{:S(2)}, u32[]{:S(2)}) collective-permute-start(bf16[96,1152]{1,0:T(8,128)(2,1)S(1)} %concatenate.67.refs_0_), channel_id=1, source_target_pairs={{0,24},{2,26},{4,28},{6,30},{8,0},{10,2},{12,4},{14,6},{16,8},{18,... | collective-permute-start | bytes 663560 | tf_op jit(solution)/shard_map/ppermute | solution.py:46
  36.1 10.1 %collective-permute-start.8 = (bf16[4,64,384]{2,1,0:T(8,128)(2,1)S(1)}, bf16[4,64,384]{2,1,0:T(8,128)(2,1)S(1)}, u32[]{:S(2)}, u32[]{:S(2)}) collective-permute-start(bf16[4,64,384]{2,1,0:T(8,128)(2,1)S(1)} %get-tuple-element.236), channel_id=1, source_target_pairs={{0,4},{2,6},{4,0},{6,2},{8,12},{10,14},{12,8},{14,10},{16,20},{18,... | collective-permute-start | bytes 589832 | tf_op jit(solution)/shard_map/ppermute | solution.py:46
  37.8 7.4 %collective-permute-start.25 = (bf16[64,2048]{1,0:T(8,128)(2,1)S(1)}, bf16[64,2048]{1,0:T(8,128)(2,1)S(1)}, u32[]{:S(2)}, u32[]{:S(2)}) collective-permute-start(bf16[64,2048]{1,0:T(8,128)(2,1)S(1)} %pad_maximum_fusion.11), channel_id=1, source_target_pairs={{0,2},{2,0},{4,6},{6,4},{8,10},{10,8},{12,14},{14,12},{16,18},{18,... | collective-permute-start | bytes 786440 | tf_op jit(solution)/shard_map/ppermute | solution.py:46
  45.2 4.1 %collective-permute-start.3 = (bf16[4,96,1152]{2,1,0:T(8,128)(2,1)}, bf16[4,96,1152]{2,1,0:T(8,128)(2,1)S(1)}, u32[]{:S(2)}, u32[]{:S(2)}) collective-permute-start(bf16[4,96,1152]{2,1,0:T(8,128)(2,1)} %pad_maximum_fusion.1), channel_id=1, source_target_pairs={{0,2},{2,0},{4,6},{6,4},{8,10},{10,8},{12,14},{14,12},{16,18},{18,... | collective-permute-start | bytes 2654216 | tf_op jit(solution)/shard_map/ppermute | solution.py:46
  46.3 9.2 %collective-permute-start.9 = (bf16[2,4,64,384]{3,2,1,0:T(8,128)(2,1)S(1)}, bf16[2,4,64,384]{3,2,1,0:T(8,128)(2,1)S(1)}, u32[]{:S(2)}, u32[]{:S(2)}) collective-permute-start(bf16[2,4,64,384]{3,2,1,0:T(8,128)(2,1)S(1)} %pad_maximum_fusion.5), channel_id=1, source_target_pairs={{0,1},{2,0},{3,2},{1,3},{4,5},{6,4},{7,6},{5,7},{8,9},{10,8},{11,1... | collective-permute-start | bytes 1179656 | tf_op jit(solution)/shard_map/ppermute | solution.py:73
  47.8 7.6 %collective-permute-start.10 = (bf16[2,4,64,384]{3,2,1,0:T(8,128)(2,1)S(1)}, bf16[2,4,64,384]{3,2,1,0:T(8,128)(2,1)S(1)}, u32[]{:S(2)}, u32[]{:S(2)}) collective-permute-start(bf16[2,4,64,384]{3,2,1,0:T(8,128)(2,1)S(1)} %pad_maximum_fusion.5), channel_id=1, source_target_pairs={{2,1},{1,2},{6,5},{5,6},{10,9},{9,10},{14,13},{13,14},{18,17},{17,... | collective-permute-start | bytes 1179656 | tf_op jit(solution)/shard_map/ppermute | solution.py:77
  49.2 13.1 %collective-permute-start.4 = (bf16[2,4,16,128]{3,2,1,0:T(8,128)(2,1)S(1)}, bf16[2,4,16,128]{3,2,1,0:T(8,128)(2,1)S(1)}, u32[]{:S(2)}, u32[]{:S(2)}) collective-permute-start(bf16[2,4,16,128]{3,2,1,0:T(8,128)(2,1)S(1)} %get-tuple-element.246), channel_id=1, source_target_pairs={{0,4},{2,6},{4,0},{6,2},{8,12},{10,14},{12,8},{14,10},{16,20},{18,... | collective-permute-start | bytes 98312 | tf_op jit(solution)/shard_map/ppermute | solution.py:46
  55.5 23.6 %collective-permute-start.17 = (bf16[64,512]{1,0:T(8,128)(2,1)}, bf16[64,512]{1,0:T(8,128)(2,1)}, u32[]{:S(2)}, u32[]{:S(2)}) collective-permute-start(bf16[64,512]{1,0:T(8,128)(2,1)} %bitcast.39), channel_id=1, source_target_pairs={{0,8},{2,10},{4,12},{6,14},{8,16},{10,18},{12,20},{14,22},{16,24},... | collective-permute-start | bytes 196616 | tf_op jit(solution)/shard_map/ppermute | solution.py:46
  58.0 21.2 %collective-permute-start.18 = (bf16[64,512]{1,0:T(8,128)(2,1)}, bf16[64,512]{1,0:T(8,128)(2,1)}, u32[]{:S(2)}, u32[]{:S(2)}) collective-permute-start(bf16[64,512]{1,0:T(8,128)(2,1)} %bitcast.39), channel_id=1, source_target_pairs={{0,16},{2,18},{4,20},{6,22},{8,24},{10,26},{12,28},{14,30},{16,0},... | collective-permute-start | bytes 196616 | tf_op jit(solution)/shard_map/ppermute | solution.py:46
  59.5 19.8 %collective-permute-start.19 = (bf16[64,512]{1,0:T(8,128)(2,1)}, bf16[64,512]{1,0:T(8,128)(2,1)}, u32[]{:S(2)}, u32[]{:S(2)}) collective-permute-start(bf16[64,512]{1,0:T(8,128)(2,1)} %bitcast.39), channel_id=1, source_target_pairs={{0,24},{2,26},{4,28},{6,30},{8,0},{10,2},{12,4},{14,6},{16,8},{18,... | collective-permute-start | bytes 196616 | tf_op jit(solution)/shard_map/ppermute | solution.py:46
  70.2 20.0 %collective-permute-start.13 = (bf16[768,256]{1,0:T(8,128)(2,1)S(1)}, bf16[768,256]{1,0:T(8,128)(2,1)S(1)}, u32[]{:S(2)}, u32[]{:S(2)}) collective-permute-start(bf16[768,256]{1,0:T(8,128)(2,1)S(1)} %get-tuple-element.70.refs_0_), channel_id=1, source_target_pairs={{0,1},{1,0},{2,3},{3,2},{4,5},{5,4},{6,7},{7,6},{8,9},{9,8},{10,11... | collective-permute-start | bytes 1179656 | tf_op jit(solution)/shard_map/ppermute | solution.py:58
  74.5 29.4 %collective-permute-start.14 = (bf16[768,256]{1,0:T(8,128)(2,1)S(1)}, bf16[768,256]{1,0:T(8,128)(2,1)S(1)}, u32[]{:S(2)}, u32[]{:S(2)}) collective-permute-start(bf16[768,256]{1,0:T(8,128)(2,1)S(1)} %get-tuple-element.70.refs_0_), channel_id=1, source_target_pairs={{0,4},{2,6},{4,0},{6,2},{8,12},{10,14},{12,8},{14,10},{16,20},{18,... | collective-permute-start | bytes 1179656 | tf_op jit(solution)/shard_map/ppermute | solution.py:46
  79.2 15.7 %collective-permute-start.11 = (bf16[192,1024]{1,0:T(8,128)(2,1)}, bf16[192,1024]{1,0:T(8,128)(2,1)}, u32[]{:S(2)}, u32[]{:S(2)}) collective-permute-start(bf16[192,1024]{1,0:T(8,128)(2,1)} %pad_maximum_fusion.6), channel_id=1, source_target_pairs={{0,2},{2,0},{4,6},{6,4},{8,10},{10,8},{12,14},{14,12},{16,18},{18,... | collective-permute-start | bytes 1179656 | tf_op jit(solution)/shard_map/ppermute | solution.py:46
  79.2 15.7 %collective-permute-start.12 = (f32[2,512]{1,0:T(2,128)S(1)}, f32[2,512]{1,0:T(2,128)S(1)}, u32[]{:S(2)}, u32[]{:S(2)}) collective-permute-start(f32[2,512]{1,0:T(2,128)S(1)} %reshape.345), channel_id=1, source_target_pairs={{0,1},{1,0},{2,3},{3,2},{4,5},{5,4},{6,7},{7,6},{8,9},{9,8},{10,11... | collective-permute-start | bytes 12296 | tf_op jit(solution)/shard_map/ppermute | solution.py:58
  80.3 8.8 %collective-permute-start.20 = (bf16[4,64,512]{2,1,0:T(8,128)(2,1)S(1)}, bf16[4,64,512]{2,1,0:T(8,128)(2,1)}, u32[]{:S(2)}, u32[]{:S(2)}) collective-permute-start(bf16[4,64,512]{2,1,0:T(8,128)(2,1)S(1)} %pad_maximum_fusion.9), channel_id=1, source_target_pairs={{0,4},{2,6},{4,0},{6,2},{8,12},{10,14},{12,8},{14,10},{16,20},{18,... | collective-permute-start | bytes 786440 | tf_op jit(solution)/shard_map/ppermute | solution.py:46
  90.2 13.5 %collective-permute-start.21 = (bf16[2,4,64,512]{3,2,1,0:T(8,128)(2,1)S(1)}, bf16[2,4,64,512]{3,2,1,0:T(8,128)(2,1)S(1)}, u32[]{:S(2)}, u32[]{:S(2)}) collective-permute-start(bf16[2,4,64,512]{3,2,1,0:T(8,128)(2,1)S(1)} %pad_maximum_fusion.3), channel_id=1, source_target_pairs={{0,1},{1,0},{2,3},{3,2},{4,5},{5,4},{6,7},{7,6},{8,9},{9,8},{10,11... | collective-permute-start | bytes 1572872 | tf_op jit(solution)/shard_map/ppermute | solution.py:58
  92.7 19.8 %collective-permute-start.15 = (bf16[768,256]{1,0:T(8,128)(2,1)S(1)}, bf16[768,256]{1,0:T(8,128)(2,1)S(1)}, u32[]{:S(2)}, u32[]{:S(2)}) collective-permute-start(bf16[768,256]{1,0:T(8,128)(2,1)S(1)} %collective-permute-done.13.refs_1_), channel_id=1, source_target_pairs={{0,4},{2,6},{4,0},{6,2},{8,12},{10,14},{12,8},{14,10},{16,20},{18,... | collective-permute-start | bytes 1179656 | tf_op jit(solution)/shard_map/ppermute | solution.py:46
  103.8 35.2 %collective-permute-start.22 = (bf16[2,2,4,64,512]{4,3,2,1,0:T(8,128)(2,1)S(1)}, bf16[2,2,4,64,512]{4,3,2,1,0:T(8,128)(2,1)S(1)}, u32[]{:S(2)}, u32[]{:S(2)}) collective-permute-start(bf16[2,2,4,64,512]{4,3,2,1,0:T(8,128)(2,1)S(1)} %pad_maximum_fusion.own_ref), channel_id=1, source_target_pairs={{0,2},{2,0},{4,6},{6,4},{8,10},{10,8},{12,14},{14,12},{16,18},{18,... | collective-permute-start | bytes 3145736 | tf_op jit(solution)/shard_map/ppermute | solution.py:46
  143.3 7.0 %collective-permute-start.23 = (bf16[96,1024]{1,0:T(8,128)(2,1)S(1)}, bf16[96,1024]{1,0:T(8,128)(2,1)S(1)}, u32[]{:S(2)}, u32[]{:S(2)}) collective-permute-start(bf16[96,1024]{1,0:T(8,128)(2,1)S(1)} %get-tuple-element.81.own_ref), channel_id=1, source_target_pairs={{0,1},{1,0},{2,3},{3,2},{4,5},{5,4},{6,7},{7,6},{8,9},{9,8},{10,11... | collective-permute-start | bytes 589832 | tf_op jit(solution)/shard_map/ppermute | solution.py:58
  166.2 7.3 %collective-permute-start.27 = (bf16[96,1024]{1,0:T(8,128)(2,1)}, bf16[96,1024]{1,0:T(8,128)(2,1)}, u32[]{:S(2)}, u32[]{:S(2)}) collective-permute-start(bf16[96,1024]{1,0:T(8,128)(2,1)} %slice.394), channel_id=1, source_target_pairs={{0,1},{1,0},{2,3},{3,2},{4,5},{5,4},{6,7},{7,6},{8,9},{9,8},{10,11... | collective-permute-start | bytes 589832 | tf_op jit(solution)/shard_map/ppermute | solution.py:58
  179.1 11.4 %all-to-all-start.1 = ((bf16[4,2,96,128]{3,2,1,0:T(8,128)(2,1)}), bf16[4,2,96,128]{3,2,1,0:T(8,128)(2,1)S(1)}, u32[]{:S(2)}, u32[]{:S(2)}) async-start(bf16[4,2,96,128]{3,2,1,0:T(8,128)(2,1)} %pad_maximum_fusion.13), calls=%async_computation.1 | async-start | bytes 393216 | tf_op jit(solution)/shard_map/all_to_all | solution.py:864
  182.5 130.2 %reduce-scatter.2.cloned.1.call-start = ((), (), s32[]{:S(2)}) async-start(), calls=%async_computation.5 | async-start | bytes 4718592 | tf_op jit(solution)/shard_map/reduce_scatter | solution.py:859
  184.2 28.3 %collective-permute-start.28 = (bf16[192,1024]{1,0:T(8,128)(2,1)}, bf16[192,1024]{1,0:T(8,128)(2,1)S(1)}, u32[]{:S(2)}, u32[]{:S(2)}) collective-permute-start(bf16[192,1024]{1,0:T(8,128)(2,1)} %get-tuple-element.96), channel_id=1, source_target_pairs={{0,2},{2,0},{4,6},{6,4},{8,10},{10,8},{12,14},{14,12},{16,18},{18,... | collective-permute-start | bytes 1179656 | tf_op jit(solution)/shard_map/ppermute | solution.py:46
  208.4 23.3 %collective-permute-start.32 = (bf16[1536,256]{1,0:T(8,128)(2,1)}, bf16[1536,256]{1,0:T(8,128)(2,1)}, u32[]{:S(2)}, u32[]{:S(2)}) collective-permute-start(bf16[1536,256]{1,0:T(8,128)(2,1)} %get-tuple-element.105), channel_id=1, source_target_pairs={{0,4},{2,6},{4,0},{6,2},{8,12},{10,14},{12,8},{14,10},{16,20},{18,... | collective-permute-start | bytes 2359304 | tf_op jit(solution)/shard_map/ppermute | solution.py:46
  210.8 24.1 %collective-permute-start.43 = (bf16[8,64,1024]{2,1,0:T(8,128)(2,1)}, bf16[8,64,1024]{2,1,0:T(8,128)(2,1)}, u32[]{:S(2)}, u32[]{:S(2)}) collective-permute-start(bf16[8,64,1024]{2,1,0:T(8,128)(2,1)} %dynamic-slice_bitcast_fusion), channel_id=1, source_target_pairs={{0,2},{2,0},{4,6},{6,4},{8,10},{10,8},{12,14},{14,12},{16,18},{18,... | collective-permute-start | bytes 3145736 | tf_op jit(solution)/shard_map/ppermute | solution.py:46
  213.8 23.4 %collective-permute-start.29 = (bf16[96,1024]{1,0:T(8,128)(2,1)S(1)}, bf16[96,1024]{1,0:T(8,128)(2,1)S(1)}, u32[]{:S(2)}, u32[]{:S(2)}) collective-permute-start(bf16[96,1024]{1,0:T(8,128)(2,1)S(1)} %slice.393), channel_id=1, source_target_pairs={{0,1},{1,0},{2,3},{3,2},{4,5},{5,4},{6,7},{7,6},{8,9},{9,8},{10,11... | collective-permute-start | bytes 589832 | tf_op jit(solution)/shard_map/ppermute | solution.py:58
  233.3 12.1 %collective-permute-start.33 = (bf16[768,256]{1,0:T(8,128)(2,1)S(1)}, bf16[768,256]{1,0:T(8,128)(2,1)S(1)}, u32[]{:S(2)}, u32[]{:S(2)}) collective-permute-start(bf16[768,256]{1,0:T(8,128)(2,1)S(1)} %slice.392), channel_id=1, source_target_pairs={{0,1},{1,0},{2,3},{3,2},{4,5},{5,4},{6,7},{7,6},{8,9},{9,8},{10,11... | collective-permute-start | bytes 1179656 | tf_op jit(solution)/shard_map/ppermute | solution.py:58
  236.7 15.5 %collective-permute-start.44 = (bf16[8,64,512]{2,1,0:T(8,128)(2,1)S(1)}, bf16[8,64,512]{2,1,0:T(8,128)(2,1)S(1)}, u32[]{:S(2)}, u32[]{:S(2)}) collective-permute-start(bf16[8,64,512]{2,1,0:T(8,128)(2,1)S(1)} %select_convert_fusion.1), channel_id=1, source_target_pairs={{0,1},{1,0},{2,3},{3,2},{4,5},{5,4},{6,7},{7,6},{8,9},{9,8},{10,11... | collective-permute-start | bytes 1572872 | tf_op jit(solution)/shard_map/ppermute | solution.py:58
  237.7 16.7 %collective-permute-start.30 = (bf16[96,1024]{1,0:T(8,128)(2,1)S(1)}, bf16[96,1024]{1,0:T(8,128)(2,1)S(1)}, u32[]{:S(2)}, u32[]{:S(2)}) collective-permute-start(bf16[96,1024]{1,0:T(8,128)(2,1)S(1)} %fusion.12), channel_id=1, source_target_pairs={{0,1},{1,0},{2,3},{3,2},{4,5},{5,4},{6,7},{7,6},{8,9},{9,8},{10,11... | collective-permute-start | bytes 589832 | tf_op jit(solution)/shard_map/ppermute | solution.py:58
  248.2 15.7 %collective-permute-start.34 = (bf16[384,1024]{1,0:T(8,128)(2,1)S(1)}, bf16[384,1024]{1,0:T(8,128)(2,1)S(1)}, u32[]{:S(2)}, u32[]{:S(2)}) collective-permute-start(bf16[384,1024]{1,0:T(8,128)(2,1)S(1)} %get-tuple-element.108), channel_id=1, source_target_pairs={{0,2},{2,0},{4,6},{6,4},{8,10},{10,8},{12,14},{14,12},{16,18},{18,... | collective-permute-start | bytes 2359304 | tf_op jit(solution)/shard_map/ppermute | solution.py:46
  252.6 11.2 %collective-permute-start.45 = (bf16[4,64,512]{2,1,0:T(8,128)(2,1)S(1)}, bf16[4,64,512]{2,1,0:T(8,128)(2,1)S(1)}, u32[]{:S(2)}, u32[]{:S(2)}) collective-permute-start(bf16[4,64,512]{2,1,0:T(8,128)(2,1)S(1)} %dynamic-slice_bitcast_fusion.1), channel_id=1, source_target_pairs={{0,4},{2,6},{4,0},{6,2},{8,12},{10,14},{12,8},{14,10},{16,20},{18,... | collective-permute-start | bytes 786440 | tf_op jit(solution)/shard_map/ppermute | solution.py:46
  266.3 11.4 %collective-permute-start.35 = (bf16[96,1024]{1,0:T(8,128)(2,1)}, bf16[96,1024]{1,0:T(8,128)(2,1)}, u32[]{:S(2)}, u32[]{:S(2)}) collective-permute-start(bf16[96,1024]{1,0:T(8,128)(2,1)} %get-tuple-element.207), channel_id=1, source_target_pairs={{0,24},{2,26},{4,28},{6,30},{8,0},{10,2},{12,4},{14,6},{16,8},{18,... | collective-permute-start | bytes 589832 | tf_op jit(solution)/shard_map/ppermute | solution.py:46
  268.3 11.5 %collective-permute-start.36 = (bf16[96,1024]{1,0:T(8,128)(2,1)}, bf16[96,1024]{1,0:T(8,128)(2,1)}, u32[]{:S(2)}, u32[]{:S(2)}) collective-permute-start(bf16[96,1024]{1,0:T(8,128)(2,1)} %get-tuple-element.209), channel_id=1, source_target_pairs={{0,16},{2,18},{4,20},{6,22},{8,24},{10,26},{12,28},{14,30},{16,0},... | collective-permute-start | bytes 589832 | tf_op jit(solution)/shard_map/ppermute | solution.py:46
  268.8 12.5 %collective-permute-start.37 = (bf16[96,1024]{1,0:T(8,128)(2,1)}, bf16[96,1024]{1,0:T(8,128)(2,1)}, u32[]{:S(2)}, u32[]{:S(2)}) collective-permute-start(bf16[96,1024]{1,0:T(8,128)(2,1)} %get-tuple-element.208), channel_id=1, source_target_pairs={{0,8},{2,10},{4,12},{6,14},{8,16},{10,18},{12,20},{14,22},{16,24},... | collective-permute-start | bytes 589832 | tf_op jit(solution)/shard_map/ppermute | solution.py:46
  276.8 9.2 %collective-permute-start.40 = (bf16[4,2,64,512]{3,2,0,1:T(8,128)(2,1)S(1)}, bf16[4,2,64,512]{3,2,0,1:T(8,128)(2,1)S(1)}, u32[]{:S(2)}, u32[]{:S(2)}) collective-permute-start(bf16[4,2,64,512]{3,2,0,1:T(8,128)(2,1)S(1)} %bitcast_select_fusion.1), channel_id=1, source_target_pairs={{1,0},{0,2},{2,3},{3,1},{5,4},{4,6},{6,7},{7,5},{9,8},{8,10},{10,1... | collective-permute-start | bytes 1572872 | tf_op jit(solution)/shard_map/ppermute | solution.py:73
  277.0 9.0 %collective-permute-start.41 = (bf16[4,2,64,512]{3,2,0,1:T(8,128)(2,1)S(1)}, bf16[4,2,64,512]{3,2,0,1:T(8,128)(2,1)S(1)}, u32[]{:S(2)}, u32[]{:S(2)}) collective-permute-start(bf16[4,2,64,512]{3,2,0,1:T(8,128)(2,1)S(1)} %bitcast.167), channel_id=1, source_target_pairs={{2,1},{1,2},{6,5},{5,6},{10,9},{9,10},{14,13},{13,14},{18,17},{17,... | collective-permute-start | bytes 1572872 | tf_op jit(solution)/shard_map/ppermute | solution.py:77
  277.7 22.6 %collective-permute-start.46 = (bf16[64,512]{1,0:T(8,128)(2,1)S(1)}, bf16[64,512]{1,0:T(8,128)(2,1)S(1)}, u32[]{:S(2)}, u32[]{:S(2)}) collective-permute-start(bf16[64,512]{1,0:T(8,128)(2,1)S(1)} %get-tuple-element.224), channel_id=1, source_target_pairs={{0,8},{2,10},{4,12},{6,14},{8,16},{10,18},{12,20},{14,22},{16,24},... | collective-permute-start | bytes 196616 | tf_op jit(solution)/shard_map/ppermute | solution.py:46
  279.9 20.4 %collective-permute-start.47 = (bf16[64,512]{1,0:T(8,128)(2,1)S(1)}, bf16[64,512]{1,0:T(8,128)(2,1)S(1)}, u32[]{:S(2)}, u32[]{:S(2)}) collective-permute-start(bf16[64,512]{1,0:T(8,128)(2,1)S(1)} %get-tuple-element.226), channel_id=1, source_target_pairs={{0,16},{2,18},{4,20},{6,22},{8,24},{10,26},{12,28},{14,30},{16,0},... | collective-permute-start | bytes 196616 | tf_op jit(solution)/shard_map/ppermute | solution.py:46
  281.3 19.0 %collective-permute-start.48 = (bf16[64,512]{1,0:T(8,128)(2,1)S(1)}, bf16[64,512]{1,0:T(8,128)(2,1)S(1)}, u32[]{:S(2)}, u32[]{:S(2)}) collective-permute-start(bf16[64,512]{1,0:T(8,128)(2,1)S(1)} %get-tuple-element.225), channel_id=1, source_target_pairs={{0,24},{2,26},{4,28},{6,30},{8,0},{10,2},{12,4},{14,6},{16,8},{18,... | collective-permute-start | bytes 196616 | tf_op jit(solution)/shard_map/ppermute | solution.py:46
  286.3 8.3 %collective-permute-start.42 = (bf16[4,64,512]{2,1,0:T(8,128)(2,1)S(1)}, bf16[4,64,512]{2,1,0:T(8,128)(2,1)S(1)}, u32[]{:S(2)}, u32[]{:S(2)}) collective-permute-start(bf16[4,64,512]{2,1,0:T(8,128)(2,1)S(1)} %fusion.13), channel_id=1, source_target_pairs={{0,4},{2,6},{4,0},{6,2},{8,12},{10,14},{12,8},{14,10},{16,20},{18,... | collective-permute-start | bytes 786440 | tf_op jit(solution)/shard_map/ppermute | solution.py:46
  288.3 12.7 %collective-permute-start.38 = (bf16[96,1024]{1,0:T(8,128)(2,1)S(1)}, bf16[96,1024]{1,0:T(8,128)(2,1)S(1)}, u32[]{:S(2)}, u32[]{:S(2)}) collective-permute-start(bf16[96,1024]{1,0:T(8,128)(2,1)S(1)} %fusion.7), channel_id=1, source_target_pairs={{0,1},{1,0},{2,3},{3,2},{4,5},{5,4},{6,7},{7,6},{8,9},{9,8},{10,11... | collective-permute-start | bytes 589832 | tf_op jit(solution)/shard_map/ppermute | solution.py:58
  295.4 15.4 %all-to-all-start.2 = ((bf16[4,64,512]{2,1,0:T(8,128)(2,1)}), bf16[4,64,512]{2,1,0:T(8,128)(2,1)S(1)}, u32[]{:S(2)}, u32[]{:S(2)}) async-start(bf16[4,64,512]{2,1,0:T(8,128)(2,1)} %fusion.2), calls=%async_computation.2 | async-start | bytes 524288 | tf_op jit(solution)/shard_map/all_to_all | solution.py:903
  (50 other events, 531.1 us)
Sparse Core Ops, SparseCore 0:
  46.2 92.6 all-gather.1
  211.0 95.3 reduce-scatter.1

commit v5 on v4

--- a/solution.py
+++ b/solution.py
@@ -150,6 +150,8 @@
 
 
 STEP = 384
+WIDE = 1536
+BACK = 768
 SMEM = pl.BlockSpec(memory_space=pltpu.SMEM)
 
 
@@ -319,32 +321,32 @@
             keys = block[span_in, pair_lanes(p)]
             for h in (2 * p, 2 * p + 1):
                 kaug[h, span, :] = jnp.where(lane_in_head(keys.shape, h), keys, code)
-        vturn[n] = jnp.transpose(block[span_in, width:])
+        vturn[:, n * STEP : (n + 1) * STEP] = jnp.transpose(block[span_in, width:])
     for p in range(heads // 2):
         part = low_ref[:, pair_lanes(p)]
         for h in (2 * p, 2 * p + 1):
             qaug[h] = jnp.where(lane_in_head(part.shape, h), part, qcode_ref[...])
-    acc[...] = jnp.zeros_like(acc)
-    stat[0] = jnp.full(stat.shape[1:], EXCLUDED, F32)
-    stat[1] = jnp.zeros(stat.shape[1:], F32)
-
-    def chunk(i, carry):
-        for h in range(heads):
-            scores = dot(kaug[h, pl.ds(i * STEP, STEP), :], qaug[h], NT)
-            top = stat[0, h : h + 1, :]
-            new_top = jnp.maximum(top, jnp.max(scores, axis=0, keepdims=True))
-            weight = jnp.exp(scores - new_top)
-            rescale = jnp.exp(top - new_top)
-            stat[0, h : h + 1, :] = new_top
-            stat[1, h : h + 1, :] = stat[1, h : h + 1, :] * rescale + jnp.sum(weight, axis=0, keepdims=True)
-            span = slice(h * HD, (h + 1) * HD)
-            acc[span, :] = acc[span, :] * rescale + dot(vturn[i, span, :], weight.astype(BF16))
-        return carry
-
-    lax.fori_loop(0, pieces * steps, chunk, 0)
+    stat[...] = jnp.ones_like(stat)
     for h in range(heads):
         span = slice(h * HD, (h + 1) * HD)
-        acc[span, :] = acc[span, :] / stat[1, h : h + 1, :]
+        top = total = out = None
+        for n in range(kaug.shape[1] // WIDE):
+            part = slice(n * WIDE, (n + 1) * WIDE)
+            scores = dot(kaug[h, part, :], qaug[h], NT)
+            peak = jnp.max(scores, axis=0, keepdims=True)
+            new_top = peak if top is None else jnp.maximum(top, peak)
+            weight = jnp.exp(scores - new_top)
+            add = jnp.sum(weight, axis=0, keepdims=True)
+            mixed = dot(vturn[span, part], weight.astype(BF16))
+            if top is None:
+                total, out = add, mixed
+            else:
+                rescale = jnp.exp(top - new_top)
+                total, out = total * rescale + add, out * rescale + mixed
+            top = new_top
+        stat[0, h : h + 1, :] = top
+        stat[1, h : h + 1, :] = total
+        acc[span, :] = out / total
     out_ref[...] = jnp.transpose(acc[...])
     lse_ref[...] = stat[0] + jnp.log(jnp.maximum(stat[1], 1e-37))
     z = at_ref[0]
@@ -370,7 +372,7 @@
         (at, q, bias, qcode, kcode, *kv_pieces),
         scratch=[
             pltpu.VMEM((heads, keys, 2 * HD), BF16),
-            pltpu.VMEM((keys // STEP, width, STEP), BF16),
+            pltpu.VMEM((width, keys), BF16),
             pltpu.VMEM((heads, count, 2 * HD), BF16),
             pltpu.VMEM((width, count), F32),
             pltpu.VMEM((2, 8, count), F32),
@@ -413,7 +415,7 @@
             keys = block[span_in, pair_lanes(p)]
             for h in (2 * p, 2 * p + 1):
                 kaug[h, span, :] = jnp.where(lane_in_head(keys.shape, h), keys, code)
-        kturn[n] = jnp.transpose(block[span_in, :width])
+        kturn[:, n * STEP : (n + 1) * STEP] = jnp.transpose(block[span_in, :width])
         vals[span, :] = block[span_in, width:]
     for p in range(heads // 2):
         part = q_ref[:, pair_lanes(p)]
@@ -423,32 +425,33 @@
             qaug[h] = jnp.where(inside, part, qcode_ref[...])
             qmask[h] = jnp.where(inside, part, jnp.zeros_like(part))
             domask[h] = jnp.where(inside, dpart, jnp.zeros_like(dpart))
-    acc[...] = jnp.zeros_like(acc)
-    each = 2 * steps
-    for j in range(nx):
-
-        def chunk(n, carry, j=j):
-            i = j * each + n
-            span = pl.ds(i * STEP, STEP)
-            span_out = pl.ds(n * STEP, STEP)
-            for p in range(heads // 2):
-                dkey = dval = None
-                for h in (2 * p, 2 * p + 1):
-                    scores = dot(kaug[h, span, :], qaug[h], NT)
-                    prob = jnp.exp(scores - lse_ref[h : h + 1, :])
-                    dprob = dot(vals[span, pair_lanes(p)], domask[h], NT)
-                    dscore = (prob * (dprob - delta[h : h + 1, :])).astype(BF16)
-                    add_val = dot(prob.astype(BF16), domask[h])
-                    add_key = dot(dscore, qmask[h])
-                    dval = add_val if dval is None else dval + add_val
-                    dkey = add_key if dkey is None else dkey + add_key
-                    turn = slice(h * HD, (h + 1) * HD)
-                    acc[turn, :] += dot(kturn[i, turn, :], dscore)
-                dkv_refs[j][span_out, pair_lanes(p)] = dkey.astype(BF16)
-                dkv_refs[j][span_out, slice(width + p * 2 * HD, width + (p + 1) * 2 * HD)] = dval.astype(BF16)
-            return carry
-
-        lax.fori_loop(0, each, chunk, 0)
+    total = [None] * heads
+    for n in range(kaug.shape[1] // BACK):
+        part = slice(n * BACK, (n + 1) * BACK)
+        for p in range(heads // 2):
+            dkey = dval = None
+            for h in (2 * p, 2 * p + 1):
+                scores = dot(kaug[h, part, :], qaug[h], NT)
+                prob = jnp.exp(scores - lse_ref[h : h + 1, :])
+                dprob = dot(vals[part, pair_lanes(p)], domask[h], NT)
+                dscore = (prob * (dprob - delta[h : h + 1, :])).astype(BF16)
+                add_val = dot(prob.astype(BF16), domask[h])
+                add_key = dot(dscore, qmask[h])
+                dval = add_val if dval is None else dval + add_val
+                dkey = add_key if dkey is None else dkey + add_key
+                add = dot(kturn[h * HD : (h + 1) * HD, part], dscore)
+                total[h] = add if total[h] is None else total[h] + add
+            each = dkv_refs[0].shape[0]
+            size = min(BACK, each)
+            for m in range(BACK // size):
+                at_row = n * BACK + m * size
+                rows_out = slice(at_row % each, at_row % each + size)
+                rows_in = slice(m * size, (m + 1) * size)
+                dkv_refs[at_row // each][rows_out, pair_lanes(p)] = dkey[rows_in].astype(BF16)
+                lanes_out = slice(width + p * 2 * HD, width + (p + 1) * 2 * HD)
+                dkv_refs[at_row // each][rows_out, lanes_out] = dval[rows_in].astype(BF16)
+    for h in range(heads):
+        acc[h * HD : (h + 1) * HD, :] = total[h]
     dq_ref[...] = (jnp.transpose(acc[...]) * (HD ** (-0.5))).astype(BF16)
 
 
@@ -464,7 +467,7 @@
         (at, q, qcode, kcode, got, full, lse, *kv_pieces),
         scratch=[
             pltpu.VMEM((heads, keys, 2 * HD), BF16),
-            pltpu.VMEM((keys // STEP, width, STEP), BF16),
+            pltpu.VMEM((width, keys), BF16),
             pltpu.VMEM((keys, width), BF16),
             pltpu.VMEM((heads, count, 2 * HD), BF16),
             pltpu.VMEM((heads, count, 2 * HD), BF16),
@@ -591,18 +594,34 @@
     )
 
 
-def outer_kernel(normed_ref, gh_ref, gz_ref, act_ref, out_ref):
+def outer_kernel(part, at_ref, normed_ref, gh_ref, gz_ref, act_ref, keep_ref, send_ref, made):
     hidden_size = gh_ref.shape[1]
+    chips = keep_ref.shape[0] // part
     step = 256
     for base, left_ref, right_ref in ((0, normed_ref, gh_ref), (hidden_size, gz_ref, act_ref)):
         for n in range(hidden_size // step):
-            made = dot(left_ref[...], right_ref[:, n * step : (n + 1) * step], TN)
-            out_ref[:, base + n * step : base + (n + 1) * step] = made.astype(BF16)
-
-
-def outer(normed, gh, gz, act):
+            made[...] = dot(left_ref[...], right_ref[:, n * step : (n + 1) * step], TN)
+            lanes = slice(base + n * step, base + (n + 1) * step)
+            for p in range(2):
+
+                def store(ref, p=p, lanes=lanes):
+                    for i in range(chips):
+                        block = made[(2 * i + p) * part : (2 * i + p + 1) * part, :]
+                        ref[i * part : (i + 1) * part, lanes] = block.astype(BF16)
+
+                pl.when(at_ref[2] == p)(functools.partial(store, keep_ref))
+                pl.when(at_ref[2] != p)(functools.partial(store, send_ref))
+
+
+def outer(at, part, normed, gh, gz, act):
+    width = normed.shape[1]
+    out = shape((width // 2, 2 * gh.shape[1]))
     return local_kernel(
-        outer_kernel, "outer", shape((normed.shape[1], 2 * gh.shape[1])), (normed, gh, gz, act), scalars=0
+        functools.partial(outer_kernel, part),
+        "outer",
+        (out, out),
+        (at, normed, gh, gz, act),
+        scratch=[pltpu.VMEM((width, 256), F32)],
     )
 
 
@@ -855,8 +874,9 @@
 
     half_n = keep_n + grid.cswap(send_n).astype(F32)
     near_n = grid.yswap(half_n[rows:].astype(BF16))
-    d_outer = outer(normed_two, grad_hidden, gz, active)
-    d_ff = lax.psum_scatter(d_outer, ("z", "x"), scatter_dimension=0, tiled=True)
+    d_outer, d_send = outer(at, part, normed_two, grad_hidden, gz, active)
+    d_both = jnp.concatenate([d_outer, grid.cswap(d_send)], axis=1)
+    d_ff = lax.psum_scatter(d_both, ("z", "x"), scatter_dimension=0, tiled=True)
     grad_middle, grad_branch, mine, send, sums_two = branch(
         at, nz, half_n, near_n, n2, s2, vecs, gz[:rows], w_proj, (d_outer,)
     )
@@ -926,8 +946,8 @@
     dp = dp_keep + grid.yswap(dp_send.astype(BF16)).astype(F32)
     d_proj = grid.scatter(dp.astype(BF16).reshape(nz, nx, part, -1))
 
-    keep, send = split(after(d_ff, grad_n1), 0, core)
-    low_cols, high_cols = in_order(keep, grid.cswap(send), core)
+    n_cols = 2 * grad_hidden.shape[1]
+    low_cols, high_cols = in_order(d_ff[:, :n_cols], d_ff[:, n_cols:], core)
     n_hidden = grad_hidden.shape[1]
     d_up = jnp.concatenate([low_cols[:, :n_hidden], high_cols[:, :n_hidden]], axis=1).astype(F32)
     d_down = jnp.concatenate([low_cols[:, n_hidden:], high_cols[:, n_hidden:]], axis=1).astype(F32)

time: 327 us -> 324 us (level)
  waiting for transfers between devices: 111 us -> 102 us
  Pallas kernels: 61.6 us -> 56.5 us
  other arithmetic: 32.2 us -> 36 us
    ppermute x36, starting transfers between devices: 35.2 us -> 42.8 us  [_move(): return lax.ppermute(block, SP, pairs)]
    ppermute x36, waiting for transfers between devices: 64.6 us -> 57.4 us  [_move(): return lax.ppermute(block, SP, pairs)]
    pallas_call x10, Pallas kernels: 59.9 us -> 54.8 us  [local_kernel(): pl.pallas_call(kernel, out_shape=out_shape, in_specs=[SMEM] * scalars + i...]
    concatenate x0 -> x1, other arithmetic: none -> 4.12 us  [per_device(): d_both = jnp.concatenate([d_outer, grid.cswap(d_send)], axis=1)]
    ppermute x10, starting transfers between devices: 20.8 us -> 17.4 us  [yswap(): return lax.ppermute(block, 'tp', [(0, 1), (1, 0)])]
    unnamed x93 -> x105, local copies, waits for them, and re-layouts: 12.9 us -> 13.4 us
  transfers between devices with their start and end apart: 54 -> 54, of which waited for: 22 -> 22; matrix products, arithmetic and copies ran while one was open for 11% -> 13% of each run, Pallas kernels for 16% -> 15%
where the time goes in v5:
time: 324 us; the launch traced here: 320 us
  waiting for transfers between devices  102 us (31%)
  starting transfers between devices  70.3 us (22%)
  Pallas kernels  56.5 us (17%)
  other arithmetic  36 us (11%)
  local copies, waits for them, and re-layouts  25 us (8%)
  between operations  15.5 us (5%)
  blocking collectives  13.8 us (4%)
    ppermute x36, waiting for transfers between devices, _move(): return lax.ppermute(block, SP, pairs)  57.4 us
    pallas_call x10, Pallas kernels, local_kernel(): pl.pallas_call(kernel, out_shape=out_shape, in_specs=[SMEM] * scalars + i...  54.8 us
    ppermute x36, starting transfers between devices, _move(): return lax.ppermute(block, SP, pairs)  42.8 us
    ppermute x10, waiting for transfers between devices, yswap(): return lax.ppermute(block, 'tp', [(0, 1), (1, 0)])  24.5 us
    ppermute x10, starting transfers between devices, yswap(): return lax.ppermute(block, 'tp', [(0, 1), (1, 0)])  17.4 us
    all_to_all x1, blocking collectives, per_device(): attn_got = lax.all_to_all(attn_send, 'z', 0, 0, tiled=True)  13.8 us
    unnamed x105, local copies, waits for them, and re-layouts  13.4 us
    all_to_all x1, waiting for transfers between devices, per_device(): dw = lax.all_to_all(dw.astype(BF16), 'z', 0, 0, tiled=True)  9.94 us
  transfers between devices with their start and end apart: 54, of which 22 were waited for; matrix products, arithmetic and copies ran while one was open for 13% of the time, Pallas kernels for 15%

profile of v5, /device:TPU:0, one launch (start us, length us, event | category | flops | bytes accessed | tf_op | source)
XLA Modules:
  0.0 320.4 jit_solution(16224043226806372580)
XLA Ops:
  12.8 3.1 collective-permute-start
  15.9 2.6 collective-permute-start.1
  22.3 5.2 %collective-permute-done.7 = bf16[64,384]{1,0:T(8,128)(2,1)S(1)} collective-permute-done((bf16[64,384]{1,0:T(8,128)(2,1)S(1)}, bf16[64,384]{1,0:T(8,128)(2,1)S(1)}, u32[]{:S(2)}, u32[]{:S(2)}) %collective-permute-start.7) | collective-permute-done | bytes 49184 | tf_op jit(solution)/shard_map/ppermute | solution.py:46
  27.5 4.3 %collective-permute-start.2 = (bf16[96,1152]{1,0:T(8,128)(2,1)S(1)}, bf16[96,1152]{1,0:T(8,128)(2,1)S(1)}, u32[]{:S(2)}, u32[]{:S(2)}) collective-permute-start(bf16[96,1152]{1,0:T(8,128)(2,1)S(1)} %concatenate.70.refs_0_), channel_id=1, source_target_pairs={{0,24},{2,26},{4,28},{6,30},{8,0},{10,2},{12,4},{14,6},{16,8},{18,... | collective-permute-start | bytes 663560 | tf_op jit(solution)/shard_map/ppermute | solution.py:46
  31.8 5.3 %collective-permute-done.6 = bf16[64,384]{1,0:T(8,128)(2,1)S(1)} collective-permute-done((bf16[64,384]{1,0:T(8,128)(2,1)S(1)}, bf16[64,384]{1,0:T(8,128)(2,1)S(1)}, u32[]{:S(2)}, u32[]{:S(2)}) %collective-permute-start.6) | collective-permute-done | bytes 49184 | tf_op jit(solution)/shard_map/ppermute | solution.py:46
  38.8 3.3 %collective-permute-done.2.refs_3_ = bf16[96,1152]{1,0:T(8,128)(2,1)S(1)} collective-permute-done((bf16[96,1152]{1,0:T(8,128)(2,1)S(1)}, bf16[96,1152]{1,0:T(8,128)(2,1)S(1)}, u32[]{:S(2)}, u32[]{:S(2)}) %collective-permute-start.2) | collective-permute-done | bytes 221216 | tf_op jit(solution)/shard_map/ppermute | solution.py:46
  48.9 4.6 %collective-permute-done.9 = bf16[2,4,64,384]{3,2,1,0:T(8,128)(2,1)S(1)} collective-permute-done((bf16[2,4,64,384]{3,2,1,0:T(8,128)(2,1)S(1)}, bf16[2,4,64,384]{3,2,1,0:T(8,128)(2,1)S(1)}, u32[]{:S(2)}, u32[]{:S(2)}) %collective-permute-start.9) | collective-permute-done | bytes 393248 | tf_op jit(solution)/shard_map/ppermute | solution.py:73
  53.6 4.9 %collective-permute-start.19 = (bf16[64,512]{1,0:T(8,128)(2,1)}, bf16[64,512]{1,0:T(8,128)(2,1)}, u32[]{:S(2)}, u32[]{:S(2)}) collective-permute-start(bf16[64,512]{1,0:T(8,128)(2,1)} %bitcast.39), channel_id=1, source_target_pairs={{0,24},{2,26},{4,28},{6,30},{8,0},{10,2},{12,4},{14,6},{16,8},{18,... | collective-permute-start | bytes 196616 | tf_op jit(solution)/shard_map/ppermute | solution.py:46
  58.5 2.0 collective-permute-start.17
  61.0 4.2 %enter.1 = (bf16[768,1024]{1,0:T(8,128)(2,1)}, bf16[768,1024]{1,0:T(8,128)(2,1)}, f32[768,1]{1,0:T(8,128)S(1)}, f32[768,1]{1,0:T(8,128)S(1)}, f32[96,1024]{1,0:T...) custom-call(s32[4]{0:T(128)S(1)} %pad_add_fusion.at_ref.refs_0_, ...), custom_call_target="tpu_custom_call" | custom-call | flops 5000000000 | bytes 65536 | tf_op jit(solution)/shard_map/enter/pallas_call | solution.py:173
  69.2 3.8 %collective-permute-start.13 = (bf16[768,256]{1,0:T(8,128)(2,1)S(1)}, bf16[768,256]{1,0:T(8,128)(2,1)S(1)}, u32[]{:S(2)}, u32[]{:S(2)}) collective-permute-start(bf16[768,256]{1,0:T(8,128)(2,1)S(1)} %get-tuple-element.71.refs_0_), channel_id=1, source_target_pairs={{0,1},{1,0},{2,3},{3,2},{4,5},{5,4},{6,7},{7,6},{8,9},{9,8},{10,11... | collective-permute-start | bytes 1179656 | tf_op jit(solution)/shard_map/ppermute | solution.py:58
  81.0 8.8 %collective-permute-done.20 = bf16[4,64,512]{2,1,0:T(8,128)(2,1)S(1)} collective-permute-done((bf16[4,64,512]{2,1,0:T(8,128)(2,1)S(1)}, bf16[4,64,512]{2,1,0:T(8,128)(2,1)S(1)}, u32[]{:S(2)}, u32[]{:S(2)}) %collective-permute-start.20) | collective-permute-done | bytes 262176 | tf_op jit(solution)/shard_map/ppermute | solution.py:46
  91.6 2.4 collective-permute-start.21
  95.7 2.1 pad_maximum_fusion.3.gz_ref
  97.8 6.6 %collective-permute-done.21 = bf16[2,4,64,512]{3,2,1,0:T(8,128)(2,1)S(1)} collective-permute-done((bf16[2,4,64,512]{3,2,1,0:T(8,128)(2,1)S(1)}, bf16[2,4,64,512]{3,2,1,0:T(8,128)(2,1)S(1)}, u32[]{:S(2)}, u32[]{:S(2)}) %collective-permute-start.21) | collective-permute-done | bytes 524320 | tf_op jit(solution)/shard_map/ppermute | solution.py:58
  104.5 9.4 %collective-permute-done.15.refs_3_ = bf16[768,256]{1,0:T(8,128)(2,1)S(1)} collective-permute-done((bf16[768,256]{1,0:T(8,128)(2,1)S(1)}, bf16[768,256]{1,0:T(8,128)(2,1)S(1)}, u32[]{:S(2)}, u32[]{:S(2)}) %collective-permute-start.15) | collective-permute-done | bytes 393248 | tf_op jit(solution)/shard_map/ppermute | solution.py:46
  114.0 7.4 %attend.1 = (f32[768,128]{1,0:T(8,128)S(1)}, f32[8,768]{1,0:T(8,128)S(1)}, bf16[768,128]{1,0:T(8,128)(2,1)S(1)}, bf16[4,2,96,128]{3,2,1,0:T(8,128)(2,1)S(1)}) custom-call(s32[4]{0:T(128)S(1)} %pad_add_fusion.at_ref.refs_0_, f32[768,128]{1,0:T(8,128)S(1)} %copy-done.32, f32[2,128]{1,0:T(2,128)S(1)} %fusion.25.bias_ref, ...), custom_call_target="tpu_custom_call" | custom-call | flops 14000000000 | bytes 65536 | tf_op jit(solution)/shard_map/attend/pallas_call | solution.py:173
  122.1 13.8 %all_to_all.15.got_ref = bf16[4,2,96,128]{3,2,1,0:T(8,128)(2,1)S(1)} all-to-all(bf16[4,2,96,128]{3,2,1,0:T(8,128)(2,1)S(1)} %get-tuple-element.74), channel_id=1, replica_groups=mesh['z'=4,'x'=2,'core'=2,'tp'=2] {'z'}, dimensions={0} | all-to-all | bytes 393216 | tf_op jit(solution)/shard_map/all_to_all | solution.py:868
  142.5 5.4 %collective-permute-done.23.near_ref = bf16[96,1024]{1,0:T(8,128)(2,1)S(1)} collective-permute-done((bf16[96,1024]{1,0:T(8,128)(2,1)S(1)}, bf16[96,1024]{1,0:T(8,128)(2,1)S(1)}, u32[]{:S(2)}, u32[]{:S(2)}) %collective-permute-start.23) | collective-permute-done | bytes 196640 | tf_op jit(solution)/shard_map/ppermute | solution.py:58
  148.0 1.8 collective-permute-done.24.far_ref
  149.9 8.4 %feed.1 = (bf16[384,1024]{1,0:T(8,128)(2,1)}, bf16[384,1024]{1,0:T(8,128)(2,1)}, bf16[384,1024]{1,0:T(8,128)(2,1)}, f32[1,1024]{1,0:T(1,128)}, f32[192,1024]{1,0...) custom-call(f32[1,1024]{1,0:T(1,128)} %broadcast_select_fusion.18.bias_ref, ...), custom_call_target="tpu_custom_call" | custom-call | bytes 65536 | tf_op jit(solution)/shard_map/feed/pallas_call | solution.py:173
  158.5 1.8 collective-permute-done.26
  161.5 1.6 collective-permute-start.27
  163.1 8.1 %outer.1 = (bf16[512,2048]{1,0:T(8,128)(2,1)S(1)}, bf16[512,2048]{1,0:T(8,128)(2,1)}) custom-call(s32[4]{0:T(128)S(1)} %pad_add_fusion.at_ref.refs_0_, bf16[384,1024]{1,0:T(8,128)(2,1)S(1)} %copy-done.12, bf16[384,1024]{1,0:T(8,128)(2,1)S(1)} %copy-done.14, bf16[384,1024]{1,0:T(8,128)(2,1)S(1)} %copy-done, bf16[384,1024]{1,0:T(8,128)(2,1)S(1)} %copy-done.13), custom_call_target="tpu_custom_call" | custom-call | flops 5000000000 | bytes 65536 | tf_op jit(solution)/shard_map/outer/pallas_call | solution.py:173
  176.2 3.4 %all-to-all-start.1 = ((bf16[4,2,96,128]{3,2,1,0:T(8,128)(2,1)}), bf16[4,2,96,128]{3,2,1,0:T(8,128)(2,1)S(1)}, u32[]{:S(2)}, u32[]{:S(2)}) async-start(bf16[4,2,96,128]{3,2,1,0:T(8,128)(2,1)} %pad_maximum_fusion.14), calls=%async_computation.1 | async-start | bytes 393216 | tf_op jit(solution)/shard_map/all_to_all | solution.py:884
  182.8 4.8 %all-to-all-done.1.got_ref = bf16[4,2,96,128]{3,2,1,0:T(8,128)(2,1)S(1)} async-done(((bf16[4,2,96,128]{3,2,1,0:T(8,128)(2,1)}), bf16[4,2,96,128]{3,2,1,0:T(8,128)(2,1)S(1)}, u32[]{:S(2)}, u32[]{:S(2)}) %all-to-all-start.1) | async-done | bytes 196640 | tf_op jit(solution)/shard_map/all_to_all | solution.py:884
  188.3 15.0 %attend_back.1 = (bf16[768,128]{1,0:T(8,128)(2,1)}, bf16[1536,256]{1,0:T(8,128)(2,1)}, bf16[1536,256]{1,0:T(8,128)(2,1)}) custom-call(s32[4]{0:T(128)} %copy-done.11, bf16[768,128]{1,0:T(8,128)(2,1)} %copy-done.34, bf16[768,128]{1,0:T(8,128)(2,1)} %copy-done.7, bf16[3072,128]{1,0:T(8,128)(2,1)} %copy-done.4, bf16[4,2,96,128]{3,2,1,0:T(8,128)(2,1)} %copy-done.48, ...), custom_call_target="tpu_custom_call" | custom-call | flops 16999999488 | bytes 65536 | tf_op jit(solution)/shard_map/attend_back/pallas_call | solution.py:173
  208.3 4.1 %pad_maximum_fusion = bf16[512,4096]{1,0:T(8,128)(2,1)} fusion(bf16[512,2048]{1,0:T(8,128)(2,1)} %collective-permute-done.49, bf16[512,2048]{1,0:T(8,128)(2,1)S(1)} %copy-done.2), kind=kLoop, calls=%fused_computation | loop fusion | flops 8388608 | bytes 8388608 | tf_op jit(solution)/shard_map/concatenate | solution.py:878
  212.4 10.8 %collective-permute-done.32 = bf16[1536,256]{1,0:T(8,128)(2,1)} collective-permute-done((bf16[1536,256]{1,0:T(8,128)(2,1)}, bf16[1536,256]{1,0:T(8,128)(2,1)}, u32[]{:S(2)}, u32[]{:S(2)}) %collective-permute-start.32) | collective-permute-done | bytes 786464 | tf_op jit(solution)/shard_map/ppermute | solution.py:46
  224.9 1.7 convert_add_fusion
  226.8 2.0 collective-permute-start.44
  229.0 7.9 %collective-permute-done.33.near_ref = bf16[768,256]{1,0:T(8,128)(2,1)S(1)} collective-permute-done((bf16[768,256]{1,0:T(8,128)(2,1)S(1)}, bf16[768,256]{1,0:T(8,128)(2,1)S(1)}, u32[]{:S(2)}, u32[]{:S(2)}) %collective-permute-start.33) | collective-permute-done | bytes 393248 | tf_op jit(solution)/shard_map/ppermute | solution.py:58
  237.0 2.7 leave.1
  239.7 4.4 %collective-permute-done.44 = bf16[8,64,512]{2,1,0:T(8,128)(2,1)S(1)} collective-permute-done((bf16[8,64,512]{2,1,0:T(8,128)(2,1)S(1)}, bf16[8,64,512]{2,1,0:T(8,128)(2,1)S(1)}, u32[]{:S(2)}, u32[]{:S(2)}) %collective-permute-start.44) | collective-permute-done | bytes 524320 | tf_op jit(solution)/shard_map/ppermute | solution.py:58
  244.4 1.6 collective-permute-start.45
  247.0 3.9 %collective-permute-done.45 = bf16[4,64,512]{2,1,0:T(8,128)(2,1)S(1)} collective-permute-done((bf16[4,64,512]{2,1,0:T(8,128)(2,1)S(1)}, bf16[4,64,512]{2,1,0:T(8,128)(2,1)S(1)}, u32[]{:S(2)}, u32[]{:S(2)}) %collective-permute-start.45) | collective-permute-done | bytes 262176 | tf_op jit(solution)/shard_map/ppermute | solution.py:46
  254.2 2.6 collective-permute-start.37
  256.7 2.1 collective-permute-start.36
  259.1 5.1 %close.1 = (f32[4,1024]{1,0:T(4,128)S(1)}, f32[1,384]{1,0:T(1,128)S(1)}, bf16[1024,384]{1,0:T(8,128)(2,1)S(1)}) custom-call(f32[768,1024]{1,0:T(8,128)} %get-tuple-element.109.refs_0_, bf16[768,1024]{1,0:T(8,128)(2,1)S(1)} %copy-done.8, f32[768,1]{1,0:T(8,128)S(1)} %copy-done.10, f32[768,1]{1,0:T(8,128)S(1)} %copy-done.29, ...), custom_call_target="tpu_custom_call" | custom-call | flops 5000000000 | bytes 65536 | tf_op jit(solution)/shard_map/close/pallas_call | solution.py:173
  267.7 2.1 collective-permute-start.48
  271.0 2.4 collective-permute-start.46
  276.2 2.2 collective-permute-start.42
  278.6 5.2 %collective-permute-start.38 = (bf16[96,1024]{1,0:T(8,128)(2,1)S(1)}, bf16[96,1024]{1,0:T(8,128)(2,1)S(1)}, u32[]{:S(2)}, u32[]{:S(2)}) collective-permute-start(bf16[96,1024]{1,0:T(8,128)(2,1)S(1)} %fusion.7), channel_id=1, source_target_pairs={{0,1},{1,0},{2,3},{3,2},{4,5},{5,4},{6,7},{7,6},{8,9},{9,8},{10,11... | collective-permute-start | bytes 589832 | tf_op jit(solution)/shard_map/ppermute | solution.py:58
  283.8 4.8 %collective-permute-done.42 = bf16[4,64,512]{2,1,0:T(8,128)(2,1)S(1)} collective-permute-done((bf16[4,64,512]{2,1,0:T(8,128)(2,1)S(1)}, bf16[4,64,512]{2,1,0:T(8,128)(2,1)S(1)}, u32[]{:S(2)}, u32[]{:S(2)}) %collective-permute-start.42) | collective-permute-done | bytes 262176 | tf_op jit(solution)/shard_map/ppermute | solution.py:46
  289.4 3.4 %all-to-all-start.2 = ((bf16[4,64,512]{2,1,0:T(8,128)(2,1)}), bf16[4,64,512]{2,1,0:T(8,128)(2,1)S(1)}, u32[]{:S(2)}, u32[]{:S(2)}) async-start(bf16[4,64,512]{2,1,0:T(8,128)(2,1)} %fusion.2), calls=%async_computation.2 | async-start | bytes 524288 | tf_op jit(solution)/shard_map/all_to_all | solution.py:923
  292.8 1.6 fusion.17
  295.4 9.9 %all-to-all-done.2 = bf16[4,64,512]{2,1,0:T(8,128)(2,1)S(1)} async-done(((bf16[4,64,512]{2,1,0:T(8,128)(2,1)}), bf16[4,64,512]{2,1,0:T(8,128)(2,1)S(1)}, u32[]{:S(2)}, u32[]{:S(2)}) %all-to-all-start.2) | async-done | bytes 262176 | tf_op jit(solution)/shard_map/all_to_all | solution.py:923
  307.9 1.7 place_qkv.1
  (315 shorter events, 78.4 us)
Async XLA Ops:
  7.2 142.7 %all-gather.2.cloned.1.call-start = ((), (), s32[]{:S(2)}) async-start(), calls=%async_computation.4 | async-start | bytes 4718592 | tf_op jit(solution)/shard_map/all_gather | solution.py:852
  12.8 26.0 %collective-permute-start = (bf16[96,1152]{1,0:T(8,128)(2,1)S(1)}, bf16[96,1152]{1,0:T(8,128)(2,1)S(1)}, u32[]{:S(2)}, u32[]{:S(2)}) collective-permute-start(bf16[96,1152]{1,0:T(8,128)(2,1)S(1)} %concatenate.70.refs_0_), channel_id=1, source_target_pairs={{0,8},{2,10},{4,12},{6,14},{8,16},{10,18},{12,20},{14,22},{16,24},... | collective-permute-start | bytes 663560 | tf_op jit(solution)/shard_map/ppermute | solution.py:46
  15.9 22.9 %collective-permute-start.1 = (bf16[96,1152]{1,0:T(8,128)(2,1)S(1)}, bf16[96,1152]{1,0:T(8,128)(2,1)S(1)}, u32[]{:S(2)}, u32[]{:S(2)}) collective-permute-start(bf16[96,1152]{1,0:T(8,128)(2,1)S(1)} %concatenate.70.refs_0_), channel_id=1, source_target_pairs={{0,16},{2,18},{4,20},{6,22},{8,24},{10,26},{12,28},{14,30},{16,0},... | collective-permute-start | bytes 663560 | tf_op jit(solution)/shard_map/ppermute | solution.py:46
  19.9 7.6 %collective-permute-start.7 = (bf16[64,384]{1,0:T(8,128)(2,1)S(1)}, bf16[64,384]{1,0:T(8,128)(2,1)S(1)}, u32[]{:S(2)}, u32[]{:S(2)}) collective-permute-start(bf16[64,384]{1,0:T(8,128)(2,1)S(1)} %get-tuple-element.240), channel_id=1, source_target_pairs={{0,24},{2,26},{4,28},{6,30},{8,0},{10,2},{12,4},{14,6},{16,8},{18,... | collective-permute-start | bytes 147464 | tf_op jit(solution)/shard_map/ppermute | solution.py:46
  21.3 15.8 %collective-permute-start.6 = (bf16[64,384]{1,0:T(8,128)(2,1)S(1)}, bf16[64,384]{1,0:T(8,128)(2,1)S(1)}, u32[]{:S(2)}, u32[]{:S(2)}) collective-permute-start(bf16[64,384]{1,0:T(8,128)(2,1)S(1)} %get-tuple-element.241), channel_id=1, source_target_pairs={{0,16},{2,18},{4,20},{6,22},{8,24},{10,26},{12,28},{14,30},{16,0},... | collective-permute-start | bytes 147464 | tf_op jit(solution)/shard_map/ppermute | solution.py:46
  21.5 15.6 %collective-permute-start.5 = (bf16[64,384]{1,0:T(8,128)(2,1)S(1)}, bf16[64,384]{1,0:T(8,128)(2,1)S(1)}, u32[]{:S(2)}, u32[]{:S(2)}) collective-permute-start(bf16[64,384]{1,0:T(8,128)(2,1)S(1)} %get-tuple-element.242), channel_id=1, source_target_pairs={{0,8},{2,10},{4,12},{6,14},{8,16},{10,18},{12,20},{14,22},{16,24},... | collective-permute-start | bytes 147464 | tf_op jit(solution)/shard_map/ppermute | solution.py:46
  27.5 14.7 %collective-permute-start.2 = (bf16[96,1152]{1,0:T(8,128)(2,1)S(1)}, bf16[96,1152]{1,0:T(8,128)(2,1)S(1)}, u32[]{:S(2)}, u32[]{:S(2)}) collective-permute-start(bf16[96,1152]{1,0:T(8,128)(2,1)S(1)} %concatenate.70.refs_0_), channel_id=1, source_target_pairs={{0,24},{2,26},{4,28},{6,30},{8,0},{10,2},{12,4},{14,6},{16,8},{18,... | collective-permute-start | bytes 663560 | tf_op jit(solution)/shard_map/ppermute | solution.py:46
  37.1 7.2 %collective-permute-start.8 = (bf16[4,64,384]{2,1,0:T(8,128)(2,1)S(1)}, bf16[4,64,384]{2,1,0:T(8,128)(2,1)S(1)}, u32[]{:S(2)}, u32[]{:S(2)}) collective-permute-start(bf16[4,64,384]{2,1,0:T(8,128)(2,1)S(1)} %get-tuple-element.238), channel_id=1, source_target_pairs={{0,4},{2,6},{4,0},{6,2},{8,12},{10,14},{12,8},{14,10},{16,20},{18,... | collective-permute-start | bytes 589832 | tf_op jit(solution)/shard_map/ppermute | solution.py:46
  38.7 4.5 %collective-permute-start.25 = (bf16[64,2048]{1,0:T(8,128)(2,1)S(1)}, bf16[64,2048]{1,0:T(8,128)(2,1)S(1)}, u32[]{:S(2)}, u32[]{:S(2)}) collective-permute-start(bf16[64,2048]{1,0:T(8,128)(2,1)S(1)} %pad_maximum_fusion.12), channel_id=1, source_target_pairs={{0,2},{2,0},{4,6},{6,4},{8,10},{10,8},{12,14},{14,12},{16,18},{18,... | collective-permute-start | bytes 786440 | tf_op jit(solution)/shard_map/ppermute | solution.py:46
  44.4 9.2 %collective-permute-start.9 = (bf16[2,4,64,384]{3,2,1,0:T(8,128)(2,1)S(1)}, bf16[2,4,64,384]{3,2,1,0:T(8,128)(2,1)S(1)}, u32[]{:S(2)}, u32[]{:S(2)}) collective-permute-start(bf16[2,4,64,384]{3,2,1,0:T(8,128)(2,1)S(1)} %pad_maximum_fusion.6), channel_id=1, source_target_pairs={{0,1},{2,0},{3,2},{1,3},{4,5},{6,4},{7,6},{5,7},{8,9},{10,8},{11,1... | collective-permute-start | bytes 1179656 | tf_op jit(solution)/shard_map/ppermute | solution.py:73
  45.9 7.6 %collective-permute-start.10 = (bf16[2,4,64,384]{3,2,1,0:T(8,128)(2,1)S(1)}, bf16[2,4,64,384]{3,2,1,0:T(8,128)(2,1)S(1)}, u32[]{:S(2)}, u32[]{:S(2)}) collective-permute-start(bf16[2,4,64,384]{3,2,1,0:T(8,128)(2,1)S(1)} %pad_maximum_fusion.6), channel_id=1, source_target_pairs={{2,1},{1,2},{6,5},{5,6},{10,9},{9,10},{14,13},{13,14},{18,17},{17,... | collective-permute-start | bytes 1179656 | tf_op jit(solution)/shard_map/ppermute | solution.py:77
  47.3 13.2 %collective-permute-start.4 = (bf16[2,4,16,128]{3,2,1,0:T(8,128)(2,1)S(1)}, bf16[2,4,16,128]{3,2,1,0:T(8,128)(2,1)S(1)}, u32[]{:S(2)}, u32[]{:S(2)}) collective-permute-start(bf16[2,4,16,128]{3,2,1,0:T(8,128)(2,1)S(1)} %get-tuple-element.248), channel_id=1, source_target_pairs={{0,4},{2,6},{4,0},{6,2},{8,12},{10,14},{12,8},{14,10},{16,20},{18,... | collective-permute-start | bytes 98312 | tf_op jit(solution)/shard_map/ppermute | solution.py:46
  53.6 23.6 %collective-permute-start.19 = (bf16[64,512]{1,0:T(8,128)(2,1)}, bf16[64,512]{1,0:T(8,128)(2,1)}, u32[]{:S(2)}, u32[]{:S(2)}) collective-permute-start(bf16[64,512]{1,0:T(8,128)(2,1)} %bitcast.39), channel_id=1, source_target_pairs={{0,24},{2,26},{4,28},{6,30},{8,0},{10,2},{12,4},{14,6},{16,8},{18,... | collective-permute-start | bytes 196616 | tf_op jit(solution)/shard_map/ppermute | solution.py:46
  58.5 18.6 %collective-permute-start.18 = (bf16[64,512]{1,0:T(8,128)(2,1)}, bf16[64,512]{1,0:T(8,128)(2,1)}, u32[]{:S(2)}, u32[]{:S(2)}) collective-permute-start(bf16[64,512]{1,0:T(8,128)(2,1)} %bitcast.39), channel_id=1, source_target_pairs={{0,16},{2,18},{4,20},{6,22},{8,24},{10,26},{12,28},{14,30},{16,0},... | collective-permute-start | bytes 196616 | tf_op jit(solution)/shard_map/ppermute | solution.py:46
  58.5 18.7 %collective-permute-start.17 = (bf16[64,512]{1,0:T(8,128)(2,1)}, bf16[64,512]{1,0:T(8,128)(2,1)}, u32[]{:S(2)}, u32[]{:S(2)}) collective-permute-start(bf16[64,512]{1,0:T(8,128)(2,1)} %bitcast.39), channel_id=1, source_target_pairs={{0,8},{2,10},{4,12},{6,14},{8,16},{10,18},{12,20},{14,22},{16,24},... | collective-permute-start | bytes 196616 | tf_op jit(solution)/shard_map/ppermute | solution.py:46
  69.2 22.4 %collective-permute-start.13 = (bf16[768,256]{1,0:T(8,128)(2,1)S(1)}, bf16[768,256]{1,0:T(8,128)(2,1)S(1)}, u32[]{:S(2)}, u32[]{:S(2)}) collective-permute-start(bf16[768,256]{1,0:T(8,128)(2,1)S(1)} %get-tuple-element.71.refs_0_), channel_id=1, source_target_pairs={{0,1},{1,0},{2,3},{3,2},{4,5},{5,4},{6,7},{7,6},{8,9},{9,8},{10,11... | collective-permute-start | bytes 1179656 | tf_op jit(solution)/shard_map/ppermute | solution.py:58
  73.0 31.5 %collective-permute-start.14 = (bf16[768,256]{1,0:T(8,128)(2,1)S(1)}, bf16[768,256]{1,0:T(8,128)(2,1)S(1)}, u32[]{:S(2)}, u32[]{:S(2)}) collective-permute-start(bf16[768,256]{1,0:T(8,128)(2,1)S(1)} %get-tuple-element.71.refs_0_), channel_id=1, source_target_pairs={{0,4},{2,6},{4,0},{6,2},{8,12},{10,14},{12,8},{14,10},{16,20},{18,... | collective-permute-start | bytes 1179656 | tf_op jit(solution)/shard_map/ppermute | solution.py:46
  77.2 18.5 %collective-permute-start.11 = (bf16[192,1024]{1,0:T(8,128)(2,1)}, bf16[192,1024]{1,0:T(8,128)(2,1)}, u32[]{:S(2)}, u32[]{:S(2)}) collective-permute-start(bf16[192,1024]{1,0:T(8,128)(2,1)} %pad_maximum_fusion.7), channel_id=1, source_target_pairs={{0,2},{2,0},{4,6},{6,4},{8,10},{10,8},{12,14},{14,12},{16,18},{18,... | collective-permute-start | bytes 1179656 | tf_op jit(solution)/shard_map/ppermute | solution.py:46
  77.2 18.5 %collective-permute-start.12 = (f32[2,512]{1,0:T(2,128)S(1)}, f32[2,512]{1,0:T(2,128)S(1)}, u32[]{:S(2)}, u32[]{:S(2)}) collective-permute-start(f32[2,512]{1,0:T(2,128)S(1)} %reshape.345), channel_id=1, source_target_pairs={{0,1},{1,0},{2,3},{3,2},{4,5},{5,4},{6,7},{7,6},{8,9},{9,8},{10,11... | collective-permute-start | bytes 12296 | tf_op jit(solution)/shard_map/ppermute | solution.py:58
  78.3 11.5 %collective-permute-start.20 = (bf16[4,64,512]{2,1,0:T(8,128)(2,1)S(1)}, bf16[4,64,512]{2,1,0:T(8,128)(2,1)S(1)}, u32[]{:S(2)}, u32[]{:S(2)}) collective-permute-start(bf16[4,64,512]{2,1,0:T(8,128)(2,1)S(1)} %pad_maximum_fusion.10), channel_id=1, source_target_pairs={{0,4},{2,6},{4,0},{6,2},{8,12},{10,14},{12,8},{14,10},{16,20},{18,... | collective-permute-start | bytes 786440 | tf_op jit(solution)/shard_map/ppermute | solution.py:46
  91.6 12.7 %collective-permute-start.21 = (bf16[2,4,64,512]{3,2,1,0:T(8,128)(2,1)S(1)}, bf16[2,4,64,512]{3,2,1,0:T(8,128)(2,1)S(1)}, u32[]{:S(2)}, u32[]{:S(2)}) collective-permute-start(bf16[2,4,64,512]{3,2,1,0:T(8,128)(2,1)S(1)} %pad_maximum_fusion.4), channel_id=1, source_target_pairs={{0,1},{1,0},{2,3},{3,2},{4,5},{5,4},{6,7},{7,6},{8,9},{9,8},{10,11... | collective-permute-start | bytes 1572872 | tf_op jit(solution)/shard_map/ppermute | solution.py:58
  94.6 19.4 %collective-permute-start.15 = (bf16[768,256]{1,0:T(8,128)(2,1)S(1)}, bf16[768,256]{1,0:T(8,128)(2,1)S(1)}, u32[]{:S(2)}, u32[]{:S(2)}) collective-permute-start(bf16[768,256]{1,0:T(8,128)(2,1)S(1)} %collective-permute-done.13.refs_1_), channel_id=1, source_target_pairs={{0,4},{2,6},{4,0},{6,2},{8,12},{10,14},{12,8},{14,10},{16,20},{18,... | collective-permute-start | bytes 1179656 | tf_op jit(solution)/shard_map/ppermute | solution.py:46
  104.4 31.6 %collective-permute-start.22 = (bf16[2,2,4,64,512]{4,3,2,1,0:T(8,128)(2,1)S(1)}, bf16[2,2,4,64,512]{4,3,2,1,0:T(8,128)(2,1)S(1)}, u32[]{:S(2)}, u32[]{:S(2)}) collective-permute-start(bf16[2,2,4,64,512]{4,3,2,1,0:T(8,128)(2,1)S(1)} %pad_maximum_fusion.1.own_ref), channel_id=1, source_target_pairs={{0,2},{2,0},{4,6},{6,4},{8,10},{10,8},{12,14},{14,12},{16,18},{18,... | collective-permute-start | bytes 3145736 | tf_op jit(solution)/shard_map/ppermute | solution.py:46
  140.9 7.0 %collective-permute-start.23 = (bf16[96,1024]{1,0:T(8,128)(2,1)S(1)}, bf16[96,1024]{1,0:T(8,128)(2,1)S(1)}, u32[]{:S(2)}, u32[]{:S(2)}) collective-permute-start(bf16[96,1024]{1,0:T(8,128)(2,1)S(1)} %get-tuple-element.82.own_ref), channel_id=1, source_target_pairs={{0,1},{1,0},{2,3},{3,2},{4,5},{5,4},{6,7},{7,6},{8,9},{9,8},{10,11... | collective-permute-start | bytes 589832 | tf_op jit(solution)/shard_map/ppermute | solution.py:58
  161.5 11.1 %collective-permute-start.27 = (bf16[96,1024]{1,0:T(8,128)(2,1)S(1)}, bf16[96,1024]{1,0:T(8,128)(2,1)S(1)}, u32[]{:S(2)}, u32[]{:S(2)}) collective-permute-start(bf16[96,1024]{1,0:T(8,128)(2,1)S(1)} %slice.390), channel_id=1, source_target_pairs={{0,1},{1,0},{2,3},{3,2},{4,5},{5,4},{6,7},{7,6},{8,9},{9,8},{10,11... | collective-permute-start | bytes 589832 | tf_op jit(solution)/shard_map/ppermute | solution.py:58
  176.2 11.4 %all-to-all-start.1 = ((bf16[4,2,96,128]{3,2,1,0:T(8,128)(2,1)}), bf16[4,2,96,128]{3,2,1,0:T(8,128)(2,1)S(1)}, u32[]{:S(2)}, u32[]{:S(2)}) async-start(bf16[4,2,96,128]{3,2,1,0:T(8,128)(2,1)} %pad_maximum_fusion.14), calls=%async_computation.1 | async-start | bytes 393216 | tf_op jit(solution)/shard_map/all_to_all | solution.py:884
  179.6 131.0 %reduce-scatter.2.cloned.1.call-start = ((), (), s32[]{:S(2)}) async-start(), calls=%async_computation.5 | async-start | bytes 4718592 | tf_op jit(solution)/shard_map/reduce_scatter | solution.py:879
  182.2 26.1 %collective-permute-start.49 = (bf16[512,2048]{1,0:T(8,128)(2,1)}, bf16[512,2048]{1,0:T(8,128)(2,1)}, u32[]{:S(2)}, u32[]{:S(2)}) collective-permute-start(bf16[512,2048]{1,0:T(8,128)(2,1)} %get-tuple-element.123), channel_id=1, source_target_pairs={{0,2},{2,0},{4,6},{6,4},{8,10},{10,8},{12,14},{14,12},{16,18},{18,... | collective-permute-start | bytes 6291464 | tf_op jit(solution)/shard_map/ppermute | solution.py:46
  182.4 24.3 %collective-permute-start.28 = (bf16[192,1024]{1,0:T(8,128)(2,1)}, bf16[192,1024]{1,0:T(8,128)(2,1)S(1)}, u32[]{:S(2)}, u32[]{:S(2)}) collective-permute-start(bf16[192,1024]{1,0:T(8,128)(2,1)} %get-tuple-element.98), channel_id=1, source_target_pairs={{0,2},{2,0},{4,6},{6,4},{8,10},{10,8},{12,14},{14,12},{16,18},{18,... | collective-permute-start | bytes 1179656 | tf_op jit(solution)/shard_map/ppermute | solution.py:46
  203.3 19.9 %collective-permute-start.32 = (bf16[1536,256]{1,0:T(8,128)(2,1)}, bf16[1536,256]{1,0:T(8,128)(2,1)}, u32[]{:S(2)}, u32[]{:S(2)}) collective-permute-start(bf16[1536,256]{1,0:T(8,128)(2,1)} %get-tuple-element.107), channel_id=1, source_target_pairs={{0,4},{2,6},{4,0},{6,2},{8,12},{10,14},{12,8},{14,10},{16,20},{18,... | collective-permute-start | bytes 2359304 | tf_op jit(solution)/shard_map/ppermute | solution.py:46
  206.4 18.5 %collective-permute-start.43 = (bf16[8,64,1024]{2,1,0:T(8,128)(2,1)}, bf16[8,64,1024]{2,1,0:T(8,128)(2,1)}, u32[]{:S(2)}, u32[]{:S(2)}) collective-permute-start(bf16[8,64,1024]{2,1,0:T(8,128)(2,1)} %dynamic-slice_bitcast_fusion), channel_id=1, source_target_pairs={{0,2},{2,0},{4,6},{6,4},{8,10},{10,8},{12,14},{14,12},{16,18},{18,... | collective-permute-start | bytes 3145736 | tf_op jit(solution)/shard_map/ppermute | solution.py:46
  207.7 21.0 %collective-permute-start.29 = (bf16[96,1024]{1,0:T(8,128)(2,1)S(1)}, bf16[96,1024]{1,0:T(8,128)(2,1)S(1)}, u32[]{:S(2)}, u32[]{:S(2)}) collective-permute-start(bf16[96,1024]{1,0:T(8,128)(2,1)S(1)} %slice.389), channel_id=1, source_target_pairs={{0,1},{1,0},{2,3},{3,2},{4,5},{5,4},{6,7},{7,6},{8,9},{9,8},{10,11... | collective-permute-start | bytes 589832 | tf_op jit(solution)/shard_map/ppermute | solution.py:58
  224.8 12.1 %collective-permute-start.33 = (bf16[768,256]{1,0:T(8,128)(2,1)S(1)}, bf16[768,256]{1,0:T(8,128)(2,1)S(1)}, u32[]{:S(2)}, u32[]{:S(2)}) collective-permute-start(bf16[768,256]{1,0:T(8,128)(2,1)S(1)} %slice.388), channel_id=1, source_target_pairs={{0,1},{1,0},{2,3},{3,2},{4,5},{5,4},{6,7},{7,6},{8,9},{9,8},{10,11... | collective-permute-start | bytes 1179656 | tf_op jit(solution)/shard_map/ppermute | solution.py:58
  226.8 17.3 %collective-permute-start.44 = (bf16[8,64,512]{2,1,0:T(8,128)(2,1)S(1)}, bf16[8,64,512]{2,1,0:T(8,128)(2,1)S(1)}, u32[]{:S(2)}, u32[]{:S(2)}) collective-permute-start(bf16[8,64,512]{2,1,0:T(8,128)(2,1)S(1)} %select_convert_fusion.1), channel_id=1, source_target_pairs={{0,1},{1,0},{2,3},{3,2},{4,5},{5,4},{6,7},{7,6},{8,9},{9,8},{10,11... | collective-permute-start | bytes 1572872 | tf_op jit(solution)/shard_map/ppermute | solution.py:58
  228.8 17.3 %collective-permute-start.30 = (bf16[96,1024]{1,0:T(8,128)(2,1)S(1)}, bf16[96,1024]{1,0:T(8,128)(2,1)S(1)}, u32[]{:S(2)}, u32[]{:S(2)}) collective-permute-start(bf16[96,1024]{1,0:T(8,128)(2,1)S(1)} %fusion.13), channel_id=1, source_target_pairs={{0,1},{1,0},{2,3},{3,2},{4,5},{5,4},{6,7},{7,6},{8,9},{9,8},{10,11... | collective-permute-start | bytes 589832 | tf_op jit(solution)/shard_map/ppermute | solution.py:58
  239.7 12.1 %collective-permute-start.34 = (bf16[384,1024]{1,0:T(8,128)(2,1)S(1)}, bf16[384,1024]{1,0:T(8,128)(2,1)S(1)}, u32[]{:S(2)}, u32[]{:S(2)}) collective-permute-start(bf16[384,1024]{1,0:T(8,128)(2,1)S(1)} %get-tuple-element.110), channel_id=1, source_target_pairs={{0,2},{2,0},{4,6},{6,4},{8,10},{10,8},{12,14},{14,12},{16,18},{18,... | collective-permute-start | bytes 2359304 | tf_op jit(solution)/shard_map/ppermute | solution.py:46
  244.4 6.4 %collective-permute-start.45 = (bf16[4,64,512]{2,1,0:T(8,128)(2,1)S(1)}, bf16[4,64,512]{2,1,0:T(8,128)(2,1)S(1)}, u32[]{:S(2)}, u32[]{:S(2)}) collective-permute-start(bf16[4,64,512]{2,1,0:T(8,128)(2,1)S(1)} %dynamic-slice_bitcast_fusion.1), channel_id=1, source_target_pairs={{0,4},{2,6},{4,0},{6,2},{8,12},{10,14},{12,8},{14,10},{16,20},{18,... | collective-permute-start | bytes 786440 | tf_op jit(solution)/shard_map/ppermute | solution.py:46
  254.2 13.5 %collective-permute-start.37 = (bf16[96,1024]{1,0:T(8,128)(2,1)}, bf16[96,1024]{1,0:T(8,128)(2,1)}, u32[]{:S(2)}, u32[]{:S(2)}) collective-permute-start(bf16[96,1024]{1,0:T(8,128)(2,1)} %get-tuple-element.208), channel_id=1, source_target_pairs={{0,8},{2,10},{4,12},{6,14},{8,16},{10,18},{12,20},{14,22},{16,24},... | collective-permute-start | bytes 589832 | tf_op jit(solution)/shard_map/ppermute | solution.py:46
  256.7 13.0 %collective-permute-start.36 = (bf16[96,1024]{1,0:T(8,128)(2,1)}, bf16[96,1024]{1,0:T(8,128)(2,1)}, u32[]{:S(2)}, u32[]{:S(2)}) collective-permute-start(bf16[96,1024]{1,0:T(8,128)(2,1)} %get-tuple-element.209), channel_id=1, source_target_pairs={{0,16},{2,18},{4,20},{6,22},{8,24},{10,26},{12,28},{14,30},{16,0},... | collective-permute-start | bytes 589832 | tf_op jit(solution)/shard_map/ppermute | solution.py:46
  258.9 12.1 %collective-permute-start.35 = (bf16[96,1024]{1,0:T(8,128)(2,1)}, bf16[96,1024]{1,0:T(8,128)(2,1)}, u32[]{:S(2)}, u32[]{:S(2)}) collective-permute-start(bf16[96,1024]{1,0:T(8,128)(2,1)} %get-tuple-element.207), channel_id=1, source_target_pairs={{0,24},{2,26},{4,28},{6,30},{8,0},{10,2},{12,4},{14,6},{16,8},{18,... | collective-permute-start | bytes 589832 | tf_op jit(solution)/shard_map/ppermute | solution.py:46
  266.7 9.2 %collective-permute-start.40 = (bf16[4,2,64,512]{3,2,0,1:T(8,128)(2,1)S(1)}, bf16[4,2,64,512]{3,2,0,1:T(8,128)(2,1)S(1)}, u32[]{:S(2)}, u32[]{:S(2)}) collective-permute-start(bf16[4,2,64,512]{3,2,0,1:T(8,128)(2,1)S(1)} %bitcast_select_fusion.1), channel_id=1, source_target_pairs={{1,0},{0,2},{2,3},{3,1},{5,4},{4,6},{6,7},{7,5},{9,8},{8,10},{10,1... | collective-permute-start | bytes 1572872 | tf_op jit(solution)/shard_map/ppermute | solution.py:73
  266.9 9.0 %collective-permute-start.41 = (bf16[4,2,64,512]{3,2,0,1:T(8,128)(2,1)S(1)}, bf16[4,2,64,512]{3,2,0,1:T(8,128)(2,1)S(1)}, u32[]{:S(2)}, u32[]{:S(2)}) collective-permute-start(bf16[4,2,64,512]{3,2,0,1:T(8,128)(2,1)S(1)} %bitcast.167), channel_id=1, source_target_pairs={{2,1},{1,2},{6,5},{5,6},{10,9},{9,10},{14,13},{13,14},{18,17},{17,... | collective-permute-start | bytes 1572872 | tf_op jit(solution)/shard_map/ppermute | solution.py:77
  267.7 25.1 %collective-permute-start.48 = (bf16[64,512]{1,0:T(8,128)(2,1)S(1)}, bf16[64,512]{1,0:T(8,128)(2,1)S(1)}, u32[]{:S(2)}, u32[]{:S(2)}) collective-permute-start(bf16[64,512]{1,0:T(8,128)(2,1)S(1)} %get-tuple-element.227), channel_id=1, source_target_pairs={{0,24},{2,26},{4,28},{6,30},{8,0},{10,2},{12,4},{14,6},{16,8},{18,... | collective-permute-start | bytes 196616 | tf_op jit(solution)/shard_map/ppermute | solution.py:46
  269.7 23.1 %collective-permute-start.47 = (bf16[64,512]{1,0:T(8,128)(2,1)S(1)}, bf16[64,512]{1,0:T(8,128)(2,1)S(1)}, u32[]{:S(2)}, u32[]{:S(2)}) collective-permute-start(bf16[64,512]{1,0:T(8,128)(2,1)S(1)} %get-tuple-element.228), channel_id=1, source_target_pairs={{0,16},{2,18},{4,20},{6,22},{8,24},{10,26},{12,28},{14,30},{16,0},... | collective-permute-start | bytes 196616 | tf_op jit(solution)/shard_map/ppermute | solution.py:46
  271.0 21.8 %collective-permute-start.46 = (bf16[64,512]{1,0:T(8,128)(2,1)S(1)}, bf16[64,512]{1,0:T(8,128)(2,1)S(1)}, u32[]{:S(2)}, u32[]{:S(2)}) collective-permute-start(bf16[64,512]{1,0:T(8,128)(2,1)S(1)} %get-tuple-element.226), channel_id=1, source_target_pairs={{0,8},{2,10},{4,12},{6,14},{8,16},{10,18},{12,20},{14,22},{16,24},... | collective-permute-start | bytes 196616 | tf_op jit(solution)/shard_map/ppermute | solution.py:46
  276.2 12.4 %collective-permute-start.42 = (bf16[4,64,512]{2,1,0:T(8,128)(2,1)S(1)}, bf16[4,64,512]{2,1,0:T(8,128)(2,1)S(1)}, u32[]{:S(2)}, u32[]{:S(2)}) collective-permute-start(bf16[4,64,512]{2,1,0:T(8,128)(2,1)S(1)} %fusion.14), channel_id=1, source_target_pairs={{0,4},{2,6},{4,0},{6,2},{8,12},{10,14},{12,8},{14,10},{16,20},{18,... | collective-permute-start | bytes 786440 | tf_op jit(solution)/shard_map/ppermute | solution.py:46
  278.6 15.8 %collective-permute-start.38 = (bf16[96,1024]{1,0:T(8,128)(2,1)S(1)}, bf16[96,1024]{1,0:T(8,128)(2,1)S(1)}, u32[]{:S(2)}, u32[]{:S(2)}) collective-permute-start(bf16[96,1024]{1,0:T(8,128)(2,1)S(1)} %fusion.7), channel_id=1, source_target_pairs={{0,1},{1,0},{2,3},{3,2},{4,5},{5,4},{6,7},{7,6},{8,9},{9,8},{10,11... | collective-permute-start | bytes 589832 | tf_op jit(solution)/shard_map/ppermute | solution.py:58
  289.4 16.0 %all-to-all-start.2 = ((bf16[4,64,512]{2,1,0:T(8,128)(2,1)}), bf16[4,64,512]{2,1,0:T(8,128)(2,1)S(1)}, u32[]{:S(2)}, u32[]{:S(2)}) async-start(bf16[4,64,512]{2,1,0:T(8,128)(2,1)} %fusion.2), calls=%async_computation.2 | async-start | bytes 524288 | tf_op jit(solution)/shard_map/all_to_all | solution.py:923
  (56 other events, 621.8 us)
Sparse Core Ops, SparseCore 0:
  44.3 91.6 all-gather.1
  212.5 91.2 reduce-scatter.1

commit v6 on v5

--- a/solution.py
+++ b/solution.py
@@ -537,14 +537,13 @@
 
 
 def feed_kernel(bias_ref, own_ref, near_ref, far_ref, gz_ref, weight, *refs):
-    normed_ref, act_ref, gh_ref, sum_ref, keep_n_ref, send_n_ref, keep_o_ref, send_o_ref = refs[:8]
-    back, out = refs[8:]
+    normed_ref, act_ref, gh_ref, sum_ref, keep_n_ref, send_n_ref, keep_o_ref, send_o_ref = refs
     rows = own_ref.shape[0]
     hidden_size = act_ref.shape[1]
     normed_ref[:rows, :] = own_ref[...]
     normed_ref[rows : 2 * rows, :] = near_ref[...]
     normed_ref[2 * rows :, :] = far_ref[...]
-    step = 256
+    step = 1024
     for n in range(hidden_size // step):
         up = slice(n * step, (n + 1) * step)
         down = slice(hidden_size + n * step, hidden_size + (n + 1) * step)
@@ -558,16 +557,12 @@
         sum_ref[:, up] = jnp.sum(low.astype(F32), axis=0, keepdims=True)
         add_back = dot(low, weight[:, up], NT)
         add_out = dot(act, weight[:, down], NT)
-        if n == 0:
-            back[...] = add_back
-            out[...] = add_out
-        else:
-            back[...] += add_back
-            out[...] += add_out
-    keep_n_ref[...] = back[: 2 * rows, :]
-    send_n_ref[...] = back[2 * rows :, :].astype(BF16)
-    keep_o_ref[...] = out[: 2 * rows, :]
-    send_o_ref[...] = out[2 * rows :, :].astype(BF16)
+        back = add_back if n == 0 else back + add_back
+        out = add_out if n == 0 else out + add_out
+    keep_n_ref[...] = back[: 2 * rows]
+    send_n_ref[...] = back[2 * rows :].astype(BF16)
+    keep_o_ref[...] = out[: 2 * rows]
+    send_o_ref[...] = out[2 * rows :].astype(BF16)
 
 
 def feed(bias, own, near, far, gz, weight):
@@ -589,7 +584,6 @@
         ),
         (bias, own, near, far, gz, weight),
         scalars=0,
-        scratch=[pltpu.VMEM((count, width), F32), pltpu.VMEM((count, width), F32)],
         megabytes=56,
     )
 
@@ -597,7 +591,7 @@
 def outer_kernel(part, at_ref, normed_ref, gh_ref, gz_ref, act_ref, keep_ref, send_ref, made):
     hidden_size = gh_ref.shape[1]
     chips = keep_ref.shape[0] // part
-    step = 256
+    step = 512
     for base, left_ref, right_ref in ((0, normed_ref, gh_ref), (hidden_size, gz_ref, act_ref)):
         for n in range(hidden_size // step):
             made[...] = dot(left_ref[...], right_ref[:, n * step : (n + 1) * step], TN)
@@ -621,7 +615,7 @@
         "outer",
         (out, out),
         (at, normed, gh, gz, act),
-        scratch=[pltpu.VMEM((width, 256), F32)],
+        scratch=[pltpu.VMEM((width, 512), F32)],
     )
 
 

time: 324 us -> 320 us (0.988)
  Pallas kernels: 56.5 us -> 52.5 us
    pallas_call x10, Pallas kernels: 54.8 us -> 50.8 us  [local_kernel(): pl.pallas_call(kernel, out_shape=out_shape, in_specs=[SMEM] * scalars + i...]
  transfers between devices with their start and end apart: 54 -> 54, of which waited for: 22 -> 22; matrix products, arithmetic and copies ran while one was open for 13% -> 13% of each run, Pallas kernels for 15% -> 14%
where the time goes in v6:
time: 320 us; the launch traced here: 316 us
  waiting for transfers between devices  102 us (32%)
  starting transfers between devices  70.1 us (22%)
  Pallas kernels  52.5 us (16%)
  other arithmetic  36 us (11%)
  local copies, waits for them, and re-layouts  25 us (8%)
  between operations  15.4 us (5%)
  blocking collectives  13.9 us (4%)
    ppermute x36, waiting for transfers between devices, _move(): return lax.ppermute(block, SP, pairs)  57.2 us
    pallas_call x10, Pallas kernels, local_kernel(): pl.pallas_call(kernel, out_shape=out_shape, in_specs=[SMEM] * scalars + i...  50.8 us
    ppermute x36, starting transfers between devices, _move(): return lax.ppermute(block, SP, pairs)  42.4 us
    ppermute x10, waiting for transfers between devices, yswap(): return lax.ppermute(block, 'tp', [(0, 1), (1, 0)])  24.7 us
    ppermute x10, starting transfers between devices, yswap(): return lax.ppermute(block, 'tp', [(0, 1), (1, 0)])  17.4 us
    all_to_all x1, blocking collectives, per_device(): attn_got = lax.all_to_all(attn_send, 'z', 0, 0, tiled=True)  13.9 us
    unnamed x105, local copies, waits for them, and re-layouts  13.4 us
    all_to_all x1, waiting for transfers between devices, per_device(): dw = lax.all_to_all(dw.astype(BF16), 'z', 0, 0, tiled=True)  10 us
  transfers between devices with their start and end apart: 54, of which 22 were waited for; matrix products, arithmetic and copies ran while one was open for 13% of the time, Pallas kernels for 14%

profile of v6, /device:TPU:0, one launch (start us, length us, event | category | flops | bytes accessed | tf_op | source)
XLA Modules:
  0.0 316.2 jit_solution(1730573103541332992)
XLA Ops:
  12.8 3.1 collective-permute-start
  15.9 2.6 collective-permute-start.1
  22.3 5.2 %collective-permute-done.7 = bf16[64,384]{1,0:T(8,128)(2,1)S(1)} collective-permute-done((bf16[64,384]{1,0:T(8,128)(2,1)S(1)}, bf16[64,384]{1,0:T(8,128)(2,1)S(1)}, u32[]{:S(2)}, u32[]{:S(2)}) %collective-permute-start.7) | collective-permute-done | bytes 49184 | tf_op jit(solution)/shard_map/ppermute | solution.py:46
  27.5 4.3 %collective-permute-start.2 = (bf16[96,1152]{1,0:T(8,128)(2,1)S(1)}, bf16[96,1152]{1,0:T(8,128)(2,1)S(1)}, u32[]{:S(2)}, u32[]{:S(2)}) collective-permute-start(bf16[96,1152]{1,0:T(8,128)(2,1)S(1)} %concatenate.70.refs_0_), channel_id=1, source_target_pairs={{0,24},{2,26},{4,28},{6,30},{8,0},{10,2},{12,4},{14,6},{16,8},{18,... | collective-permute-start | bytes 663560 | tf_op jit(solution)/shard_map/ppermute | solution.py:46
  31.8 5.3 %collective-permute-done.6 = bf16[64,384]{1,0:T(8,128)(2,1)S(1)} collective-permute-done((bf16[64,384]{1,0:T(8,128)(2,1)S(1)}, bf16[64,384]{1,0:T(8,128)(2,1)S(1)}, u32[]{:S(2)}, u32[]{:S(2)}) %collective-permute-start.6) | collective-permute-done | bytes 49184 | tf_op jit(solution)/shard_map/ppermute | solution.py:46
  37.1 1.6 collective-permute-start.8
  38.8 3.3 %collective-permute-done.2.refs_3_ = bf16[96,1152]{1,0:T(8,128)(2,1)S(1)} collective-permute-done((bf16[96,1152]{1,0:T(8,128)(2,1)S(1)}, bf16[96,1152]{1,0:T(8,128)(2,1)S(1)}, u32[]{:S(2)}, u32[]{:S(2)}) %collective-permute-start.2) | collective-permute-done | bytes 221216 | tf_op jit(solution)/shard_map/ppermute | solution.py:46
  48.9 4.6 %collective-permute-done.9 = bf16[2,4,64,384]{3,2,1,0:T(8,128)(2,1)S(1)} collective-permute-done((bf16[2,4,64,384]{3,2,1,0:T(8,128)(2,1)S(1)}, bf16[2,4,64,384]{3,2,1,0:T(8,128)(2,1)S(1)}, u32[]{:S(2)}, u32[]{:S(2)}) %collective-permute-start.9) | collective-permute-done | bytes 393248 | tf_op jit(solution)/shard_map/ppermute | solution.py:73
  53.6 4.9 %collective-permute-start.19 = (bf16[64,512]{1,0:T(8,128)(2,1)}, bf16[64,512]{1,0:T(8,128)(2,1)}, u32[]{:S(2)}, u32[]{:S(2)}) collective-permute-start(bf16[64,512]{1,0:T(8,128)(2,1)} %bitcast.39), channel_id=1, source_target_pairs={{0,24},{2,26},{4,28},{6,30},{8,0},{10,2},{12,4},{14,6},{16,8},{18,... | collective-permute-start | bytes 196616 | tf_op jit(solution)/shard_map/ppermute | solution.py:46
  58.5 1.9 collective-permute-start.17
  60.9 4.2 %enter.1 = (bf16[768,1024]{1,0:T(8,128)(2,1)}, bf16[768,1024]{1,0:T(8,128)(2,1)}, f32[768,1]{1,0:T(8,128)S(1)}, f32[768,1]{1,0:T(8,128)S(1)}, f32[96,1024]{1,0:T...) custom-call(s32[4]{0:T(128)S(1)} %pad_add_fusion.at_ref.refs_0_, ...), custom_call_target="tpu_custom_call" | custom-call | flops 5000000000 | bytes 65536 | tf_op jit(solution)/shard_map/enter/pallas_call | solution.py:173
  69.1 3.8 %collective-permute-start.13 = (bf16[768,256]{1,0:T(8,128)(2,1)S(1)}, bf16[768,256]{1,0:T(8,128)(2,1)S(1)}, u32[]{:S(2)}, u32[]{:S(2)}) collective-permute-start(bf16[768,256]{1,0:T(8,128)(2,1)S(1)} %get-tuple-element.71.refs_0_), channel_id=1, source_target_pairs={{0,1},{1,0},{2,3},{3,2},{4,5},{5,4},{6,7},{7,6},{8,9},{9,8},{10,11... | collective-permute-start | bytes 1179656 | tf_op jit(solution)/shard_map/ppermute | solution.py:58
  80.9 8.7 %collective-permute-done.20 = bf16[4,64,512]{2,1,0:T(8,128)(2,1)S(1)} collective-permute-done((bf16[4,64,512]{2,1,0:T(8,128)(2,1)S(1)}, bf16[4,64,512]{2,1,0:T(8,128)(2,1)S(1)}, u32[]{:S(2)}, u32[]{:S(2)}) %collective-permute-start.20) | collective-permute-done | bytes 262176 | tf_op jit(solution)/shard_map/ppermute | solution.py:46
  91.4 2.3 collective-permute-start.21
  95.5 2.1 pad_maximum_fusion.3.gz_ref
  97.5 6.6 %collective-permute-done.21 = bf16[2,4,64,512]{3,2,1,0:T(8,128)(2,1)S(1)} collective-permute-done((bf16[2,4,64,512]{3,2,1,0:T(8,128)(2,1)S(1)}, bf16[2,4,64,512]{3,2,1,0:T(8,128)(2,1)S(1)}, u32[]{:S(2)}, u32[]{:S(2)}) %collective-permute-start.21) | collective-permute-done | bytes 524320 | tf_op jit(solution)/shard_map/ppermute | solution.py:58
  104.3 9.4 %collective-permute-done.15.refs_3_ = bf16[768,256]{1,0:T(8,128)(2,1)S(1)} collective-permute-done((bf16[768,256]{1,0:T(8,128)(2,1)S(1)}, bf16[768,256]{1,0:T(8,128)(2,1)S(1)}, u32[]{:S(2)}, u32[]{:S(2)}) %collective-permute-start.15) | collective-permute-done | bytes 393248 | tf_op jit(solution)/shard_map/ppermute | solution.py:46
  113.8 7.4 %attend.1 = (f32[768,128]{1,0:T(8,128)S(1)}, f32[8,768]{1,0:T(8,128)S(1)}, bf16[768,128]{1,0:T(8,128)(2,1)S(1)}, bf16[4,2,96,128]{3,2,1,0:T(8,128)(2,1)S(1)}) custom-call(s32[4]{0:T(128)S(1)} %pad_add_fusion.at_ref.refs_0_, f32[768,128]{1,0:T(8,128)S(1)} %copy-done.32, f32[2,128]{1,0:T(2,128)S(1)} %fusion.25.bias_ref, ...), custom_call_target="tpu_custom_call" | custom-call | flops 14000000000 | bytes 65536 | tf_op jit(solution)/shard_map/attend/pallas_call | solution.py:173
  121.9 13.9 %all_to_all.15.got_ref = bf16[4,2,96,128]{3,2,1,0:T(8,128)(2,1)S(1)} all-to-all(bf16[4,2,96,128]{3,2,1,0:T(8,128)(2,1)S(1)} %get-tuple-element.74), channel_id=1, replica_groups=mesh['z'=4,'x'=2,'core'=2,'tp'=2] {'z'}, dimensions={0} | all-to-all | bytes 393216 | tf_op jit(solution)/shard_map/all_to_all | solution.py:862
  142.3 5.4 %collective-permute-done.23.near_ref = bf16[96,1024]{1,0:T(8,128)(2,1)S(1)} collective-permute-done((bf16[96,1024]{1,0:T(8,128)(2,1)S(1)}, bf16[96,1024]{1,0:T(8,128)(2,1)S(1)}, u32[]{:S(2)}, u32[]{:S(2)}) %collective-permute-start.23) | collective-permute-done | bytes 196640 | tf_op jit(solution)/shard_map/ppermute | solution.py:58
  147.9 1.8 collective-permute-done.24.far_ref
  149.8 7.3 %feed.1 = (bf16[384,1024]{1,0:T(8,128)(2,1)}, bf16[384,1024]{1,0:T(8,128)(2,1)}, bf16[384,1024]{1,0:T(8,128)(2,1)}, f32[1,1024]{1,0:T(1,128)}, f32[192,1024]{1,0...) custom-call(f32[1,1024]{1,0:T(1,128)} %broadcast_select_fusion.18.bias_ref, ...), custom_call_target="tpu_custom_call" | custom-call | bytes 65536 | tf_op jit(solution)/shard_map/feed/pallas_call | solution.py:173
  157.2 1.8 collective-permute-done.26
  160.2 1.6 collective-permute-start.27
  161.8 5.3 %outer.1 = (bf16[512,2048]{1,0:T(8,128)(2,1)S(1)}, bf16[512,2048]{1,0:T(8,128)(2,1)}) custom-call(s32[4]{0:T(128)S(1)} %pad_add_fusion.at_ref.refs_0_, bf16[384,1024]{1,0:T(8,128)(2,1)S(1)} %copy-done.12, bf16[384,1024]{1,0:T(8,128)(2,1)S(1)} %copy-done.14, bf16[384,1024]{1,0:T(8,128)(2,1)S(1)} %copy-done, bf16[384,1024]{1,0:T(8,128)(2,1)S(1)} %copy-done.13), custom_call_target="tpu_custom_call" | custom-call | flops 5000000000 | bytes 65536 | tf_op jit(solution)/shard_map/outer/pallas_call | solution.py:173
  172.0 3.4 %all-to-all-start.1 = ((bf16[4,2,96,128]{3,2,1,0:T(8,128)(2,1)}), bf16[4,2,96,128]{3,2,1,0:T(8,128)(2,1)S(1)}, u32[]{:S(2)}, u32[]{:S(2)}) async-start(bf16[4,2,96,128]{3,2,1,0:T(8,128)(2,1)} %pad_maximum_fusion.14), calls=%async_computation.1 | async-start | bytes 393216 | tf_op jit(solution)/shard_map/all_to_all | solution.py:878
  178.9 4.6 %all-to-all-done.1.got_ref = bf16[4,2,96,128]{3,2,1,0:T(8,128)(2,1)S(1)} async-done(((bf16[4,2,96,128]{3,2,1,0:T(8,128)(2,1)}), bf16[4,2,96,128]{3,2,1,0:T(8,128)(2,1)S(1)}, u32[]{:S(2)}, u32[]{:S(2)}) %all-to-all-start.1) | async-done | bytes 196640 | tf_op jit(solution)/shard_map/all_to_all | solution.py:878
  184.1 15.0 %attend_back.1 = (bf16[768,128]{1,0:T(8,128)(2,1)}, bf16[1536,256]{1,0:T(8,128)(2,1)}, bf16[1536,256]{1,0:T(8,128)(2,1)}) custom-call(s32[4]{0:T(128)} %copy-done.11, bf16[768,128]{1,0:T(8,128)(2,1)} %copy-done.34, bf16[768,128]{1,0:T(8,128)(2,1)} %copy-done.7, bf16[3072,128]{1,0:T(8,128)(2,1)} %copy-done.4, bf16[4,2,96,128]{3,2,1,0:T(8,128)(2,1)} %copy-done.48, ...), custom_call_target="tpu_custom_call" | custom-call | flops 16999999488 | bytes 65536 | tf_op jit(solution)/shard_map/attend_back/pallas_call | solution.py:173
  204.0 4.1 %pad_maximum_fusion = bf16[512,4096]{1,0:T(8,128)(2,1)} fusion(bf16[512,2048]{1,0:T(8,128)(2,1)} %collective-permute-done.49, bf16[512,2048]{1,0:T(8,128)(2,1)S(1)} %copy-done.2), kind=kLoop, calls=%fused_computation | loop fusion | flops 8388608 | bytes 8388608 | tf_op jit(solution)/shard_map/concatenate | solution.py:872
  208.2 10.8 %collective-permute-done.32 = bf16[1536,256]{1,0:T(8,128)(2,1)} collective-permute-done((bf16[1536,256]{1,0:T(8,128)(2,1)}, bf16[1536,256]{1,0:T(8,128)(2,1)}, u32[]{:S(2)}, u32[]{:S(2)}) %collective-permute-start.32) | collective-permute-done | bytes 786464 | tf_op jit(solution)/shard_map/ppermute | solution.py:46
  220.7 1.7 convert_add_fusion
  222.5 2.0 collective-permute-start.44
  224.8 7.9 %collective-permute-done.33.near_ref = bf16[768,256]{1,0:T(8,128)(2,1)S(1)} collective-permute-done((bf16[768,256]{1,0:T(8,128)(2,1)S(1)}, bf16[768,256]{1,0:T(8,128)(2,1)S(1)}, u32[]{:S(2)}, u32[]{:S(2)}) %collective-permute-start.33) | collective-permute-done | bytes 393248 | tf_op jit(solution)/shard_map/ppermute | solution.py:58
  232.7 2.7 leave.1
  235.4 4.5 %collective-permute-done.44 = bf16[8,64,512]{2,1,0:T(8,128)(2,1)S(1)} collective-permute-done((bf16[8,64,512]{2,1,0:T(8,128)(2,1)S(1)}, bf16[8,64,512]{2,1,0:T(8,128)(2,1)S(1)}, u32[]{:S(2)}, u32[]{:S(2)}) %collective-permute-start.44) | collective-permute-done | bytes 524320 | tf_op jit(solution)/shard_map/ppermute | solution.py:58
  242.8 3.9 %collective-permute-done.45 = bf16[4,64,512]{2,1,0:T(8,128)(2,1)S(1)} collective-permute-done((bf16[4,64,512]{2,1,0:T(8,128)(2,1)S(1)}, bf16[4,64,512]{2,1,0:T(8,128)(2,1)S(1)}, u32[]{:S(2)}, u32[]{:S(2)}) %collective-permute-start.45) | collective-permute-done | bytes 262176 | tf_op jit(solution)/shard_map/ppermute | solution.py:46
  250.0 2.6 collective-permute-start.37
  252.6 2.1 collective-permute-start.36
  255.0 5.1 %close.1 = (f32[4,1024]{1,0:T(4,128)S(1)}, f32[1,384]{1,0:T(1,128)S(1)}, bf16[1024,384]{1,0:T(8,128)(2,1)S(1)}) custom-call(f32[768,1024]{1,0:T(8,128)} %get-tuple-element.109.refs_0_, bf16[768,1024]{1,0:T(8,128)(2,1)S(1)} %copy-done.8, f32[768,1]{1,0:T(8,128)S(1)} %copy-done.10, f32[768,1]{1,0:T(8,128)S(1)} %copy-done.29, ...), custom_call_target="tpu_custom_call" | custom-call | flops 5000000000 | bytes 65536 | tf_op jit(solution)/shard_map/close/pallas_call | solution.py:173
  263.5 2.0 collective-permute-start.48
  266.8 2.4 collective-permute-start.46
  272.1 2.1 collective-permute-start.42
  274.4 5.2 %collective-permute-start.38 = (bf16[96,1024]{1,0:T(8,128)(2,1)S(1)}, bf16[96,1024]{1,0:T(8,128)(2,1)S(1)}, u32[]{:S(2)}, u32[]{:S(2)}) collective-permute-start(bf16[96,1024]{1,0:T(8,128)(2,1)S(1)} %fusion.7), channel_id=1, source_target_pairs={{0,1},{1,0},{2,3},{3,2},{4,5},{5,4},{6,7},{7,6},{8,9},{9,8},{10,11... | collective-permute-start | bytes 589832 | tf_op jit(solution)/shard_map/ppermute | solution.py:58
  279.6 4.8 %collective-permute-done.42 = bf16[4,64,512]{2,1,0:T(8,128)(2,1)S(1)} collective-permute-done((bf16[4,64,512]{2,1,0:T(8,128)(2,1)S(1)}, bf16[4,64,512]{2,1,0:T(8,128)(2,1)S(1)}, u32[]{:S(2)}, u32[]{:S(2)}) %collective-permute-start.42) | collective-permute-done | bytes 262176 | tf_op jit(solution)/shard_map/ppermute | solution.py:46
  285.2 3.4 %all-to-all-start.2 = ((bf16[4,64,512]{2,1,0:T(8,128)(2,1)}), bf16[4,64,512]{2,1,0:T(8,128)(2,1)S(1)}, u32[]{:S(2)}, u32[]{:S(2)}) async-start(bf16[4,64,512]{2,1,0:T(8,128)(2,1)} %fusion.2), calls=%async_computation.2 | async-start | bytes 524288 | tf_op jit(solution)/shard_map/all_to_all | solution.py:917
  288.6 1.6 fusion.17
  291.2 10.0 %all-to-all-done.2 = bf16[4,64,512]{2,1,0:T(8,128)(2,1)S(1)} async-done(((bf16[4,64,512]{2,1,0:T(8,128)(2,1)}), bf16[4,64,512]{2,1,0:T(8,128)(2,1)S(1)}, u32[]{:S(2)}, u32[]{:S(2)}) %all-to-all-start.2) | async-done | bytes 262176 | tf_op jit(solution)/shard_map/all_to_all | solution.py:917
  303.8 1.7 place_qkv.1
  (315 shorter events, 78.7 us)
Async XLA Ops:
  7.2 142.5 %all-gather.2.cloned.1.call-start = ((), (), s32[]{:S(2)}) async-start(), calls=%async_computation.4 | async-start | bytes 4718592 | tf_op jit(solution)/shard_map/all_gather | solution.py:846
  12.8 26.0 %collective-permute-start = (bf16[96,1152]{1,0:T(8,128)(2,1)S(1)}, bf16[96,1152]{1,0:T(8,128)(2,1)S(1)}, u32[]{:S(2)}, u32[]{:S(2)}) collective-permute-start(bf16[96,1152]{1,0:T(8,128)(2,1)S(1)} %concatenate.70.refs_0_), channel_id=1, source_target_pairs={{0,8},{2,10},{4,12},{6,14},{8,16},{10,18},{12,20},{14,22},{16,24},... | collective-permute-start | bytes 663560 | tf_op jit(solution)/shard_map/ppermute | solution.py:46
  15.9 22.9 %collective-permute-start.1 = (bf16[96,1152]{1,0:T(8,128)(2,1)S(1)}, bf16[96,1152]{1,0:T(8,128)(2,1)S(1)}, u32[]{:S(2)}, u32[]{:S(2)}) collective-permute-start(bf16[96,1152]{1,0:T(8,128)(2,1)S(1)} %concatenate.70.refs_0_), channel_id=1, source_target_pairs={{0,16},{2,18},{4,20},{6,22},{8,24},{10,26},{12,28},{14,30},{16,0},... | collective-permute-start | bytes 663560 | tf_op jit(solution)/shard_map/ppermute | solution.py:46
  19.9 7.6 %collective-permute-start.7 = (bf16[64,384]{1,0:T(8,128)(2,1)S(1)}, bf16[64,384]{1,0:T(8,128)(2,1)S(1)}, u32[]{:S(2)}, u32[]{:S(2)}) collective-permute-start(bf16[64,384]{1,0:T(8,128)(2,1)S(1)} %get-tuple-element.240), channel_id=1, source_target_pairs={{0,24},{2,26},{4,28},{6,30},{8,0},{10,2},{12,4},{14,6},{16,8},{18,... | collective-permute-start | bytes 147464 | tf_op jit(solution)/shard_map/ppermute | solution.py:46
  21.3 15.8 %collective-permute-start.6 = (bf16[64,384]{1,0:T(8,128)(2,1)S(1)}, bf16[64,384]{1,0:T(8,128)(2,1)S(1)}, u32[]{:S(2)}, u32[]{:S(2)}) collective-permute-start(bf16[64,384]{1,0:T(8,128)(2,1)S(1)} %get-tuple-element.241), channel_id=1, source_target_pairs={{0,16},{2,18},{4,20},{6,22},{8,24},{10,26},{12,28},{14,30},{16,0},... | collective-permute-start | bytes 147464 | tf_op jit(solution)/shard_map/ppermute | solution.py:46
  21.5 15.6 %collective-permute-start.5 = (bf16[64,384]{1,0:T(8,128)(2,1)S(1)}, bf16[64,384]{1,0:T(8,128)(2,1)S(1)}, u32[]{:S(2)}, u32[]{:S(2)}) collective-permute-start(bf16[64,384]{1,0:T(8,128)(2,1)S(1)} %get-tuple-element.242), channel_id=1, source_target_pairs={{0,8},{2,10},{4,12},{6,14},{8,16},{10,18},{12,20},{14,22},{16,24},... | collective-permute-start | bytes 147464 | tf_op jit(solution)/shard_map/ppermute | solution.py:46
  27.5 14.7 %collective-permute-start.2 = (bf16[96,1152]{1,0:T(8,128)(2,1)S(1)}, bf16[96,1152]{1,0:T(8,128)(2,1)S(1)}, u32[]{:S(2)}, u32[]{:S(2)}) collective-permute-start(bf16[96,1152]{1,0:T(8,128)(2,1)S(1)} %concatenate.70.refs_0_), channel_id=1, source_target_pairs={{0,24},{2,26},{4,28},{6,30},{8,0},{10,2},{12,4},{14,6},{16,8},{18,... | collective-permute-start | bytes 663560 | tf_op jit(solution)/shard_map/ppermute | solution.py:46
  37.1 7.2 %collective-permute-start.8 = (bf16[4,64,384]{2,1,0:T(8,128)(2,1)S(1)}, bf16[4,64,384]{2,1,0:T(8,128)(2,1)S(1)}, u32[]{:S(2)}, u32[]{:S(2)}) collective-permute-start(bf16[4,64,384]{2,1,0:T(8,128)(2,1)S(1)} %get-tuple-element.238), channel_id=1, source_target_pairs={{0,4},{2,6},{4,0},{6,2},{8,12},{10,14},{12,8},{14,10},{16,20},{18,... | collective-permute-start | bytes 589832 | tf_op jit(solution)/shard_map/ppermute | solution.py:46
  38.7 4.5 %collective-permute-start.25 = (bf16[64,2048]{1,0:T(8,128)(2,1)S(1)}, bf16[64,2048]{1,0:T(8,128)(2,1)S(1)}, u32[]{:S(2)}, u32[]{:S(2)}) collective-permute-start(bf16[64,2048]{1,0:T(8,128)(2,1)S(1)} %pad_maximum_fusion.12), channel_id=1, source_target_pairs={{0,2},{2,0},{4,6},{6,4},{8,10},{10,8},{12,14},{14,12},{16,18},{18,... | collective-permute-start | bytes 786440 | tf_op jit(solution)/shard_map/ppermute | solution.py:46
  44.4 9.2 %collective-permute-start.9 = (bf16[2,4,64,384]{3,2,1,0:T(8,128)(2,1)S(1)}, bf16[2,4,64,384]{3,2,1,0:T(8,128)(2,1)S(1)}, u32[]{:S(2)}, u32[]{:S(2)}) collective-permute-start(bf16[2,4,64,384]{3,2,1,0:T(8,128)(2,1)S(1)} %pad_maximum_fusion.6), channel_id=1, source_target_pairs={{0,1},{2,0},{3,2},{1,3},{4,5},{6,4},{7,6},{5,7},{8,9},{10,8},{11,1... | collective-permute-start | bytes 1179656 | tf_op jit(solution)/shard_map/ppermute | solution.py:73
  45.9 7.6 %collective-permute-start.10 = (bf16[2,4,64,384]{3,2,1,0:T(8,128)(2,1)S(1)}, bf16[2,4,64,384]{3,2,1,0:T(8,128)(2,1)S(1)}, u32[]{:S(2)}, u32[]{:S(2)}) collective-permute-start(bf16[2,4,64,384]{3,2,1,0:T(8,128)(2,1)S(1)} %pad_maximum_fusion.6), channel_id=1, source_target_pairs={{2,1},{1,2},{6,5},{5,6},{10,9},{9,10},{14,13},{13,14},{18,17},{17,... | collective-permute-start | bytes 1179656 | tf_op jit(solution)/shard_map/ppermute | solution.py:77
  47.3 13.1 %collective-permute-start.4 = (bf16[2,4,16,128]{3,2,1,0:T(8,128)(2,1)S(1)}, bf16[2,4,16,128]{3,2,1,0:T(8,128)(2,1)S(1)}, u32[]{:S(2)}, u32[]{:S(2)}) collective-permute-start(bf16[2,4,16,128]{3,2,1,0:T(8,128)(2,1)S(1)} %get-tuple-element.248), channel_id=1, source_target_pairs={{0,4},{2,6},{4,0},{6,2},{8,12},{10,14},{12,8},{14,10},{16,20},{18,... | collective-permute-start | bytes 98312 | tf_op jit(solution)/shard_map/ppermute | solution.py:46
  53.6 23.4 %collective-permute-start.19 = (bf16[64,512]{1,0:T(8,128)(2,1)}, bf16[64,512]{1,0:T(8,128)(2,1)}, u32[]{:S(2)}, u32[]{:S(2)}) collective-permute-start(bf16[64,512]{1,0:T(8,128)(2,1)} %bitcast.39), channel_id=1, source_target_pairs={{0,24},{2,26},{4,28},{6,30},{8,0},{10,2},{12,4},{14,6},{16,8},{18,... | collective-permute-start | bytes 196616 | tf_op jit(solution)/shard_map/ppermute | solution.py:46
  58.5 18.5 %collective-permute-start.18 = (bf16[64,512]{1,0:T(8,128)(2,1)}, bf16[64,512]{1,0:T(8,128)(2,1)}, u32[]{:S(2)}, u32[]{:S(2)}) collective-permute-start(bf16[64,512]{1,0:T(8,128)(2,1)} %bitcast.39), channel_id=1, source_target_pairs={{0,16},{2,18},{4,20},{6,22},{8,24},{10,26},{12,28},{14,30},{16,0},... | collective-permute-start | bytes 196616 | tf_op jit(solution)/shard_map/ppermute | solution.py:46
  58.5 18.6 %collective-permute-start.17 = (bf16[64,512]{1,0:T(8,128)(2,1)}, bf16[64,512]{1,0:T(8,128)(2,1)}, u32[]{:S(2)}, u32[]{:S(2)}) collective-permute-start(bf16[64,512]{1,0:T(8,128)(2,1)} %bitcast.39), channel_id=1, source_target_pairs={{0,8},{2,10},{4,12},{6,14},{8,16},{10,18},{12,20},{14,22},{16,24},... | collective-permute-start | bytes 196616 | tf_op jit(solution)/shard_map/ppermute | solution.py:46
  69.1 22.3 %collective-permute-start.13 = (bf16[768,256]{1,0:T(8,128)(2,1)S(1)}, bf16[768,256]{1,0:T(8,128)(2,1)S(1)}, u32[]{:S(2)}, u32[]{:S(2)}) collective-permute-start(bf16[768,256]{1,0:T(8,128)(2,1)S(1)} %get-tuple-element.71.refs_0_), channel_id=1, source_target_pairs={{0,1},{1,0},{2,3},{3,2},{4,5},{5,4},{6,7},{7,6},{8,9},{9,8},{10,11... | collective-permute-start | bytes 1179656 | tf_op jit(solution)/shard_map/ppermute | solution.py:58
  72.9 31.4 %collective-permute-start.14 = (bf16[768,256]{1,0:T(8,128)(2,1)S(1)}, bf16[768,256]{1,0:T(8,128)(2,1)S(1)}, u32[]{:S(2)}, u32[]{:S(2)}) collective-permute-start(bf16[768,256]{1,0:T(8,128)(2,1)S(1)} %get-tuple-element.71.refs_0_), channel_id=1, source_target_pairs={{0,4},{2,6},{4,0},{6,2},{8,12},{10,14},{12,8},{14,10},{16,20},{18,... | collective-permute-start | bytes 1179656 | tf_op jit(solution)/shard_map/ppermute | solution.py:46
  77.1 18.4 %collective-permute-start.11 = (bf16[192,1024]{1,0:T(8,128)(2,1)}, bf16[192,1024]{1,0:T(8,128)(2,1)}, u32[]{:S(2)}, u32[]{:S(2)}) collective-permute-start(bf16[192,1024]{1,0:T(8,128)(2,1)} %pad_maximum_fusion.7), channel_id=1, source_target_pairs={{0,2},{2,0},{4,6},{6,4},{8,10},{10,8},{12,14},{14,12},{16,18},{18,... | collective-permute-start | bytes 1179656 | tf_op jit(solution)/shard_map/ppermute | solution.py:46
  77.1 18.4 %collective-permute-start.12 = (f32[2,512]{1,0:T(2,128)S(1)}, f32[2,512]{1,0:T(2,128)S(1)}, u32[]{:S(2)}, u32[]{:S(2)}) collective-permute-start(f32[2,512]{1,0:T(2,128)S(1)} %reshape.345), channel_id=1, source_target_pairs={{0,1},{1,0},{2,3},{3,2},{4,5},{5,4},{6,7},{7,6},{8,9},{9,8},{10,11... | collective-permute-start | bytes 12296 | tf_op jit(solution)/shard_map/ppermute | solution.py:58
  78.1 11.4 %collective-permute-start.20 = (bf16[4,64,512]{2,1,0:T(8,128)(2,1)S(1)}, bf16[4,64,512]{2,1,0:T(8,128)(2,1)S(1)}, u32[]{:S(2)}, u32[]{:S(2)}) collective-permute-start(bf16[4,64,512]{2,1,0:T(8,128)(2,1)S(1)} %pad_maximum_fusion.10), channel_id=1, source_target_pairs={{0,4},{2,6},{4,0},{6,2},{8,12},{10,14},{12,8},{14,10},{16,20},{18,... | collective-permute-start | bytes 786440 | tf_op jit(solution)/shard_map/ppermute | solution.py:46
  91.4 12.7 %collective-permute-start.21 = (bf16[2,4,64,512]{3,2,1,0:T(8,128)(2,1)S(1)}, bf16[2,4,64,512]{3,2,1,0:T(8,128)(2,1)S(1)}, u32[]{:S(2)}, u32[]{:S(2)}) collective-permute-start(bf16[2,4,64,512]{3,2,1,0:T(8,128)(2,1)S(1)} %pad_maximum_fusion.4), channel_id=1, source_target_pairs={{0,1},{1,0},{2,3},{3,2},{4,5},{5,4},{6,7},{7,6},{8,9},{9,8},{10,11... | collective-permute-start | bytes 1572872 | tf_op jit(solution)/shard_map/ppermute | solution.py:58
  94.3 19.4 %collective-permute-start.15 = (bf16[768,256]{1,0:T(8,128)(2,1)S(1)}, bf16[768,256]{1,0:T(8,128)(2,1)S(1)}, u32[]{:S(2)}, u32[]{:S(2)}) collective-permute-start(bf16[768,256]{1,0:T(8,128)(2,1)S(1)} %collective-permute-done.13.refs_1_), channel_id=1, source_target_pairs={{0,4},{2,6},{4,0},{6,2},{8,12},{10,14},{12,8},{14,10},{16,20},{18,... | collective-permute-start | bytes 1179656 | tf_op jit(solution)/shard_map/ppermute | solution.py:46
  104.2 31.7 %collective-permute-start.22 = (bf16[2,2,4,64,512]{4,3,2,1,0:T(8,128)(2,1)S(1)}, bf16[2,2,4,64,512]{4,3,2,1,0:T(8,128)(2,1)S(1)}, u32[]{:S(2)}, u32[]{:S(2)}) collective-permute-start(bf16[2,2,4,64,512]{4,3,2,1,0:T(8,128)(2,1)S(1)} %pad_maximum_fusion.1.own_ref), channel_id=1, source_target_pairs={{0,2},{2,0},{4,6},{6,4},{8,10},{10,8},{12,14},{14,12},{16,18},{18,... | collective-permute-start | bytes 3145736 | tf_op jit(solution)/shard_map/ppermute | solution.py:46
  140.8 7.0 %collective-permute-start.23 = (bf16[96,1024]{1,0:T(8,128)(2,1)S(1)}, bf16[96,1024]{1,0:T(8,128)(2,1)S(1)}, u32[]{:S(2)}, u32[]{:S(2)}) collective-permute-start(bf16[96,1024]{1,0:T(8,128)(2,1)S(1)} %get-tuple-element.82.own_ref), channel_id=1, source_target_pairs={{0,1},{1,0},{2,3},{3,2},{4,5},{5,4},{6,7},{7,6},{8,9},{9,8},{10,11... | collective-permute-start | bytes 589832 | tf_op jit(solution)/shard_map/ppermute | solution.py:58
  160.2 8.3 %collective-permute-start.27 = (bf16[96,1024]{1,0:T(8,128)(2,1)S(1)}, bf16[96,1024]{1,0:T(8,128)(2,1)S(1)}, u32[]{:S(2)}, u32[]{:S(2)}) collective-permute-start(bf16[96,1024]{1,0:T(8,128)(2,1)S(1)} %slice.390), channel_id=1, source_target_pairs={{0,1},{1,0},{2,3},{3,2},{4,5},{5,4},{6,7},{7,6},{8,9},{9,8},{10,11... | collective-permute-start | bytes 589832 | tf_op jit(solution)/shard_map/ppermute | solution.py:58
  172.0 11.4 %all-to-all-start.1 = ((bf16[4,2,96,128]{3,2,1,0:T(8,128)(2,1)}), bf16[4,2,96,128]{3,2,1,0:T(8,128)(2,1)S(1)}, u32[]{:S(2)}, u32[]{:S(2)}) async-start(bf16[4,2,96,128]{3,2,1,0:T(8,128)(2,1)} %pad_maximum_fusion.14), calls=%async_computation.1 | async-start | bytes 393216 | tf_op jit(solution)/shard_map/all_to_all | solution.py:878
  175.4 131.0 %reduce-scatter.2.cloned.1.call-start = ((), (), s32[]{:S(2)}) async-start(), calls=%async_computation.5 | async-start | bytes 4718592 | tf_op jit(solution)/shard_map/reduce_scatter | solution.py:873
  178.3 25.7 %collective-permute-start.49 = (bf16[512,2048]{1,0:T(8,128)(2,1)}, bf16[512,2048]{1,0:T(8,128)(2,1)}, u32[]{:S(2)}, u32[]{:S(2)}) collective-permute-start(bf16[512,2048]{1,0:T(8,128)(2,1)} %get-tuple-element.123), channel_id=1, source_target_pairs={{0,2},{2,0},{4,6},{6,4},{8,10},{10,8},{12,14},{14,12},{16,18},{18,... | collective-permute-start | bytes 6291464 | tf_op jit(solution)/shard_map/ppermute | solution.py:46
  178.5 23.9 %collective-permute-start.28 = (bf16[192,1024]{1,0:T(8,128)(2,1)}, bf16[192,1024]{1,0:T(8,128)(2,1)S(1)}, u32[]{:S(2)}, u32[]{:S(2)}) collective-permute-start(bf16[192,1024]{1,0:T(8,128)(2,1)} %get-tuple-element.98), channel_id=1, source_target_pairs={{0,2},{2,0},{4,6},{6,4},{8,10},{10,8},{12,14},{14,12},{16,18},{18,... | collective-permute-start | bytes 1179656 | tf_op jit(solution)/shard_map/ppermute | solution.py:46
  199.1 19.8 %collective-permute-start.32 = (bf16[1536,256]{1,0:T(8,128)(2,1)}, bf16[1536,256]{1,0:T(8,128)(2,1)}, u32[]{:S(2)}, u32[]{:S(2)}) collective-permute-start(bf16[1536,256]{1,0:T(8,128)(2,1)} %get-tuple-element.107), channel_id=1, source_target_pairs={{0,4},{2,6},{4,0},{6,2},{8,12},{10,14},{12,8},{14,10},{16,20},{18,... | collective-permute-start | bytes 2359304 | tf_op jit(solution)/shard_map/ppermute | solution.py:46
  202.2 18.4 %collective-permute-start.43 = (bf16[8,64,1024]{2,1,0:T(8,128)(2,1)}, bf16[8,64,1024]{2,1,0:T(8,128)(2,1)}, u32[]{:S(2)}, u32[]{:S(2)}) collective-permute-start(bf16[8,64,1024]{2,1,0:T(8,128)(2,1)} %dynamic-slice_bitcast_fusion), channel_id=1, source_target_pairs={{0,2},{2,0},{4,6},{6,4},{8,10},{10,8},{12,14},{14,12},{16,18},{18,... | collective-permute-start | bytes 3145736 | tf_op jit(solution)/shard_map/ppermute | solution.py:46
  203.5 21.0 %collective-permute-start.29 = (bf16[96,1024]{1,0:T(8,128)(2,1)S(1)}, bf16[96,1024]{1,0:T(8,128)(2,1)S(1)}, u32[]{:S(2)}, u32[]{:S(2)}) collective-permute-start(bf16[96,1024]{1,0:T(8,128)(2,1)S(1)} %slice.389), channel_id=1, source_target_pairs={{0,1},{1,0},{2,3},{3,2},{4,5},{5,4},{6,7},{7,6},{8,9},{9,8},{10,11... | collective-permute-start | bytes 589832 | tf_op jit(solution)/shard_map/ppermute | solution.py:58
  220.6 12.1 %collective-permute-start.33 = (bf16[768,256]{1,0:T(8,128)(2,1)S(1)}, bf16[768,256]{1,0:T(8,128)(2,1)S(1)}, u32[]{:S(2)}, u32[]{:S(2)}) collective-permute-start(bf16[768,256]{1,0:T(8,128)(2,1)S(1)} %slice.388), channel_id=1, source_target_pairs={{0,1},{1,0},{2,3},{3,2},{4,5},{5,4},{6,7},{7,6},{8,9},{9,8},{10,11... | collective-permute-start | bytes 1179656 | tf_op jit(solution)/shard_map/ppermute | solution.py:58
  222.5 17.4 %collective-permute-start.44 = (bf16[8,64,512]{2,1,0:T(8,128)(2,1)S(1)}, bf16[8,64,512]{2,1,0:T(8,128)(2,1)S(1)}, u32[]{:S(2)}, u32[]{:S(2)}) collective-permute-start(bf16[8,64,512]{2,1,0:T(8,128)(2,1)S(1)} %select_convert_fusion.1), channel_id=1, source_target_pairs={{0,1},{1,0},{2,3},{3,2},{4,5},{5,4},{6,7},{7,6},{8,9},{9,8},{10,11... | collective-permute-start | bytes 1572872 | tf_op jit(solution)/shard_map/ppermute | solution.py:58
  224.6 17.4 %collective-permute-start.30 = (bf16[96,1024]{1,0:T(8,128)(2,1)S(1)}, bf16[96,1024]{1,0:T(8,128)(2,1)S(1)}, u32[]{:S(2)}, u32[]{:S(2)}) collective-permute-start(bf16[96,1024]{1,0:T(8,128)(2,1)S(1)} %fusion.13), channel_id=1, source_target_pairs={{0,1},{1,0},{2,3},{3,2},{4,5},{5,4},{6,7},{7,6},{8,9},{9,8},{10,11... | collective-permute-start | bytes 589832 | tf_op jit(solution)/shard_map/ppermute | solution.py:58
  235.4 12.2 %collective-permute-start.34 = (bf16[384,1024]{1,0:T(8,128)(2,1)S(1)}, bf16[384,1024]{1,0:T(8,128)(2,1)S(1)}, u32[]{:S(2)}, u32[]{:S(2)}) collective-permute-start(bf16[384,1024]{1,0:T(8,128)(2,1)S(1)} %get-tuple-element.110), channel_id=1, source_target_pairs={{0,2},{2,0},{4,6},{6,4},{8,10},{10,8},{12,14},{14,12},{16,18},{18,... | collective-permute-start | bytes 2359304 | tf_op jit(solution)/shard_map/ppermute | solution.py:46
  240.2 6.4 %collective-permute-start.45 = (bf16[4,64,512]{2,1,0:T(8,128)(2,1)S(1)}, bf16[4,64,512]{2,1,0:T(8,128)(2,1)S(1)}, u32[]{:S(2)}, u32[]{:S(2)}) collective-permute-start(bf16[4,64,512]{2,1,0:T(8,128)(2,1)S(1)} %dynamic-slice_bitcast_fusion.1), channel_id=1, source_target_pairs={{0,4},{2,6},{4,0},{6,2},{8,12},{10,14},{12,8},{14,10},{16,20},{18,... | collective-permute-start | bytes 786440 | tf_op jit(solution)/shard_map/ppermute | solution.py:46
  250.0 13.5 %collective-permute-start.37 = (bf16[96,1024]{1,0:T(8,128)(2,1)}, bf16[96,1024]{1,0:T(8,128)(2,1)}, u32[]{:S(2)}, u32[]{:S(2)}) collective-permute-start(bf16[96,1024]{1,0:T(8,128)(2,1)} %get-tuple-element.208), channel_id=1, source_target_pairs={{0,8},{2,10},{4,12},{6,14},{8,16},{10,18},{12,20},{14,22},{16,24},... | collective-permute-start | bytes 589832 | tf_op jit(solution)/shard_map/ppermute | solution.py:46
  252.6 13.0 %collective-permute-start.36 = (bf16[96,1024]{1,0:T(8,128)(2,1)}, bf16[96,1024]{1,0:T(8,128)(2,1)}, u32[]{:S(2)}, u32[]{:S(2)}) collective-permute-start(bf16[96,1024]{1,0:T(8,128)(2,1)} %get-tuple-element.209), channel_id=1, source_target_pairs={{0,16},{2,18},{4,20},{6,22},{8,24},{10,26},{12,28},{14,30},{16,0},... | collective-permute-start | bytes 589832 | tf_op jit(solution)/shard_map/ppermute | solution.py:46
  254.7 12.1 %collective-permute-start.35 = (bf16[96,1024]{1,0:T(8,128)(2,1)}, bf16[96,1024]{1,0:T(8,128)(2,1)}, u32[]{:S(2)}, u32[]{:S(2)}) collective-permute-start(bf16[96,1024]{1,0:T(8,128)(2,1)} %get-tuple-element.207), channel_id=1, source_target_pairs={{0,24},{2,26},{4,28},{6,30},{8,0},{10,2},{12,4},{14,6},{16,8},{18,... | collective-permute-start | bytes 589832 | tf_op jit(solution)/shard_map/ppermute | solution.py:46
  262.6 9.2 %collective-permute-start.40 = (bf16[4,2,64,512]{3,2,0,1:T(8,128)(2,1)S(1)}, bf16[4,2,64,512]{3,2,0,1:T(8,128)(2,1)S(1)}, u32[]{:S(2)}, u32[]{:S(2)}) collective-permute-start(bf16[4,2,64,512]{3,2,0,1:T(8,128)(2,1)S(1)} %bitcast_select_fusion.1), channel_id=1, source_target_pairs={{1,0},{0,2},{2,3},{3,1},{5,4},{4,6},{6,7},{7,5},{9,8},{8,10},{10,1... | collective-permute-start | bytes 1572872 | tf_op jit(solution)/shard_map/ppermute | solution.py:73
  262.8 9.0 %collective-permute-start.41 = (bf16[4,2,64,512]{3,2,0,1:T(8,128)(2,1)S(1)}, bf16[4,2,64,512]{3,2,0,1:T(8,128)(2,1)S(1)}, u32[]{:S(2)}, u32[]{:S(2)}) collective-permute-start(bf16[4,2,64,512]{3,2,0,1:T(8,128)(2,1)S(1)} %bitcast.167), channel_id=1, source_target_pairs={{2,1},{1,2},{6,5},{5,6},{10,9},{9,10},{14,13},{13,14},{18,17},{17,... | collective-permute-start | bytes 1572872 | tf_op jit(solution)/shard_map/ppermute | solution.py:77
  263.5 25.0 %collective-permute-start.48 = (bf16[64,512]{1,0:T(8,128)(2,1)S(1)}, bf16[64,512]{1,0:T(8,128)(2,1)S(1)}, u32[]{:S(2)}, u32[]{:S(2)}) collective-permute-start(bf16[64,512]{1,0:T(8,128)(2,1)S(1)} %get-tuple-element.227), channel_id=1, source_target_pairs={{0,24},{2,26},{4,28},{6,30},{8,0},{10,2},{12,4},{14,6},{16,8},{18,... | collective-permute-start | bytes 196616 | tf_op jit(solution)/shard_map/ppermute | solution.py:46
  265.6 23.0 %collective-permute-start.47 = (bf16[64,512]{1,0:T(8,128)(2,1)S(1)}, bf16[64,512]{1,0:T(8,128)(2,1)S(1)}, u32[]{:S(2)}, u32[]{:S(2)}) collective-permute-start(bf16[64,512]{1,0:T(8,128)(2,1)S(1)} %get-tuple-element.228), channel_id=1, source_target_pairs={{0,16},{2,18},{4,20},{6,22},{8,24},{10,26},{12,28},{14,30},{16,0},... | collective-permute-start | bytes 196616 | tf_op jit(solution)/shard_map/ppermute | solution.py:46
  266.8 21.8 %collective-permute-start.46 = (bf16[64,512]{1,0:T(8,128)(2,1)S(1)}, bf16[64,512]{1,0:T(8,128)(2,1)S(1)}, u32[]{:S(2)}, u32[]{:S(2)}) collective-permute-start(bf16[64,512]{1,0:T(8,128)(2,1)S(1)} %get-tuple-element.226), channel_id=1, source_target_pairs={{0,8},{2,10},{4,12},{6,14},{8,16},{10,18},{12,20},{14,22},{16,24},... | collective-permute-start | bytes 196616 | tf_op jit(solution)/shard_map/ppermute | solution.py:46
  272.1 12.3 %collective-permute-start.42 = (bf16[4,64,512]{2,1,0:T(8,128)(2,1)S(1)}, bf16[4,64,512]{2,1,0:T(8,128)(2,1)S(1)}, u32[]{:S(2)}, u32[]{:S(2)}) collective-permute-start(bf16[4,64,512]{2,1,0:T(8,128)(2,1)S(1)} %fusion.14), channel_id=1, source_target_pairs={{0,4},{2,6},{4,0},{6,2},{8,12},{10,14},{12,8},{14,10},{16,20},{18,... | collective-permute-start | bytes 786440 | tf_op jit(solution)/shard_map/ppermute | solution.py:46
  274.4 15.9 %collective-permute-start.38 = (bf16[96,1024]{1,0:T(8,128)(2,1)S(1)}, bf16[96,1024]{1,0:T(8,128)(2,1)S(1)}, u32[]{:S(2)}, u32[]{:S(2)}) collective-permute-start(bf16[96,1024]{1,0:T(8,128)(2,1)S(1)} %fusion.7), channel_id=1, source_target_pairs={{0,1},{1,0},{2,3},{3,2},{4,5},{5,4},{6,7},{7,6},{8,9},{9,8},{10,11... | collective-permute-start | bytes 589832 | tf_op jit(solution)/shard_map/ppermute | solution.py:58
  285.2 16.1 %all-to-all-start.2 = ((bf16[4,64,512]{2,1,0:T(8,128)(2,1)}), bf16[4,64,512]{2,1,0:T(8,128)(2,1)S(1)}, u32[]{:S(2)}, u32[]{:S(2)}) async-start(bf16[4,64,512]{2,1,0:T(8,128)(2,1)} %fusion.2), calls=%async_computation.2 | async-start | bytes 524288 | tf_op jit(solution)/shard_map/all_to_all | solution.py:917
  (56 other events, 610.5 us)
Sparse Core Ops, SparseCore 0:
  44.3 91.8 all-gather.1
  208.3 91.1 reduce-scatter.1

commit v7 on v6

--- a/solution.py
+++ b/solution.py
@@ -591,7 +591,7 @@
 def outer_kernel(part, at_ref, normed_ref, gh_ref, gz_ref, act_ref, keep_ref, send_ref, made):
     hidden_size = gh_ref.shape[1]
     chips = keep_ref.shape[0] // part
-    step = 512
+    step = 1024
     for base, left_ref, right_ref in ((0, normed_ref, gh_ref), (hidden_size, gz_ref, act_ref)):
         for n in range(hidden_size // step):
             made[...] = dot(left_ref[...], right_ref[:, n * step : (n + 1) * step], TN)
@@ -615,7 +615,7 @@
         "outer",
         (out, out),
         (at, normed, gh, gz, act),
-        scratch=[pltpu.VMEM((width, 512), F32)],
+        scratch=[pltpu.VMEM((width, 1024), F32)],
     )
 
 
@@ -696,7 +696,6 @@
 def close_kernel(rows, full_ref, unit_ref, scale_ref, lead_ref, vec_ref, middle_ref, normed_ref, stack_ref, *refs):
     sum_ref, bias_ref, out_ref = refs
     count, width = full_ref.shape
-    lead_row = jnp.zeros((4, width), F32)
     for n in range(count // rows):
         span = slice(n * rows, (n + 1) * rows)
         grad = full_ref[span, :]
@@ -704,16 +703,11 @@
         back = norm_back(unit, scale_ref[span, :], vec_ref[2:3, :], grad)
         if n == 0:
             back = back + middle_ref[...]
-        lead_row = lead_row + jnp.concatenate(
-            [
-                jnp.sum(back * lead_ref[span, :], axis=0, keepdims=True),
-                jnp.sum(back, axis=0, keepdims=True),
-                jnp.sum(grad * unit, axis=0, keepdims=True),
-                jnp.sum(grad, axis=0, keepdims=True),
-            ],
-            axis=0,
-        )
-    sum_ref[...] = lead_row
+        parts = (back * lead_ref[span, :], back, grad * unit, grad)
+        added = [jnp.sum(block, axis=0, keepdims=True) for block in parts]
+        total = added if n == 0 else [x + y for x, y in zip(total, added)]
+    for n, row in enumerate(total):
+        sum_ref[n : n + 1, :] = row
     bias_ref[...] = jnp.sum(stack_ref[...].astype(F32), axis=0, keepdims=True)
     out_ref[...] = dot(normed_ref[...], stack_ref[...], TN).astype(BF16)
 

time: 320 us -> 320 us (level)
  no operation moved by 1% of the time
where the time goes in v7:
time: 320 us; the launch traced here: 316 us
  waiting for transfers between devices  102 us (32%)
  starting transfers between devices  70.1 us (22%)
  Pallas kernels  52.2 us (16%)
  other arithmetic  36 us (11%)
  local copies, waits for them, and re-layouts  25 us (8%)
  between operations  15.4 us (5%)
  blocking collectives  13.9 us (4%)
    ppermute x36, waiting for transfers between devices, _move(): return lax.ppermute(block, SP, pairs)  57 us
    pallas_call x10, Pallas kernels, local_kernel(): pl.pallas_call(kernel, out_shape=out_shape, in_specs=[SMEM] * scalars + i...  50.5 us
    ppermute x36, starting transfers between devices, _move(): return lax.ppermute(block, SP, pairs)  42.3 us
    ppermute x10, waiting for transfers between devices, yswap(): return lax.ppermute(block, 'tp', [(0, 1), (1, 0)])  24.7 us
    ppermute x10, starting transfers between devices, yswap(): return lax.ppermute(block, 'tp', [(0, 1), (1, 0)])  17.5 us
    all_to_all x1, blocking collectives, per_device(): attn_got = lax.all_to_all(attn_send, 'z', 0, 0, tiled=True)  13.9 us
    unnamed x105, local copies, waits for them, and re-layouts  13.4 us
    all_to_all x1, waiting for transfers between devices, per_device(): dw = lax.all_to_all(dw.astype(BF16), 'z', 0, 0, tiled=True)  10.1 us
  transfers between devices with their start and end apart: 54, of which 22 were waited for; matrix products, arithmetic and copies ran while one was open for 13% of the time, Pallas kernels for 14%

profile of v7, /device:TPU:0, one launch (start us, length us, event | category | flops | bytes accessed | tf_op | source)
XLA Modules:
  0.0 315.9 jit_solution(498586591897280012)
XLA Ops:
  12.8 3.1 collective-permute-start
  15.9 2.6 collective-permute-start.1
  22.3 5.2 %collective-permute-done.7 = bf16[64,384]{1,0:T(8,128)(2,1)S(1)} collective-permute-done((bf16[64,384]{1,0:T(8,128)(2,1)S(1)}, bf16[64,384]{1,0:T(8,128)(2,1)S(1)}, u32[]{:S(2)}, u32[]{:S(2)}) %collective-permute-start.7) | collective-permute-done | bytes 49184 | tf_op jit(solution)/shard_map/ppermute | solution.py:46
  27.5 4.3 %collective-permute-start.2 = (bf16[96,1152]{1,0:T(8,128)(2,1)S(1)}, bf16[96,1152]{1,0:T(8,128)(2,1)S(1)}, u32[]{:S(2)}, u32[]{:S(2)}) collective-permute-start(bf16[96,1152]{1,0:T(8,128)(2,1)S(1)} %concatenate.70.refs_0_), channel_id=1, source_target_pairs={{0,24},{2,26},{4,28},{6,30},{8,0},{10,2},{12,4},{14,6},{16,8},{18,... | collective-permute-start | bytes 663560 | tf_op jit(solution)/shard_map/ppermute | solution.py:46
  31.8 5.3 %collective-permute-done.6 = bf16[64,384]{1,0:T(8,128)(2,1)S(1)} collective-permute-done((bf16[64,384]{1,0:T(8,128)(2,1)S(1)}, bf16[64,384]{1,0:T(8,128)(2,1)S(1)}, u32[]{:S(2)}, u32[]{:S(2)}) %collective-permute-start.6) | collective-permute-done | bytes 49184 | tf_op jit(solution)/shard_map/ppermute | solution.py:46
  38.8 3.3 %collective-permute-done.2.refs_3_ = bf16[96,1152]{1,0:T(8,128)(2,1)S(1)} collective-permute-done((bf16[96,1152]{1,0:T(8,128)(2,1)S(1)}, bf16[96,1152]{1,0:T(8,128)(2,1)S(1)}, u32[]{:S(2)}, u32[]{:S(2)}) %collective-permute-start.2) | collective-permute-done | bytes 221216 | tf_op jit(solution)/shard_map/ppermute | solution.py:46
  48.9 4.6 %collective-permute-done.9 = bf16[2,4,64,384]{3,2,1,0:T(8,128)(2,1)S(1)} collective-permute-done((bf16[2,4,64,384]{3,2,1,0:T(8,128)(2,1)S(1)}, bf16[2,4,64,384]{3,2,1,0:T(8,128)(2,1)S(1)}, u32[]{:S(2)}, u32[]{:S(2)}) %collective-permute-start.9) | collective-permute-done | bytes 393248 | tf_op jit(solution)/shard_map/ppermute | solution.py:73
  53.6 4.9 %collective-permute-start.19 = (bf16[64,512]{1,0:T(8,128)(2,1)}, bf16[64,512]{1,0:T(8,128)(2,1)}, u32[]{:S(2)}, u32[]{:S(2)}) collective-permute-start(bf16[64,512]{1,0:T(8,128)(2,1)} %bitcast.39), channel_id=1, source_target_pairs={{0,24},{2,26},{4,28},{6,30},{8,0},{10,2},{12,4},{14,6},{16,8},{18,... | collective-permute-start | bytes 196616 | tf_op jit(solution)/shard_map/ppermute | solution.py:46
  58.5 1.9 collective-permute-start.17
  60.9 4.2 %enter.1 = (bf16[768,1024]{1,0:T(8,128)(2,1)}, bf16[768,1024]{1,0:T(8,128)(2,1)}, f32[768,1]{1,0:T(8,128)S(1)}, f32[768,1]{1,0:T(8,128)S(1)}, f32[96,1024]{1,0:T...) custom-call(s32[4]{0:T(128)S(1)} %pad_add_fusion.at_ref.refs_0_, ...), custom_call_target="tpu_custom_call" | custom-call | flops 5000000000 | bytes 65536 | tf_op jit(solution)/shard_map/enter/pallas_call | solution.py:173
  69.1 3.8 %collective-permute-start.13 = (bf16[768,256]{1,0:T(8,128)(2,1)S(1)}, bf16[768,256]{1,0:T(8,128)(2,1)S(1)}, u32[]{:S(2)}, u32[]{:S(2)}) collective-permute-start(bf16[768,256]{1,0:T(8,128)(2,1)S(1)} %get-tuple-element.71.refs_0_), channel_id=1, source_target_pairs={{0,1},{1,0},{2,3},{3,2},{4,5},{5,4},{6,7},{7,6},{8,9},{9,8},{10,11... | collective-permute-start | bytes 1179656 | tf_op jit(solution)/shard_map/ppermute | solution.py:58
  80.9 8.7 %collective-permute-done.20 = bf16[4,64,512]{2,1,0:T(8,128)(2,1)S(1)} collective-permute-done((bf16[4,64,512]{2,1,0:T(8,128)(2,1)S(1)}, bf16[4,64,512]{2,1,0:T(8,128)(2,1)S(1)}, u32[]{:S(2)}, u32[]{:S(2)}) %collective-permute-start.20) | collective-permute-done | bytes 262176 | tf_op jit(solution)/shard_map/ppermute | solution.py:46
  91.4 2.3 collective-permute-start.21
  95.5 2.1 pad_maximum_fusion.3.gz_ref
  97.5 6.6 %collective-permute-done.21 = bf16[2,4,64,512]{3,2,1,0:T(8,128)(2,1)S(1)} collective-permute-done((bf16[2,4,64,512]{3,2,1,0:T(8,128)(2,1)S(1)}, bf16[2,4,64,512]{3,2,1,0:T(8,128)(2,1)S(1)}, u32[]{:S(2)}, u32[]{:S(2)}) %collective-permute-start.21) | collective-permute-done | bytes 524320 | tf_op jit(solution)/shard_map/ppermute | solution.py:58
  104.3 9.4 %collective-permute-done.15.refs_3_ = bf16[768,256]{1,0:T(8,128)(2,1)S(1)} collective-permute-done((bf16[768,256]{1,0:T(8,128)(2,1)S(1)}, bf16[768,256]{1,0:T(8,128)(2,1)S(1)}, u32[]{:S(2)}, u32[]{:S(2)}) %collective-permute-start.15) | collective-permute-done | bytes 393248 | tf_op jit(solution)/shard_map/ppermute | solution.py:46
  113.8 7.4 %attend.1 = (f32[768,128]{1,0:T(8,128)S(1)}, f32[8,768]{1,0:T(8,128)S(1)}, bf16[768,128]{1,0:T(8,128)(2,1)S(1)}, bf16[4,2,96,128]{3,2,1,0:T(8,128)(2,1)S(1)}) custom-call(s32[4]{0:T(128)S(1)} %pad_add_fusion.at_ref.refs_0_, f32[768,128]{1,0:T(8,128)S(1)} %copy-done.32, f32[2,128]{1,0:T(2,128)S(1)} %fusion.25.bias_ref, ...), custom_call_target="tpu_custom_call" | custom-call | flops 14000000000 | bytes 65536 | tf_op jit(solution)/shard_map/attend/pallas_call | solution.py:173
  121.9 13.9 %all_to_all.15.got_ref = bf16[4,2,96,128]{3,2,1,0:T(8,128)(2,1)S(1)} all-to-all(bf16[4,2,96,128]{3,2,1,0:T(8,128)(2,1)S(1)} %get-tuple-element.74), channel_id=1, replica_groups=mesh['z'=4,'x'=2,'core'=2,'tp'=2] {'z'}, dimensions={0} | all-to-all | bytes 393216 | tf_op jit(solution)/shard_map/all_to_all | solution.py:856
  142.3 5.4 %collective-permute-done.23.near_ref = bf16[96,1024]{1,0:T(8,128)(2,1)S(1)} collective-permute-done((bf16[96,1024]{1,0:T(8,128)(2,1)S(1)}, bf16[96,1024]{1,0:T(8,128)(2,1)S(1)}, u32[]{:S(2)}, u32[]{:S(2)}) %collective-permute-start.23) | collective-permute-done | bytes 196640 | tf_op jit(solution)/shard_map/ppermute | solution.py:58
  147.9 1.8 collective-permute-done.24.far_ref
  149.8 7.3 %feed.1 = (bf16[384,1024]{1,0:T(8,128)(2,1)}, bf16[384,1024]{1,0:T(8,128)(2,1)}, bf16[384,1024]{1,0:T(8,128)(2,1)}, f32[1,1024]{1,0:T(1,128)}, f32[192,1024]{1,0...) custom-call(f32[1,1024]{1,0:T(1,128)} %broadcast_select_fusion.18.bias_ref, ...), custom_call_target="tpu_custom_call" | custom-call | bytes 65536 | tf_op jit(solution)/shard_map/feed/pallas_call | solution.py:173
  157.2 1.8 collective-permute-done.26
  160.2 1.6 collective-permute-start.27
  161.8 4.9 %outer.1 = (bf16[512,2048]{1,0:T(8,128)(2,1)S(1)}, bf16[512,2048]{1,0:T(8,128)(2,1)}) custom-call(s32[4]{0:T(128)S(1)} %pad_add_fusion.at_ref.refs_0_, bf16[384,1024]{1,0:T(8,128)(2,1)S(1)} %copy-done.12, bf16[384,1024]{1,0:T(8,128)(2,1)S(1)} %copy-done.14, bf16[384,1024]{1,0:T(8,128)(2,1)S(1)} %copy-done, bf16[384,1024]{1,0:T(8,128)(2,1)S(1)} %copy-done.13), custom_call_target="tpu_custom_call" | custom-call | flops 5000000000 | bytes 65536 | tf_op jit(solution)/shard_map/outer/pallas_call | solution.py:173
  171.6 3.4 %all-to-all-start.1 = ((bf16[4,2,96,128]{3,2,1,0:T(8,128)(2,1)}), bf16[4,2,96,128]{3,2,1,0:T(8,128)(2,1)S(1)}, u32[]{:S(2)}, u32[]{:S(2)}) async-start(bf16[4,2,96,128]{3,2,1,0:T(8,128)(2,1)} %pad_maximum_fusion.14), calls=%async_computation.1 | async-start | bytes 393216 | tf_op jit(solution)/shard_map/all_to_all | solution.py:872
  178.4 4.6 %all-to-all-done.1.got_ref = bf16[4,2,96,128]{3,2,1,0:T(8,128)(2,1)S(1)} async-done(((bf16[4,2,96,128]{3,2,1,0:T(8,128)(2,1)}), bf16[4,2,96,128]{3,2,1,0:T(8,128)(2,1)S(1)}, u32[]{:S(2)}, u32[]{:S(2)}) %all-to-all-start.1) | async-done | bytes 196640 | tf_op jit(solution)/shard_map/all_to_all | solution.py:872
  183.7 15.0 %attend_back.1 = (bf16[768,128]{1,0:T(8,128)(2,1)}, bf16[1536,256]{1,0:T(8,128)(2,1)}, bf16[1536,256]{1,0:T(8,128)(2,1)}) custom-call(s32[4]{0:T(128)} %copy-done.11, bf16[768,128]{1,0:T(8,128)(2,1)} %copy-done.34, bf16[768,128]{1,0:T(8,128)(2,1)} %copy-done.7, bf16[3072,128]{1,0:T(8,128)(2,1)} %copy-done.4, bf16[4,2,96,128]{3,2,1,0:T(8,128)(2,1)} %copy-done.48, ...), custom_call_target="tpu_custom_call" | custom-call | flops 16999999488 | bytes 65536 | tf_op jit(solution)/shard_map/attend_back/pallas_call | solution.py:173
  203.8 4.1 %pad_maximum_fusion = bf16[512,4096]{1,0:T(8,128)(2,1)} fusion(bf16[512,2048]{1,0:T(8,128)(2,1)} %collective-permute-done.49, bf16[512,2048]{1,0:T(8,128)(2,1)S(1)} %copy-done.2), kind=kLoop, calls=%fused_computation | loop fusion | flops 8388608 | bytes 8388608 | tf_op jit(solution)/shard_map/concatenate | solution.py:866
  207.9 10.6 %collective-permute-done.32 = bf16[1536,256]{1,0:T(8,128)(2,1)} collective-permute-done((bf16[1536,256]{1,0:T(8,128)(2,1)}, bf16[1536,256]{1,0:T(8,128)(2,1)}, u32[]{:S(2)}, u32[]{:S(2)}) %collective-permute-start.32) | collective-permute-done | bytes 786464 | tf_op jit(solution)/shard_map/ppermute | solution.py:46
  220.2 1.7 convert_add_fusion
  222.1 2.0 collective-permute-start.44
  224.3 7.9 %collective-permute-done.33.near_ref = bf16[768,256]{1,0:T(8,128)(2,1)S(1)} collective-permute-done((bf16[768,256]{1,0:T(8,128)(2,1)S(1)}, bf16[768,256]{1,0:T(8,128)(2,1)S(1)}, u32[]{:S(2)}, u32[]{:S(2)}) %collective-permute-start.33) | collective-permute-done | bytes 393248 | tf_op jit(solution)/shard_map/ppermute | solution.py:58
  232.3 2.7 leave.1
  235.0 4.5 %collective-permute-done.44 = bf16[8,64,512]{2,1,0:T(8,128)(2,1)S(1)} collective-permute-done((bf16[8,64,512]{2,1,0:T(8,128)(2,1)S(1)}, bf16[8,64,512]{2,1,0:T(8,128)(2,1)S(1)}, u32[]{:S(2)}, u32[]{:S(2)}) %collective-permute-start.44) | collective-permute-done | bytes 524320 | tf_op jit(solution)/shard_map/ppermute | solution.py:58
  239.8 1.6 collective-permute-start.45
  242.4 3.9 %collective-permute-done.45 = bf16[4,64,512]{2,1,0:T(8,128)(2,1)S(1)} collective-permute-done((bf16[4,64,512]{2,1,0:T(8,128)(2,1)S(1)}, bf16[4,64,512]{2,1,0:T(8,128)(2,1)S(1)}, u32[]{:S(2)}, u32[]{:S(2)}) %collective-permute-start.45) | collective-permute-done | bytes 262176 | tf_op jit(solution)/shard_map/ppermute | solution.py:46
  249.6 2.6 collective-permute-start.37
  252.2 2.1 collective-permute-start.36
  254.6 5.3 %close.1 = (f32[4,1024]{1,0:T(4,128)S(1)}, f32[1,384]{1,0:T(1,128)S(1)}, bf16[1024,384]{1,0:T(8,128)(2,1)S(1)}) custom-call(f32[768,1024]{1,0:T(8,128)} %get-tuple-element.109.refs_0_, bf16[768,1024]{1,0:T(8,128)(2,1)S(1)} %copy-done.8, f32[768,1]{1,0:T(8,128)S(1)} %copy-done.10, f32[768,1]{1,0:T(8,128)S(1)} %copy-done.29, ...), custom_call_target="tpu_custom_call" | custom-call | flops 5000000000 | bytes 65536 | tf_op jit(solution)/shard_map/close/pallas_call | solution.py:173
  263.3 2.0 collective-permute-start.48
  266.5 2.2 collective-permute-start.46
  271.8 2.1 collective-permute-start.42
  274.1 5.2 %collective-permute-start.38 = (bf16[96,1024]{1,0:T(8,128)(2,1)S(1)}, bf16[96,1024]{1,0:T(8,128)(2,1)S(1)}, u32[]{:S(2)}, u32[]{:S(2)}) collective-permute-start(bf16[96,1024]{1,0:T(8,128)(2,1)S(1)} %fusion.7), channel_id=1, source_target_pairs={{0,1},{1,0},{2,3},{3,2},{4,5},{5,4},{6,7},{7,6},{8,9},{9,8},{10,11... | collective-permute-start | bytes 589832 | tf_op jit(solution)/shard_map/ppermute | solution.py:58
  279.3 4.7 %collective-permute-done.42 = bf16[4,64,512]{2,1,0:T(8,128)(2,1)S(1)} collective-permute-done((bf16[4,64,512]{2,1,0:T(8,128)(2,1)S(1)}, bf16[4,64,512]{2,1,0:T(8,128)(2,1)S(1)}, u32[]{:S(2)}, u32[]{:S(2)}) %collective-permute-start.42) | collective-permute-done | bytes 262176 | tf_op jit(solution)/shard_map/ppermute | solution.py:46
  284.8 3.4 %all-to-all-start.2 = ((bf16[4,64,512]{2,1,0:T(8,128)(2,1)}), bf16[4,64,512]{2,1,0:T(8,128)(2,1)S(1)}, u32[]{:S(2)}, u32[]{:S(2)}) async-start(bf16[4,64,512]{2,1,0:T(8,128)(2,1)} %fusion.2), calls=%async_computation.2 | async-start | bytes 524288 | tf_op jit(solution)/shard_map/all_to_all | solution.py:911
  288.3 1.6 fusion.17
  290.9 10.1 %all-to-all-done.2 = bf16[4,64,512]{2,1,0:T(8,128)(2,1)S(1)} async-done(((bf16[4,64,512]{2,1,0:T(8,128)(2,1)}), bf16[4,64,512]{2,1,0:T(8,128)(2,1)S(1)}, u32[]{:S(2)}, u32[]{:S(2)}) %all-to-all-start.2) | async-done | bytes 262176 | tf_op jit(solution)/shard_map/all_to_all | solution.py:911
  303.5 1.7 place_qkv.1
  (315 shorter events, 79.1 us)
Async XLA Ops:
  7.2 142.5 %all-gather.2.cloned.1.call-start = ((), (), s32[]{:S(2)}) async-start(), calls=%async_computation.4 | async-start | bytes 4718592 | tf_op jit(solution)/shard_map/all_gather | solution.py:840
  12.8 26.0 %collective-permute-start = (bf16[96,1152]{1,0:T(8,128)(2,1)S(1)}, bf16[96,1152]{1,0:T(8,128)(2,1)S(1)}, u32[]{:S(2)}, u32[]{:S(2)}) collective-permute-start(bf16[96,1152]{1,0:T(8,128)(2,1)S(1)} %concatenate.70.refs_0_), channel_id=1, source_target_pairs={{0,8},{2,10},{4,12},{6,14},{8,16},{10,18},{12,20},{14,22},{16,24},... | collective-permute-start | bytes 663560 | tf_op jit(solution)/shard_map/ppermute | solution.py:46
  15.9 22.9 %collective-permute-start.1 = (bf16[96,1152]{1,0:T(8,128)(2,1)S(1)}, bf16[96,1152]{1,0:T(8,128)(2,1)S(1)}, u32[]{:S(2)}, u32[]{:S(2)}) collective-permute-start(bf16[96,1152]{1,0:T(8,128)(2,1)S(1)} %concatenate.70.refs_0_), channel_id=1, source_target_pairs={{0,16},{2,18},{4,20},{6,22},{8,24},{10,26},{12,28},{14,30},{16,0},... | collective-permute-start | bytes 663560 | tf_op jit(solution)/shard_map/ppermute | solution.py:46
  19.9 7.6 %collective-permute-start.7 = (bf16[64,384]{1,0:T(8,128)(2,1)S(1)}, bf16[64,384]{1,0:T(8,128)(2,1)S(1)}, u32[]{:S(2)}, u32[]{:S(2)}) collective-permute-start(bf16[64,384]{1,0:T(8,128)(2,1)S(1)} %get-tuple-element.240), channel_id=1, source_target_pairs={{0,24},{2,26},{4,28},{6,30},{8,0},{10,2},{12,4},{14,6},{16,8},{18,... | collective-permute-start | bytes 147464 | tf_op jit(solution)/shard_map/ppermute | solution.py:46
  21.3 15.8 %collective-permute-start.6 = (bf16[64,384]{1,0:T(8,128)(2,1)S(1)}, bf16[64,384]{1,0:T(8,128)(2,1)S(1)}, u32[]{:S(2)}, u32[]{:S(2)}) collective-permute-start(bf16[64,384]{1,0:T(8,128)(2,1)S(1)} %get-tuple-element.241), channel_id=1, source_target_pairs={{0,16},{2,18},{4,20},{6,22},{8,24},{10,26},{12,28},{14,30},{16,0},... | collective-permute-start | bytes 147464 | tf_op jit(solution)/shard_map/ppermute | solution.py:46
  21.5 15.6 %collective-permute-start.5 = (bf16[64,384]{1,0:T(8,128)(2,1)S(1)}, bf16[64,384]{1,0:T(8,128)(2,1)S(1)}, u32[]{:S(2)}, u32[]{:S(2)}) collective-permute-start(bf16[64,384]{1,0:T(8,128)(2,1)S(1)} %get-tuple-element.242), channel_id=1, source_target_pairs={{0,8},{2,10},{4,12},{6,14},{8,16},{10,18},{12,20},{14,22},{16,24},... | collective-permute-start | bytes 147464 | tf_op jit(solution)/shard_map/ppermute | solution.py:46
  27.5 14.7 %collective-permute-start.2 = (bf16[96,1152]{1,0:T(8,128)(2,1)S(1)}, bf16[96,1152]{1,0:T(8,128)(2,1)S(1)}, u32[]{:S(2)}, u32[]{:S(2)}) collective-permute-start(bf16[96,1152]{1,0:T(8,128)(2,1)S(1)} %concatenate.70.refs_0_), channel_id=1, source_target_pairs={{0,24},{2,26},{4,28},{6,30},{8,0},{10,2},{12,4},{14,6},{16,8},{18,... | collective-permute-start | bytes 663560 | tf_op jit(solution)/shard_map/ppermute | solution.py:46
  37.1 7.2 %collective-permute-start.8 = (bf16[4,64,384]{2,1,0:T(8,128)(2,1)S(1)}, bf16[4,64,384]{2,1,0:T(8,128)(2,1)S(1)}, u32[]{:S(2)}, u32[]{:S(2)}) collective-permute-start(bf16[4,64,384]{2,1,0:T(8,128)(2,1)S(1)} %get-tuple-element.238), channel_id=1, source_target_pairs={{0,4},{2,6},{4,0},{6,2},{8,12},{10,14},{12,8},{14,10},{16,20},{18,... | collective-permute-start | bytes 589832 | tf_op jit(solution)/shard_map/ppermute | solution.py:46
  38.7 4.5 %collective-permute-start.25 = (bf16[64,2048]{1,0:T(8,128)(2,1)S(1)}, bf16[64,2048]{1,0:T(8,128)(2,1)S(1)}, u32[]{:S(2)}, u32[]{:S(2)}) collective-permute-start(bf16[64,2048]{1,0:T(8,128)(2,1)S(1)} %pad_maximum_fusion.12), channel_id=1, source_target_pairs={{0,2},{2,0},{4,6},{6,4},{8,10},{10,8},{12,14},{14,12},{16,18},{18,... | collective-permute-start | bytes 786440 | tf_op jit(solution)/shard_map/ppermute | solution.py:46
  44.4 9.2 %collective-permute-start.9 = (bf16[2,4,64,384]{3,2,1,0:T(8,128)(2,1)S(1)}, bf16[2,4,64,384]{3,2,1,0:T(8,128)(2,1)S(1)}, u32[]{:S(2)}, u32[]{:S(2)}) collective-permute-start(bf16[2,4,64,384]{3,2,1,0:T(8,128)(2,1)S(1)} %pad_maximum_fusion.6), channel_id=1, source_target_pairs={{0,1},{2,0},{3,2},{1,3},{4,5},{6,4},{7,6},{5,7},{8,9},{10,8},{11,1... | collective-permute-start | bytes 1179656 | tf_op jit(solution)/shard_map/ppermute | solution.py:73
  45.9 7.6 %collective-permute-start.10 = (bf16[2,4,64,384]{3,2,1,0:T(8,128)(2,1)S(1)}, bf16[2,4,64,384]{3,2,1,0:T(8,128)(2,1)S(1)}, u32[]{:S(2)}, u32[]{:S(2)}) collective-permute-start(bf16[2,4,64,384]{3,2,1,0:T(8,128)(2,1)S(1)} %pad_maximum_fusion.6), channel_id=1, source_target_pairs={{2,1},{1,2},{6,5},{5,6},{10,9},{9,10},{14,13},{13,14},{18,17},{17,... | collective-permute-start | bytes 1179656 | tf_op jit(solution)/shard_map/ppermute | solution.py:77
  47.3 13.1 %collective-permute-start.4 = (bf16[2,4,16,128]{3,2,1,0:T(8,128)(2,1)S(1)}, bf16[2,4,16,128]{3,2,1,0:T(8,128)(2,1)S(1)}, u32[]{:S(2)}, u32[]{:S(2)}) collective-permute-start(bf16[2,4,16,128]{3,2,1,0:T(8,128)(2,1)S(1)} %get-tuple-element.248), channel_id=1, source_target_pairs={{0,4},{2,6},{4,0},{6,2},{8,12},{10,14},{12,8},{14,10},{16,20},{18,... | collective-permute-start | bytes 98312 | tf_op jit(solution)/shard_map/ppermute | solution.py:46
  53.6 23.4 %collective-permute-start.19 = (bf16[64,512]{1,0:T(8,128)(2,1)}, bf16[64,512]{1,0:T(8,128)(2,1)}, u32[]{:S(2)}, u32[]{:S(2)}) collective-permute-start(bf16[64,512]{1,0:T(8,128)(2,1)} %bitcast.39), channel_id=1, source_target_pairs={{0,24},{2,26},{4,28},{6,30},{8,0},{10,2},{12,4},{14,6},{16,8},{18,... | collective-permute-start | bytes 196616 | tf_op jit(solution)/shard_map/ppermute | solution.py:46
  58.5 18.5 %collective-permute-start.18 = (bf16[64,512]{1,0:T(8,128)(2,1)}, bf16[64,512]{1,0:T(8,128)(2,1)}, u32[]{:S(2)}, u32[]{:S(2)}) collective-permute-start(bf16[64,512]{1,0:T(8,128)(2,1)} %bitcast.39), channel_id=1, source_target_pairs={{0,16},{2,18},{4,20},{6,22},{8,24},{10,26},{12,28},{14,30},{16,0},... | collective-permute-start | bytes 196616 | tf_op jit(solution)/shard_map/ppermute | solution.py:46
  58.5 18.6 %collective-permute-start.17 = (bf16[64,512]{1,0:T(8,128)(2,1)}, bf16[64,512]{1,0:T(8,128)(2,1)}, u32[]{:S(2)}, u32[]{:S(2)}) collective-permute-start(bf16[64,512]{1,0:T(8,128)(2,1)} %bitcast.39), channel_id=1, source_target_pairs={{0,8},{2,10},{4,12},{6,14},{8,16},{10,18},{12,20},{14,22},{16,24},... | collective-permute-start | bytes 196616 | tf_op jit(solution)/shard_map/ppermute | solution.py:46
  69.1 22.3 %collective-permute-start.13 = (bf16[768,256]{1,0:T(8,128)(2,1)S(1)}, bf16[768,256]{1,0:T(8,128)(2,1)S(1)}, u32[]{:S(2)}, u32[]{:S(2)}) collective-permute-start(bf16[768,256]{1,0:T(8,128)(2,1)S(1)} %get-tuple-element.71.refs_0_), channel_id=1, source_target_pairs={{0,1},{1,0},{2,3},{3,2},{4,5},{5,4},{6,7},{7,6},{8,9},{9,8},{10,11... | collective-permute-start | bytes 1179656 | tf_op jit(solution)/shard_map/ppermute | solution.py:58
  72.9 31.4 %collective-permute-start.14 = (bf16[768,256]{1,0:T(8,128)(2,1)S(1)}, bf16[768,256]{1,0:T(8,128)(2,1)S(1)}, u32[]{:S(2)}, u32[]{:S(2)}) collective-permute-start(bf16[768,256]{1,0:T(8,128)(2,1)S(1)} %get-tuple-element.71.refs_0_), channel_id=1, source_target_pairs={{0,4},{2,6},{4,0},{6,2},{8,12},{10,14},{12,8},{14,10},{16,20},{18,... | collective-permute-start | bytes 1179656 | tf_op jit(solution)/shard_map/ppermute | solution.py:46
  77.1 18.4 %collective-permute-start.11 = (bf16[192,1024]{1,0:T(8,128)(2,1)}, bf16[192,1024]{1,0:T(8,128)(2,1)}, u32[]{:S(2)}, u32[]{:S(2)}) collective-permute-start(bf16[192,1024]{1,0:T(8,128)(2,1)} %pad_maximum_fusion.7), channel_id=1, source_target_pairs={{0,2},{2,0},{4,6},{6,4},{8,10},{10,8},{12,14},{14,12},{16,18},{18,... | collective-permute-start | bytes 1179656 | tf_op jit(solution)/shard_map/ppermute | solution.py:46
  77.1 18.4 %collective-permute-start.12 = (f32[2,512]{1,0:T(2,128)S(1)}, f32[2,512]{1,0:T(2,128)S(1)}, u32[]{:S(2)}, u32[]{:S(2)}) collective-permute-start(f32[2,512]{1,0:T(2,128)S(1)} %reshape.345), channel_id=1, source_target_pairs={{0,1},{1,0},{2,3},{3,2},{4,5},{5,4},{6,7},{7,6},{8,9},{9,8},{10,11... | collective-permute-start | bytes 12296 | tf_op jit(solution)/shard_map/ppermute | solution.py:58
  78.1 11.4 %collective-permute-start.20 = (bf16[4,64,512]{2,1,0:T(8,128)(2,1)S(1)}, bf16[4,64,512]{2,1,0:T(8,128)(2,1)S(1)}, u32[]{:S(2)}, u32[]{:S(2)}) collective-permute-start(bf16[4,64,512]{2,1,0:T(8,128)(2,1)S(1)} %pad_maximum_fusion.10), channel_id=1, source_target_pairs={{0,4},{2,6},{4,0},{6,2},{8,12},{10,14},{12,8},{14,10},{16,20},{18,... | collective-permute-start | bytes 786440 | tf_op jit(solution)/shard_map/ppermute | solution.py:46
  91.4 12.7 %collective-permute-start.21 = (bf16[2,4,64,512]{3,2,1,0:T(8,128)(2,1)S(1)}, bf16[2,4,64,512]{3,2,1,0:T(8,128)(2,1)S(1)}, u32[]{:S(2)}, u32[]{:S(2)}) collective-permute-start(bf16[2,4,64,512]{3,2,1,0:T(8,128)(2,1)S(1)} %pad_maximum_fusion.4), channel_id=1, source_target_pairs={{0,1},{1,0},{2,3},{3,2},{4,5},{5,4},{6,7},{7,6},{8,9},{9,8},{10,11... | collective-permute-start | bytes 1572872 | tf_op jit(solution)/shard_map/ppermute | solution.py:58
  94.3 19.4 %collective-permute-start.15 = (bf16[768,256]{1,0:T(8,128)(2,1)S(1)}, bf16[768,256]{1,0:T(8,128)(2,1)S(1)}, u32[]{:S(2)}, u32[]{:S(2)}) collective-permute-start(bf16[768,256]{1,0:T(8,128)(2,1)S(1)} %collective-permute-done.13.refs_1_), channel_id=1, source_target_pairs={{0,4},{2,6},{4,0},{6,2},{8,12},{10,14},{12,8},{14,10},{16,20},{18,... | collective-permute-start | bytes 1179656 | tf_op jit(solution)/shard_map/ppermute | solution.py:46
  104.2 31.7 %collective-permute-start.22 = (bf16[2,2,4,64,512]{4,3,2,1,0:T(8,128)(2,1)S(1)}, bf16[2,2,4,64,512]{4,3,2,1,0:T(8,128)(2,1)S(1)}, u32[]{:S(2)}, u32[]{:S(2)}) collective-permute-start(bf16[2,2,4,64,512]{4,3,2,1,0:T(8,128)(2,1)S(1)} %pad_maximum_fusion.1.own_ref), channel_id=1, source_target_pairs={{0,2},{2,0},{4,6},{6,4},{8,10},{10,8},{12,14},{14,12},{16,18},{18,... | collective-permute-start | bytes 3145736 | tf_op jit(solution)/shard_map/ppermute | solution.py:46
  140.8 7.0 %collective-permute-start.23 = (bf16[96,1024]{1,0:T(8,128)(2,1)S(1)}, bf16[96,1024]{1,0:T(8,128)(2,1)S(1)}, u32[]{:S(2)}, u32[]{:S(2)}) collective-permute-start(bf16[96,1024]{1,0:T(8,128)(2,1)S(1)} %get-tuple-element.82.own_ref), channel_id=1, source_target_pairs={{0,1},{1,0},{2,3},{3,2},{4,5},{5,4},{6,7},{7,6},{8,9},{9,8},{10,11... | collective-permute-start | bytes 589832 | tf_op jit(solution)/shard_map/ppermute | solution.py:58
  160.2 7.9 %collective-permute-start.27 = (bf16[96,1024]{1,0:T(8,128)(2,1)S(1)}, bf16[96,1024]{1,0:T(8,128)(2,1)S(1)}, u32[]{:S(2)}, u32[]{:S(2)}) collective-permute-start(bf16[96,1024]{1,0:T(8,128)(2,1)S(1)} %slice.390), channel_id=1, source_target_pairs={{0,1},{1,0},{2,3},{3,2},{4,5},{5,4},{6,7},{7,6},{8,9},{9,8},{10,11... | collective-permute-start | bytes 589832 | tf_op jit(solution)/shard_map/ppermute | solution.py:58
  171.6 11.4 %all-to-all-start.1 = ((bf16[4,2,96,128]{3,2,1,0:T(8,128)(2,1)}), bf16[4,2,96,128]{3,2,1,0:T(8,128)(2,1)S(1)}, u32[]{:S(2)}, u32[]{:S(2)}) async-start(bf16[4,2,96,128]{3,2,1,0:T(8,128)(2,1)} %pad_maximum_fusion.14), calls=%async_computation.1 | async-start | bytes 393216 | tf_op jit(solution)/shard_map/all_to_all | solution.py:872
  175.0 131.1 %reduce-scatter.2.cloned.1.call-start = ((), (), s32[]{:S(2)}) async-start(), calls=%async_computation.5 | async-start | bytes 4718592 | tf_op jit(solution)/shard_map/reduce_scatter | solution.py:867
  177.9 25.9 %collective-permute-start.49 = (bf16[512,2048]{1,0:T(8,128)(2,1)}, bf16[512,2048]{1,0:T(8,128)(2,1)}, u32[]{:S(2)}, u32[]{:S(2)}) collective-permute-start(bf16[512,2048]{1,0:T(8,128)(2,1)} %get-tuple-element.123), channel_id=1, source_target_pairs={{0,2},{2,0},{4,6},{6,4},{8,10},{10,8},{12,14},{14,12},{16,18},{18,... | collective-permute-start | bytes 6291464 | tf_op jit(solution)/shard_map/ppermute | solution.py:46
  178.1 23.9 %collective-permute-start.28 = (bf16[192,1024]{1,0:T(8,128)(2,1)}, bf16[192,1024]{1,0:T(8,128)(2,1)S(1)}, u32[]{:S(2)}, u32[]{:S(2)}) collective-permute-start(bf16[192,1024]{1,0:T(8,128)(2,1)} %get-tuple-element.98), channel_id=1, source_target_pairs={{0,2},{2,0},{4,6},{6,4},{8,10},{10,8},{12,14},{14,12},{16,18},{18,... | collective-permute-start | bytes 1179656 | tf_op jit(solution)/shard_map/ppermute | solution.py:46
  198.7 19.8 %collective-permute-start.32 = (bf16[1536,256]{1,0:T(8,128)(2,1)}, bf16[1536,256]{1,0:T(8,128)(2,1)}, u32[]{:S(2)}, u32[]{:S(2)}) collective-permute-start(bf16[1536,256]{1,0:T(8,128)(2,1)} %get-tuple-element.107), channel_id=1, source_target_pairs={{0,4},{2,6},{4,0},{6,2},{8,12},{10,14},{12,8},{14,10},{16,20},{18,... | collective-permute-start | bytes 2359304 | tf_op jit(solution)/shard_map/ppermute | solution.py:46
  201.8 18.4 %collective-permute-start.43 = (bf16[8,64,1024]{2,1,0:T(8,128)(2,1)}, bf16[8,64,1024]{2,1,0:T(8,128)(2,1)}, u32[]{:S(2)}, u32[]{:S(2)}) collective-permute-start(bf16[8,64,1024]{2,1,0:T(8,128)(2,1)} %dynamic-slice_bitcast_fusion), channel_id=1, source_target_pairs={{0,2},{2,0},{4,6},{6,4},{8,10},{10,8},{12,14},{14,12},{16,18},{18,... | collective-permute-start | bytes 3145736 | tf_op jit(solution)/shard_map/ppermute | solution.py:46
  203.0 21.0 %collective-permute-start.29 = (bf16[96,1024]{1,0:T(8,128)(2,1)S(1)}, bf16[96,1024]{1,0:T(8,128)(2,1)S(1)}, u32[]{:S(2)}, u32[]{:S(2)}) collective-permute-start(bf16[96,1024]{1,0:T(8,128)(2,1)S(1)} %slice.389), channel_id=1, source_target_pairs={{0,1},{1,0},{2,3},{3,2},{4,5},{5,4},{6,7},{7,6},{8,9},{9,8},{10,11... | collective-permute-start | bytes 589832 | tf_op jit(solution)/shard_map/ppermute | solution.py:58
  220.2 12.1 %collective-permute-start.33 = (bf16[768,256]{1,0:T(8,128)(2,1)S(1)}, bf16[768,256]{1,0:T(8,128)(2,1)S(1)}, u32[]{:S(2)}, u32[]{:S(2)}) collective-permute-start(bf16[768,256]{1,0:T(8,128)(2,1)S(1)} %slice.388), channel_id=1, source_target_pairs={{0,1},{1,0},{2,3},{3,2},{4,5},{5,4},{6,7},{7,6},{8,9},{9,8},{10,11... | collective-permute-start | bytes 1179656 | tf_op jit(solution)/shard_map/ppermute | solution.py:58
  222.1 17.4 %collective-permute-start.44 = (bf16[8,64,512]{2,1,0:T(8,128)(2,1)S(1)}, bf16[8,64,512]{2,1,0:T(8,128)(2,1)S(1)}, u32[]{:S(2)}, u32[]{:S(2)}) collective-permute-start(bf16[8,64,512]{2,1,0:T(8,128)(2,1)S(1)} %select_convert_fusion.1), channel_id=1, source_target_pairs={{0,1},{1,0},{2,3},{3,2},{4,5},{5,4},{6,7},{7,6},{8,9},{9,8},{10,11... | collective-permute-start | bytes 1572872 | tf_op jit(solution)/shard_map/ppermute | solution.py:58
  224.2 17.4 %collective-permute-start.30 = (bf16[96,1024]{1,0:T(8,128)(2,1)S(1)}, bf16[96,1024]{1,0:T(8,128)(2,1)S(1)}, u32[]{:S(2)}, u32[]{:S(2)}) collective-permute-start(bf16[96,1024]{1,0:T(8,128)(2,1)S(1)} %fusion.13), channel_id=1, source_target_pairs={{0,1},{1,0},{2,3},{3,2},{4,5},{5,4},{6,7},{7,6},{8,9},{9,8},{10,11... | collective-permute-start | bytes 589832 | tf_op jit(solution)/shard_map/ppermute | solution.py:58
  235.0 12.2 %collective-permute-start.34 = (bf16[384,1024]{1,0:T(8,128)(2,1)S(1)}, bf16[384,1024]{1,0:T(8,128)(2,1)S(1)}, u32[]{:S(2)}, u32[]{:S(2)}) collective-permute-start(bf16[384,1024]{1,0:T(8,128)(2,1)S(1)} %get-tuple-element.110), channel_id=1, source_target_pairs={{0,2},{2,0},{4,6},{6,4},{8,10},{10,8},{12,14},{14,12},{16,18},{18,... | collective-permute-start | bytes 2359304 | tf_op jit(solution)/shard_map/ppermute | solution.py:46
  239.8 6.4 %collective-permute-start.45 = (bf16[4,64,512]{2,1,0:T(8,128)(2,1)S(1)}, bf16[4,64,512]{2,1,0:T(8,128)(2,1)S(1)}, u32[]{:S(2)}, u32[]{:S(2)}) collective-permute-start(bf16[4,64,512]{2,1,0:T(8,128)(2,1)S(1)} %dynamic-slice_bitcast_fusion.1), channel_id=1, source_target_pairs={{0,4},{2,6},{4,0},{6,2},{8,12},{10,14},{12,8},{14,10},{16,20},{18,... | collective-permute-start | bytes 786440 | tf_op jit(solution)/shard_map/ppermute | solution.py:46
  249.6 13.7 %collective-permute-start.37 = (bf16[96,1024]{1,0:T(8,128)(2,1)}, bf16[96,1024]{1,0:T(8,128)(2,1)}, u32[]{:S(2)}, u32[]{:S(2)}) collective-permute-start(bf16[96,1024]{1,0:T(8,128)(2,1)} %get-tuple-element.208), channel_id=1, source_target_pairs={{0,8},{2,10},{4,12},{6,14},{8,16},{10,18},{12,20},{14,22},{16,24},... | collective-permute-start | bytes 589832 | tf_op jit(solution)/shard_map/ppermute | solution.py:46
  252.2 13.1 %collective-permute-start.36 = (bf16[96,1024]{1,0:T(8,128)(2,1)}, bf16[96,1024]{1,0:T(8,128)(2,1)}, u32[]{:S(2)}, u32[]{:S(2)}) collective-permute-start(bf16[96,1024]{1,0:T(8,128)(2,1)} %get-tuple-element.209), channel_id=1, source_target_pairs={{0,16},{2,18},{4,20},{6,22},{8,24},{10,26},{12,28},{14,30},{16,0},... | collective-permute-start | bytes 589832 | tf_op jit(solution)/shard_map/ppermute | solution.py:46
  254.3 12.2 %collective-permute-start.35 = (bf16[96,1024]{1,0:T(8,128)(2,1)}, bf16[96,1024]{1,0:T(8,128)(2,1)}, u32[]{:S(2)}, u32[]{:S(2)}) collective-permute-start(bf16[96,1024]{1,0:T(8,128)(2,1)} %get-tuple-element.207), channel_id=1, source_target_pairs={{0,24},{2,26},{4,28},{6,30},{8,0},{10,2},{12,4},{14,6},{16,8},{18,... | collective-permute-start | bytes 589832 | tf_op jit(solution)/shard_map/ppermute | solution.py:46
  262.4 9.2 %collective-permute-start.40 = (bf16[4,2,64,512]{3,2,0,1:T(8,128)(2,1)S(1)}, bf16[4,2,64,512]{3,2,0,1:T(8,128)(2,1)S(1)}, u32[]{:S(2)}, u32[]{:S(2)}) collective-permute-start(bf16[4,2,64,512]{3,2,0,1:T(8,128)(2,1)S(1)} %bitcast_select_fusion.1), channel_id=1, source_target_pairs={{1,0},{0,2},{2,3},{3,1},{5,4},{4,6},{6,7},{7,5},{9,8},{8,10},{10,1... | collective-permute-start | bytes 1572872 | tf_op jit(solution)/shard_map/ppermute | solution.py:73
  262.6 9.0 %collective-permute-start.41 = (bf16[4,2,64,512]{3,2,0,1:T(8,128)(2,1)S(1)}, bf16[4,2,64,512]{3,2,0,1:T(8,128)(2,1)S(1)}, u32[]{:S(2)}, u32[]{:S(2)}) collective-permute-start(bf16[4,2,64,512]{3,2,0,1:T(8,128)(2,1)S(1)} %bitcast.167), channel_id=1, source_target_pairs={{2,1},{1,2},{6,5},{5,6},{10,9},{9,10},{14,13},{13,14},{18,17},{17,... | collective-permute-start | bytes 1572872 | tf_op jit(solution)/shard_map/ppermute | solution.py:77
  263.3 24.9 %collective-permute-start.48 = (bf16[64,512]{1,0:T(8,128)(2,1)S(1)}, bf16[64,512]{1,0:T(8,128)(2,1)S(1)}, u32[]{:S(2)}, u32[]{:S(2)}) collective-permute-start(bf16[64,512]{1,0:T(8,128)(2,1)S(1)} %get-tuple-element.227), channel_id=1, source_target_pairs={{0,24},{2,26},{4,28},{6,30},{8,0},{10,2},{12,4},{14,6},{16,8},{18,... | collective-permute-start | bytes 196616 | tf_op jit(solution)/shard_map/ppermute | solution.py:46
  265.3 22.9 %collective-permute-start.47 = (bf16[64,512]{1,0:T(8,128)(2,1)S(1)}, bf16[64,512]{1,0:T(8,128)(2,1)S(1)}, u32[]{:S(2)}, u32[]{:S(2)}) collective-permute-start(bf16[64,512]{1,0:T(8,128)(2,1)S(1)} %get-tuple-element.228), channel_id=1, source_target_pairs={{0,16},{2,18},{4,20},{6,22},{8,24},{10,26},{12,28},{14,30},{16,0},... | collective-permute-start | bytes 196616 | tf_op jit(solution)/shard_map/ppermute | solution.py:46
  266.5 21.7 %collective-permute-start.46 = (bf16[64,512]{1,0:T(8,128)(2,1)S(1)}, bf16[64,512]{1,0:T(8,128)(2,1)S(1)}, u32[]{:S(2)}, u32[]{:S(2)}) collective-permute-start(bf16[64,512]{1,0:T(8,128)(2,1)S(1)} %get-tuple-element.226), channel_id=1, source_target_pairs={{0,8},{2,10},{4,12},{6,14},{8,16},{10,18},{12,20},{14,22},{16,24},... | collective-permute-start | bytes 196616 | tf_op jit(solution)/shard_map/ppermute | solution.py:46
  271.8 12.2 %collective-permute-start.42 = (bf16[4,64,512]{2,1,0:T(8,128)(2,1)S(1)}, bf16[4,64,512]{2,1,0:T(8,128)(2,1)S(1)}, u32[]{:S(2)}, u32[]{:S(2)}) collective-permute-start(bf16[4,64,512]{2,1,0:T(8,128)(2,1)S(1)} %fusion.14), channel_id=1, source_target_pairs={{0,4},{2,6},{4,0},{6,2},{8,12},{10,14},{12,8},{14,10},{16,20},{18,... | collective-permute-start | bytes 786440 | tf_op jit(solution)/shard_map/ppermute | solution.py:46
  274.1 15.8 %collective-permute-start.38 = (bf16[96,1024]{1,0:T(8,128)(2,1)S(1)}, bf16[96,1024]{1,0:T(8,128)(2,1)S(1)}, u32[]{:S(2)}, u32[]{:S(2)}) collective-permute-start(bf16[96,1024]{1,0:T(8,128)(2,1)S(1)} %fusion.7), channel_id=1, source_target_pairs={{0,1},{1,0},{2,3},{3,2},{4,5},{5,4},{6,7},{7,6},{8,9},{9,8},{10,11... | collective-permute-start | bytes 589832 | tf_op jit(solution)/shard_map/ppermute | solution.py:58
  284.8 16.2 %all-to-all-start.2 = ((bf16[4,64,512]{2,1,0:T(8,128)(2,1)}), bf16[4,64,512]{2,1,0:T(8,128)(2,1)S(1)}, u32[]{:S(2)}, u32[]{:S(2)}) async-start(bf16[4,64,512]{2,1,0:T(8,128)(2,1)} %fusion.2), calls=%async_computation.2 | async-start | bytes 524288 | tf_op jit(solution)/shard_map/all_to_all | solution.py:911
  (56 other events, 609.5 us)
Sparse Core Ops, SparseCore 0:
  44.3 91.8 all-gather.1
  208.1 91.1 reduce-scatter.1
